TPU v7x, 128 devices: a whole 4x4x4 slice. The times are simulated.
128 devices in a mesh: rows: 16 (over x, z), rep: 8 (over y, core).
Axes of the slice: x: 4, y: 4, z: 4, core: 2. Of those that a mesh axis runs over, the one named last changes fastest.
Arguments:
- features: bfloat16 [131072, 256], P(('rows', 'rep')), may hold values from -6 to 6
- weight: bfloat16 [256, 256], replicated, may hold values from -0.375 to 0.375
- tile_values: bfloat16 [1024, 48, 128, 128], P(('rows', 'rep')), may hold values from -0.125 to 0.125
- tile_cols: int32 [1024, 48], P(('rows', 'rep')), may hold values from 0 to 1023, as said below
- tile_live: int32 [1024, 48], P(('rows', 'rep')), may hold values from 0 to 1, as said below
- cotangent: bfloat16 [131072, 256], P(('rows', 'rep')), may hold values from -6 to 6
Outputs:
- output: bfloat16 [131072, 256], P(('rows', 'rep'))
- feature_grad: bfloat16 [131072, 256], P(('rows', 'rep'))
- weight_grad: float32 [256, 256], replicated
Inputs may be any that keep to these rules, and one draw needn't show every extreme that they name: `tile_cols`: row tile t names only column tiles of node groups g - 1, g and g + 1 modulo 16, where g = t // 64 and group k holds column tiles k * 64 to (k + 1) * 64 - 1; a column tile may repeat. `tile_live`: the live slots of each row tile come first; every row tile has at least one; row tiles whose index is a multiple of 8 have all 48 live.
All inputs are finite; a program needn't handle non-finite values.
Results may differ from a plain program's by a relative error of at most 0.02.
Values may be sent and summed in bfloat16 or wider, within the bound.
No kernel may reach another device: no remote copies, remote signals or barrier semaphores. Data moves between devices by JAX's collectives and lax.ppermute only.
A program may use at most 192 MiB of HBM per device.

v0:
```python
import jax
import jax.numpy as jnp
from jax import lax
from jax.sharding import PartitionSpec as P


def extended(block, sides, width):
    for axis, dim in sides:
        count = lax.axis_size(axis)
        forward = [(i, i + 1) for i in range(count - 1)]
        forward.append((count - 1, 0))
        backward = [(target, source) for source, target in forward]
        low = lax.ppermute(
            lax.slice_in_dim(block, block.shape[dim] - width, None, axis=dim), axis, forward
        )
        high = lax.ppermute(lax.slice_in_dim(block, 0, width, axis=dim), axis, backward)
        block = jnp.concatenate([low, block, high], axis=dim)
    return block


def local(features, weight, tile_values, tile_cols, tile_live, cotangent):
    n_rows = lax.axis_size("rows")
    n_rep = lax.axis_size("rep")
    row_group = lax.axis_index("rows")
    node_dev, width = features.shape
    tile = tile_values.shape[2]
    group_nodes = node_dev * n_rep
    group_tiles = group_nodes // tile
    hidden = jnp.dot(features, weight, preferred_element_type=jnp.float32).astype(jnp.bfloat16)
    panel = lax.all_gather(hidden, "rep", axis=0, tiled=True)
    window = extended(panel, (("rows", 0),), group_nodes)
    win_tiles = window.reshape(3 * group_tiles, tile, width)
    col_group = tile_cols // group_tiles
    place = jnp.mod(col_group - row_group + 1, n_rows)
    win_index = place * group_tiles + tile_cols % group_tiles

    def forward_row(item):
        values, columns, live = item
        chosen = win_tiles[columns]
        masked = values * live.astype(jnp.bfloat16)[:, None, None]
        return jnp.einsum("sij,sjf->if", masked, chosen, preferred_element_type=jnp.float32)

    pre = lax.map(forward_row, (tile_values, win_index, tile_live)).reshape(node_dev, width)
    sig = jax.nn.sigmoid(pre)
    output = (pre * sig).astype(jnp.bfloat16)
    grad_pre = (cotangent.astype(jnp.float32) * sig * (1.0 + pre * (1.0 - sig))).astype(
        jnp.bfloat16
    )
    grad_tiles = grad_pre.reshape(node_dev // tile, tile, width)

    def backward_row(accum, item):
        values, columns, live, grads = item
        masked = values * live.astype(jnp.bfloat16)[:, None, None]
        contrib = jnp.einsum("sij,if->sjf", masked, grads, preferred_element_type=jnp.float32)
        return (accum.at[columns].add(contrib), None)

    start = jnp.zeros((3 * group_tiles, tile, width), jnp.float32)
    accum, _ = lax.scan(backward_row, start, (tile_values, win_index, tile_live, grad_tiles))
    accum = accum.reshape(3, group_nodes, width)
    outer = jnp.concatenate([accum[0], accum[2]], axis=0)
    spread = extended(outer.astype(jnp.bfloat16), (("rows", 0),), 2 * group_nodes).astype(
        outer.dtype
    )
    from_left = spread[group_nodes : 2 * group_nodes]
    from_right = spread[4 * group_nodes : 5 * group_nodes]
    total = accum[1] + from_left + from_right
    grad_sum = lax.psum_scatter(total.astype(jnp.bfloat16), "rep", scatter_dimension=0, tiled=True)
    feature_grad = jnp.dot(grad_sum, weight.T, preferred_element_type=jnp.float32).astype(
        jnp.bfloat16
    )
    weight_term = lax.dot_general(
        features, grad_sum, (((0,), (0,)), ((), ())), preferred_element_type=jnp.float32
    )
    weight_grad = lax.psum(weight_term, ("rows", "rep"))
    return (output, feature_grad, weight_grad)


def solution(mesh):
    placed = (
        P(("rows", "rep"), None),
        P(),
        P(("rows", "rep"), None, None, None),
        P(("rows", "rep"), None),
        P(("rows", "rep"), None),
        P(("rows", "rep"), None),
    )
    return jax.shard_map(
        local,
        mesh=mesh,
        in_specs=placed,
        out_specs=(P(("rows", "rep"), None), P(("rows", "rep"), None), P()),
        check_vma=False,
    )
```

profile of v0, /device:TPU:0, one launch (start us, length us, event | category | flops | bytes accessed | tf_op | source)
XLA Modules:
  0.0 893.5 jit_solution(14997732995010619561)
XLA Ops:
  10.3 34.7 %all-gather.2.cloned.1.call-done = bf16[8192,256]{1,0:T(8,128)(2,1)} async-done(((bf16[1024,256]{1,0:T(8,128)(2,1)}), bf16[8192,256]{1,0:T(8,128)(2,1)}) %all-gather.2.cloned.1.call-update) | async-done | bytes 4194320 | tf_op jit(solution)/shard_map/all_gather | solution.py:30
  50.8 89.8 %collective-permute-done.1 = bf16[8192,256]{1,0:T(8,128)(2,1)} collective-permute-done((bf16[8192,256]{1,0:T(8,128)(2,1)}, bf16[8192,256]{1,0:T(8,128)(2,1)}, u32[]{:S(2)}, u32[]{:S(2)}) %collective-permute-start.1) | collective-permute-done | bytes 4194336 | tf_op jit(solution)/shard_map/ppermute | solution.py:16
  146.1 15.4 %pad_maximum_fusion = bf16[24576,256]{1,0:T(8,128)(2,1)} fusion(bf16[8192,256]{1,0:T(8,128)(2,1)} %collective-permute-done.1, bf16[8192,256]{1,0:T(8,128)(2,1)} %all-gather.2.cloned.1.call-done, bf16[8192,256]{1,0:T(8,128)(2,1)} %collective-permute-done), kind=kLoop, calls=%fused_computation.32 | loop fusion | flops 37748736 | bytes 25165824 | tf_op jit(solution)/shard_map/concatenate | solution.py:17
  161.5 86.4 %while.20 = (s32[]{:T(128)}, f32[8,128,256]{2,1,0:T(8,128)S(1)}, bf16[8,48,128,128]{3,2,1,0:T(8,128)(2,1)}, s32[8,48]{1,0:T(8,128)}, s32[8,48]{1,0:T(8,128)S(1)}, /*index=5*/bf16[192,128,256]{2,1,0:T(8,128)(2,1)}, s32[]{:T(128)}) while((s32[]{:T(128)}, f32[8,128,256]{2,1,0:T(8,128)S(1)}, bf16[8,48,128,128]{3,2,1,0:T(8,128)(2,1)}, ...), condition=%wide.region_1.2_spmd, body=%wide.region_0.1_spmd.sunk | while | flops 403440832 | bytes 11147901 | solution.py:43
  162.3 7.1 gather_fusion
  173.1 7.1 gather_fusion
  194.7 7.1 gather_fusion
  205.5 7.1 gather_fusion
  249.2 11.5 %broadcast_in_dim.15 = f32[192,128,256]{2,1,0:T(8,128)} broadcast(f32[]{:T(128)} %constant.70.clone.1), dimensions={} | broadcast | bytes 25165828 | tf_op jit(solution)/shard_map/broadcast_in_dim | solution.py:57
  260.7 192.2 %while.21 = (s32[]{:T(128)}, f32[192,128,256]{2,1,0:T(8,128)}, s32[8,48]{1,0:T(8,128)S(1)}, bf16[8,48,128,128]{3,2,1,0:T(8,128)(2,1)}, s32[8,48]{1,0:T(8,128)}, /*index=5*/bf16[8,128,256]{2,1,0:T(8,128)(2,1)S(1)}, s32[]{:T(128)}) while((s32[]{:T(128)}, f32[192,128,256]{2,1,0:T(8,128)}, s32[8,48]{1,0:T(8,128)S(1)}, ...), condition=%wide.region_4.5_spmd, body=%wide.region_2.4_spmd.sunk | while | flops 405012672 | bytes 33097156 | solution.py:58
  269.8 15.0 %scatter_fusion = f32[192,128,256]{2,1,0:T(8,128)} fusion(f32[192,128,256]{2,1,0:T(8,128)} %get-tuple-element.209, s32[48]{0:T(128)S(1)} %fusion.59, f32[48,128,256]{2,1,0:T(8,128)} %fusion.61), kind=kCustom, calls=%fused_computation.1.clone.1 | custom fusion | flops 1572864 | bytes 18874560 | tf_op jit(solution)/shard_map/while/body/eval_jaxpr/scatter-add | solution.py:55
  293.9 14.8 %scatter_fusion = f32[192,128,256]{2,1,0:T(8,128)} fusion(f32[192,128,256]{2,1,0:T(8,128)} %get-tuple-element.209, s32[48]{0:T(128)S(1)} %fusion.59, f32[48,128,256]{2,1,0:T(8,128)} %fusion.61), kind=kCustom, calls=%fused_computation.1.clone.1 | custom fusion | flops 1572864 | bytes 18874560 | tf_op jit(solution)/shard_map/while/body/eval_jaxpr/scatter-add | solution.py:55
  317.8 14.9 %scatter_fusion = f32[192,128,256]{2,1,0:T(8,128)} fusion(f32[192,128,256]{2,1,0:T(8,128)} %get-tuple-element.209, s32[48]{0:T(128)S(1)} %fusion.59, f32[48,128,256]{2,1,0:T(8,128)} %fusion.61), kind=kCustom, calls=%fused_computation.1.clone.1 | custom fusion | flops 1572864 | bytes 18874560 | tf_op jit(solution)/shard_map/while/body/eval_jaxpr/scatter-add | solution.py:55
  341.8 14.9 %scatter_fusion = f32[192,128,256]{2,1,0:T(8,128)} fusion(f32[192,128,256]{2,1,0:T(8,128)} %get-tuple-element.209, s32[48]{0:T(128)S(1)} %fusion.59, f32[48,128,256]{2,1,0:T(8,128)} %fusion.61), kind=kCustom, calls=%fused_computation.1.clone.1 | custom fusion | flops 1572864 | bytes 18874560 | tf_op jit(solution)/shard_map/while/body/eval_jaxpr/scatter-add | solution.py:55
  365.8 14.9 %scatter_fusion = f32[192,128,256]{2,1,0:T(8,128)} fusion(f32[192,128,256]{2,1,0:T(8,128)} %get-tuple-element.209, s32[48]{0:T(128)S(1)} %fusion.59, f32[48,128,256]{2,1,0:T(8,128)} %fusion.61), kind=kCustom, calls=%fused_computation.1.clone.1 | custom fusion | flops 1572864 | bytes 18874560 | tf_op jit(solution)/shard_map/while/body/eval_jaxpr/scatter-add | solution.py:55
  389.8 14.9 %scatter_fusion = f32[192,128,256]{2,1,0:T(8,128)} fusion(f32[192,128,256]{2,1,0:T(8,128)} %get-tuple-element.209, s32[48]{0:T(128)S(1)} %fusion.59, f32[48,128,256]{2,1,0:T(8,128)} %fusion.61), kind=kCustom, calls=%fused_computation.1.clone.1 | custom fusion | flops 1572864 | bytes 18874560 | tf_op jit(solution)/shard_map/while/body/eval_jaxpr/scatter-add | solution.py:55
  413.8 14.9 %scatter_fusion = f32[192,128,256]{2,1,0:T(8,128)} fusion(f32[192,128,256]{2,1,0:T(8,128)} %get-tuple-element.209, s32[48]{0:T(128)S(1)} %fusion.59, f32[48,128,256]{2,1,0:T(8,128)} %fusion.61), kind=kCustom, calls=%fused_computation.1.clone.1 | custom fusion | flops 1572864 | bytes 18874560 | tf_op jit(solution)/shard_map/while/body/eval_jaxpr/scatter-add | solution.py:55
  437.8 15.0 %scatter_fusion = f32[192,128,256]{2,1,0:T(8,128)} fusion(f32[192,128,256]{2,1,0:T(8,128)} %get-tuple-element.209, s32[48]{0:T(128)S(1)} %fusion.59, f32[48,128,256]{2,1,0:T(8,128)} %fusion.61), kind=kCustom, calls=%fused_computation.1.clone.1 | custom fusion | flops 1572864 | bytes 18874560 | tf_op jit(solution)/shard_map/while/body/eval_jaxpr/scatter-add | solution.py:55
  452.8 9.2 %convert.8 = bf16[192,128,256]{2,1,0:T(8,128)(2,1)S(1)} convert(f32[192,128,256]{2,1,0:T(8,128)} %get-tuple-element.68) | non-fusion elementwise | flops 6291456 | bytes 37748736 | tf_op jit(solution)/shard_map/convert.5
  462.6 25.0 %pad_maximum_fusion.1 = bf16[16384,256]{1,0:T(8,128)(2,1)} fusion(bf16[8192,256]{1,0:T(8,128)(2,1)S(1)} %bitcast.101, bf16[8192,256]{1,0:T(8,128)(2,1)S(1)} %bitcast.99), kind=kLoop, calls=%fused_computation.36 | loop fusion | flops 16777216 | bytes 16777216 | tf_op jit(solution)/shard_map/concatenate | solution.py:60
  493.6 176.1 %collective-permute-done.3 = bf16[16384,256]{1,0:T(8,128)(2,1)} collective-permute-done((bf16[16384,256]{1,0:T(8,128)(2,1)}, bf16[16384,256]{1,0:T(8,128)(2,1)}, u32[]{:S(2)}, u32[]{:S(2)}) %collective-permute-start.3) | collective-permute-done | bytes 8388640 | tf_op jit(solution)/shard_map/ppermute | solution.py:16
  673.2 32.8 %fusion.22 = bf16[8192,256]{1,0:T(8,128)(2,1)} fusion(f32[64,128,256]{2,1,0:T(8,128)S(1)} %slice.20, bf16[16384,256]{1,0:T(8,128)(2,1)} %collective-permute-done.3, bf16[8192,256]{1,0:T(8,128)(2,1)S(1)} %bitcast.102, bf16[8192,256]{1,0:T(8,128)(2,1)S(1)} %bitcast.100, bf16[16384,256]{1,0:T(8,128)(2,1)} %collective-permute-done.2), kind=kLoop, calls=%fused_computation.35 | loop fusion | flops 39845888 | bytes 37748736 | tf_op jit(solution)/shard_map/convert_element_type | solution.py:67
  706.1 32.9 %reduce-scatter.2.cloned.1.call-done = bf16[1024,256]{1,0:T(8,128)(2,1)} async-done(((bf16[8192,256]{1,0:T(8,128)(2,1)}), bf16[1024,256]{1,0:T(8,128)(2,1)}) %reduce-scatter.2.cloned.1.call-update) | async-done | bytes 524304 | tf_op jit(solution)/shard_map/reduce_scatter | solution.py:67
  743.3 141.9 %all-reduce.2.cloned.1.call-done = f32[256,256]{0,1:T(8,128)} async-done(((f32[256,256]{0,1:T(8,128)}), f32[256,256]{0,1:T(8,128)}) %all-reduce.2.cloned.1.call-update) | async-done | bytes 262160 | tf_op jit(solution)/shard_map/psum | solution.py:74
  (103 shorter events, 162.5 us)
Async XLA Ops:
  7.2 1.0 copy-start
  7.2 37.8 %all-gather.2.cloned.1.call-start = ((), (), s32[]{:S(2)}) async-start(), calls=%async_computation.1 | async-start | bytes 4718592 | tf_op jit(solution)/shard_map/all_gather | solution.py:30
  10.2 728.8 %reduce-scatter.2.cloned.1.call-start = ((), (), s32[]{:S(2)}) async-start(), calls=%async_computation.2 | async-start | bytes 4718592 | tf_op jit(solution)/shard_map/reduce_scatter | solution.py:67
  45.0 95.6 %collective-permute-start.1 = (bf16[8192,256]{1,0:T(8,128)(2,1)}, bf16[8192,256]{1,0:T(8,128)(2,1)}, u32[]{:S(2)}, u32[]{:S(2)}) collective-permute-start(bf16[8192,256]{1,0:T(8,128)(2,1)} %all-gather.2.cloned.1.call-done), channel_id=1, source_target_pairs={{8,0},{16,8},{24,16},{32,24},{40,32},{48,40},{56,48},{64,56},{72,6... | collective-permute-start | bytes 12582920 | tf_op jit(solution)/shard_map/ppermute | solution.py:16
  50.0 96.1 %collective-permute-start = (bf16[8192,256]{1,0:T(8,128)(2,1)}, bf16[8192,256]{1,0:T(8,128)(2,1)}, u32[]{:S(2)}, u32[]{:S(2)}) collective-permute-start(bf16[8192,256]{1,0:T(8,128)(2,1)} %all-gather.2.cloned.1.call-done), channel_id=1, source_target_pairs={{0,8},{8,16},{16,24},{24,32},{32,40},{40,48},{48,56},{56,64},{64,7... | collective-permute-start | bytes 12582920 | tf_op jit(solution)/shard_map/ppermute | solution.py:13
  161.5 86.4 %copy-start.1 = (bf16[1024,256]{1,0:T(8,128)(2,1)S(1)}, bf16[1024,256]{1,0:T(8,128)(2,1)}, u32[]{:S(2)}) copy-start(bf16[1024,256]{1,0:T(8,128)(2,1)} %param.15) | copy-start | bytes 1572868
  487.6 182.1 %collective-permute-start.3 = (bf16[16384,256]{1,0:T(8,128)(2,1)}, bf16[16384,256]{1,0:T(8,128)(2,1)}, u32[]{:S(2)}, u32[]{:S(2)}) collective-permute-start(bf16[16384,256]{1,0:T(8,128)(2,1)} %pad_maximum_fusion.1), channel_id=1, source_target_pairs={{8,0},{16,8},{24,16},{32,24},{40,32},{48,40},{56,48},{64,56},{72,6... | collective-permute-start | bytes 25165832 | tf_op jit(solution)/shard_map/ppermute | solution.py:16
  488.0 185.2 %collective-permute-start.2 = (bf16[16384,256]{1,0:T(8,128)(2,1)}, bf16[16384,256]{1,0:T(8,128)(2,1)}, u32[]{:S(2)}, u32[]{:S(2)}) collective-permute-start(bf16[16384,256]{1,0:T(8,128)(2,1)} %pad_maximum_fusion.1), channel_id=1, source_target_pairs={{0,8},{8,16},{16,24},{24,32},{32,40},{40,48},{48,56},{56,64},{64,7... | collective-permute-start | bytes 25165832 | tf_op jit(solution)/shard_map/ppermute | solution.py:13
  493.6 247.5 %copy-start.2 = (bf16[256,256]{1,0:T(8,128)(2,1)S(1)}, bf16[256,256]{1,0:T(8,128)(2,1)}, u32[]{:S(2)}) copy-start(bf16[256,256]{1,0:T(8,128)(2,1)} %param.11) | copy-start | bytes 393220
  706.1 179.1 %all-reduce.2.cloned.1.call-start = ((), (), s32[]{:S(2)}) async-start(), calls=%async_computation.3 | async-start | bytes 524288 | tf_op jit(solution)/shard_map/psum | solution.py:74
Sparse Core Ops, SparseCore 0:
  10.4 34.5 all-gather.1
  706.2 32.7 reduce-scatter.1
  744.3 140.8 all-reduce.1
where the time goes:
time: 896 us; the launch traced here: 894 us
  waiting for transfers between devices  485 us (54%)
  other arithmetic  215 us (24%)
  local copies, waits for them, and re-layouts  113 us (13%)
  matrix products  59.9 us (7%)
  between operations  13.8 us (2%)
    ppermute x2, waiting for transfers between devices, extended(): lax.ppermute(lax.slice_in_dim(block, 0, width, axis=dim), axis, backward)  266 us
    psum x1, waiting for transfers between devices, local(): weight_grad = lax.psum(weight_term, ('rows', 'rep'))  142 us
    scatter-add x8, other arithmetic, backward_row(): return (accum.at[columns].add(contrib), None)  119 us
    gather x8, local copies, waits for them, and re-layouts, forward_row(): chosen = win_tiles[columns]  56.5 us
    dynamic_slice x16, local copies, waits for them, and re-layouts, local(): lax.map(forward_row, (tile_values, win_index, tile_live))  37.5 us
    all_gather x1, waiting for transfers between devices, local(): panel = lax.all_gather(hidden, 'rep', axis=0, tiled=True)  34.7 us
    reduce_scatter x1, waiting for transfers between devices, local(): lax.psum_scatter(total.astype(jnp.bfloat16), 'rep', scatter_dimension=0,...  32.9 us
    convert_element_type x1, other arithmetic, local(): total.astype(jnp.bfloat16)  32.8 us
  transfers between devices with their start and end apart: 7, of which 7 were waited for; matrix products, arithmetic and copies ran while one was open for 1% of the time, Pallas kernels for 0%

commit v1 on v0

v1 whole, which is shorter than its diff:
```python
import jax, jax.numpy as jnp
from jax import lax
from jax.experimental import pallas as pl
from jax.experimental.pallas import tpu as pltpu
from jax.sharding import PartitionSpec as P

bf16, f32 = jnp.bfloat16, jnp.float32
U = 4

def pairs(a_ref, t_n, k0):
    tiles = []
    for u in range(U):
        a = a_ref[0, k0 + u]
        tiles.append(jnp.where(k0 + u < t_n, a, jnp.zeros_like(a)))
    return [jnp.concatenate(tiles[u:u+2], axis=1) for u in range(0, U, 2)]

def kernel(idx, cnt, a_ref, win_ref, w_ref, cot_ref, out_ref, wg_ref, grad_hbm, acc, stage, sem):
    t = pl.program_id(0)
    nt = pl.num_programs(0)
    n_win = acc.shape[0]
    @pl.when(t == 0)
    def _():
        wg_ref[...] = jnp.zeros_like(wg_ref)
        def zero(i, _):
            acc[i] = jnp.zeros(acc.shape[1:], f32)
            return 0
        lax.fori_loop(0, n_win, zero, 0)
    n = cnt[t]
    trips = (n + U - 1) // U
    def fwd(i, af):
        k0 = i * U
        for p, a in enumerate(pairs(a_ref, n, k0)):
            w = jnp.concatenate([win_ref[pl.ds(pl.multiple_of(idx[t, k0 + 2*p + u] * 128, 128), 128), :] for u in range(2)], axis=0)
            af = af + jnp.dot(a, w, preferred_element_type=f32)
        return af
    af = lax.fori_loop(0, trips, fwd, jnp.zeros((128, 256), f32))
    afb = af.astype(bf16)
    pre = jnp.dot(afb, w_ref[...], preferred_element_type=f32)
    sig = jax.nn.sigmoid(pre)
    out_ref[...] = (pre * sig).astype(bf16)
    g = (cot_ref[...].astype(f32) * sig * (1.0 + pre * (1.0 - sig))).astype(bf16)
    wg_ref[...] += lax.dot_general(afb, g, (((0,), (0,)), ((), ())), preferred_element_type=f32)
    gwt = lax.dot_general(w_ref[...], g, (((1,), (1,)), ((), ())), preferred_element_type=f32).astype(bf16)
    def bwd(i, _):
        k0 = i * U
        for p, a in enumerate(pairs(a_ref, n, k0)):
            r = jnp.dot(gwt, a, preferred_element_type=f32)
            for u in range(2):
                c = idx[t, k0 + 2*p + u]
                acc[c] += r[:, u*128:(u+1)*128]
        return 0
    lax.fori_loop(0, trips, bwd, 0)
    @pl.when(t == nt - 1)
    def _():
        per = stage.shape[1]
        steps = n_win // per
        def copy(i):
            return pltpu.make_async_copy(stage.at[i % 2], grad_hbm.at[pl.ds(i * per, per)], sem.at[i % 2])
        def emit(i, _):
            @pl.when(i >= 2)
            def _():
                copy(i - 2).wait()
            stage[i % 2] = acc[pl.ds(i * per, per)].astype(bf16)
            copy(i).start()
            return 0
        lax.fori_loop(0, steps, emit, 0)
        copy(steps - 2).wait()
        copy(steps - 1).wait()

def layer(idx, cnt, tile_values, win, weight, cotangent):
    nt, slots, tile, _ = tile_values.shape
    width = weight.shape[0]
    n_win = win.shape[0] // tile
    whole = lambda *s: pl.BlockSpec(s, lambda t, *_: (0,) * len(s), pipeline_mode=pl.Buffered(1))
    return pl.pallas_call(
        kernel,
        grid_spec=pltpu.PrefetchScalarGridSpec(
            num_scalar_prefetch=2, grid=(nt,),
            in_specs=[pl.BlockSpec((1, slots, tile, tile), lambda t, *_: (t, 0, 0, 0)),
                      whole(*win.shape), whole(width, width),
                      pl.BlockSpec((tile, width), lambda t, *_: (t, 0))],
            out_specs=[pl.BlockSpec((tile, width), lambda t, *_: (t, 0)),
                       pl.BlockSpec((width, width), lambda t, *_: (0, 0)),
                       pl.BlockSpec(memory_space=pl.ANY)],
            scratch_shapes=[pltpu.VMEM((n_win, width, tile), f32), pltpu.VMEM((2, 8, width, tile), bf16), pltpu.SemaphoreType.DMA((2,))]),
        out_shape=[jax.ShapeDtypeStruct((nt*tile, width), bf16), jax.ShapeDtypeStruct((width, width), f32),
                   jax.ShapeDtypeStruct((n_win, width, tile), bf16)],
        compiler_params=pltpu.CompilerParams(vmem_limit_bytes=60*2**20),
    )(idx, cnt, tile_values, win, weight, cotangent)


def ring(count, step):
    return [(i, (i + step) % count) for i in range(count)]


def weight_sum(term, n_rows, n_rep):
    rep = lax.axis_index("rep")
    height = term.shape[0] // n_rep
    pieces = term.reshape(n_rep, height, term.shape[1])

    def piece(at):
        return lax.dynamic_index_in_dim(pieces, jnp.mod(at, n_rep), 0, keepdims=False)

    own = piece(rep)
    for step in range(1, n_rep):
        own = own + lax.ppermute(piece(rep + step), "rep", ring(n_rep, step))
    part = 4
    for inner in (True, False):
        got = own
        for step in range(1, part):
            if inner:
                route = [(r, r // part * part + (r % part + step) % part) for r in range(n_rows)]
            else:
                route = [(r, (r + step * part) % n_rows) for r in range(n_rows)]
            got = got + lax.ppermute(own, "rows", route)
        own = got
    blocks = jnp.zeros_like(pieces)
    blocks = lax.dynamic_update_index_in_dim(blocks, own, rep, 0)
    for step in range(1, n_rep):
        got = lax.ppermute(own, "rep", ring(n_rep, step))
        blocks = lax.dynamic_update_index_in_dim(blocks, got, jnp.mod(rep - step, n_rep), 0)
    return blocks.reshape(term.shape)


def local(features, weight, tile_values, tile_cols, tile_live, cotangent):
    n_rows = lax.axis_size("rows")
    n_rep = lax.axis_size("rep")
    row_group = lax.axis_index("rows")
    node_dev, width = features.shape
    tile = tile_values.shape[2]
    own_tiles = node_dev // tile
    group_tiles = own_tiles * n_rep
    place = jnp.mod(tile_cols // group_tiles - row_group + 1, n_rows)
    inner = tile_cols % group_tiles
    idx = ((inner // own_tiles) * 3 + place) * own_tiles + inner % own_tiles
    cnt = jnp.sum(tile_live, axis=1)
    low = lax.ppermute(features, "rows", ring(n_rows, 1))
    high = lax.ppermute(features, "rows", ring(n_rows, -1))
    win = lax.all_gather(jnp.concatenate([low, features, high]), "rep", axis=0, tiled=True)
    output, term, grads = layer(idx, cnt, tile_values, win, weight, cotangent)
    weight_grad = weight_sum(term, n_rows, n_rep)
    grads = lax.psum_scatter(grads, "rep", scatter_dimension=0, tiled=True)
    down, mid, up = (grads[i * own_tiles : (i + 1) * own_tiles] for i in range(3))
    from_high = lax.ppermute(down, "rows", ring(n_rows, -1))
    from_low = lax.ppermute(up, "rows", ring(n_rows, 1))
    total = mid.astype(f32) + from_high.astype(f32) + from_low.astype(f32)
    feature_grad = jnp.swapaxes(total, 1, 2).reshape(node_dev, width).astype(bf16)
    return (output, feature_grad, weight_grad)


def solution(mesh):
    placed = (
        P(("rows", "rep"), None),
        P(),
        P(("rows", "rep"), None, None, None),
        P(("rows", "rep"), None),
        P(("rows", "rep"), None),
        P(("rows", "rep"), None),
    )
    return jax.shard_map(
        local,
        mesh=mesh,
        in_specs=placed,
        out_specs=(P(("rows", "rep"), None), P(("rows", "rep"), None), P()),
        check_vma=False,
    )
```

time: 896 us -> 253 us (0.28)
  waiting for transfers between devices: 485 us -> 140 us
  other arithmetic: 215 us -> 4.84 us
  local copies, waits for them, and re-layouts: 113 us -> 3.2 us
  matrix products: 59.9 us -> 0 us
  starting transfers between devices: 7.22 us -> 51.3 us
  Pallas kernels: 0 us -> 39.8 us
    ppermute x4 -> x24, waiting for transfers between devices: 275 us -> 41.8 us  [the longest x1 11.5 us: local(): high = lax.ppermute(features, 'rows', ring(n_rows, -1))]
    psum x1 -> x0, waiting for transfers between devices: 142 us -> none  [local(): weight_grad = lax.psum(weight_term, ('rows', 'rep'))]
    scatter-add x8 -> x0, other arithmetic: 119 us -> none  [backward_row(): return (accum.at[columns].add(contrib), None)]
    dot_general x19 -> x0, matrix products: 59.9 us -> none  [the longest x8 29.7 us: backward_row(): jnp.einsum('sij,if->sjf', masked, grads, preferred_element_type=jnp.float32)]
    gather x8 -> x0, local copies, waits for them, and re-layouts: 56.5 us -> none  [forward_row(): chosen = win_tiles[columns]]
    ppermute x4 -> x24, starting transfers between devices: 7.1 us -> 51.3 us  [the longest x7 18 us: weight_sum(): own = own + lax.ppermute(piece(rep + step), 'rep', ring(n_rep, step))]
    convert_element_type x18 -> x1, other arithmetic: 45.3 us -> 1.25 us  [local(): jnp.swapaxes(total, 1, 2).reshape(node_dev, width).astype(bf16)]
    pallas_call x0 -> x1, Pallas kernels: none -> 39.8 us  [layer(): pl.pallas_call(kernel, grid_spec=pltpu.PrefetchScalarGridSpec(num_scalar_...]
  transfers between devices with their start and end apart: 7 -> 26, of which waited for: 7 -> 14; matrix products, arithmetic and copies ran while one was open for 1% -> 1% of each run, Pallas kernels for 0% -> 0%
where the time goes in v1:
time: 253 us
  waiting for transfers between devices  140 us (55%)
  starting transfers between devices  51.3 us (20%)
  Pallas kernels  39.8 us (16%)
  between operations  14.4 us (6%)
  other arithmetic  4.84 us (2%)
  local copies, waits for them, and re-layouts  3.2 us (1%)
    all_gather x1, waiting for transfers between devices, local(): lax.all_gather(jnp.concatenate([low, features, high]), 'rep', axis=0, til...  62.6 us
    pallas_call x1, Pallas kernels, layer(): pl.pallas_call(kernel, grid_spec=pltpu.PrefetchScalarGridSpec(num_scalar_...  39.8 us
    reduce_scatter x1, waiting for transfers between devices, local(): grads = lax.psum_scatter(grads, 'rep', scatter_dimension=0, tiled=True)  35.2 us
    ppermute x7, starting transfers between devices, weight_sum(): own = own + lax.ppermute(piece(rep + step), 'rep', ring(n_rep, step))  18 us
    ppermute x6, starting transfers between devices, weight_sum(): got = got + lax.ppermute(own, 'rows', route)  14.6 us
    ppermute x1, waiting for transfers between devices, local(): high = lax.ppermute(features, 'rows', ring(n_rows, -1))  11.5 us
    ppermute x1, waiting for transfers between devices, local(): from_low = lax.ppermute(up, 'rows', ring(n_rows, 1))  11 us
    ppermute x6, waiting for transfers between devices, weight_sum(): got = got + lax.ppermute(own, 'rows', route)  8.33 us
  transfers between devices with their start and end apart: 26, of which 14 were waited for; matrix products, arithmetic and copies ran while one was open for 1% of the time, Pallas kernels for 0%

profile of v1, /device:TPU:0, one launch (start us, length us, event | category | flops | bytes accessed | tf_op | source)
XLA Modules:
  0.0 253.3 jit_solution(12748418167856391340)
XLA Ops:
  7.2 6.4 %collective-permute-start.1 = (bf16[1024,256]{1,0:T(8,128)(2,1)}, bf16[1024,256]{1,0:T(8,128)(2,1)S(1)}, u32[]{:S(2)}, u32[]{:S(2)}) collective-permute-start(bf16[1024,256]{1,0:T(8,128)(2,1)} %param.6), channel_id=1, source_target_pairs={{0,120},{8,0},{16,8},{24,16},{32,24},{40,32},{48,40},{56,48},{64,5... | collective-permute-start | bytes 1572872 | tf_op jit(solution)/shard_map/ppermute | solution.py:138
  13.6 11.5 %collective-permute-done.1 = bf16[1024,256]{1,0:T(8,128)(2,1)S(1)} collective-permute-done((bf16[1024,256]{1,0:T(8,128)(2,1)}, bf16[1024,256]{1,0:T(8,128)(2,1)S(1)}, u32[]{:S(2)}, u32[]{:S(2)}) %collective-permute-start.1) | collective-permute-done | bytes 524320 | tf_op jit(solution)/shard_map/ppermute | solution.py:138
  25.1 5.4 %collective-permute-done = bf16[1024,256]{1,0:T(8,128)(2,1)S(1)} collective-permute-done((bf16[1024,256]{1,0:T(8,128)(2,1)}, bf16[1024,256]{1,0:T(8,128)(2,1)S(1)}, u32[]{:S(2)}, u32[]{:S(2)}) %collective-permute-start) | collective-permute-done | bytes 524320 | tf_op jit(solution)/shard_map/ppermute | solution.py:137
  30.5 2.3 pad_maximum_fusion
  34.2 62.6 %all-gather.2.cloned.1.call-done.win_ref = bf16[24576,256]{1,0:T(8,128)(2,1)} async-done(((bf16[3072,256]{1,0:T(8,128)(2,1)}), bf16[24576,256]{1,0:T(8,128)(2,1)}) %all-gather.2.cloned.1.call-update) | async-done | bytes 12582928 | tf_op jit(solution)/shard_map/all_gather | solution.py:139
  96.8 39.8 %shard_map.85 = (bf16[1024,256]{1,0:T(8,128)(2,1)}, f32[256,256]{1,0:T(8,128)}, bf16[192,256,128]{2,1,0:T(8,128)(2,1)}) custom-call(s32[8,48]{1,0:T(8,128)} %fusion.10.idx, s32[8]{0:T(128)} %reduce_sum.9.cnt, bf16[8,48,128,128]{3,2,1,0:T(8,128)(2,1)} %a_ref.1, bf16[24576,256]{1,0:T(8,128)(2,1)} %all-gather.2.cloned.1.call-done.win_ref, ...), custom_call_target="tpu_custom_call" | custom-call | tf_op jit(solution)/shard_map/pallas_call | solution.py:75
  137.6 2.1 collective-permute-start.10
  139.7 11.9 %collective-permute-start.9 = (f32[32,256]{1,0:T(8,128)S(1)}, f32[32,256]{1,0:T(8,128)S(1)}, u32[]{:S(2)}, u32[]{:S(2)}) collective-permute-start(f32[32,256]{1,0:T(8,128)S(1)} %get-tuple-element.15), channel_id=1, source_target_pairs={{0,6},{1,7},{2,0},{3,1},{4,2},{5,3},{6,4},{7,5},{8,14},{9,15},{10,... | collective-permute-start | bytes 98312 | tf_op jit(solution)/shard_map/ppermute | solution.py:106
  151.5 1.7 collective-permute-start.6
  155.6 1.4 collective-permute-done.7
  157.0 1.4 collective-permute-done.5
  159.7 5.0 %collective-permute-start.13 = (f32[32,256]{1,0:T(8,128)S(1)}, f32[32,256]{1,0:T(8,128)S(1)}, u32[]{:S(2)}, u32[]{:S(2)}) collective-permute-start(f32[32,256]{1,0:T(8,128)S(1)} %fusion.6), channel_id=1, source_target_pairs={{0,24},{8,0},{16,8},{24,16},{32,56},{40,32},{48,40},{56,48},{64,88... | collective-permute-start | bytes 98312 | tf_op jit(solution)/shard_map/ppermute | solution.py:115
  166.3 3.9 %collective-permute-done.12 = f32[32,256]{1,0:T(8,128)S(1)} collective-permute-done((f32[32,256]{1,0:T(8,128)S(1)}, f32[32,256]{1,0:T(8,128)S(1)}, u32[]{:S(2)}, u32[]{:S(2)}) %collective-permute-start.12) | collective-permute-done | bytes 32800 | tf_op jit(solution)/shard_map/ppermute | solution.py:115
  170.2 5.4 %collective-permute-start.16 = (f32[32,256]{1,0:T(8,128)S(1)}, f32[32,256]{1,0:T(8,128)S(1)}, u32[]{:S(2)}, u32[]{:S(2)}) collective-permute-start(f32[32,256]{1,0:T(8,128)S(1)} %add_add_fusion.1), channel_id=1, source_target_pairs={{0,96},{8,104},{16,112},{24,120},{32,0},{40,8},{48,16},{56,24},{64... | collective-permute-start | bytes 98312 | tf_op jit(solution)/shard_map/ppermute | solution.py:115
  175.6 2.0 collective-permute-start.15
  178.9 2.1 collective-permute-done.15
  181.0 1.7 collective-permute-done.14
  183.0 2.1 collective-permute-start.19
  185.1 2.1 collective-permute-start.20
  187.2 1.7 collective-permute-start.21
  191.3 35.2 %reduce-scatter.2.cloned.1.call-done = bf16[24,256,128]{2,1,0:T(8,128)(2,1)} async-done(((bf16[192,256,128]{2,1,0:T(8,128)(2,1)}), bf16[24,256,128]{2,1,0:T(8,128)(2,1)}) %reduce-scatter.2.cloned.1.call-update) | async-done | bytes 1572880 | tf_op jit(solution)/shard_map/reduce_scatter | solution.py:142
  227.7 1.6 collective-permute-start.3
  229.4 3.8 %collective-permute-start.2 = (bf16[8,256,128]{2,1,0:T(8,128)(2,1)S(1)}, bf16[8,256,128]{2,1,0:T(8,128)(2,1)S(1)}, u32[]{:S(2)}, u32[]{:S(2)}) collective-permute-start(bf16[8,256,128]{2,1,0:T(8,128)(2,1)S(1)} %get-tuple-element.11), channel_id=1, source_target_pairs={{0,120},{8,0},{16,8},{24,16},{32,24},{40,32},{48,40},{56,48},{64,5... | collective-permute-start | bytes 1572872 | tf_op jit(solution)/shard_map/ppermute | solution.py:144
  233.2 11.0 %collective-permute-done.3 = bf16[8,256,128]{2,1,0:T(8,128)(2,1)S(1)} collective-permute-done((bf16[8,256,128]{2,1,0:T(8,128)(2,1)S(1)}, bf16[8,256,128]{2,1,0:T(8,128)(2,1)S(1)}, u32[]{:S(2)}, u32[]{:S(2)}) %collective-permute-start.3) | collective-permute-done | bytes 524320 | tf_op jit(solution)/shard_map/ppermute | solution.py:145
  (57 shorter events, 14.8 us)
Async XLA Ops:
  7.2 89.6 %all-gather.2.cloned.1.call-start = ((), (), s32[]{:S(2)}) async-start(), calls=%async_computation.1 | async-start | bytes 14155776 | tf_op jit(solution)/shard_map/all_gather | solution.py:139
  7.2 17.9 %collective-permute-start.1 = (bf16[1024,256]{1,0:T(8,128)(2,1)}, bf16[1024,256]{1,0:T(8,128)(2,1)S(1)}, u32[]{:S(2)}, u32[]{:S(2)}) collective-permute-start(bf16[1024,256]{1,0:T(8,128)(2,1)} %param.6), channel_id=1, source_target_pairs={{0,120},{8,0},{16,8},{24,16},{32,24},{40,32},{48,40},{56,48},{64,5... | collective-permute-start | bytes 1572872 | tf_op jit(solution)/shard_map/ppermute | solution.py:138
  13.6 16.9 %collective-permute-start = (bf16[1024,256]{1,0:T(8,128)(2,1)}, bf16[1024,256]{1,0:T(8,128)(2,1)S(1)}, u32[]{:S(2)}, u32[]{:S(2)}) collective-permute-start(bf16[1024,256]{1,0:T(8,128)(2,1)} %param.6), channel_id=1, source_target_pairs={{0,8},{8,16},{16,24},{24,32},{32,40},{40,48},{48,56},{56,64},{64,7... | collective-permute-start | bytes 1572872 | tf_op jit(solution)/shard_map/ppermute | solution.py:137
  32.8 193.6 %reduce-scatter.2.cloned.1.call-start = ((), (), s32[]{:S(2)}) async-start(), calls=%async_computation.2 | async-start | bytes 14155776 | tf_op jit(solution)/shard_map/reduce_scatter | solution.py:142
  137.6 15.7 %collective-permute-start.10 = (f32[32,256]{1,0:T(8,128)S(1)}, f32[32,256]{1,0:T(8,128)S(1)}, u32[]{:S(2)}, u32[]{:S(2)}) collective-permute-start(f32[32,256]{1,0:T(8,128)S(1)} %get-tuple-element.14), channel_id=1, source_target_pairs={{0,7},{1,0},{2,1},{3,2},{4,3},{5,4},{6,5},{7,6},{8,15},{9,8},{10,9... | collective-permute-start | bytes 98312 | tf_op jit(solution)/shard_map/ppermute | solution.py:106
  139.7 14.8 %collective-permute-start.9 = (f32[32,256]{1,0:T(8,128)S(1)}, f32[32,256]{1,0:T(8,128)S(1)}, u32[]{:S(2)}, u32[]{:S(2)}) collective-permute-start(f32[32,256]{1,0:T(8,128)S(1)} %get-tuple-element.15), channel_id=1, source_target_pairs={{0,6},{1,7},{2,0},{3,1},{4,2},{5,3},{6,4},{7,5},{8,14},{9,15},{10,... | collective-permute-start | bytes 98312 | tf_op jit(solution)/shard_map/ppermute | solution.py:106
  151.5 5.5 %collective-permute-start.7 = (f32[32,256]{1,0:T(8,128)S(1)}, f32[32,256]{1,0:T(8,128)S(1)}, u32[]{:S(2)}, u32[]{:S(2)}) collective-permute-start(f32[32,256]{1,0:T(8,128)S(1)} %get-tuple-element.17), channel_id=1, source_target_pairs={{0,4},{1,5},{2,6},{3,7},{4,0},{5,1},{6,2},{7,3},{8,12},{9,13},{10,... | collective-permute-start | bytes 98312 | tf_op jit(solution)/shard_map/ppermute | solution.py:106
  151.5 5.5 %collective-permute-start.6 = (f32[32,256]{1,0:T(8,128)S(1)}, f32[32,256]{1,0:T(8,128)S(1)}, u32[]{:S(2)}, u32[]{:S(2)}) collective-permute-start(f32[32,256]{1,0:T(8,128)S(1)} %get-tuple-element.18), channel_id=1, source_target_pairs={{0,3},{1,4},{2,5},{3,6},{4,7},{5,0},{6,1},{7,2},{8,11},{9,12},{10,... | collective-permute-start | bytes 98312 | tf_op jit(solution)/shard_map/ppermute | solution.py:106
  153.3 5.1 %collective-permute-start.5 = (f32[32,256]{1,0:T(8,128)S(1)}, f32[32,256]{1,0:T(8,128)S(1)}, u32[]{:S(2)}, u32[]{:S(2)}) collective-permute-start(f32[32,256]{1,0:T(8,128)S(1)} %get-tuple-element.19), channel_id=1, source_target_pairs={{0,2},{1,3},{2,4},{3,5},{4,6},{5,7},{6,0},{7,1},{8,10},{9,11},{10,... | collective-permute-start | bytes 98312 | tf_op jit(solution)/shard_map/ppermute | solution.py:106
  154.5 5.2 %collective-permute-start.4 = (f32[32,256]{1,0:T(8,128)S(1)}, f32[32,256]{1,0:T(8,128)S(1)}, u32[]{:S(2)}, u32[]{:S(2)}) collective-permute-start(f32[32,256]{1,0:T(8,128)S(1)} %get-tuple-element.13), channel_id=1, source_target_pairs={{0,1},{1,2},{2,3},{3,4},{4,5},{5,6},{6,7},{7,0},{8,9},{9,10},{10,1... | collective-permute-start | bytes 98312 | tf_op jit(solution)/shard_map/ppermute | solution.py:106
  159.7 6.6 %collective-permute-start.13 = (f32[32,256]{1,0:T(8,128)S(1)}, f32[32,256]{1,0:T(8,128)S(1)}, u32[]{:S(2)}, u32[]{:S(2)}) collective-permute-start(f32[32,256]{1,0:T(8,128)S(1)} %fusion.6), channel_id=1, source_target_pairs={{0,24},{8,0},{16,8},{24,16},{32,56},{40,32},{48,40},{56,48},{64,88... | collective-permute-start | bytes 98312 | tf_op jit(solution)/shard_map/ppermute | solution.py:115
  164.7 5.5 %collective-permute-start.12 = (f32[32,256]{1,0:T(8,128)S(1)}, f32[32,256]{1,0:T(8,128)S(1)}, u32[]{:S(2)}, u32[]{:S(2)}) collective-permute-start(f32[32,256]{1,0:T(8,128)S(1)} %fusion.6), channel_id=1, source_target_pairs={{0,16},{8,24},{16,0},{24,8},{32,48},{40,56},{48,32},{56,40},{64,80... | collective-permute-start | bytes 98312 | tf_op jit(solution)/shard_map/ppermute | solution.py:115
  164.7 5.5 %collective-permute-start.11 = (f32[32,256]{1,0:T(8,128)S(1)}, f32[32,256]{1,0:T(8,128)S(1)}, u32[]{:S(2)}, u32[]{:S(2)}) collective-permute-start(f32[32,256]{1,0:T(8,128)S(1)} %fusion.6), channel_id=1, source_target_pairs={{0,8},{8,16},{16,24},{24,0},{32,40},{40,48},{48,56},{56,32},{64,72... | collective-permute-start | bytes 98312 | tf_op jit(solution)/shard_map/ppermute | solution.py:115
  170.2 8.7 %collective-permute-start.16 = (f32[32,256]{1,0:T(8,128)S(1)}, f32[32,256]{1,0:T(8,128)S(1)}, u32[]{:S(2)}, u32[]{:S(2)}) collective-permute-start(f32[32,256]{1,0:T(8,128)S(1)} %add_add_fusion.1), channel_id=1, source_target_pairs={{0,96},{8,104},{16,112},{24,120},{32,0},{40,8},{48,16},{56,24},{64... | collective-permute-start | bytes 98312 | tf_op jit(solution)/shard_map/ppermute | solution.py:115
  175.6 5.4 %collective-permute-start.15 = (f32[32,256]{1,0:T(8,128)S(1)}, f32[32,256]{1,0:T(8,128)S(1)}, u32[]{:S(2)}, u32[]{:S(2)}) collective-permute-start(f32[32,256]{1,0:T(8,128)S(1)} %add_add_fusion.1), channel_id=1, source_target_pairs={{0,64},{8,72},{16,80},{24,88},{32,96},{40,104},{48,112},{56,120},{... | collective-permute-start | bytes 98312 | tf_op jit(solution)/shard_map/ppermute | solution.py:115
  182.7 6.1 %collective-permute-start.17 = (f32[32,256]{1,0:T(8,128)S(1)}, f32[32,256]{1,0:T(8,128)S(1)}, u32[]{:S(2)}, u32[]{:S(2)}) collective-permute-start(f32[32,256]{1,0:T(8,128)S(1)} %get-tuple-element.10), channel_id=1, source_target_pairs={{0,1},{1,2},{2,3},{3,4},{4,5},{5,6},{6,7},{7,0},{8,9},{9,10},{10,1... | collective-permute-start | bytes 98312 | tf_op jit(solution)/shard_map/ppermute | solution.py:120
  182.9 6.8 %collective-permute-start.18 = (f32[32,256]{1,0:T(8,128)S(1)}, f32[32,256]{1,0:T(8,128)S(1)}, u32[]{:S(2)}, u32[]{:S(2)}) collective-permute-start(f32[32,256]{1,0:T(8,128)S(1)} %get-tuple-element.10), channel_id=1, source_target_pairs={{0,2},{1,3},{2,4},{3,5},{4,6},{5,7},{6,0},{7,1},{8,10},{9,11},{10,... | collective-permute-start | bytes 98312 | tf_op jit(solution)/shard_map/ppermute | solution.py:120
  183.0 7.0 %collective-permute-start.19 = (f32[32,256]{1,0:T(8,128)S(1)}, f32[32,256]{1,0:T(8,128)S(1)}, u32[]{:S(2)}, u32[]{:S(2)}) collective-permute-start(f32[32,256]{1,0:T(8,128)S(1)} %get-tuple-element.10), channel_id=1, source_target_pairs={{0,3},{1,4},{2,5},{3,6},{4,7},{5,0},{6,1},{7,2},{8,11},{9,12},{10,... | collective-permute-start | bytes 98312 | tf_op jit(solution)/shard_map/ppermute | solution.py:120
  185.1 6.2 %collective-permute-start.20 = (f32[32,256]{1,0:T(8,128)S(1)}, f32[32,256]{1,0:T(8,128)S(1)}, u32[]{:S(2)}, u32[]{:S(2)}) collective-permute-start(f32[32,256]{1,0:T(8,128)S(1)} %get-tuple-element.10), channel_id=1, source_target_pairs={{0,4},{1,5},{2,6},{3,7},{4,0},{5,1},{6,2},{7,3},{8,12},{9,13},{10,... | collective-permute-start | bytes 98312 | tf_op jit(solution)/shard_map/ppermute | solution.py:120
  187.2 45.9 %collective-permute-start.21 = (f32[32,256]{1,0:T(8,128)S(1)}, f32[32,256]{1,0:T(8,128)S(1)}, u32[]{:S(2)}, u32[]{:S(2)}) collective-permute-start(f32[32,256]{1,0:T(8,128)S(1)} %get-tuple-element.10), channel_id=1, source_target_pairs={{0,5},{1,6},{2,7},{3,0},{4,1},{5,2},{6,3},{7,4},{8,13},{9,14},{10,... | collective-permute-start | bytes 98312 | tf_op jit(solution)/shard_map/ppermute | solution.py:120
  188.9 44.3 %collective-permute-start.22 = (f32[32,256]{1,0:T(8,128)S(1)}, f32[32,256]{1,0:T(8,128)S(1)}, u32[]{:S(2)}, u32[]{:S(2)}) collective-permute-start(f32[32,256]{1,0:T(8,128)S(1)} %get-tuple-element.10), channel_id=1, source_target_pairs={{0,6},{1,7},{2,0},{3,1},{4,2},{5,3},{6,4},{7,5},{8,14},{9,15},{10,... | collective-permute-start | bytes 98312 | tf_op jit(solution)/shard_map/ppermute | solution.py:120
  189.7 43.4 %collective-permute-start.23 = (f32[32,256]{1,0:T(8,128)S(1)}, f32[32,256]{1,0:T(8,128)S(1)}, u32[]{:S(2)}, u32[]{:S(2)}) collective-permute-start(f32[32,256]{1,0:T(8,128)S(1)} %get-tuple-element.10), channel_id=1, source_target_pairs={{0,7},{1,0},{2,1},{3,2},{4,3},{5,4},{6,5},{7,6},{8,15},{9,8},{10,9... | collective-permute-start | bytes 98312 | tf_op jit(solution)/shard_map/ppermute | solution.py:120
  227.7 16.5 %collective-permute-start.3 = (bf16[8,256,128]{2,1,0:T(8,128)(2,1)S(1)}, bf16[8,256,128]{2,1,0:T(8,128)(2,1)S(1)}, u32[]{:S(2)}, u32[]{:S(2)}) collective-permute-start(bf16[8,256,128]{2,1,0:T(8,128)(2,1)S(1)} %get-tuple-element.12), channel_id=1, source_target_pairs={{0,8},{8,16},{16,24},{24,32},{32,40},{40,48},{48,56},{56,64},{64,7... | collective-permute-start | bytes 1572872 | tf_op jit(solution)/shard_map/ppermute | solution.py:145
  229.4 14.9 %collective-permute-start.2 = (bf16[8,256,128]{2,1,0:T(8,128)(2,1)S(1)}, bf16[8,256,128]{2,1,0:T(8,128)(2,1)S(1)}, u32[]{:S(2)}, u32[]{:S(2)}) collective-permute-start(bf16[8,256,128]{2,1,0:T(8,128)(2,1)S(1)} %get-tuple-element.11), channel_id=1, source_target_pairs={{0,120},{8,0},{16,8},{24,16},{32,24},{40,32},{48,40},{56,48},{64,5... | collective-permute-start | bytes 1572872 | tf_op jit(solution)/shard_map/ppermute | solution.py:144
  (6 other events, 75.5 us)
Sparse Core Ops, SparseCore 0:
  33.0 63.7 all-gather.1
  136.8 89.6 reduce-scatter.1

commit v2 on v0

v2 whole, which is shorter than its diff:
```python
import functools
import math

import jax
import jax.numpy as jnp
import numpy as np
from jax import lax
from jax.experimental import pallas as pl
from jax.experimental.pallas import tpu as pltpu
from jax.sharding import PartitionSpec as P

bf16, f32 = jnp.bfloat16, jnp.float32

CROSS = 4
FWD_SLOTS = 12
BWD_SLOTS = 8
STAGES = 4


def pieces_of(own):
    a = range(CROSS)
    b = range(CROSS, own)
    full = range(own)
    a2 = [(p, 2, i) for p in (1, 0, 2) for i in a]
    half = len(a2) // 2
    return [
        ("lz1", [(0, dy, i) for dy in (1, 3) for i in b]),
        ("lz2", [(0, 2, i) for i in b]),
        ("hz1", [(2, dy, i) for dy in (1, 3) for i in b]),
        ("hz2", [(2, 2, i) for i in b]),
        ("a2lo", a2[:half]),
        ("a2hi", a2[half:]),
        ("a1", [(p, 1, i) for p in (1, 0, 2) for i in a]),
        ("a3", [(p, 3, i) for p in (1, 0, 2) for i in a]),
        ("bb", [(1, dy, i) for dy in (1, 3) for i in b]),
        ("b2", [(1, 2, i) for i in b]),
        ("own", [(1, 0, i) for i in full]),
        ("low", [(0, 0, i) for i in full]),
        ("high", [(2, 0, i) for i in full]),
    ]


GROUPS = [
    ("lz1", "lz2"),
    ("hz1", "hz2"),
    ("a2lo", "a2hi"),
    ("a1", "a3"),
    ("bb", "b2"),
    ("own", "low", "high"),
]


def kernel(sizes, groups, chunk, idx, cnt, a_ref, *refs):
    n_in = 2 * len(sizes)
    n_out = 2 * len(groups)
    parts = refs[:n_in]
    w_ref, cot_ref, out_ref, wg_ref = refs[n_in : n_in + 4]
    outs = refs[n_in + 4 : n_in + 4 + n_out]
    win, acc, stage, in_sem, out_sem = refs[n_in + 4 + n_out :]
    t = pl.program_id(0)
    tile = a_ref.shape[2]

    @pl.when(t == 0)
    def _():
        copies, at = [], 0
        for k, part in enumerate(parts):
            rows = part.shape[0]
            copies.append(pltpu.make_async_copy(part, win.at[pl.ds(at, rows)], in_sem.at[k]))
            copies[-1].start()
            at += rows
        wg_ref[...] = jnp.zeros_like(wg_ref)

        def zero(i, _):
            acc[pl.ds(i * 4, 4)] = jnp.zeros((4,) + acc.shape[1:], f32)
            return 0

        lax.fori_loop(0, acc.shape[0] // 4, zero, 0)
        for copy in copies:
            copy.wait()

    n = cnt[t]

    def lanes(k0, count):
        got = []
        for j in range(count):
            a = a_ref[0, k0 + j]
            got.append(jnp.where(k0 + j < n, a, jnp.zeros_like(a)))
        return jnp.concatenate(got, axis=1)

    def forward(i, af):
        k0 = i * FWD_SLOTS
        rows = [
            win[pl.ds(pl.multiple_of(idx[t, k0 + j] * tile, tile), tile), :]
            for j in range(FWD_SLOTS)
        ]
        return af + jnp.dot(
            lanes(k0, FWD_SLOTS), jnp.concatenate(rows, axis=0), preferred_element_type=f32
        )

    width = w_ref.shape[0]
    trips = (n + FWD_SLOTS - 1) // FWD_SLOTS
    af = lax.fori_loop(0, trips, forward, jnp.zeros((tile, width), f32)).astype(bf16)
    pre = jnp.dot(af, w_ref[...], preferred_element_type=f32)
    sig = jax.nn.sigmoid(pre)
    out_ref[...] = (pre * sig).astype(bf16)
    g = (cot_ref[...].astype(f32) * sig * (1.0 + pre * (1.0 - sig))).astype(bf16)
    wg_ref[...] += lax.dot_general(af, g, (((0,), (0,)), ((), ())), preferred_element_type=f32)
    gwt = lax.dot_general(
        w_ref[...], g, (((1,), (1,)), ((), ())), preferred_element_type=f32
    ).astype(bf16)

    def backward(i, _):
        k0 = i * BWD_SLOTS
        r = jnp.dot(gwt, lanes(k0, BWD_SLOTS), preferred_element_type=f32)
        for j in range(BWD_SLOTS):
            acc[idx[t, k0 + j]] += r[:, j * tile : (j + 1) * tile]
        return 0

    lax.fori_loop(0, (n + BWD_SLOTS - 1) // BWD_SLOTS, backward, 0)

    @pl.when(t == pl.num_programs(0) - 1)
    def _():
        def copy(slot, out, at):
            return pltpu.make_async_copy(stage.at[slot], out.at[pl.ds(at, chunk)], out_sem.at[slot])

        done = 0
        for out in outs:
            steps = out.shape[0] // chunk

            def emit(i, _, out=out, done=done):
                number = done + i
                slot = lax.rem(number, STAGES)

                @pl.when(number >= STAGES)
                def _():
                    copy(slot, out, 0).wait()

                stage[slot] = acc[pl.ds(number * chunk, chunk)].astype(bf16)
                copy(slot, out, i * chunk).start()
                return 0

            lax.fori_loop(0, steps, emit, 0)
            done += steps
        for slot in range(STAGES):
            copy(slot, outs[0], 0).wait()


def layer(idx, cnt, tile_values, parts, weight, cotangent, sizes, groups):
    nt, slots, tile, _ = tile_values.shape
    width = weight.shape[0]
    n_win = 2 * sum(sizes)
    chunk = math.gcd(*groups)
    anywhere = pl.BlockSpec(memory_space=pl.ANY)
    return pl.pallas_call(
        functools.partial(kernel, sizes, groups, chunk),
        grid_spec=pltpu.PrefetchScalarGridSpec(
            num_scalar_prefetch=2,
            grid=(nt,),
            in_specs=[pl.BlockSpec((1, slots, tile, tile), lambda t, *_: (t, 0, 0, 0))]
            + [anywhere] * len(parts)
            + [
                pl.BlockSpec((width, width), lambda t, *_: (0, 0)),
                pl.BlockSpec((tile, width), lambda t, *_: (t, 0)),
            ],
            out_specs=[
                pl.BlockSpec((tile, width), lambda t, *_: (t, 0)),
                pl.BlockSpec((width, width), lambda t, *_: (0, 0)),
            ]
            + [anywhere] * (2 * len(groups)),
            scratch_shapes=[
                pltpu.VMEM((n_win * tile, width), bf16),
                pltpu.VMEM((n_win, width, tile), f32),
                pltpu.VMEM((STAGES, chunk, width, tile), bf16),
                pltpu.SemaphoreType.DMA((len(parts),)),
                pltpu.SemaphoreType.DMA((STAGES,)),
            ],
        ),
        out_shape=[
            jax.ShapeDtypeStruct((nt * tile, width), bf16),
            jax.ShapeDtypeStruct((width, width), f32),
        ]
        + [jax.ShapeDtypeStruct((g, width, tile), bf16) for _ in range(2) for g in groups],
        compiler_params=pltpu.CompilerParams(vmem_limit_bytes=60 * 2**20),
    )(idx, cnt, tile_values, *parts, weight, cotangent)


def ring(count, step):
    return [(i, (i + step) % count) for i in range(count)]


def from_z(x, step):
    return lax.ppermute(x, "rows", ring(lax.axis_size("rows"), -step))


def from_y(x, step):
    return lax.ppermute(x, "rep", ring(lax.axis_size("rep"), -2 * step))


def from_core(x):
    return lax.ppermute(x, "rep", [(i, i ^ 1) for i in range(lax.axis_size("rep"))])


def gather(features, tile, own):
    ha, hb = features[: CROSS * tile], features[CROSS * tile :]
    got = {"own": features}
    got["low"], got["high"] = from_z(features, -1), from_z(features, 1)
    b1, b3 = from_y(hb, 1), from_y(hb, -1)
    half = (own - CROSS) // 2 * tile
    got["bb"] = jnp.concatenate([b1, b3])
    got["lz1"], got["hz1"] = from_z(got["bb"], -1), from_z(got["bb"], 1)
    got["b2"] = jnp.concatenate([from_y(b1[:half], 1), from_y(b3[half:], -1)])
    got["lz2"], got["hz2"] = from_z(got["b2"], -1), from_z(got["b2"], 1)
    ycat = jnp.concatenate([ha, got["low"][: CROSS * tile], got["high"][: CROSS * tile]])
    got["a1"], got["a3"] = from_y(ycat, 1), from_y(ycat, -1)
    half = 3 * CROSS // 2 * tile
    got["a2lo"] = from_y(got["a1"][:half], 1)
    got["a2hi"] = from_y(got["a3"][half:], -1)
    return got


def scatter(mine, other, own):
    s = [m.astype(f32) + from_core(o).astype(f32) for m, o in zip(mine, other)]
    lz, hz, a2, a13, bb2, home = s
    nb = own - CROSS
    b = bb2 + from_z(lz.astype(bf16), 1).astype(f32) + from_z(hz.astype(bf16), -1).astype(f32)
    half, na = 3 * CROSS // 2, 3 * CROSS
    a2 = a2.astype(bf16)
    lo, hi = from_y(a2[:half], -1).astype(f32), from_y(a2[half:], 1).astype(f32)
    a1 = jnp.concatenate([a13[:half] + lo, a13[half:na]]).astype(bf16)
    a3 = jnp.concatenate([a13[na : na + half], a13[na + half :] + hi]).astype(bf16)
    ycat = from_y(a1, -1).astype(f32) + from_y(a3, 1).astype(f32)
    h, low, high = home[:own], home[own : 2 * own], home[2 * own :]
    ha = h[:CROSS] + ycat[:CROSS]
    low = jnp.concatenate([low[:CROSS] + ycat[CROSS : 2 * CROSS], low[CROSS:]]).astype(bf16)
    high = jnp.concatenate([high[:CROSS] + ycat[2 * CROSS :], high[CROSS:]]).astype(bf16)
    half = nb // 2
    b2 = b[2 * nb :].astype(bf16)
    lo, hi = from_y(b2[:half], -1).astype(f32), from_y(b2[half:], 1).astype(f32)
    b1 = jnp.concatenate([b[:half] + lo, b[half:nb]]).astype(bf16)
    b3 = jnp.concatenate([b[nb : nb + half], b[nb + half : 2 * nb] + hi]).astype(bf16)
    hb = h[CROSS:] + from_y(b1, -1).astype(f32) + from_y(b3, 1).astype(f32)
    return (
        jnp.concatenate([ha, hb]) + from_z(low, 1).astype(f32) + from_z(high, -1).astype(f32)
    )


def weight_sum(term, n_rows, n_rep):
    rep = lax.axis_index("rep")
    core, y = rep % 2, rep // 2
    n_y = n_rep // 2

    def piece(x, count, at):
        x = x.reshape(count, x.shape[0] // count, x.shape[1])
        return lax.dynamic_index_in_dim(x, jnp.mod(at, count), 0, keepdims=False)

    half = piece(term, 2, core) + from_core(piece(term, 2, core + 1))
    own = piece(half, n_y, y)
    for step in range(1, n_y):
        own = own + from_y(piece(half, n_y, y - step), step)
    part = 4
    for inner in (True, False):
        got = own
        for step in range(1, part):
            if inner:
                route = [(r, r // part * part + (r % part + step) % part) for r in range(n_rows)]
            else:
                route = ring(n_rows, step * part)
            got = got + lax.ppermute(own, "rows", route)
        own = got
    blocks = jnp.zeros((n_y,) + own.shape, f32)
    blocks = lax.dynamic_update_index_in_dim(blocks, own, y, 0)
    for step in range(1, n_y):
        blocks = lax.dynamic_update_index_in_dim(blocks, from_y(own, step), jnp.mod(y + step, n_y), 0)
    half = blocks.reshape(half.shape)
    other = from_core(half)
    return jnp.where(core == 0, jnp.concatenate([half, other]), jnp.concatenate([other, half]))


def local(features, weight, tile_values, tile_cols, tile_live, cotangent):
    n_rows = lax.axis_size("rows")
    n_rep = lax.axis_size("rep")
    rep = lax.axis_index("rep")
    node_dev, width = features.shape
    tile = tile_values.shape[2]
    own = node_dev // tile
    group_tiles = own * n_rep
    pieces = pieces_of(own)
    order = [key for _, keys in pieces for key in keys]
    table = np.zeros((3, n_rep // 2, own), np.int32)
    for at, key in enumerate(order):
        table[key] = at
    place = jnp.mod(tile_cols // group_tiles - lax.axis_index("rows") + 1, n_rows)
    inner = tile_cols % group_tiles
    owner = inner // own
    dy = jnp.mod(owner // 2 - rep // 2, n_rep // 2)
    dcore = jnp.mod(owner + rep, 2)
    key = (place * (n_rep // 2) + dy) * own + inner % own
    hit = key[:, :, None] == jnp.arange(table.size, dtype=jnp.int32)
    at = jnp.sum(jnp.where(hit, jnp.asarray(table.reshape(-1)), 0), axis=2)
    idx = dcore * table.size + at
    cnt = jnp.sum(tile_live, axis=1)

    got = gather(features, tile, own)
    mine = [got[name] for name, _ in pieces]
    parts = mine + [from_core(x) for x in mine]
    size = {name: len(keys) for name, keys in pieces}
    groups = [sum(size[name] for name in names) for names in GROUPS]
    output, term, *grads = layer(
        idx, cnt, tile_values, parts, weight, cotangent, list(size.values()), groups
    )
    total = scatter(grads[: len(groups)], grads[len(groups) :], own)
    weight_grad = weight_sum(term, n_rows, n_rep)
    feature_grad = jnp.swapaxes(total, 1, 2).reshape(node_dev, width).astype(bf16)
    return (output, feature_grad, weight_grad)


def solution(mesh):
    placed = (
        P(("rows", "rep"), None),
        P(),
        P(("rows", "rep"), None, None, None),
        P(("rows", "rep"), None),
        P(("rows", "rep"), None),
        P(("rows", "rep"), None),
    )
    return jax.shard_map(
        local,
        mesh=mesh,
        in_specs=placed,
        out_specs=(P(("rows", "rep"), None), P(("rows", "rep"), None), P()),
        check_vma=False,
    )
```

time: 896 us -> 216 us (0.24)
  waiting for transfers between devices: 485 us -> 101 us
  other arithmetic: 215 us -> 13.7 us
  local copies, waits for them, and re-layouts: 113 us -> 8.11 us
  matrix products: 59.9 us -> 0 us
  starting transfers between devices: 7.22 us -> 63 us
  Pallas kernels: 0 us -> 28.9 us
  between operations: 13.8 us -> 1.35 us
    ppermute x4 -> x59, waiting for transfers between devices: 275 us -> 101 us  [the longest x22 52.9 us: from_y(): return lax.ppermute(x, 'rep', ring(lax.axis_size('rep'), -2 * step))]
    psum x1 -> x0, waiting for transfers between devices: 142 us -> none  [local(): weight_grad = lax.psum(weight_term, ('rows', 'rep'))]
    scatter-add x8 -> x0, other arithmetic: 119 us -> none  [backward_row(): return (accum.at[columns].add(contrib), None)]
    dot_general x19 -> x0, matrix products: 59.9 us -> none  [the longest x8 29.7 us: backward_row(): jnp.einsum('sij,if->sjf', masked, grads, preferred_element_type=jnp.float32)]
    gather x8 -> x0, local copies, waits for them, and re-layouts: 56.5 us -> none  [forward_row(): chosen = win_tiles[columns]]
    ppermute x4 -> x59, starting transfers between devices: 7.1 us -> 63 us  [the longest x22 27.9 us: from_y(): return lax.ppermute(x, 'rep', ring(lax.axis_size('rep'), -2 * step))]
    concatenate x2 -> x7, other arithmetic: 40.4 us -> 0.34 us  [the longest x1 0.07 us: scatter(): a1 = jnp.concatenate([a13[:half] + lo, a13[half:na]]).astype(bf16)]
    convert_element_type x18 -> x4, other arithmetic: 45.3 us -> 6.13 us  [the longest x1 2.27 us: scatter(): lz.astype(bf16)]
  transfers between devices with their start and end apart: 7 -> 59, of which waited for: 7 -> 25; matrix products, arithmetic and copies ran while one was open for 1% -> 7% of each run, Pallas kernels for 0% -> 0%
where the time goes in v2:
time: 216 us
  waiting for transfers between devices  101 us (47%)
  starting transfers between devices  63 us (29%)
  Pallas kernels  28.9 us (13%)
  other arithmetic  13.7 us (6%)
  local copies, waits for them, and re-layouts  8.11 us (4%)
    ppermute x22, waiting for transfers between devices, from_y(): return lax.ppermute(x, 'rep', ring(lax.axis_size('rep'), -2 * step))  52.9 us
    ppermute x10, waiting for transfers between devices, from_z(): return lax.ppermute(x, 'rows', ring(lax.axis_size('rows'), -step))  40.3 us
    pallas_call x1, Pallas kernels, layer(): pl.pallas_call(functools.partial(kernel, sizes, groups, chunk), grid_spec...  28.9 us
    ppermute x22, starting transfers between devices, from_y(): return lax.ppermute(x, 'rep', ring(lax.axis_size('rep'), -2 * step))  27.9 us
    ppermute x10, starting transfers between devices, from_z(): return lax.ppermute(x, 'rows', ring(lax.axis_size('rows'), -step))  22.8 us
    ppermute x6, starting transfers between devices, weight_sum(): got = got + lax.ppermute(own, 'rows', route)  8.8 us
    ppermute x6, waiting for transfers between devices, weight_sum(): got = got + lax.ppermute(own, 'rows', route)  5.04 us
  transfers between devices with their start and end apart: 59, of which 25 were waited for; matrix products, arithmetic and copies ran while one was open for 7% of the time, Pallas kernels for 0%

profile of v2, /device:TPU:0, one launch (start us, length us, event | category | flops | bytes accessed | tf_op | source)
XLA Modules:
  0.0 215.8 jit_solution(17882259344349195380)
XLA Ops:
  1.8 3.2 %collective-permute-start = (bf16[512,256]{1,0:T(8,128)(2,1)S(1)}, bf16[512,256]{1,0:T(8,128)(2,1)S(1)}, u32[]{:S(2)}, u32[]{:S(2)}) collective-permute-start(bf16[512,256]{1,0:T(8,128)(2,1)S(1)} %get-tuple-element.58), channel_id=1, source_target_pairs={{0,6},{1,7},{2,0},{3,1},{4,2},{5,3},{6,4},{7,5},{8,14},{9,15},{10,... | collective-permute-start | bytes 786440 | tf_op jit(solution)/shard_map/ppermute | solution.py:196
  6.8 4.3 %collective-permute-start.9 = (bf16[1024,256]{1,0:T(8,128)(2,1)}, bf16[1024,256]{1,0:T(8,128)(2,1)S(1)}, u32[]{:S(2)}, u32[]{:S(2)}) collective-permute-start(bf16[1024,256]{1,0:T(8,128)(2,1)} %refs_10_.1), channel_id=1, source_target_pairs={{0,120},{8,0},{16,8},{24,16},{32,24},{40,32},{48,40},{56,48},{64,5... | collective-permute-start | bytes 1572872 | tf_op jit(solution)/shard_map/ppermute | solution.py:192
  11.2 3.3 %collective-permute-start.3 = (bf16[256,256]{1,0:T(8,128)(2,1)S(1)}, bf16[256,256]{1,0:T(8,128)(2,1)S(1)}, u32[]{:S(2)}, u32[]{:S(2)}) collective-permute-start(bf16[256,256]{1,0:T(8,128)(2,1)S(1)} %slice.135), channel_id=1, source_target_pairs={{0,6},{1,7},{2,0},{3,1},{4,2},{5,3},{6,4},{7,5},{8,14},{9,15},{10,... | collective-permute-start | bytes 393224 | tf_op jit(solution)/shard_map/ppermute | solution.py:196
  14.5 5.4 %collective-permute-done.1 = bf16[512,256]{1,0:T(8,128)(2,1)S(1)} collective-permute-done((bf16[512,256]{1,0:T(8,128)(2,1)S(1)}, bf16[512,256]{1,0:T(8,128)(2,1)S(1)}, u32[]{:S(2)}, u32[]{:S(2)}) %collective-permute-start.1) | collective-permute-done | bytes 262176 | tf_op jit(solution)/shard_map/ppermute | solution.py:196
  20.1 6.0 %collective-permute-done.4 = bf16[256,256]{1,0:T(8,128)(2,1)S(1)} collective-permute-done((bf16[256,256]{1,0:T(8,128)(2,1)S(1)}, bf16[256,256]{1,0:T(8,128)(2,1)S(1)}, u32[]{:S(2)}, u32[]{:S(2)}) %collective-permute-start.4) | collective-permute-done | bytes 131104 | tf_op jit(solution)/shard_map/ppermute | solution.py:196
  26.2 5.3 %collective-permute-start.7 = (bf16[512,256]{1,0:T(8,128)(2,1)S(1)}, bf16[512,256]{1,0:T(8,128)(2,1)S(1)}, u32[]{:S(2)}, u32[]{:S(2)}) collective-permute-start(bf16[512,256]{1,0:T(8,128)(2,1)S(1)} %constant_dynamic-update-slice_fusion.2.refs_9_), channel_id=1, source_target_pairs={{0,120},{8,0},{16,8},{24,16},{32,24},{40,32},{48,40},{56,48},{64,5... | collective-permute-start | bytes 786440 | tf_op jit(solution)/shard_map/ppermute | solution.py:192
  35.9 5.3 %collective-permute-start.6 = (bf16[1024,256]{1,0:T(8,128)(2,1)S(1)}, bf16[1024,256]{1,0:T(8,128)(2,1)}, u32[]{:S(2)}, u32[]{:S(2)}) collective-permute-start(bf16[1024,256]{1,0:T(8,128)(2,1)S(1)} %constant_dynamic-update-slice_fusion.refs_8_), channel_id=1, source_target_pairs={{0,120},{8,0},{16,8},{24,16},{32,24},{40,32},{48,40},{56,48},{64,5... | collective-permute-start | bytes 1572872 | tf_op jit(solution)/shard_map/ppermute | solution.py:192
  41.3 9.9 %collective-permute-done.2.refs_0_ = bf16[1024,256]{1,0:T(8,128)(2,1)S(1)} collective-permute-done((bf16[1024,256]{1,0:T(8,128)(2,1)S(1)}, bf16[1024,256]{1,0:T(8,128)(2,1)S(1)}, u32[]{:S(2)}, u32[]{:S(2)}) %collective-permute-start.2) | collective-permute-done | bytes 524320 | tf_op jit(solution)/shard_map/ppermute | solution.py:192
  58.6 8.0 %collective-permute-done.11.refs_4_ = bf16[768,256]{1,0:T(8,128)(2,1)} collective-permute-done((bf16[768,256]{1,0:T(8,128)(2,1)}, bf16[768,256]{1,0:T(8,128)(2,1)}, u32[]{:S(2)}, u32[]{:S(2)}) %collective-permute-start.11) | collective-permute-done | bytes 393248 | tf_op jit(solution)/shard_map/ppermute | solution.py:196
  71.9 28.9 %shard_map.94 = (bf16[1024,256]{1,0:T(8,128)(2,1)}, f32[256,256]{1,0:T(8,128)}, bf16[12,256,128]{2,1,0:T(8,128)(2,1)}, bf16[12,256,128]{2,1,0:T(8,128)(2,1)}, bf...) custom-call(s32[8,48]{1,0:T(8,128)} %fusion.14.idx, ...), custom_call_target="tpu_custom_call" | custom-call | tf_op jit(solution)/shard_map/pallas_call | solution.py:154
  105.5 3.1 %collective-permute-start.46 = (f32[32,256]{1,0:T(8,128)S(1)}, f32[32,256]{1,0:T(8,128)S(1)}, u32[]{:S(2)}, u32[]{:S(2)}) collective-permute-start(f32[32,256]{1,0:T(8,128)S(1)} %get-tuple-element.59), channel_id=1, source_target_pairs={{0,6},{1,7},{2,0},{3,1},{4,2},{5,3},{6,4},{7,5},{8,14},{9,15},{10,... | collective-permute-start | bytes 98312 | tf_op jit(solution)/shard_map/ppermute | solution.py:196
  111.7 2.3 %collective-permute-done.47 = f32[32,256]{1,0:T(8,128)S(1)} collective-permute-done((f32[32,256]{1,0:T(8,128)S(1)}, f32[32,256]{1,0:T(8,128)S(1)}, u32[]{:S(2)}, u32[]{:S(2)}) %collective-permute-start.47) | collective-permute-done | bytes 32800 | tf_op jit(solution)/shard_map/ppermute | solution.py:196
  116.5 2.3 %collective-permute-start.51 = (f32[32,256]{1,0:T(8,128)S(1)}, f32[32,256]{1,0:T(8,128)S(1)}, u32[]{:S(2)}, u32[]{:S(2)}) collective-permute-start(f32[32,256]{1,0:T(8,128)S(1)} %fusion.11), channel_id=1, source_target_pairs={{0,24},{8,0},{16,8},{24,16},{32,56},{40,32},{48,40},{56,48},{64,88... | collective-permute-start | bytes 98312 | tf_op jit(solution)/shard_map/ppermute | solution.py:268
  131.5 2.3 %add_convert_fusion.1 = bf16[12,256,128]{2,1,0:T(8,128)(2,1)} fusion(bf16[12,256,128]{2,1,0:T(8,128)(2,1)} %collective-permute-done.35, bf16[12,256,128]{2,1,0:T(8,128)(2,1)S(1)} %copy-done.11), kind=kLoop, calls=%fused_computation.4 | loop fusion | flops 1572864 | bytes 2359296 | tf_op jit(solution)/shard_map/convert_element_type | solution.py:225
  133.8 3.7 %collective-permute-start.36 = (bf16[12,256,128]{2,1,0:T(8,128)(2,1)}, bf16[12,256,128]{2,1,0:T(8,128)(2,1)}, u32[]{:S(2)}, u32[]{:S(2)}) collective-permute-start(bf16[12,256,128]{2,1,0:T(8,128)(2,1)} %add_convert_fusion.1), channel_id=1, source_target_pairs={{0,120},{8,0},{16,8},{24,16},{32,24},{40,32},{48,40},{56,48},{64,5... | collective-permute-start | bytes 2359304 | tf_op jit(solution)/shard_map/ppermute | solution.py:192
  142.3 12.6 %collective-permute-done.36 = bf16[12,256,128]{2,1,0:T(8,128)(2,1)} collective-permute-done((bf16[12,256,128]{2,1,0:T(8,128)(2,1)}, bf16[12,256,128]{2,1,0:T(8,128)(2,1)}, u32[]{:S(2)}, u32[]{:S(2)}) %collective-permute-start.36) | collective-permute-done | bytes 786464 | tf_op jit(solution)/shard_map/ppermute | solution.py:192
  155.2 7.4 %collective-permute-done.38 = bf16[12,256,128]{2,1,0:T(8,128)(2,1)S(1)} collective-permute-done((bf16[12,256,128]{2,1,0:T(8,128)(2,1)}, bf16[12,256,128]{2,1,0:T(8,128)(2,1)S(1)}, u32[]{:S(2)}, u32[]{:S(2)}) %collective-permute-start.38) | collective-permute-done | bytes 786464 | tf_op jit(solution)/shard_map/ppermute | solution.py:192
  169.0 5.2 %collective-permute-done.32 = bf16[6,256,128]{2,1,0:T(8,128)(2,1)S(1)} collective-permute-done((bf16[6,256,128]{2,1,0:T(8,128)(2,1)S(1)}, bf16[6,256,128]{2,1,0:T(8,128)(2,1)S(1)}, u32[]{:S(2)}, u32[]{:S(2)}) %collective-permute-start.32) | collective-permute-done | bytes 393248 | tf_op jit(solution)/shard_map/ppermute | solution.py:196
  174.9 3.1 %collective-permute-start.33 = (bf16[12,256,128]{2,1,0:T(8,128)(2,1)S(1)}, bf16[12,256,128]{2,1,0:T(8,128)(2,1)S(1)}, u32[]{:S(2)}, u32[]{:S(2)}) collective-permute-start(bf16[12,256,128]{2,1,0:T(8,128)(2,1)S(1)} %pad_maximum_fusion.2), channel_id=1, source_target_pairs={{0,6},{1,7},{2,0},{3,1},{4,2},{5,3},{6,4},{7,5},{8,14},{9,15},{10,... | collective-permute-start | bytes 2359304 | tf_op jit(solution)/shard_map/ppermute | solution.py:196
  179.2 15.9 %collective-permute-done.31 = bf16[12,256,128]{2,1,0:T(8,128)(2,1)S(1)} collective-permute-done((bf16[12,256,128]{2,1,0:T(8,128)(2,1)S(1)}, bf16[12,256,128]{2,1,0:T(8,128)(2,1)S(1)}, u32[]{:S(2)}, u32[]{:S(2)}) %collective-permute-start.31) | collective-permute-done | bytes 786464 | tf_op jit(solution)/shard_map/ppermute | solution.py:196
  195.6 2.6 %collective-permute-done.40 = bf16[4,256,128]{2,1,0:T(8,128)(2,1)S(1)} collective-permute-done((bf16[4,256,128]{2,1,0:T(8,128)(2,1)S(1)}, bf16[4,256,128]{2,1,0:T(8,128)(2,1)S(1)}, u32[]{:S(2)}, u32[]{:S(2)}) %collective-permute-start.40) | collective-permute-done | bytes 262176 | tf_op jit(solution)/shard_map/ppermute | solution.py:196
  198.3 3.2 %collective-permute-done.42 = bf16[4,256,128]{2,1,0:T(8,128)(2,1)S(1)} collective-permute-done((bf16[4,256,128]{2,1,0:T(8,128)(2,1)S(1)}, bf16[4,256,128]{2,1,0:T(8,128)(2,1)S(1)}, u32[]{:S(2)}, u32[]{:S(2)}) %collective-permute-start.42) | collective-permute-done | bytes 262176 | tf_op jit(solution)/shard_map/ppermute | solution.py:196
  206.2 4.8 %collective-permute-done.43 = bf16[8,256,128]{2,1,0:T(8,128)(2,1)S(1)} collective-permute-done((bf16[8,256,128]{2,1,0:T(8,128)(2,1)S(1)}, bf16[8,256,128]{2,1,0:T(8,128)(2,1)S(1)}, u32[]{:S(2)}, u32[]{:S(2)}) %collective-permute-start.43) | collective-permute-done | bytes 524320 | tf_op jit(solution)/shard_map/ppermute | solution.py:192
  211.1 3.6 %collective-permute-done.44 = bf16[8,256,128]{2,1,0:T(8,128)(2,1)S(1)} collective-permute-done((bf16[8,256,128]{2,1,0:T(8,128)(2,1)S(1)}, bf16[8,256,128]{2,1,0:T(8,128)(2,1)S(1)}, u32[]{:S(2)}, u32[]{:S(2)}) %collective-permute-start.44) | collective-permute-done | bytes 524320 | tf_op jit(solution)/shard_map/ppermute | solution.py:192
  (198 shorter events, 62.8 us)
Async XLA Ops:
  4.9 26.6 %collective-permute-start.8 = (bf16[1024,256]{1,0:T(8,128)(2,1)}, bf16[1024,256]{1,0:T(8,128)(2,1)S(1)}, u32[]{:S(2)}, u32[]{:S(2)}) collective-permute-start(bf16[1024,256]{1,0:T(8,128)(2,1)} %refs_10_.1), channel_id=1, source_target_pairs={{0,8},{8,16},{16,24},{24,32},{32,40},{40,48},{48,56},{56,64},{64,7... | collective-permute-start | bytes 1572872 | tf_op jit(solution)/shard_map/ppermute | solution.py:192
  6.8 24.8 %collective-permute-start.9 = (bf16[1024,256]{1,0:T(8,128)(2,1)}, bf16[1024,256]{1,0:T(8,128)(2,1)S(1)}, u32[]{:S(2)}, u32[]{:S(2)}) collective-permute-start(bf16[1024,256]{1,0:T(8,128)(2,1)} %refs_10_.1), channel_id=1, source_target_pairs={{0,120},{8,0},{16,8},{24,16},{32,24},{40,32},{48,40},{56,48},{64,5... | collective-permute-start | bytes 1572872 | tf_op jit(solution)/shard_map/ppermute | solution.py:192
  31.7 20.0 %collective-permute-start.10 = (bf16[1536,256]{1,0:T(8,128)(2,1)S(1)}, bf16[1536,256]{1,0:T(8,128)(2,1)S(1)}, u32[]{:S(2)}, u32[]{:S(2)}) collective-permute-start(bf16[1536,256]{1,0:T(8,128)(2,1)S(1)} %pad_maximum_fusion), channel_id=1, source_target_pairs={{0,6},{1,7},{2,0},{3,1},{4,2},{5,3},{6,4},{7,5},{8,14},{9,15},{10,... | collective-permute-start | bytes 2359304 | tf_op jit(solution)/shard_map/ppermute | solution.py:196
  31.9 21.2 %collective-permute-start.12 = (bf16[1536,256]{1,0:T(8,128)(2,1)S(1)}, bf16[1536,256]{1,0:T(8,128)(2,1)S(1)}, u32[]{:S(2)}, u32[]{:S(2)}) collective-permute-start(bf16[1536,256]{1,0:T(8,128)(2,1)S(1)} %pad_maximum_fusion), channel_id=1, source_target_pairs={{0,2},{1,3},{2,4},{3,5},{4,6},{5,7},{6,0},{7,1},{8,10},{9,11},{10,... | collective-permute-start | bytes 2359304 | tf_op jit(solution)/shard_map/ppermute | solution.py:196
  35.9 15.3 %collective-permute-start.2 = (bf16[1024,256]{1,0:T(8,128)(2,1)S(1)}, bf16[1024,256]{1,0:T(8,128)(2,1)S(1)}, u32[]{:S(2)}, u32[]{:S(2)}) collective-permute-start(bf16[1024,256]{1,0:T(8,128)(2,1)S(1)} %constant_dynamic-update-slice_fusion.refs_8_), channel_id=1, source_target_pairs={{0,8},{8,16},{16,24},{24,32},{32,40},{40,48},{48,56},{56,64},{64,7... | collective-permute-start | bytes 1572872 | tf_op jit(solution)/shard_map/ppermute | solution.py:192
  35.9 15.2 %collective-permute-start.6 = (bf16[1024,256]{1,0:T(8,128)(2,1)S(1)}, bf16[1024,256]{1,0:T(8,128)(2,1)}, u32[]{:S(2)}, u32[]{:S(2)}) collective-permute-start(bf16[1024,256]{1,0:T(8,128)(2,1)S(1)} %constant_dynamic-update-slice_fusion.refs_8_), channel_id=1, source_target_pairs={{0,120},{8,0},{16,8},{24,16},{32,24},{40,32},{48,40},{56,48},{64,5... | collective-permute-start | bytes 1572872 | tf_op jit(solution)/shard_map/ppermute | solution.py:192
  56.1 12.4 %collective-permute-start.13 = (bf16[768,256]{1,0:T(8,128)(2,1)}, bf16[768,256]{1,0:T(8,128)(2,1)}, u32[]{:S(2)}, u32[]{:S(2)}) collective-permute-start(bf16[768,256]{1,0:T(8,128)(2,1)} %slice.140), channel_id=1, source_target_pairs={{0,2},{1,3},{2,4},{3,5},{4,6},{5,7},{6,0},{7,1},{8,10},{9,11},{10,... | collective-permute-start | bytes 1179656 | tf_op jit(solution)/shard_map/ppermute | solution.py:196
  56.9 13.7 %collective-permute-start.20 = (bf16[1536,256]{1,0:T(8,128)(2,1)S(1)}, bf16[1536,256]{1,0:T(8,128)(2,1)}, u32[]{:S(2)}, u32[]{:S(2)}) collective-permute-start(bf16[1536,256]{1,0:T(8,128)(2,1)S(1)} %collective-permute-done.10.refs_6_), channel_id=1, source_target_pairs={{0,1},{1,0},{2,3},{3,2},{4,5},{5,4},{6,7},{7,6},{8,9},{9,8},{10,11... | collective-permute-start | bytes 2359304 | tf_op jit(solution)/shard_map/ppermute | solution.py:200
  57.7 12.9 %collective-permute-start.21 = (bf16[1536,256]{1,0:T(8,128)(2,1)S(1)}, bf16[1536,256]{1,0:T(8,128)(2,1)S(1)}, u32[]{:S(2)}, u32[]{:S(2)}) collective-permute-start(bf16[1536,256]{1,0:T(8,128)(2,1)S(1)} %collective-permute-done.12.refs_7_), channel_id=1, source_target_pairs={{0,1},{1,0},{2,3},{3,2},{4,5},{5,4},{6,7},{7,6},{8,9},{9,8},{10,11... | collective-permute-start | bytes 2359304 | tf_op jit(solution)/shard_map/ppermute | solution.py:200
  103.5 26.0 %collective-permute-start.35 = (bf16[12,256,128]{2,1,0:T(8,128)(2,1)}, bf16[12,256,128]{2,1,0:T(8,128)(2,1)}, u32[]{:S(2)}, u32[]{:S(2)}) collective-permute-start(bf16[12,256,128]{2,1,0:T(8,128)(2,1)} %get-tuple-element.27), channel_id=1, source_target_pairs={{0,1},{1,0},{2,3},{3,2},{4,5},{5,4},{6,7},{7,6},{8,9},{9,8},{10,11... | collective-permute-start | bytes 2359304 | tf_op jit(solution)/shard_map/ppermute | solution.py:200
  118.8 15.0 %collective-permute-start.37 = (bf16[12,256,128]{2,1,0:T(8,128)(2,1)}, bf16[12,256,128]{2,1,0:T(8,128)(2,1)}, u32[]{:S(2)}, u32[]{:S(2)}) collective-permute-start(bf16[12,256,128]{2,1,0:T(8,128)(2,1)} %get-tuple-element.29), channel_id=1, source_target_pairs={{0,1},{1,0},{2,3},{3,2},{4,5},{5,4},{6,7},{7,6},{8,9},{9,8},{10,11... | collective-permute-start | bytes 2359304 | tf_op jit(solution)/shard_map/ppermute | solution.py:200
  127.4 14.0 %collective-permute-start.34 = (bf16[12,256,128]{2,1,0:T(8,128)(2,1)}, bf16[12,256,128]{2,1,0:T(8,128)(2,1)}, u32[]{:S(2)}, u32[]{:S(2)}) collective-permute-start(bf16[12,256,128]{2,1,0:T(8,128)(2,1)} %get-tuple-element.25), channel_id=1, source_target_pairs={{0,1},{1,0},{2,3},{3,2},{4,5},{5,4},{6,7},{7,6},{8,9},{9,8},{10,11... | collective-permute-start | bytes 2359304 | tf_op jit(solution)/shard_map/ppermute | solution.py:200
  129.3 35.6 %collective-permute-start.28 = (bf16[24,256,128]{2,1,0:T(8,128)(2,1)}, bf16[24,256,128]{2,1,0:T(8,128)(2,1)S(1)}, u32[]{:S(2)}, u32[]{:S(2)}) collective-permute-start(bf16[24,256,128]{2,1,0:T(8,128)(2,1)} %get-tuple-element.21), channel_id=1, source_target_pairs={{0,1},{1,0},{2,3},{3,2},{4,5},{5,4},{6,7},{7,6},{8,9},{9,8},{10,11... | collective-permute-start | bytes 4718600 | tf_op jit(solution)/shard_map/ppermute | solution.py:200
  133.8 21.2 %collective-permute-start.36 = (bf16[12,256,128]{2,1,0:T(8,128)(2,1)}, bf16[12,256,128]{2,1,0:T(8,128)(2,1)}, u32[]{:S(2)}, u32[]{:S(2)}) collective-permute-start(bf16[12,256,128]{2,1,0:T(8,128)(2,1)} %add_convert_fusion.1), channel_id=1, source_target_pairs={{0,120},{8,0},{16,8},{24,16},{32,24},{40,32},{48,40},{56,48},{64,5... | collective-permute-start | bytes 2359304 | tf_op jit(solution)/shard_map/ppermute | solution.py:192
  139.7 22.9 %collective-permute-start.38 = (bf16[12,256,128]{2,1,0:T(8,128)(2,1)}, bf16[12,256,128]{2,1,0:T(8,128)(2,1)S(1)}, u32[]{:S(2)}, u32[]{:S(2)}) collective-permute-start(bf16[12,256,128]{2,1,0:T(8,128)(2,1)} %add_convert_fusion), channel_id=1, source_target_pairs={{0,8},{8,16},{16,24},{24,32},{32,40},{40,48},{48,56},{56,64},{64,7... | collective-permute-start | bytes 2359304 | tf_op jit(solution)/shard_map/ppermute | solution.py:192
  139.7 35.1 %collective-permute-start.27 = (bf16[24,256,128]{2,1,0:T(8,128)(2,1)}, bf16[24,256,128]{2,1,0:T(8,128)(2,1)S(1)}, u32[]{:S(2)}, u32[]{:S(2)}) collective-permute-start(bf16[24,256,128]{2,1,0:T(8,128)(2,1)} %get-tuple-element.19), channel_id=1, source_target_pairs={{0,1},{1,0},{2,3},{3,2},{4,5},{5,4},{6,7},{7,6},{8,9},{9,8},{10,11... | collective-permute-start | bytes 4718600 | tf_op jit(solution)/shard_map/ppermute | solution.py:200
  141.4 62.7 %collective-permute-start.56 = (f32[32,256]{1,0:T(8,128)S(1)}, f32[32,256]{1,0:T(8,128)S(1)}, u32[]{:S(2)}, u32[]{:S(2)}) collective-permute-start(f32[32,256]{1,0:T(8,128)S(1)} %get-tuple-element.32), channel_id=1, source_target_pairs={{0,4},{1,5},{2,6},{3,7},{4,0},{5,1},{6,2},{7,3},{8,12},{9,13},{10,... | collective-permute-start | bytes 98312 | tf_op jit(solution)/shard_map/ppermute | solution.py:196
  155.0 12.4 %collective-permute-start.30 = (bf16[6,256,128]{2,1,0:T(8,128)(2,1)S(1)}, bf16[6,256,128]{2,1,0:T(8,128)(2,1)S(1)}, u32[]{:S(2)}, u32[]{:S(2)}) collective-permute-start(bf16[6,256,128]{2,1,0:T(8,128)(2,1)S(1)} %get-tuple-element.55), channel_id=1, source_target_pairs={{0,2},{1,3},{2,4},{3,5},{4,6},{5,7},{6,0},{7,1},{8,10},{9,11},{10,... | collective-permute-start | bytes 1179656 | tf_op jit(solution)/shard_map/ppermute | solution.py:196
  165.0 13.7 %collective-permute-start.39 = (bf16[2,256,128]{2,1,0:T(8,128)(2,1)S(1)}, bf16[2,256,128]{2,1,0:T(8,128)(2,1)S(1)}, u32[]{:S(2)}, u32[]{:S(2)}) collective-permute-start(bf16[2,256,128]{2,1,0:T(8,128)(2,1)S(1)} %get-tuple-element.51), channel_id=1, source_target_pairs={{0,2},{1,3},{2,4},{3,5},{4,6},{5,7},{6,0},{7,1},{8,10},{9,11},{10,... | collective-permute-start | bytes 393224 | tf_op jit(solution)/shard_map/ppermute | solution.py:196
  174.5 20.6 %collective-permute-start.31 = (bf16[12,256,128]{2,1,0:T(8,128)(2,1)S(1)}, bf16[12,256,128]{2,1,0:T(8,128)(2,1)S(1)}, u32[]{:S(2)}, u32[]{:S(2)}) collective-permute-start(bf16[12,256,128]{2,1,0:T(8,128)(2,1)S(1)} %pad_maximum_fusion.1), channel_id=1, source_target_pairs={{0,2},{1,3},{2,4},{3,5},{4,6},{5,7},{6,0},{7,1},{8,10},{9,11},{10,... | collective-permute-start | bytes 2359304 | tf_op jit(solution)/shard_map/ppermute | solution.py:196
  174.9 20.6 %collective-permute-start.33 = (bf16[12,256,128]{2,1,0:T(8,128)(2,1)S(1)}, bf16[12,256,128]{2,1,0:T(8,128)(2,1)S(1)}, u32[]{:S(2)}, u32[]{:S(2)}) collective-permute-start(bf16[12,256,128]{2,1,0:T(8,128)(2,1)S(1)} %pad_maximum_fusion.2), channel_id=1, source_target_pairs={{0,6},{1,7},{2,0},{3,1},{4,2},{5,3},{6,4},{7,5},{8,14},{9,15},{10,... | collective-permute-start | bytes 2359304 | tf_op jit(solution)/shard_map/ppermute | solution.py:196
  178.7 25.4 %collective-permute-start.57 = (f32[32,256]{1,0:T(8,128)S(1)}, f32[32,256]{1,0:T(8,128)S(1)}, u32[]{:S(2)}, u32[]{:S(2)}) collective-permute-start(f32[32,256]{1,0:T(8,128)S(1)} %get-tuple-element.32), channel_id=1, source_target_pairs={{0,2},{1,3},{2,4},{3,5},{4,6},{5,7},{6,0},{7,1},{8,10},{9,11},{10,... | collective-permute-start | bytes 98312 | tf_op jit(solution)/shard_map/ppermute | solution.py:196
  178.9 19.4 %collective-permute-start.40 = (bf16[4,256,128]{2,1,0:T(8,128)(2,1)S(1)}, bf16[4,256,128]{2,1,0:T(8,128)(2,1)S(1)}, u32[]{:S(2)}, u32[]{:S(2)}) collective-permute-start(bf16[4,256,128]{2,1,0:T(8,128)(2,1)S(1)} %pad_maximum_fusion.5), channel_id=1, source_target_pairs={{0,2},{1,3},{2,4},{3,5},{4,6},{5,7},{6,0},{7,1},{8,10},{9,11},{10,... | collective-permute-start | bytes 786440 | tf_op jit(solution)/shard_map/ppermute | solution.py:196
  202.1 12.6 %collective-permute-start.44 = (bf16[8,256,128]{2,1,0:T(8,128)(2,1)S(1)}, bf16[8,256,128]{2,1,0:T(8,128)(2,1)S(1)}, u32[]{:S(2)}, u32[]{:S(2)}) collective-permute-start(bf16[8,256,128]{2,1,0:T(8,128)(2,1)S(1)} %pad_maximum_fusion.4), channel_id=1, source_target_pairs={{0,8},{8,16},{16,24},{24,32},{32,40},{40,48},{48,56},{56,64},{64,7... | collective-permute-start | bytes 1572872 | tf_op jit(solution)/shard_map/ppermute | solution.py:192
  (62 other events, 668.2 us)

commit v3 on v2

v3 whole, which is shorter than its diff:
```python
import functools
import math

import jax
import jax.numpy as jnp
import numpy as np
from jax import lax
from jax.experimental import pallas as pl
from jax.experimental.pallas import tpu as pltpu
from jax.sharding import PartitionSpec as P

bf16, f32 = jnp.bfloat16, jnp.float32

FWD_SLOTS = 12
BWD_SLOTS = 8
STAGES = 4


def layout(own, core):
    half = own // 2

    def shards(*keys):
        return [(p, dy, i) for p, dy in keys for i in range(own)]

    if core == 0:
        last = shards((1, 2), (0, 2), (2, 2))
        middle = shards((1, 1), (0, 1), (2, 1), (1, 3), (0, 3), (2, 3))
        first = [None] * own + shards((1, 0), (0, 0), (2, 0))
    else:
        last = shards((0, 2)) + [None] * half + shards((2, 2)) + [None] * half
        middle = shards((0, 0), (0, 1), (0, 3), (2, 0), (2, 1), (2, 3))
        first = shards((1, 2), (1, 0), (1, 1), (1, 3))
    return last, middle, first


def kernel(n_in, n_out, chunk, idx, cnt, a_ref, *refs):
    parts = refs[:n_in]
    w_ref, cot_ref, out_ref, wg_ref = refs[n_in : n_in + 4]
    outs = refs[n_in + 4 : n_in + 4 + n_out]
    win, acc, stage, in_sem, out_sem = refs[n_in + 4 + n_out :]
    t = pl.program_id(0)
    tile = a_ref.shape[2]

    @pl.when(t == 0)
    def _():
        copies, at = [], 0
        for k, part in enumerate(parts):
            rows = part.shape[0]
            copies.append(pltpu.make_async_copy(part, win.at[pl.ds(at, rows)], in_sem.at[k]))
            copies[-1].start()
            at += rows
        wg_ref[...] = jnp.zeros_like(wg_ref)

        def zero(i, _):
            acc[pl.ds(i * 4, 4)] = jnp.zeros((4,) + acc.shape[1:], f32)
            return 0

        lax.fori_loop(0, acc.shape[0] // 4, zero, 0)
        for copy in copies:
            copy.wait()

    n = cnt[t]

    def lanes(k0, count):
        got = []
        for j in range(count):
            a = a_ref[0, k0 + j]
            got.append(jnp.where(k0 + j < n, a, jnp.zeros_like(a)))
        return jnp.concatenate(got, axis=1)

    def forward(i, af):
        k0 = i * FWD_SLOTS
        rows = [
            win[pl.ds(pl.multiple_of(idx[t, k0 + j] * tile, tile), tile), :]
            for j in range(FWD_SLOTS)
        ]
        return af + jnp.dot(
            lanes(k0, FWD_SLOTS), jnp.concatenate(rows, axis=0), preferred_element_type=f32
        )

    width = w_ref.shape[0]
    trips = (n + FWD_SLOTS - 1) // FWD_SLOTS
    af = lax.fori_loop(0, trips, forward, jnp.zeros((tile, width), f32)).astype(bf16)
    pre = jnp.dot(af, w_ref[...], preferred_element_type=f32)
    sig = jax.nn.sigmoid(pre)
    out_ref[...] = (pre * sig).astype(bf16)
    g = (cot_ref[...].astype(f32) * sig * (1.0 + pre * (1.0 - sig))).astype(bf16)
    wg_ref[...] += lax.dot_general(af, g, (((0,), (0,)), ((), ())), preferred_element_type=f32)
    gwt = lax.dot_general(
        w_ref[...], g, (((1,), (1,)), ((), ())), preferred_element_type=f32
    ).astype(bf16)

    def backward(i, _):
        k0 = i * BWD_SLOTS
        r = jnp.dot(gwt, lanes(k0, BWD_SLOTS), preferred_element_type=f32)
        for j in range(BWD_SLOTS):
            acc[idx[t, k0 + j]] += r[:, j * tile : (j + 1) * tile]
        return 0

    lax.fori_loop(0, (n + BWD_SLOTS - 1) // BWD_SLOTS, backward, 0)

    @pl.when(t == pl.num_programs(0) - 1)
    def _():
        def copy(slot, out, at):
            return pltpu.make_async_copy(stage.at[slot], out.at[pl.ds(at, chunk)], out_sem.at[slot])

        done = 0
        for out in outs:
            steps = out.shape[0] // chunk

            def emit(i, _, out=out, done=done):
                number = done + i
                slot = lax.rem(number, STAGES)

                @pl.when(number >= STAGES)
                def _():
                    copy(slot, out, 0).wait()

                stage[slot] = acc[pl.ds(number * chunk, chunk)].astype(bf16)
                copy(slot, out, i * chunk).start()
                return 0

            lax.fori_loop(0, steps, emit, 0)
            done += steps
        for slot in range(STAGES):
            copy(slot, outs[0], 0).wait()


def layer(idx, cnt, tile_values, parts, weight, cotangent, groups):
    nt, slots, tile, _ = tile_values.shape
    width = weight.shape[0]
    n_win = 2 * sum(groups)
    chunk = math.gcd(*groups)
    anywhere = pl.BlockSpec(memory_space=pl.ANY)
    return pl.pallas_call(
        functools.partial(kernel, len(parts), 2 * len(groups), chunk),
        grid_spec=pltpu.PrefetchScalarGridSpec(
            num_scalar_prefetch=2,
            grid=(nt,),
            in_specs=[pl.BlockSpec((1, slots, tile, tile), lambda t, *_: (t, 0, 0, 0))]
            + [anywhere] * len(parts)
            + [
                pl.BlockSpec((width, width), lambda t, *_: (0, 0)),
                pl.BlockSpec((tile, width), lambda t, *_: (t, 0)),
            ],
            out_specs=[
                pl.BlockSpec((tile, width), lambda t, *_: (t, 0)),
                pl.BlockSpec((width, width), lambda t, *_: (0, 0)),
            ]
            + [anywhere] * (2 * len(groups)),
            scratch_shapes=[
                pltpu.VMEM((n_win * tile, width), bf16),
                pltpu.VMEM((n_win, width, tile), f32),
                pltpu.VMEM((STAGES, chunk, width, tile), bf16),
                pltpu.SemaphoreType.DMA((len(parts),)),
                pltpu.SemaphoreType.DMA((STAGES,)),
            ],
        ),
        out_shape=[
            jax.ShapeDtypeStruct((nt * tile, width), bf16),
            jax.ShapeDtypeStruct((width, width), f32),
        ]
        + [jax.ShapeDtypeStruct((g, width, tile), bf16) for _ in range(2) for g in groups],
        compiler_params=pltpu.CompilerParams(vmem_limit_bytes=60 * 2**20),
    )(idx, cnt, tile_values, *parts, weight, cotangent)


def near(group, rep, axis, step, n_rows, n_rep):
    if axis == "z":
        return (group + step) % n_rows * n_rep + rep
    return group * n_rep + (rep + 2 * step) % n_rep


def moved(x, moves, back=False):
    n_rows, n_rep = lax.axis_size("rows"), lax.axis_size("rep")
    pairs = []
    for group in range(n_rows):
        for rep in range(n_rep):
            if moves[rep % 2]:
                source = near(group, rep, *moves[rep % 2], n_rows, n_rep)
                pairs.append((source, group * n_rep + rep))
    if back:
        pairs = [(target, source) for source, target in pairs]
    return lax.ppermute(x, ("rows", "rep"), pairs)


FIRST_UP, FIRST_DOWN = (("z", -1), ("y", 1)), (("z", 1), ("y", -1))
HALF_UP, HALF_DOWN = (None, ("y", 1)), (None, ("y", -1))
NEXT_UP, NEXT_DOWN = (("y", 1), ("z", -1)), (("y", -1), ("z", 1))


def from_core(x):
    return lax.ppermute(x, "rep", [(i, i ^ 1) for i in range(lax.axis_size("rep"))])


def gather(features, core):
    rows = features.shape[0]
    half = rows // 2
    up, down = moved(features, FIRST_UP), moved(features, FIRST_DOWN)
    near3 = jnp.concatenate([features, up, down])
    far = jnp.concatenate([moved(up[:half], HALF_UP), moved(down[half:], HALF_DOWN)])
    up, down = moved(near3, NEXT_UP), moved(near3, NEXT_DOWN)
    crossing = jnp.concatenate([far, far[:half]])
    last_up = moved(jnp.where(core == 0, up[: 3 * half], crossing), NEXT_UP)
    last_down = moved(jnp.where(core == 0, down[3 * half :], crossing), NEXT_DOWN)
    mine = [last_up, last_down, up, down, far, near3]
    return mine + [from_core(x) for x in mine]


def scatter(mine, other, own, core):
    last, middle, first = (
        m.astype(f32) + from_core(o).astype(f32) for m, o in zip(mine, other)
    )
    half = own // 2
    cut = 3 * half
    last = last.astype(bf16)
    last_up = moved(last[:cut], NEXT_UP, back=True).astype(f32)
    last_down = moved(last[cut:], NEXT_DOWN, back=True).astype(f32)
    up, down = middle[: 2 * cut], middle[2 * cut :]
    along = (core == 0).astype(f32)
    up = jnp.concatenate([up[:cut] + along * last_up, up[cut:]]).astype(bf16)
    down = jnp.concatenate([down[:cut], down[cut:] + along * last_down]).astype(bf16)
    far = (first[:own] + (1.0 - along) * (last_up[:own] + last_down[:own])).astype(bf16)
    half_up = moved(far[:half], HALF_UP, back=True).astype(f32)
    half_down = moved(far[half:], HALF_DOWN, back=True).astype(f32)
    near3 = (
        first[own:]
        + moved(up, NEXT_UP, back=True).astype(f32)
        + moved(down, NEXT_DOWN, back=True).astype(f32)
    )
    home, up, down = near3[:own], near3[own : 2 * own], near3[2 * own :]
    up = jnp.concatenate([up[:half] + half_up, up[half:]]).astype(bf16)
    down = jnp.concatenate([down[:half], down[half:] + half_down]).astype(bf16)
    return (
        home
        + moved(up, FIRST_UP, back=True).astype(f32)
        + moved(down, FIRST_DOWN, back=True).astype(f32)
    )


def weight_sum(term, core):
    height = term.shape[0] // 2
    low, high = term[:height], term[height:]
    x = jnp.where(core == 0, low, high) + from_core(jnp.where(core == 0, high, low))
    for axis, first in (("rep", 2), ("rows", 1)):
        bit = first
        while bit < lax.axis_size(axis):
            pairs = [(i, i ^ bit) for i in range(lax.axis_size(axis))]
            x = x + lax.ppermute(x, axis, pairs)
            bit *= 2
    other = from_core(x)
    return jnp.where(core == 0, jnp.concatenate([x, other]), jnp.concatenate([other, x]))


def local(features, weight, tile_values, tile_cols, tile_live, cotangent):
    n_rows, n_rep = lax.axis_size("rows"), lax.axis_size("rep")
    rep = lax.axis_index("rep")
    node_dev, width = features.shape
    tile = tile_values.shape[2]
    own = node_dev // tile
    group_tiles = own * n_rep
    core = rep % 2
    plans = [layout(own, c) for c in range(2)]
    groups = [len(keys) for keys in plans[0]]
    table = np.zeros((2, 3, n_rep // 2, own), np.int32)
    for c, plan in enumerate(plans):
        for at, key in enumerate(sum(plan, [])):
            if key:
                table[(c, *key)] = at
    place = jnp.mod(tile_cols // group_tiles - lax.axis_index("rows") + 1, n_rows)
    inner = tile_cols % group_tiles
    owner = inner // own
    dy = jnp.mod(owner // 2 - rep // 2, n_rep // 2)
    key = (((owner % 2) * 3 + place) * (n_rep // 2) + dy) * own + inner % own
    hit = key[:, :, None] == jnp.arange(table.size, dtype=jnp.int32)
    at = jnp.sum(jnp.where(hit, jnp.asarray(table.reshape(-1)), 0), axis=2)
    idx = jnp.mod(owner + rep, 2) * sum(groups) + at
    cnt = jnp.sum(tile_live, axis=1)

    parts = gather(features, core)
    output, term, *grads = layer(idx, cnt, tile_values, parts, weight, cotangent, groups)
    total = scatter(grads[: len(groups)], grads[len(groups) :], own, core)
    weight_grad = weight_sum(term, core)
    feature_grad = jnp.swapaxes(total, 1, 2).reshape(node_dev, width).astype(bf16)
    return (output, feature_grad, weight_grad)


def solution(mesh):
    placed = (
        P(("rows", "rep"), None),
        P(),
        P(("rows", "rep"), None, None, None),
        P(("rows", "rep"), None),
        P(("rows", "rep"), None),
        P(("rows", "rep"), None),
    )
    return jax.shard_map(
        local,
        mesh=mesh,
        in_specs=placed,
        out_specs=(P(("rows", "rep"), None), P(("rows", "rep"), None), P()),
        check_vma=False,
    )
```

time: 216 us -> 194 us (0.90)
  waiting for transfers between devices: 101 us -> 85.2 us
  starting transfers between devices: 63 us -> 53 us
  other arithmetic: 13.7 us -> 17.1 us
    ppermute x38 -> x22, waiting for transfers between devices: 98.2 us -> 74.8 us  [the longest x6 43.3 us: weight_sum(): x = x + lax.ppermute(x, axis, pairs)]
    ppermute x38 -> x22, starting transfers between devices: 59.6 us -> 38 us  [the longest x16 31 us: moved(): return lax.ppermute(x, ('rows', 'rep'), pairs)]
    ppermute x21 -> x11, starting transfers between devices: 3.42 us -> 15.1 us  [from_core(): lax.ppermute(x, 'rep', [(i, i ^ 1) for i in range(lax.axis_size('rep'))])]
    ppermute x21 -> x11, waiting for transfers between devices: 2.55 us -> 10.4 us  [from_core(): lax.ppermute(x, 'rep', [(i, i ^ 1) for i in range(lax.axis_size('rep'))])]
    another operation x4, other arithmetic: 2.77 us -> 6.44 us
    convert_element_type x3 -> x4, other arithmetic: 5.96 us -> 2.32 us  [the longest x1 1.89 us: scatter(): last = last.astype(bf16)]
  transfers between devices with their start and end apart: 59 -> 33, of which waited for: 25 -> 15; matrix products, arithmetic and copies ran while one was open for 7% -> 12% of each run, Pallas kernels for 0% -> 0%
where the time goes in v3:
time: 194 us; the launch traced here: 193 us
  waiting for transfers between devices  85.2 us (44%)
  starting transfers between devices  53 us (27%)
  Pallas kernels  28.7 us (15%)
  other arithmetic  17.1 us (9%)
  local copies, waits for them, and re-layouts  7.5 us (4%)
    ppermute x6, waiting for transfers between devices, weight_sum(): x = x + lax.ppermute(x, axis, pairs)  43.3 us
    ppermute x16, waiting for transfers between devices, moved(): return lax.ppermute(x, ('rows', 'rep'), pairs)  31.5 us
    ppermute x16, starting transfers between devices, moved(): return lax.ppermute(x, ('rows', 'rep'), pairs)  31 us
    pallas_call x1, Pallas kernels, layer(): pl.pallas_call(functools.partial(kernel, len(parts), 2 * len(groups), chu...  28.7 us
    ppermute x11, starting transfers between devices, from_core(): lax.ppermute(x, 'rep', [(i, i ^ 1) for i in range(lax.axis_size('rep'))])  15.1 us
    ppermute x11, waiting for transfers between devices, from_core(): lax.ppermute(x, 'rep', [(i, i ^ 1) for i in range(lax.axis_size('rep'))])  10.4 us
    ppermute x6, starting transfers between devices, weight_sum(): x = x + lax.ppermute(x, axis, pairs)  6.94 us
    another operation x4, other arithmetic  6.44 us
  transfers between devices with their start and end apart: 33, of which 15 were waited for; matrix products, arithmetic and copies ran while one was open for 12% of the time, Pallas kernels for 0%

profile of v3, /device:TPU:0, one launch (start us, length us, event | category | flops | bytes accessed | tf_op | source)
XLA Modules:
  0.0 192.6 jit_solution(12227881192215568987)
XLA Ops:
  2.7 4.4 %collective-permute-start.1 = (bf16[1024,256]{1,0:T(8,128)(2,1)}, bf16[1024,256]{1,0:T(8,128)(2,1)S(1)}, u32[]{:S(2)}, u32[]{:S(2)}) collective-permute-start(bf16[1024,256]{1,0:T(8,128)(2,1)} %param.7), channel_id=1, source_target_pairs={{8,0},{7,1},{10,2},{1,3},{12,4},{3,5},{14,6},{5,7},{16,8},{15,9},{... | collective-permute-start | bytes 1572872 | tf_op jit(solution)/shard_map/ppermute | solution.py:184
  9.0 5.4 %collective-permute-done = bf16[1024,256]{1,0:T(8,128)(2,1)S(1)} collective-permute-done((bf16[1024,256]{1,0:T(8,128)(2,1)}, bf16[1024,256]{1,0:T(8,128)(2,1)S(1)}, u32[]{:S(2)}, u32[]{:S(2)}) %collective-permute-start) | collective-permute-done | bytes 524320 | tf_op jit(solution)/shard_map/ppermute | solution.py:184
  16.1 3.0 %collective-permute-start.2 = (bf16[3072,256]{1,0:T(8,128)(2,1)}, bf16[3072,256]{1,0:T(8,128)(2,1)S(1)}, u32[]{:S(2)}, u32[]{:S(2)}) collective-permute-start(bf16[3072,256]{1,0:T(8,128)(2,1)} %constant_dynamic-update-slice_fusion.refs_5_), channel_id=1, source_target_pairs={{2,0},{121,1},{4,2},{123,3},{6,4},{125,5},{0,6},{127,7},{10,8},{1,... | collective-permute-start | bytes 4718600 | tf_op jit(solution)/shard_map/ppermute | solution.py:184
  22.6 4.1 %collective-permute-start.13 = (bf16[3072,256]{1,0:T(8,128)(2,1)}, bf16[3072,256]{1,0:T(8,128)(2,1)}, u32[]{:S(2)}, u32[]{:S(2)}) collective-permute-start(bf16[3072,256]{1,0:T(8,128)(2,1)} %constant_dynamic-update-slice_fusion.refs_5_), channel_id=1, source_target_pairs={{0,1},{1,0},{2,3},{3,2},{4,5},{5,4},{6,7},{7,6},{8,9},{9,8},{10,11... | collective-permute-start | bytes 4718600 | tf_op jit(solution)/shard_map/ppermute | solution.py:193
  27.7 9.1 %collective-permute-start.12 = (bf16[1024,256]{1,0:T(8,128)(2,1)S(1)}, bf16[1024,256]{1,0:T(8,128)(2,1)S(1)}, u32[]{:S(2)}, u32[]{:S(2)}) collective-permute-start(bf16[1024,256]{1,0:T(8,128)(2,1)S(1)} %get-tuple-element.37.refs_4_), channel_id=1, source_target_pairs={{0,1},{1,0},{2,3},{3,2},{4,5},{5,4},{6,7},{7,6},{8,9},{9,8},{10,11... | collective-permute-start | bytes 1572872 | tf_op jit(solution)/shard_map/ppermute | solution.py:193
  36.9 3.2 %collective-permute-done.2.refs_2_ = bf16[3072,256]{1,0:T(8,128)(2,1)S(1)} collective-permute-done((bf16[3072,256]{1,0:T(8,128)(2,1)}, bf16[3072,256]{1,0:T(8,128)(2,1)S(1)}, u32[]{:S(2)}, u32[]{:S(2)}) %collective-permute-start.2) | collective-permute-done | bytes 1572896 | tf_op jit(solution)/shard_map/ppermute | solution.py:184
  40.1 3.6 %collective-permute-done.6.refs_3_ = bf16[3072,256]{1,0:T(8,128)(2,1)S(1)} collective-permute-done((bf16[3072,256]{1,0:T(8,128)(2,1)}, bf16[3072,256]{1,0:T(8,128)(2,1)S(1)}, u32[]{:S(2)}, u32[]{:S(2)}) %collective-permute-start.6) | collective-permute-done | bytes 1572896 | tf_op jit(solution)/shard_map/ppermute | solution.py:184
  46.6 9.5 %collective-permute-done.5.refs_0_ = bf16[1536,256]{1,0:T(8,128)(2,1)} collective-permute-done((bf16[1536,256]{1,0:T(8,128)(2,1)S(1)}, bf16[1536,256]{1,0:T(8,128)(2,1)}, u32[]{:S(2)}, u32[]{:S(2)}) %collective-permute-start.5) | collective-permute-done | bytes 786464 | tf_op jit(solution)/shard_map/ppermute | solution.py:184
  60.0 28.7 %shard_map.94 = (bf16[1024,256]{1,0:T(8,128)(2,1)}, f32[256,256]{1,0:T(8,128)}, bf16[24,256,128]{2,1,0:T(8,128)(2,1)}, bf16[48,256,128]{2,1,0:T(8,128)(2,1)}, bf...) custom-call(s32[8,48]{1,0:T(8,128)} %fusion.13.idx, ...), custom_call_target="tpu_custom_call" | custom-call | tf_op jit(solution)/shard_map/pallas_call | solution.py:135
  90.9 8.1 %collective-permute-done.16 = bf16[24,256,128]{2,1,0:T(8,128)(2,1)S(1)} collective-permute-done((bf16[24,256,128]{2,1,0:T(8,128)(2,1)}, bf16[24,256,128]{2,1,0:T(8,128)(2,1)S(1)}, u32[]{:S(2)}, u32[]{:S(2)}) %collective-permute-start.16) | collective-permute-done | bytes 1572896 | tf_op jit(solution)/shard_map/ppermute | solution.py:193
  101.0 9.0 %collective-permute-start.17 = (bf16[12,256,128]{2,1,0:T(8,128)(2,1)S(1)}, bf16[12,256,128]{2,1,0:T(8,128)(2,1)S(1)}, u32[]{:S(2)}, u32[]{:S(2)}) collective-permute-start(bf16[12,256,128]{2,1,0:T(8,128)(2,1)S(1)} %get-tuple-element.31), channel_id=1, source_target_pairs={{0,2},{1,121},{2,4},{3,123},{4,6},{5,125},{6,0},{7,127},{8,10},{9,... | collective-permute-start | bytes 2359304 | tf_op jit(solution)/shard_map/ppermute | solution.py:184
  110.0 3.2 %fusion.31 = (bf16[48,256,128]{2,1,0:T(8,128)(2,1)S(1)}, f32[48,256,128]{2,1,0:T(8,128)S(1)}) fusion(bf16[48,256,128]{2,1,0:T(8,128)(2,1)} %collective-permute-done.15, bf16[48,256,128]{2,1,0:T(8,128)(2,1)S(1)} %copy-done.2), kind=kLoop, calls=%fused_computation.87 | loop fusion | flops 6291456 | bytes 15728640 | tf_op jit(solution)/shard_map/convert.11
  113.4 6.1 %collective-permute-done.17 = bf16[12,256,128]{2,1,0:T(8,128)(2,1)S(1)} collective-permute-done((bf16[12,256,128]{2,1,0:T(8,128)(2,1)S(1)}, bf16[12,256,128]{2,1,0:T(8,128)(2,1)S(1)}, u32[]{:S(2)}, u32[]{:S(2)}) %collective-permute-start.17) | collective-permute-done | bytes 786464 | tf_op jit(solution)/shard_map/ppermute | solution.py:184
  119.5 2.5 %collective-permute-done.19 = bf16[12,256,128]{2,1,0:T(8,128)(2,1)S(1)} collective-permute-done((bf16[12,256,128]{2,1,0:T(8,128)(2,1)S(1)}, bf16[12,256,128]{2,1,0:T(8,128)(2,1)S(1)}, u32[]{:S(2)}, u32[]{:S(2)}) %collective-permute-start.19) | collective-permute-done | bytes 786464 | tf_op jit(solution)/shard_map/ppermute | solution.py:184
  124.1 3.2 %collective-permute-start.20 = (bf16[24,256,128]{2,1,0:T(8,128)(2,1)}, bf16[24,256,128]{2,1,0:T(8,128)(2,1)}, u32[]{:S(2)}, u32[]{:S(2)}) collective-permute-start(bf16[24,256,128]{2,1,0:T(8,128)(2,1)} %pad_maximum_fusion.1), channel_id=1, source_target_pairs={{0,6},{1,9},{2,0},{3,11},{4,2},{5,13},{6,4},{7,15},{8,14},{9,17},{... | collective-permute-start | bytes 4718600 | tf_op jit(solution)/shard_map/ppermute | solution.py:184
  127.3 21.6 %collective-permute-done.26 = f32[128,256]{1,0:T(8,128)S(1)} collective-permute-done((f32[128,256]{1,0:T(8,128)S(1)}, f32[128,256]{1,0:T(8,128)S(1)}, u32[]{:S(2)}, u32[]{:S(2)}) %collective-permute-start.26) | collective-permute-done | bytes 131104 | tf_op jit(solution)/shard_map/ppermute | solution.py:249
  148.9 2.7 %collective-permute-start.27 = (f32[128,256]{1,0:T(8,128)S(1)}, f32[128,256]{1,0:T(8,128)S(1)}, u32[]{:S(2)}, u32[]{:S(2)}) collective-permute-start(f32[128,256]{1,0:T(8,128)S(1)} %add.144), channel_id=1, source_target_pairs={{0,4},{1,5},{2,6},{3,7},{4,0},{5,1},{6,2},{7,3},{8,12},{9,13},{10,... | collective-permute-start | bytes 393224 | tf_op jit(solution)/shard_map/ppermute | solution.py:249
  151.6 3.9 %collective-permute-done.27 = f32[128,256]{1,0:T(8,128)S(1)} collective-permute-done((f32[128,256]{1,0:T(8,128)S(1)}, f32[128,256]{1,0:T(8,128)S(1)}, u32[]{:S(2)}, u32[]{:S(2)}) %collective-permute-start.27) | collective-permute-done | bytes 131104 | tf_op jit(solution)/shard_map/ppermute | solution.py:249
  155.8 5.0 %collective-permute-done.28 = f32[128,256]{1,0:T(8,128)S(1)} collective-permute-done((f32[128,256]{1,0:T(8,128)S(1)}, f32[128,256]{1,0:T(8,128)S(1)}, u32[]{:S(2)}, u32[]{:S(2)}) %collective-permute-start.28) | collective-permute-done | bytes 131104 | tf_op jit(solution)/shard_map/ppermute | solution.py:249
  162.4 2.9 %convert_add_fusion.1 = f32[32,256,128]{2,1,0:T(8,128)S(1)} fusion(bf16[32,256,128]{2,1,0:T(8,128)(2,1)} %collective-permute-done.14, bf16[32,256,128]{2,1,0:T(8,128)(2,1)} %get-tuple-element.12), kind=kLoop, calls=%fused_computation.1 | loop fusion | flops 3145728 | bytes 8388608 | tf_op jit(solution)/shard_map/add | solution.py:212
  167.2 2.7 %fusion.32 = (bf16[24,256,128]{2,1,0:T(8,128)(2,1)S(1)}, f32[24,256,128]{2,1,0:T(8,128)S(1)}) fusion(bf16[24,256,128]{2,1,0:T(8,128)(2,1)} %collective-permute-done.20, bf16[24,256,128]{2,1,0:T(8,128)(2,1)} %collective-permute-done.18, f32[32,256,128]{2,1,0:T(8,128)S(1)} %convert_add_fusion.1), kind=kLoop, calls=%fused_computation.88 | loop fusion | flops 3932160 | bytes 11010048 | tf_op jit(solution)/shard_map/convert.5
  170.2 3.7 %collective-permute-start.22 = (bf16[8,256,128]{2,1,0:T(8,128)(2,1)S(1)}, bf16[8,256,128]{2,1,0:T(8,128)(2,1)S(1)}, u32[]{:S(2)}, u32[]{:S(2)}) collective-permute-start(bf16[8,256,128]{2,1,0:T(8,128)(2,1)S(1)} %pad_maximum_fusion.2), channel_id=1, source_target_pairs={{0,120},{1,3},{2,122},{3,5},{4,124},{5,7},{6,126},{7,1},{8,0},{9,1... | collective-permute-start | bytes 1572872 | tf_op jit(solution)/shard_map/ppermute | solution.py:184
  174.1 8.5 %collective-permute-done.30 = f32[128,256]{1,0:T(8,128)S(1)} collective-permute-done((f32[128,256]{1,0:T(8,128)S(1)}, f32[128,256]{1,0:T(8,128)S(1)}, u32[]{:S(2)}, u32[]{:S(2)}) %collective-permute-start.30) | collective-permute-done | bytes 131104 | tf_op jit(solution)/shard_map/ppermute | solution.py:249
  184.8 4.4 %collective-permute-done.31 = f32[128,256]{1,0:T(8,128)S(1)} collective-permute-done((f32[128,256]{1,0:T(8,128)S(1)}, f32[128,256]{1,0:T(8,128)S(1)}, u32[]{:S(2)}, u32[]{:S(2)}) %collective-permute-start.31) | collective-permute-done | bytes 131104 | tf_op jit(solution)/shard_map/ppermute | solution.py:249
  (102 shorter events, 33.2 us)
Async XLA Ops:
  0.6 13.8 %collective-permute-start = (bf16[1024,256]{1,0:T(8,128)(2,1)}, bf16[1024,256]{1,0:T(8,128)(2,1)S(1)}, u32[]{:S(2)}, u32[]{:S(2)}) collective-permute-start(bf16[1024,256]{1,0:T(8,128)(2,1)} %param.7), channel_id=1, source_target_pairs={{120,0},{3,1},{122,2},{5,3},{124,4},{7,5},{126,6},{1,7},{0,8},{11,... | collective-permute-start | bytes 1572872 | tf_op jit(solution)/shard_map/ppermute | solution.py:184
  2.7 12.5 %collective-permute-start.1 = (bf16[1024,256]{1,0:T(8,128)(2,1)}, bf16[1024,256]{1,0:T(8,128)(2,1)S(1)}, u32[]{:S(2)}, u32[]{:S(2)}) collective-permute-start(bf16[1024,256]{1,0:T(8,128)(2,1)} %param.7), channel_id=1, source_target_pairs={{8,0},{7,1},{10,2},{1,3},{12,4},{3,5},{14,6},{5,7},{16,8},{15,9},{... | collective-permute-start | bytes 1572872 | tf_op jit(solution)/shard_map/ppermute | solution.py:184
  16.1 24.1 %collective-permute-start.2 = (bf16[3072,256]{1,0:T(8,128)(2,1)}, bf16[3072,256]{1,0:T(8,128)(2,1)S(1)}, u32[]{:S(2)}, u32[]{:S(2)}) collective-permute-start(bf16[3072,256]{1,0:T(8,128)(2,1)} %constant_dynamic-update-slice_fusion.refs_5_), channel_id=1, source_target_pairs={{2,0},{121,1},{4,2},{123,3},{6,4},{125,5},{0,6},{127,7},{10,8},{1,... | collective-permute-start | bytes 4718600 | tf_op jit(solution)/shard_map/ppermute | solution.py:184
  19.1 24.6 %collective-permute-start.6 = (bf16[3072,256]{1,0:T(8,128)(2,1)}, bf16[3072,256]{1,0:T(8,128)(2,1)S(1)}, u32[]{:S(2)}, u32[]{:S(2)}) collective-permute-start(bf16[3072,256]{1,0:T(8,128)(2,1)} %constant_dynamic-update-slice_fusion.refs_5_), channel_id=1, source_target_pairs={{6,0},{9,1},{0,2},{11,3},{2,4},{13,5},{4,6},{15,7},{14,8},{17,9},{... | collective-permute-start | bytes 4718600 | tf_op jit(solution)/shard_map/ppermute | solution.py:184
  19.8 6.9 %collective-permute-start.3 = (bf16[512,256]{1,0:T(8,128)(2,1)}, bf16[512,256]{1,0:T(8,128)(2,1)S(1)}, u32[]{:S(2)}, u32[]{:S(2)}) collective-permute-start(bf16[512,256]{1,0:T(8,128)(2,1)} %slice.109), channel_id=1, source_target_pairs={{3,1},{5,3},{7,5},{1,7},{11,9},{13,11},{15,13},{9,15},{19,17},{21,... | collective-permute-start | bytes 786440 | tf_op jit(solution)/shard_map/ppermute | solution.py:184
  22.6 36.5 %collective-permute-start.13 = (bf16[3072,256]{1,0:T(8,128)(2,1)}, bf16[3072,256]{1,0:T(8,128)(2,1)}, u32[]{:S(2)}, u32[]{:S(2)}) collective-permute-start(bf16[3072,256]{1,0:T(8,128)(2,1)} %constant_dynamic-update-slice_fusion.refs_5_), channel_id=1, source_target_pairs={{0,1},{1,0},{2,3},{3,2},{4,5},{5,4},{6,7},{7,6},{8,9},{9,8},{10,11... | collective-permute-start | bytes 4718600 | tf_op jit(solution)/shard_map/ppermute | solution.py:193
  27.7 18.2 %collective-permute-start.12 = (bf16[1024,256]{1,0:T(8,128)(2,1)S(1)}, bf16[1024,256]{1,0:T(8,128)(2,1)S(1)}, u32[]{:S(2)}, u32[]{:S(2)}) collective-permute-start(bf16[1024,256]{1,0:T(8,128)(2,1)S(1)} %get-tuple-element.37.refs_4_), channel_id=1, source_target_pairs={{0,1},{1,0},{2,3},{3,2},{4,5},{5,4},{6,7},{7,6},{8,9},{9,8},{10,11... | collective-permute-start | bytes 1572872 | tf_op jit(solution)/shard_map/ppermute | solution.py:193
  43.9 12.2 %collective-permute-start.5 = (bf16[1536,256]{1,0:T(8,128)(2,1)S(1)}, bf16[1536,256]{1,0:T(8,128)(2,1)}, u32[]{:S(2)}, u32[]{:S(2)}) collective-permute-start(bf16[1536,256]{1,0:T(8,128)(2,1)S(1)} %get-tuple-element.34), channel_id=1, source_target_pairs={{2,0},{121,1},{4,2},{123,3},{6,4},{125,5},{0,6},{127,7},{10,8},{1,... | collective-permute-start | bytes 2359304 | tf_op jit(solution)/shard_map/ppermute | solution.py:184
  44.0 13.4 %collective-permute-start.7 = (bf16[1536,256]{1,0:T(8,128)(2,1)S(1)}, bf16[1536,256]{1,0:T(8,128)(2,1)}, u32[]{:S(2)}, u32[]{:S(2)}) collective-permute-start(bf16[1536,256]{1,0:T(8,128)(2,1)S(1)} %get-tuple-element.33), channel_id=1, source_target_pairs={{6,0},{9,1},{0,2},{11,3},{2,4},{13,5},{4,6},{15,7},{14,8},{17,9},{... | collective-permute-start | bytes 2359304 | tf_op jit(solution)/shard_map/ppermute | solution.py:184
  46.0 14.0 %collective-permute-start.10 = (bf16[3072,256]{1,0:T(8,128)(2,1)S(1)}, bf16[3072,256]{1,0:T(8,128)(2,1)}, u32[]{:S(2)}, u32[]{:S(2)}) collective-permute-start(bf16[3072,256]{1,0:T(8,128)(2,1)S(1)} %collective-permute-done.2.refs_2_), channel_id=1, source_target_pairs={{0,1},{1,0},{2,3},{3,2},{4,5},{5,4},{6,7},{7,6},{8,9},{9,8},{10,11... | collective-permute-start | bytes 4718600 | tf_op jit(solution)/shard_map/ppermute | solution.py:193
  46.0 14.0 %collective-permute-start.11 = (bf16[3072,256]{1,0:T(8,128)(2,1)S(1)}, bf16[3072,256]{1,0:T(8,128)(2,1)}, u32[]{:S(2)}, u32[]{:S(2)}) collective-permute-start(bf16[3072,256]{1,0:T(8,128)(2,1)S(1)} %collective-permute-done.6.refs_3_), channel_id=1, source_target_pairs={{0,1},{1,0},{2,3},{3,2},{4,5},{5,4},{6,7},{7,6},{8,9},{9,8},{10,11... | collective-permute-start | bytes 4718600 | tf_op jit(solution)/shard_map/ppermute | solution.py:193
  88.7 21.3 %collective-permute-start.15 = (bf16[48,256,128]{2,1,0:T(8,128)(2,1)}, bf16[48,256,128]{2,1,0:T(8,128)(2,1)}, u32[]{:S(2)}, u32[]{:S(2)}) collective-permute-start(bf16[48,256,128]{2,1,0:T(8,128)(2,1)} %get-tuple-element.15), channel_id=1, source_target_pairs={{0,1},{1,0},{2,3},{3,2},{4,5},{5,4},{6,7},{7,6},{8,9},{9,8},{10,11... | collective-permute-start | bytes 9437192 | tf_op jit(solution)/shard_map/ppermute | solution.py:193
  88.8 10.2 %collective-permute-start.16 = (bf16[24,256,128]{2,1,0:T(8,128)(2,1)}, bf16[24,256,128]{2,1,0:T(8,128)(2,1)S(1)}, u32[]{:S(2)}, u32[]{:S(2)}) collective-permute-start(bf16[24,256,128]{2,1,0:T(8,128)(2,1)} %get-tuple-element.17), channel_id=1, source_target_pairs={{0,1},{1,0},{2,3},{3,2},{4,5},{5,4},{6,7},{7,6},{8,9},{9,8},{10,11... | collective-permute-start | bytes 4718600 | tf_op jit(solution)/shard_map/ppermute | solution.py:193
  90.3 36.9 %collective-permute-start.25 = (f32[128,256]{1,0:T(8,128)S(1)}, f32[128,256]{1,0:T(8,128)S(1)}, u32[]{:S(2)}, u32[]{:S(2)}) collective-permute-start(f32[128,256]{1,0:T(8,128)S(1)} %slice_select_fusion.2), channel_id=1, source_target_pairs={{0,1},{1,0},{2,3},{3,2},{4,5},{5,4},{6,7},{7,6},{8,9},{9,8},{10,11... | collective-permute-start | bytes 393224 | tf_op jit(solution)/shard_map/ppermute | solution.py:193
  90.5 72.0 %collective-permute-start.14 = (bf16[32,256,128]{2,1,0:T(8,128)(2,1)}, bf16[32,256,128]{2,1,0:T(8,128)(2,1)}, u32[]{:S(2)}, u32[]{:S(2)}) collective-permute-start(bf16[32,256,128]{2,1,0:T(8,128)(2,1)} %get-tuple-element.13), channel_id=1, source_target_pairs={{0,1},{1,0},{2,3},{3,2},{4,5},{5,4},{6,7},{7,6},{8,9},{9,8},{10,11... | collective-permute-start | bytes 6291464 | tf_op jit(solution)/shard_map/ppermute | solution.py:193
  101.0 18.5 %collective-permute-start.17 = (bf16[12,256,128]{2,1,0:T(8,128)(2,1)S(1)}, bf16[12,256,128]{2,1,0:T(8,128)(2,1)S(1)}, u32[]{:S(2)}, u32[]{:S(2)}) collective-permute-start(bf16[12,256,128]{2,1,0:T(8,128)(2,1)S(1)} %get-tuple-element.31), channel_id=1, source_target_pairs={{0,2},{1,121},{2,4},{3,123},{4,6},{5,125},{6,0},{7,127},{8,10},{9,... | collective-permute-start | bytes 2359304 | tf_op jit(solution)/shard_map/ppermute | solution.py:184
  110.0 12.0 %collective-permute-start.19 = (bf16[12,256,128]{2,1,0:T(8,128)(2,1)S(1)}, bf16[12,256,128]{2,1,0:T(8,128)(2,1)S(1)}, u32[]{:S(2)}, u32[]{:S(2)}) collective-permute-start(bf16[12,256,128]{2,1,0:T(8,128)(2,1)S(1)} %get-tuple-element.32), channel_id=1, source_target_pairs={{0,6},{1,9},{2,0},{3,11},{4,2},{5,13},{6,4},{7,15},{8,14},{9,17},{... | collective-permute-start | bytes 2359304 | tf_op jit(solution)/shard_map/ppermute | solution.py:184
  122.6 44.6 %collective-permute-start.18 = (bf16[24,256,128]{2,1,0:T(8,128)(2,1)S(1)}, bf16[24,256,128]{2,1,0:T(8,128)(2,1)}, u32[]{:S(2)}, u32[]{:S(2)}) collective-permute-start(bf16[24,256,128]{2,1,0:T(8,128)(2,1)S(1)} %pad_maximum_fusion), channel_id=1, source_target_pairs={{0,2},{1,121},{2,4},{3,123},{4,6},{5,125},{6,0},{7,127},{8,10},{9,... | collective-permute-start | bytes 4718600 | tf_op jit(solution)/shard_map/ppermute | solution.py:184
  124.1 43.2 %collective-permute-start.20 = (bf16[24,256,128]{2,1,0:T(8,128)(2,1)}, bf16[24,256,128]{2,1,0:T(8,128)(2,1)}, u32[]{:S(2)}, u32[]{:S(2)}) collective-permute-start(bf16[24,256,128]{2,1,0:T(8,128)(2,1)} %pad_maximum_fusion.1), channel_id=1, source_target_pairs={{0,6},{1,9},{2,0},{3,11},{4,2},{5,13},{6,4},{7,15},{8,14},{9,17},{... | collective-permute-start | bytes 4718600 | tf_op jit(solution)/shard_map/ppermute | solution.py:184
  127.2 21.6 %collective-permute-start.26 = (f32[128,256]{1,0:T(8,128)S(1)}, f32[128,256]{1,0:T(8,128)S(1)}, u32[]{:S(2)}, u32[]{:S(2)}) collective-permute-start(f32[128,256]{1,0:T(8,128)S(1)} %select_add_fusion), channel_id=1, source_target_pairs={{0,2},{1,3},{2,0},{3,1},{4,6},{5,7},{6,4},{7,5},{8,10},{9,11},{10,... | collective-permute-start | bytes 393224 | tf_op jit(solution)/shard_map/ppermute | solution.py:249
  160.7 13.3 %collective-permute-start.29 = (f32[128,256]{1,0:T(8,128)S(1)}, f32[128,256]{1,0:T(8,128)S(1)}, u32[]{:S(2)}, u32[]{:S(2)}) collective-permute-start(f32[128,256]{1,0:T(8,128)S(1)} %add.146), channel_id=1, source_target_pairs={{0,16},{8,24},{16,0},{24,8},{32,48},{40,56},{48,32},{56,40},{64,80... | collective-permute-start | bytes 393224 | tf_op jit(solution)/shard_map/ppermute | solution.py:249
  170.2 21.2 %collective-permute-start.22 = (bf16[8,256,128]{2,1,0:T(8,128)(2,1)S(1)}, bf16[8,256,128]{2,1,0:T(8,128)(2,1)S(1)}, u32[]{:S(2)}, u32[]{:S(2)}) collective-permute-start(bf16[8,256,128]{2,1,0:T(8,128)(2,1)S(1)} %pad_maximum_fusion.2), channel_id=1, source_target_pairs={{0,120},{1,3},{2,122},{3,5},{4,124},{5,7},{6,126},{7,1},{8,0},{9,1... | collective-permute-start | bytes 1572872 | tf_op jit(solution)/shard_map/ppermute | solution.py:184
  173.9 17.4 %collective-permute-start.24 = (bf16[8,256,128]{2,1,0:T(8,128)(2,1)S(1)}, bf16[8,256,128]{2,1,0:T(8,128)(2,1)S(1)}, u32[]{:S(2)}, u32[]{:S(2)}) collective-permute-start(bf16[8,256,128]{2,1,0:T(8,128)(2,1)S(1)} %pad_maximum_fusion.3), channel_id=1, source_target_pairs={{0,8},{1,7},{2,10},{3,1},{4,12},{5,3},{6,14},{7,5},{8,16},{9,15},{... | collective-permute-start | bytes 1572872 | tf_op jit(solution)/shard_map/ppermute | solution.py:184
  174.0 8.6 %collective-permute-start.30 = (f32[128,256]{1,0:T(8,128)S(1)}, f32[128,256]{1,0:T(8,128)S(1)}, u32[]{:S(2)}, u32[]{:S(2)}) collective-permute-start(f32[128,256]{1,0:T(8,128)S(1)} %add.147), channel_id=1, source_target_pairs={{0,32},{8,40},{16,48},{24,56},{32,0},{40,8},{48,16},{56,24},{64,96... | collective-permute-start | bytes 393224 | tf_op jit(solution)/shard_map/ppermute | solution.py:249
  (18 other events, 150.5 us)

commit v4 on v3

v4 whole, which is shorter than its diff:
```python
import functools

import jax
import jax.numpy as jnp
import numpy as np
from jax import lax
from jax.experimental import pallas as pl
from jax.experimental.pallas import tpu as pltpu
from jax.sharding import PartitionSpec as P

bf16, f32 = jnp.bfloat16, jnp.float32

FWD_SLOTS = 12
BWD_SLOTS = 8
STAGES = 4


def layout(own, core):
    half = own // 2

    def shards(*keys):
        return [(p, dy, i) for p, dy in keys for i in range(own)]

    if core == 0:
        last = shards((1, 2), (0, 2), (2, 2))
        middle = shards((1, 1), (0, 1), (2, 1), (1, 3), (0, 3), (2, 3))
        first = [None] * own + shards((1, 0), (0, 0), (2, 0))
    else:
        last = shards((0, 2)) + [None] * half + shards((2, 2)) + [None] * half
        middle = shards((0, 0), (0, 1), (0, 3), (2, 0), (2, 1), (2, 3))
        first = shards((1, 2), (1, 0), (1, 1), (1, 3))
    return last, middle, first


def lanes(a_ref, order, t, k0, end, count):
    got = []
    for j in range(count):
        a = a_ref[0, order[t, k0 + j]]
        got.append(jnp.where(k0 + j < end, a, jnp.zeros_like(a)))
    return jnp.concatenate(got, axis=1)


def clear(acc):
    def zero(i, _):
        acc[pl.ds(i * 4, 4)] = jnp.zeros((4,) + acc.shape[1:], f32)
        return 0

    lax.fori_loop(0, acc.shape[0] // 4, zero, 0)


def spread(a_ref, acc, gwt, order, at, t, begin, end, base):
    tile = a_ref.shape[2]

    def body(i, _):
        k0 = begin + i * BWD_SLOTS
        r = jnp.dot(gwt, lanes(a_ref, order, t, k0, end, BWD_SLOTS), preferred_element_type=f32)
        for j in range(BWD_SLOTS):
            c = jnp.where(k0 + j < end, at[t, k0 + j] - base, 0)
            acc[c] += r[:, j * tile : (j + 1) * tile]
        return 0

    lax.fori_loop(0, (end - begin + BWD_SLOTS - 1) // BWD_SLOTS, body, 0)


def hand_out(acc, outs, stage, sem):
    chunk = stage.shape[1]

    def copy(slot, out, at):
        return pltpu.make_async_copy(stage.at[slot], out.at[pl.ds(at, chunk)], sem.at[slot])

    done = 0
    for out in outs:
        steps = out.shape[0] // chunk

        def emit(i, _, out=out, done=done):
            number = done + i
            slot = lax.rem(number, STAGES)

            @pl.when(number >= STAGES)
            def _():
                copy(slot, out, 0).wait()

            stage[slot] = acc[pl.ds(number * chunk, chunk)].astype(bf16)
            copy(slot, out, i * chunk).start()
            return 0

        lax.fori_loop(0, steps, emit, 0)
        done += steps
    for slot in range(STAGES):
        copy(slot, outs[0], 0).wait()


def whole_kernel(n_in, order, at, ends, a_ref, *refs):
    parts = refs[:n_in]
    w_ref, cot_ref, out_ref, wg_ref, gwt_ref = refs[n_in : n_in + 5]
    outs = refs[n_in + 5 : n_in + 7]
    win, acc, stage, in_sem, out_sem = refs[n_in + 7 :]
    t = pl.program_id(0)
    tile, width = a_ref.shape[2], w_ref.shape[0]

    @pl.when(t == 0)
    def _():
        copies, row = [], 0
        for k, part in enumerate(parts):
            rows = part.shape[0]
            copies.append(pltpu.make_async_copy(part, win.at[pl.ds(row, rows)], in_sem.at[k]))
            copies[-1].start()
            row += rows
        wg_ref[...] = jnp.zeros_like(wg_ref)
        clear(acc)
        for copy in copies:
            copy.wait()

    n = ends[t, 2]

    def forward(i, af):
        k0 = i * FWD_SLOTS
        rows = [
            win[pl.ds(pl.multiple_of(at[t, k0 + j] * tile, tile), tile), :]
            for j in range(FWD_SLOTS)
        ]
        a = lanes(a_ref, order, t, k0, n, FWD_SLOTS)
        return af + jnp.dot(a, jnp.concatenate(rows, axis=0), preferred_element_type=f32)

    trips = (n + FWD_SLOTS - 1) // FWD_SLOTS
    af = lax.fori_loop(0, trips, forward, jnp.zeros((tile, width), f32)).astype(bf16)
    pre = jnp.dot(af, w_ref[...], preferred_element_type=f32)
    sig = jax.nn.sigmoid(pre)
    out_ref[...] = (pre * sig).astype(bf16)
    g = (cot_ref[...].astype(f32) * sig * (1.0 + pre * (1.0 - sig))).astype(bf16)
    wg_ref[...] += lax.dot_general(af, g, (((0,), (0,)), ((), ())), preferred_element_type=f32)
    gwt = lax.dot_general(
        w_ref[...], g, (((1,), (1,)), ((), ())), preferred_element_type=f32
    ).astype(bf16)
    gwt_ref[0] = gwt
    spread(a_ref, acc, gwt, order, at, t, 0, ends[t, 0], 0)

    @pl.when(t == pl.num_programs(0) - 1)
    def _():
        hand_out(acc, outs, stage, out_sem)


def back_kernel(group, base, order, at, ends, a_ref, gwt_ref, *refs):
    mine, other, acc, stage, sem = refs[-5:]
    t = pl.program_id(0)

    @pl.when(t == 0)
    def _():
        clear(acc)

    spread(a_ref, acc, gwt_ref[0], order, at, t, ends[t, group - 1], ends[t, group], base)

    @pl.when(t == pl.num_programs(0) - 1)
    def _():
        hand_out(acc, (mine, other), stage, sem)


ANYWHERE = pl.BlockSpec(memory_space=pl.ANY)
CHUNK = 8


def back_scratch(size, width, tile):
    return [
        pltpu.VMEM((2 * size, width, tile), f32),
        pltpu.VMEM((STAGES, CHUNK, width, tile), bf16),
    ]


def values_block(tile_values):
    return pl.BlockSpec((1,) + tile_values.shape[1:], lambda t, *_: (t, 0, 0, 0))


def handed(size, width, tile):
    return [jax.ShapeDtypeStruct((size, width, tile), bf16)] * 2


def cost(tile_values, width, products, passes):
    return pl.CostEstimate(
        flops=products * tile_values.size * width,
        bytes_accessed=passes * 2 * tile_values.size,
        transcendentals=0,
    )


def front(lists, tile_values, parts, weight, cotangent, groups):
    nt, _, tile, _ = tile_values.shape
    width = weight.shape[0]
    output, term, gwt, mine, other = pl.pallas_call(
        functools.partial(whole_kernel, len(parts)),
        grid_spec=pltpu.PrefetchScalarGridSpec(
            num_scalar_prefetch=3,
            grid=(nt,),
            in_specs=[values_block(tile_values)]
            + [ANYWHERE] * len(parts)
            + [
                pl.BlockSpec((width, width), lambda t, *_: (0, 0)),
                pl.BlockSpec((tile, width), lambda t, *_: (t, 0)),
            ],
            out_specs=[
                pl.BlockSpec((tile, width), lambda t, *_: (t, 0)),
                pl.BlockSpec((width, width), lambda t, *_: (0, 0)),
                pl.BlockSpec((1, width, tile), lambda t, *_: (t, 0, 0)),
                ANYWHERE,
                ANYWHERE,
            ],
            scratch_shapes=[pltpu.VMEM((2 * sum(groups) * tile, width), bf16)]
            + back_scratch(groups[0], width, tile)
            + [pltpu.SemaphoreType.DMA((len(parts),)), pltpu.SemaphoreType.DMA((STAGES,))],
        ),
        out_shape=[
            jax.ShapeDtypeStruct((nt * tile, width), bf16),
            jax.ShapeDtypeStruct((width, width), f32),
            jax.ShapeDtypeStruct((nt, width, tile), bf16),
        ]
        + handed(groups[0], width, tile),
        compiler_params=pltpu.CompilerParams(vmem_limit_bytes=60 * 2**20),
        cost_estimate=cost(tile_values, width, 3, 3),
    )(*lists, tile_values, *parts, weight, cotangent)
    return output, term, gwt, mine, other


def rest(lists, tile_values, gwt, group, groups, earlier=()):
    nt, _, tile, _ = tile_values.shape
    width = gwt.shape[1]
    return pl.pallas_call(
        functools.partial(back_kernel, group, 2 * sum(groups[:group])),
        grid_spec=pltpu.PrefetchScalarGridSpec(
            num_scalar_prefetch=3,
            grid=(nt,),
            in_specs=[
                values_block(tile_values),
                pl.BlockSpec((1, width, tile), lambda t, *_: (t, 0, 0)),
            ]
            + [ANYWHERE] * len(earlier),
            out_specs=[ANYWHERE, ANYWHERE],
            scratch_shapes=back_scratch(groups[group], width, tile)
            + [pltpu.SemaphoreType.DMA((STAGES,))],
        ),
        out_shape=handed(groups[group], width, tile),
        compiler_params=pltpu.CompilerParams(vmem_limit_bytes=60 * 2**20),
        cost_estimate=cost(tile_values, width, 1, 2),
    )(*lists, tile_values, gwt, *earlier)


def tied(x, *earlier):
    return pl.pallas_call(
        lambda *refs: None,
        in_specs=[ANYWHERE] * (1 + len(earlier)),
        out_specs=ANYWHERE,
        out_shape=jax.ShapeDtypeStruct(x.shape, x.dtype),
        input_output_aliases={0: 0},
    )(x, *earlier)


def near(group, rep, axis, step, n_rows, n_rep):
    if axis == "z":
        return (group + step) % n_rows * n_rep + rep
    return group * n_rep + (rep + 2 * step) % n_rep


def moved(x, moves, back=False):
    n_rows, n_rep = lax.axis_size("rows"), lax.axis_size("rep")
    pairs = []
    for group in range(n_rows):
        for rep in range(n_rep):
            if moves[rep % 2]:
                source = near(group, rep, *moves[rep % 2], n_rows, n_rep)
                pairs.append((source, group * n_rep + rep))
    if back:
        pairs = [(target, source) for source, target in pairs]
    return lax.ppermute(x, ("rows", "rep"), pairs)


FIRST_UP, FIRST_DOWN = (("z", -1), ("y", 1)), (("z", 1), ("y", -1))
HALF_UP, HALF_DOWN = (None, ("y", 1)), (None, ("y", -1))
NEXT_UP, NEXT_DOWN = (("y", 1), ("z", -1)), (("y", -1), ("z", 1))


def from_core(x):
    return lax.ppermute(x, "rep", [(i, i ^ 1) for i in range(lax.axis_size("rep"))])


def gather(features, core):
    rows = features.shape[0]
    half = rows // 2
    up, down = moved(features, FIRST_UP), moved(features, FIRST_DOWN)
    near3 = jnp.concatenate([features, up, down])
    far = jnp.concatenate([moved(up[:half], HALF_UP), moved(down[half:], HALF_DOWN)])
    up, down = moved(near3, NEXT_UP), moved(near3, NEXT_DOWN)
    crossing = jnp.concatenate([far, far[:half]])
    last_up = moved(jnp.where(core == 0, up[: 3 * half], crossing), NEXT_UP)
    last_down = moved(jnp.where(core == 0, down[3 * half :], crossing), NEXT_DOWN)
    mine = ((last_up, last_down), (up, down), (far, near3))
    return [x for pair in mine for part in (pair, [from_core(x) for x in pair]) for x in part]


def joined(mine, other):
    return mine.astype(f32) + from_core(other).astype(f32)


def scatter(last, middle, first, own, core, steps):
    half = own // 2
    cut = 3 * half
    last_up, last_down = (x.astype(f32) for x in last)
    up, down = middle[: 2 * cut], middle[2 * cut :]
    along = (core == 0).astype(f32)
    up = jnp.concatenate([up[:cut] + along * last_up, up[cut:]]).astype(bf16)
    down = jnp.concatenate([down[:cut], down[cut:] + along * last_down]).astype(bf16)
    next_up, next_down = moved(up, NEXT_UP, back=True), moved(down, NEXT_DOWN, back=True)
    steps.go(2)
    far = (first[:own] + (1.0 - along) * (last_up[:own] + last_down[:own])).astype(bf16)
    half_up = moved(far[:half], HALF_UP, back=True)
    half_down = moved(far[half:], HALF_DOWN, back=True)
    steps.tie(half_up, half_down)
    steps.go(2)
    near3 = first[own:] + next_up.astype(f32) + next_down.astype(f32)
    home, up, down = near3[:own], near3[own : 2 * own], near3[2 * own :]
    up = jnp.concatenate([up[:half] + half_up.astype(f32), up[half:]]).astype(bf16)
    down = jnp.concatenate([down[:half], down[half:] + half_down.astype(f32)]).astype(bf16)
    up = tied(up, steps.x)
    return (
        home
        + moved(up, FIRST_UP, back=True).astype(f32)
        + moved(down, FIRST_DOWN, back=True).astype(f32)
    )


class Steps:
    def __init__(self, term, core):
        height = term.shape[0] // 2
        low, high = term[:height], term[height:]
        self.got = from_core(jnp.where(core == 0, high, low))
        self.x = jnp.where(core == 0, low, high) + self.got
        self.left = [
            (axis, bit)
            for axis, first in (("rep", 2), ("rows", 1))
            for bit in (1 << k for k in range(10))
            if first <= bit < lax.axis_size(axis)
        ]

    def go(self, count):
        for axis, bit in self.left[:count]:
            pairs = [(i, i ^ bit) for i in range(lax.axis_size(axis))]
            self.got = lax.ppermute(self.x, axis, pairs)
            self.x = self.x + self.got
        self.left = self.left[count:]

    def tie(self, *earlier):
        self.x = tied(self.x, *earlier)

    def whole(self, core):
        self.go(len(self.left))
        other = from_core(self.x)
        halves = [self.x, other], [other, self.x]
        return jnp.where(core == 0, *(jnp.concatenate(h) for h in halves))


def by_group(at, live, starts):
    slots = at.shape[1]
    group = sum((at >= start).astype(jnp.int32) for start in starts[1:])
    group = jnp.where(live > 0, group, len(starts))
    ends = jnp.stack([jnp.sum(group <= g, axis=1) for g in range(len(starts))], axis=1)
    s = jnp.arange(slots, dtype=jnp.int32)
    a, b = group[:, :, None], group[:, None, :]
    before = (b < a) | ((b == a) & (s[None, :] < s[:, None]))
    rank = jnp.sum(before, axis=2)
    k = jnp.arange(slots + 16, dtype=jnp.int32)
    hit = (rank[:, None, :] == k[:, None]) & (live > 0)[:, None, :]
    order = jnp.sum(jnp.where(hit, s, 0), axis=2)
    place = jnp.sum(jnp.where(hit, at[:, None, :], 0), axis=2)
    return order.astype(jnp.int32), place.astype(jnp.int32), ends.astype(jnp.int32)


def local(features, weight, tile_values, tile_cols, tile_live, cotangent):
    n_rows, n_rep = lax.axis_size("rows"), lax.axis_size("rep")
    rep = lax.axis_index("rep")
    node_dev, width = features.shape
    tile = tile_values.shape[2]
    own = node_dev // tile
    group_tiles = own * n_rep
    core = rep % 2
    plans = [layout(own, c) for c in range(2)]
    groups = [len(keys) for keys in plans[0]]
    starts = [2 * sum(groups[:g]) for g in range(len(groups))]
    table = np.zeros((2, 3, n_rep // 2, own), np.int32)
    stride = np.zeros_like(table)
    for c, plan in enumerate(plans):
        for start, keys in zip(starts, plan):
            for at, key in enumerate(keys):
                if key:
                    table[(c, *key)] = start + at
                    stride[(c, *key)] = len(keys)
    place = jnp.mod(tile_cols // group_tiles - lax.axis_index("rows") + 1, n_rows)
    inner = tile_cols % group_tiles
    owner = inner // own
    dy = jnp.mod(owner // 2 - rep // 2, n_rep // 2)
    key = (((owner % 2) * 3 + place) * (n_rep // 2) + dy) * own + inner % own
    hit = key[:, :, None] == jnp.arange(table.size, dtype=jnp.int32)
    turn = jnp.mod(owner + rep, 2)[:, :, None]
    spot = jnp.asarray(table.reshape(-1)) + turn * jnp.asarray(stride.reshape(-1))
    at = jnp.sum(jnp.where(hit, spot, 0), axis=2)
    lists = by_group(at, tile_live, starts)

    parts = gather(features, core)
    output, term, gwt, mine, other = front(lists, tile_values, parts, weight, cotangent, groups)
    last = joined(mine, other).astype(bf16)
    steps = Steps(term, core)
    cut = groups[0] // 2
    sent = last[:cut], last[cut:]
    mine, other = rest(lists, tile_values, gwt, 1, groups)
    other = tied(other, steps.got)
    mine2, other2 = rest(lists, tile_values, gwt, 2, groups, (*sent, other))
    last = moved(sent[0], NEXT_UP, back=True), moved(sent[1], NEXT_DOWN, back=True)
    middle = joined(mine, other)
    steps.go(1)
    first = joined(mine2, tied(other2, *last, steps.got))
    total = scatter(last, middle, first, own, core, steps)
    weight_grad = steps.whole(core)
    feature_grad = jnp.swapaxes(total, 1, 2).reshape(node_dev, width).astype(bf16)
    return (output, feature_grad, weight_grad)


def solution(mesh):
    placed = (
        P(("rows", "rep"), None),
        P(),
        P(("rows", "rep"), None, None, None),
        P(("rows", "rep"), None),
        P(("rows", "rep"), None),
        P(("rows", "rep"), None),
    )
    return jax.shard_map(
        local,
        mesh=mesh,
        in_specs=placed,
        out_specs=(P(("rows", "rep"), None), P(("rows", "rep"), None), P()),
        check_vma=False,
    )
```

time: 194 us -> 202 us (1.041)
  the two profiles are of different devices: /device:TPU:0 before, /device:TPU:7 now
where the time goes in v4:
time: 202 us; the launch traced here: 201 us
  starting transfers between devices  67.2 us (33%)
  Pallas kernels  48.9 us (24%)
  waiting for transfers between devices  40.5 us (20%)
  other arithmetic  25.4 us (13%)
  local copies, waits for them, and re-layouts  18.1 us (9%)
    ppermute x16, starting transfers between devices, moved(): return lax.ppermute(x, ('rows', 'rep'), pairs)  30.5 us
    ppermute x16, waiting for transfers between devices, moved(): return lax.ppermute(x, ('rows', 'rep'), pairs)  28.4 us
    pallas_call x2, Pallas kernels, rest(): pl.pallas_call(functools.partial(back_kernel, group, 2 * sum(groups[:grou...  26.5 us
    ppermute x11, starting transfers between devices, from_core(): lax.ppermute(x, 'rep', [(i, i ^ 1) for i in range(lax.axis_size('rep'))])  25.9 us
    pallas_call x1, Pallas kernels, front(): pl.pallas_call(functools.partial(whole_kernel, len(parts)), grid_spec=plt...  22.4 us
    unnamed x55, local copies, waits for them, and re-layouts  12.2 us
    ppermute x6, starting transfers between devices, go(): self.got = lax.ppermute(self.x, axis, pairs)  10.8 us
    ppermute x6, waiting for transfers between devices, go(): self.got = lax.ppermute(self.x, axis, pairs)  10.6 us
  transfers between devices with their start and end apart: 33, of which 14 were waited for; matrix products, arithmetic and copies ran while one was open for 15% of the time, Pallas kernels for 13%

profile of v4, /device:TPU:7, one launch (start us, length us, event | category | flops | bytes accessed | tf_op | source)
XLA Modules:
  0.0 201.2 jit_solution(17394860416407086864)
XLA Ops:
  0.6 2.8 %collective-permute-start = (bf16[1024,256]{1,0:T(8,128)(2,1)}, bf16[1024,256]{1,0:T(8,128)(2,1)S(1)}, u32[]{:S(2)}, u32[]{:S(2)}) collective-permute-start(bf16[1024,256]{1,0:T(8,128)(2,1)} %param.8), channel_id=1, source_target_pairs={{120,0},{3,1},{122,2},{5,3},{124,4},{7,5},{126,6},{1,7},{0,8},{11,... | collective-permute-start | bytes 1572872 | tf_op jit(solution)/shard_map/ppermute | solution.py:271
  5.4 4.4 %collective-permute-done = bf16[1024,256]{1,0:T(8,128)(2,1)S(1)} collective-permute-done((bf16[1024,256]{1,0:T(8,128)(2,1)}, bf16[1024,256]{1,0:T(8,128)(2,1)S(1)}, u32[]{:S(2)}, u32[]{:S(2)}) %collective-permute-start) | collective-permute-done | bytes 524320 | tf_op jit(solution)/shard_map/ppermute | solution.py:271
  13.7 4.0 %collective-permute-start.6 = (bf16[3072,256]{1,0:T(8,128)(2,1)}, bf16[3072,256]{1,0:T(8,128)(2,1)S(1)}, u32[]{:S(2)}, u32[]{:S(2)}) collective-permute-start(bf16[3072,256]{1,0:T(8,128)(2,1)} %constant_dynamic-update-slice_fusion.refs_9_), channel_id=1, source_target_pairs={{6,0},{9,1},{0,2},{11,3},{2,4},{13,5},{4,6},{15,7},{14,8},{17,9},{... | collective-permute-start | bytes 4718600 | tf_op jit(solution)/shard_map/ppermute | solution.py:271
  18.5 3.0 %collective-permute-start.3 = (bf16[512,256]{1,0:T(8,128)(2,1)}, bf16[512,256]{1,0:T(8,128)(2,1)S(1)}, u32[]{:S(2)}, u32[]{:S(2)}) collective-permute-start(bf16[512,256]{1,0:T(8,128)(2,1)} %slice.109), channel_id=1, source_target_pairs={{3,1},{5,3},{7,5},{1,7},{11,9},{13,11},{15,13},{9,15},{19,17},{21,... | collective-permute-start | bytes 786440 | tf_op jit(solution)/shard_map/ppermute | solution.py:271
  24.5 4.5 %collective-permute-done.3 = bf16[512,256]{1,0:T(8,128)(2,1)S(1)} collective-permute-done((bf16[512,256]{1,0:T(8,128)(2,1)}, bf16[512,256]{1,0:T(8,128)(2,1)S(1)}, u32[]{:S(2)}, u32[]{:S(2)}) %collective-permute-start.3) | collective-permute-done | bytes 262176 | tf_op jit(solution)/shard_map/ppermute | solution.py:271
  29.0 4.9 %collective-permute-done.4 = bf16[512,256]{1,0:T(8,128)(2,1)} collective-permute-done((bf16[512,256]{1,0:T(8,128)(2,1)}, bf16[512,256]{1,0:T(8,128)(2,1)}, u32[]{:S(2)}, u32[]{:S(2)}) %collective-permute-start.4) | collective-permute-done | bytes 262176 | tf_op jit(solution)/shard_map/ppermute | solution.py:271
  35.4 3.9 %collective-permute-done.2.refs_4_ = bf16[3072,256]{1,0:T(8,128)(2,1)S(1)} collective-permute-done((bf16[3072,256]{1,0:T(8,128)(2,1)}, bf16[3072,256]{1,0:T(8,128)(2,1)S(1)}, u32[]{:S(2)}, u32[]{:S(2)}) %collective-permute-start.2) | collective-permute-done | bytes 1572896 | tf_op jit(solution)/shard_map/ppermute | solution.py:271
  45.9 6.3 %collective-permute-done.7.refs_1_ = bf16[1536,256]{1,0:T(8,128)(2,1)} collective-permute-done((bf16[1536,256]{1,0:T(8,128)(2,1)}, bf16[1536,256]{1,0:T(8,128)(2,1)}, u32[]{:S(2)}, u32[]{:S(2)}) %collective-permute-start.7) | collective-permute-done | bytes 786464 | tf_op jit(solution)/shard_map/ppermute | solution.py:271
  52.2 2.6 %collective-permute-start.9 = (bf16[1536,256]{1,0:T(8,128)(2,1)}, bf16[1536,256]{1,0:T(8,128)(2,1)}, u32[]{:S(2)}, u32[]{:S(2)}) collective-permute-start(bf16[1536,256]{1,0:T(8,128)(2,1)} %collective-permute-done.7.refs_1_), channel_id=1, source_target_pairs={{0,1},{1,0},{2,3},{3,2},{4,5},{5,4},{6,7},{7,6},{8,9},{9,8},{10,11... | collective-permute-start | bytes 2359304 | tf_op jit(solution)/shard_map/ppermute | solution.py:280
  58.2 22.4 %shard_map.103 = (bf16[1024,256]{1,0:T(8,128)(2,1)}, f32[256,256]{1,0:T(8,128)}, bf16[8,256,128]{2,1,0:T(8,128)(2,1)}, bf16[24,256,128]{2,1,0:T(8,128)(2,1)}, bf16[24,256,128]{2,1,0:T(8,128)(2,1)}) custom-call(s32[8,64]{1,0:T(8,128)} %get-tuple-element.22.order, s32[8,64]{1,0:T(8,128)} %get-tuple-element.21.at, s32[8,3]{1,0:T(8,128)} %pad_add_fusion.ends, ...), custom_call_target="tpu_custom_call" | custom-call | flops 4831838208 | bytes 37748736 | tf_op jit(solution)/shard_map/pallas_call | solution.py:188
  82.2 14.2 %shard_map.104 = (bf16[48,256,128]{2,1,0:T(8,128)(2,1)}, bf16[48,256,128]{2,1,0:T(8,128)(2,1)}) custom-call(s32[8,64]{1,0:T(8,128)} %get-tuple-element.22.order, s32[8,64]{1,0:T(8,128)} %get-tuple-element.21.at, s32[8,3]{1,0:T(8,128)} %pad_add_fusion.ends, bf16[8,48,128,128]{3,2,1,0:T(8,128)(2,1)} %a_ref.5, bf16[8,256,128]{2,1,0:T(8,128)(2,1)} %get-tuple-element.13.gwt_ref), custom_call_target="tpu_custom_call" | custom-call | flops 1610612736 | bytes 25165824 | tf_op jit(solution)/shard_map/pallas_call | solution.py:225
  99.2 4.7 %collective-permute-start.16 = (bf16[12,256,128]{2,1,0:T(8,128)(2,1)S(1)}, bf16[12,256,128]{2,1,0:T(8,128)(2,1)S(1)}, u32[]{:S(2)}, u32[]{:S(2)}) collective-permute-start(bf16[12,256,128]{2,1,0:T(8,128)(2,1)S(1)} %get-tuple-element.40.refs_0_), channel_id=1, source_target_pairs={{0,2},{1,121},{2,4},{3,123},{4,6},{5,125},{6,0},{7,127},{8,10},{9,... | collective-permute-start | bytes 2359304 | tf_op jit(solution)/shard_map/ppermute | solution.py:271
  103.9 3.2 %collective-permute-start.18 = (f32[128,256]{1,0:T(8,128)S(1)}, f32[128,256]{1,0:T(8,128)S(1)}, u32[]{:S(2)}, u32[]{:S(2)}) collective-permute-start(f32[128,256]{1,0:T(8,128)S(1)} %select_add_fusion), channel_id=1, source_target_pairs={{0,2},{1,3},{2,0},{3,1},{4,6},{5,7},{6,4},{7,5},{8,10},{9,11},{10,... | collective-permute-start | bytes 393224 | tf_op jit(solution)/shard_map/ppermute | solution.py:344
  107.1 12.3 %shard_map.106 = (bf16[32,256,128]{2,1,0:T(8,128)(2,1)}, bf16[32,256,128]{2,1,0:T(8,128)(2,1)}) custom-call(s32[8,64]{1,0:T(8,128)} %get-tuple-element.22.order, s32[8,64]{1,0:T(8,128)} %get-tuple-element.21.at, s32[8,3]{1,0:T(8,128)} %pad_add_fusion.ends, bf16[8,48,128,128]{3,2,1,0:T(8,128)(2,1)} %a_ref.5, bf16[8,256,128]{2,1,0:T(8,128)(2,1)} %get-tuple-element.13.gwt_ref, ...), custom_call_target="tpu_custom_call" | custom-call | flops 1610612736 | bytes 25165824 | tf_op jit(solution)/shard_map/pallas_call | solution.py:225
  120.6 4.0 %fusion.30 = (bf16[48,256,128]{2,1,0:T(8,128)(2,1)S(1)}, f32[48,256,128]{2,1,0:T(8,128)S(1)}) fusion(bf16[48,256,128]{2,1,0:T(8,128)(2,1)} %collective-permute-done.20, bf16[48,256,128]{2,1,0:T(8,128)(2,1)} %get-tuple-element.20), kind=kLoop, calls=%fused_computation.97 | loop fusion | flops 6291456 | bytes 15728640 | tf_op jit(solution)/shard_map/convert.11
  128.2 4.0 %collective-permute-start.21 = (bf16[24,256,128]{2,1,0:T(8,128)(2,1)}, bf16[24,256,128]{2,1,0:T(8,128)(2,1)}, u32[]{:S(2)}, u32[]{:S(2)}) collective-permute-start(bf16[24,256,128]{2,1,0:T(8,128)(2,1)} %pad_maximum_fusion), channel_id=1, source_target_pairs={{0,2},{1,121},{2,4},{3,123},{4,6},{5,125},{6,0},{7,127},{8,10},{9,... | collective-permute-start | bytes 4718600 | tf_op jit(solution)/shard_map/ppermute | solution.py:271
  140.9 4.3 %collective-permute-start.26 = (bf16[4,256,128]{2,1,0:T(8,128)(2,1)S(1)}, bf16[4,256,128]{2,1,0:T(8,128)(2,1)S(1)}, u32[]{:S(2)}, u32[]{:S(2)}) collective-permute-start(bf16[4,256,128]{2,1,0:T(8,128)(2,1)S(1)} %get-tuple-element.45), channel_id=1, source_target_pairs={{1,7},{3,1},{5,3},{7,5},{9,15},{11,9},{13,11},{15,13},{17,23},{19,... | collective-permute-start | bytes 786440 | tf_op jit(solution)/shard_map/ppermute | solution.py:271
  145.4 4.2 %collective-permute-done.25 = f32[128,256]{1,0:T(8,128)S(1)} collective-permute-done((f32[128,256]{1,0:T(8,128)S(1)}, f32[128,256]{1,0:T(8,128)S(1)}, u32[]{:S(2)}, u32[]{:S(2)}) %collective-permute-start.25) | collective-permute-done | bytes 131104 | tf_op jit(solution)/shard_map/ppermute | solution.py:344
  152.7 3.2 %collective-permute-start.27 = (f32[128,256]{1,0:T(8,128)}, f32[128,256]{1,0:T(8,128)S(1)}, u32[]{:S(2)}, u32[]{:S(2)}) collective-permute-start(f32[128,256]{1,0:T(8,128)} %shard_map.108), channel_id=1, source_target_pairs={{0,16},{8,24},{16,0},{24,8},{32,48},{40,56},{48,32},{56,40},{64,80... | collective-permute-start | bytes 393224 | tf_op jit(solution)/shard_map/ppermute | solution.py:344
  155.9 3.3 %collective-permute-done.27 = f32[128,256]{1,0:T(8,128)S(1)} collective-permute-done((f32[128,256]{1,0:T(8,128)}, f32[128,256]{1,0:T(8,128)S(1)}, u32[]{:S(2)}, u32[]{:S(2)}) %collective-permute-start.27) | collective-permute-done | bytes 131104 | tf_op jit(solution)/shard_map/ppermute | solution.py:344
  160.6 3.5 %fusion.31 = (bf16[24,256,128]{2,1,0:T(8,128)(2,1)S(1)}, f32[24,256,128]{2,1,0:T(8,128)S(1)}) fusion(bf16[24,256,128]{2,1,0:T(8,128)(2,1)} %collective-permute-done.22, bf16[24,256,128]{2,1,0:T(8,128)(2,1)} %collective-permute-done.21, f32[32,256,128]{2,1,0:T(8,128)} %copy-done), kind=kLoop, calls=%fused_computation.98 | loop fusion | flops 3932160 | bytes 11010048 | tf_op jit(solution)/shard_map/convert.5
  168.1 3.9 %collective-permute-start.31 = (f32[128,256]{1,0:T(8,128)}, f32[128,256]{1,0:T(8,128)S(1)}, u32[]{:S(2)}, u32[]{:S(2)}) collective-permute-start(f32[128,256]{1,0:T(8,128)} %add.154.refs_1_), channel_id=1, source_target_pairs={{0,64},{8,72},{16,80},{24,88},{32,96},{40,104},{48,112},{56,120},{... | collective-permute-start | bytes 393224 | tf_op jit(solution)/shard_map/ppermute | solution.py:344
  172.0 3.0 %collective-permute-done.31 = f32[128,256]{1,0:T(8,128)S(1)} collective-permute-done((f32[128,256]{1,0:T(8,128)}, f32[128,256]{1,0:T(8,128)S(1)}, u32[]{:S(2)}, u32[]{:S(2)}) %collective-permute-start.31) | collective-permute-done | bytes 131104 | tf_op jit(solution)/shard_map/ppermute | solution.py:344
  176.0 19.5 %collective-permute-start.32 = (f32[128,256]{1,0:T(8,128)S(1)}, f32[128,256]{1,0:T(8,128)S(1)}, u32[]{:S(2)}, u32[]{:S(2)}) collective-permute-start(f32[128,256]{1,0:T(8,128)S(1)} %add.158), channel_id=1, source_target_pairs={{0,1},{1,0},{2,3},{3,2},{4,5},{5,4},{6,7},{7,6},{8,9},{9,8},{10,11... | collective-permute-start | bytes 393224 | tf_op jit(solution)/shard_map/ppermute | solution.py:280
  (148 shorter events, 53.7 us)
Async XLA Ops:
  13.7 21.7 %collective-permute-start.6 = (bf16[3072,256]{1,0:T(8,128)(2,1)}, bf16[3072,256]{1,0:T(8,128)(2,1)S(1)}, u32[]{:S(2)}, u32[]{:S(2)}) collective-permute-start(bf16[3072,256]{1,0:T(8,128)(2,1)} %constant_dynamic-update-slice_fusion.refs_9_), channel_id=1, source_target_pairs={{6,0},{9,1},{0,2},{11,3},{2,4},{13,5},{4,6},{15,7},{14,8},{17,9},{... | collective-permute-start | bytes 4718600 | tf_op jit(solution)/shard_map/ppermute | solution.py:271
  17.7 21.6 %collective-permute-start.2 = (bf16[3072,256]{1,0:T(8,128)(2,1)}, bf16[3072,256]{1,0:T(8,128)(2,1)S(1)}, u32[]{:S(2)}, u32[]{:S(2)}) collective-permute-start(bf16[3072,256]{1,0:T(8,128)(2,1)} %constant_dynamic-update-slice_fusion.refs_9_), channel_id=1, source_target_pairs={{2,0},{121,1},{4,2},{123,3},{6,4},{125,5},{0,6},{127,7},{10,8},{1,... | collective-permute-start | bytes 4718600 | tf_op jit(solution)/shard_map/ppermute | solution.py:271
  18.5 10.5 %collective-permute-start.3 = (bf16[512,256]{1,0:T(8,128)(2,1)}, bf16[512,256]{1,0:T(8,128)(2,1)S(1)}, u32[]{:S(2)}, u32[]{:S(2)}) collective-permute-start(bf16[512,256]{1,0:T(8,128)(2,1)} %slice.109), channel_id=1, source_target_pairs={{3,1},{5,3},{7,5},{1,7},{11,9},{13,11},{15,13},{9,15},{19,17},{21,... | collective-permute-start | bytes 786440 | tf_op jit(solution)/shard_map/ppermute | solution.py:271
  22.2 11.7 %collective-permute-start.4 = (bf16[512,256]{1,0:T(8,128)(2,1)}, bf16[512,256]{1,0:T(8,128)(2,1)}, u32[]{:S(2)}, u32[]{:S(2)}) collective-permute-start(bf16[512,256]{1,0:T(8,128)(2,1)} %slice.110), channel_id=1, source_target_pairs={{7,1},{1,3},{3,5},{5,7},{15,9},{9,11},{11,13},{13,15},{23,17},{17,... | collective-permute-start | bytes 786440 | tf_op jit(solution)/shard_map/ppermute | solution.py:271
  40.7 11.5 %collective-permute-start.7 = (bf16[1536,256]{1,0:T(8,128)(2,1)}, bf16[1536,256]{1,0:T(8,128)(2,1)}, u32[]{:S(2)}, u32[]{:S(2)}) collective-permute-start(bf16[1536,256]{1,0:T(8,128)(2,1)} %get-tuple-element.42), channel_id=1, source_target_pairs={{6,0},{9,1},{0,2},{11,3},{2,4},{13,5},{4,6},{15,7},{14,8},{17,9},{... | collective-permute-start | bytes 2359304 | tf_op jit(solution)/shard_map/ppermute | solution.py:271
  40.8 14.0 %collective-permute-start.5 = (bf16[1536,256]{1,0:T(8,128)(2,1)}, bf16[1536,256]{1,0:T(8,128)(2,1)}, u32[]{:S(2)}, u32[]{:S(2)}) collective-permute-start(bf16[1536,256]{1,0:T(8,128)(2,1)} %get-tuple-element.43), channel_id=1, source_target_pairs={{2,0},{121,1},{4,2},{123,3},{6,4},{125,5},{0,6},{127,7},{10,8},{1,... | collective-permute-start | bytes 2359304 | tf_op jit(solution)/shard_map/ppermute | solution.py:271
  42.2 15.4 %collective-permute-start.13 = (bf16[3072,256]{1,0:T(8,128)(2,1)}, bf16[3072,256]{1,0:T(8,128)(2,1)}, u32[]{:S(2)}, u32[]{:S(2)}) collective-permute-start(bf16[3072,256]{1,0:T(8,128)(2,1)} %constant_dynamic-update-slice_fusion.refs_9_), channel_id=1, source_target_pairs={{0,1},{1,0},{2,3},{3,2},{4,5},{5,4},{6,7},{7,6},{8,9},{9,8},{10,11... | collective-permute-start | bytes 4718600 | tf_op jit(solution)/shard_map/ppermute | solution.py:280
  44.5 13.1 %collective-permute-start.11 = (bf16[3072,256]{1,0:T(8,128)(2,1)S(1)}, bf16[3072,256]{1,0:T(8,128)(2,1)}, u32[]{:S(2)}, u32[]{:S(2)}) collective-permute-start(bf16[3072,256]{1,0:T(8,128)(2,1)S(1)} %collective-permute-done.6.refs_5_), channel_id=1, source_target_pairs={{0,1},{1,0},{2,3},{3,2},{4,5},{5,4},{6,7},{7,6},{8,9},{9,8},{10,11... | collective-permute-start | bytes 4718600 | tf_op jit(solution)/shard_map/ppermute | solution.py:280
  45.3 12.8 %collective-permute-start.10 = (bf16[3072,256]{1,0:T(8,128)(2,1)S(1)}, bf16[3072,256]{1,0:T(8,128)(2,1)}, u32[]{:S(2)}, u32[]{:S(2)}) collective-permute-start(bf16[3072,256]{1,0:T(8,128)(2,1)S(1)} %collective-permute-done.2.refs_4_), channel_id=1, source_target_pairs={{0,1},{1,0},{2,3},{3,2},{4,5},{5,4},{6,7},{7,6},{8,9},{9,8},{10,11... | collective-permute-start | bytes 4718600 | tf_op jit(solution)/shard_map/ppermute | solution.py:280
  80.6 16.5 %collective-permute-start.14 = (bf16[24,256,128]{2,1,0:T(8,128)(2,1)}, bf16[24,256,128]{2,1,0:T(8,128)(2,1)S(1)}, u32[]{:S(2)}, u32[]{:S(2)}) collective-permute-start(bf16[24,256,128]{2,1,0:T(8,128)(2,1)} %get-tuple-element.15), channel_id=1, source_target_pairs={{0,1},{1,0},{2,3},{3,2},{4,5},{5,4},{6,7},{7,6},{8,9},{9,8},{10,11... | collective-permute-start | bytes 4718600 | tf_op jit(solution)/shard_map/ppermute | solution.py:280
  81.7 14.8 %collective-permute-start.15 = (f32[128,256]{1,0:T(8,128)S(1)}, f32[128,256]{1,0:T(8,128)S(1)}, u32[]{:S(2)}, u32[]{:S(2)}) collective-permute-start(f32[128,256]{1,0:T(8,128)S(1)} %slice_select_fusion.2), channel_id=1, source_target_pairs={{0,1},{1,0},{2,3},{3,2},{4,5},{5,4},{6,7},{7,6},{8,9},{9,8},{10,11... | collective-permute-start | bytes 393224 | tf_op jit(solution)/shard_map/ppermute | solution.py:280
  97.1 23.5 %collective-permute-start.20 = (bf16[48,256,128]{2,1,0:T(8,128)(2,1)}, bf16[48,256,128]{2,1,0:T(8,128)(2,1)}, u32[]{:S(2)}, u32[]{:S(2)}) collective-permute-start(bf16[48,256,128]{2,1,0:T(8,128)(2,1)} %shard_map.105.refs_2_), channel_id=1, source_target_pairs={{0,1},{1,0},{2,3},{3,2},{4,5},{5,4},{6,7},{7,6},{8,9},{9,8},{10,11... | collective-permute-start | bytes 9437192 | tf_op jit(solution)/shard_map/ppermute | solution.py:280
  99.2 20.3 %collective-permute-start.16 = (bf16[12,256,128]{2,1,0:T(8,128)(2,1)S(1)}, bf16[12,256,128]{2,1,0:T(8,128)(2,1)S(1)}, u32[]{:S(2)}, u32[]{:S(2)}) collective-permute-start(bf16[12,256,128]{2,1,0:T(8,128)(2,1)S(1)} %get-tuple-element.40.refs_0_), channel_id=1, source_target_pairs={{0,2},{1,121},{2,4},{3,123},{4,6},{5,125},{6,0},{7,127},{8,10},{9,... | collective-permute-start | bytes 2359304 | tf_op jit(solution)/shard_map/ppermute | solution.py:271
  103.9 15.6 %collective-permute-start.17 = (bf16[12,256,128]{2,1,0:T(8,128)(2,1)S(1)}, bf16[12,256,128]{2,1,0:T(8,128)(2,1)S(1)}, u32[]{:S(2)}, u32[]{:S(2)}) collective-permute-start(bf16[12,256,128]{2,1,0:T(8,128)(2,1)S(1)} %get-tuple-element.41.refs_1_), channel_id=1, source_target_pairs={{0,6},{1,9},{2,0},{3,11},{4,2},{5,13},{6,4},{7,15},{8,14},{9,17},{... | collective-permute-start | bytes 2359304 | tf_op jit(solution)/shard_map/ppermute | solution.py:271
  103.9 15.5 %collective-permute-start.18 = (f32[128,256]{1,0:T(8,128)S(1)}, f32[128,256]{1,0:T(8,128)S(1)}, u32[]{:S(2)}, u32[]{:S(2)}) collective-permute-start(f32[128,256]{1,0:T(8,128)S(1)} %select_add_fusion), channel_id=1, source_target_pairs={{0,2},{1,3},{2,0},{3,1},{4,6},{5,7},{6,4},{7,5},{8,10},{9,11},{10,... | collective-permute-start | bytes 393224 | tf_op jit(solution)/shard_map/ppermute | solution.py:344
  120.6 11.9 %collective-permute-start.19 = (bf16[32,256,128]{2,1,0:T(8,128)(2,1)}, bf16[32,256,128]{2,1,0:T(8,128)(2,1)}, u32[]{:S(2)}, u32[]{:S(2)}) collective-permute-start(bf16[32,256,128]{2,1,0:T(8,128)(2,1)} %shard_map.107), channel_id=1, source_target_pairs={{0,1},{1,0},{2,3},{3,2},{4,5},{5,4},{6,7},{7,6},{8,9},{9,8},{10,11... | collective-permute-start | bytes 6291464 | tf_op jit(solution)/shard_map/ppermute | solution.py:280
  126.7 33.8 %collective-permute-start.22 = (bf16[24,256,128]{2,1,0:T(8,128)(2,1)S(1)}, bf16[24,256,128]{2,1,0:T(8,128)(2,1)}, u32[]{:S(2)}, u32[]{:S(2)}) collective-permute-start(bf16[24,256,128]{2,1,0:T(8,128)(2,1)S(1)} %pad_maximum_fusion.1), channel_id=1, source_target_pairs={{0,6},{1,9},{2,0},{3,11},{4,2},{5,13},{6,4},{7,15},{8,14},{9,17},{... | collective-permute-start | bytes 4718600 | tf_op jit(solution)/shard_map/ppermute | solution.py:271
  128.2 32.4 %collective-permute-start.21 = (bf16[24,256,128]{2,1,0:T(8,128)(2,1)}, bf16[24,256,128]{2,1,0:T(8,128)(2,1)}, u32[]{:S(2)}, u32[]{:S(2)}) collective-permute-start(bf16[24,256,128]{2,1,0:T(8,128)(2,1)} %pad_maximum_fusion), channel_id=1, source_target_pairs={{0,2},{1,121},{2,4},{3,123},{4,6},{5,125},{6,0},{7,127},{8,10},{9,... | collective-permute-start | bytes 4718600 | tf_op jit(solution)/shard_map/ppermute | solution.py:271
  132.2 13.0 %collective-permute-start.24 = (f32[128,256]{1,0:T(8,128)S(1)}, f32[128,256]{1,0:T(8,128)S(1)}, u32[]{:S(2)}, u32[]{:S(2)}) collective-permute-start(f32[128,256]{1,0:T(8,128)S(1)} %add.150), channel_id=1, source_target_pairs={{0,4},{1,5},{2,6},{3,7},{4,0},{5,1},{6,2},{7,3},{8,12},{9,13},{10,... | collective-permute-start | bytes 393224 | tf_op jit(solution)/shard_map/ppermute | solution.py:344
  138.5 11.8 %collective-permute-start.23 = (bf16[4,256,128]{2,1,0:T(8,128)(2,1)S(1)}, bf16[4,256,128]{2,1,0:T(8,128)(2,1)S(1)}, u32[]{:S(2)}, u32[]{:S(2)}) collective-permute-start(bf16[4,256,128]{2,1,0:T(8,128)(2,1)S(1)} %get-tuple-element.44), channel_id=1, source_target_pairs={{1,3},{3,5},{5,7},{7,1},{9,11},{11,13},{13,15},{15,9},{17,19},{19,... | collective-permute-start | bytes 786440 | tf_op jit(solution)/shard_map/ppermute | solution.py:271
  140.9 11.0 %collective-permute-start.26 = (bf16[4,256,128]{2,1,0:T(8,128)(2,1)S(1)}, bf16[4,256,128]{2,1,0:T(8,128)(2,1)S(1)}, u32[]{:S(2)}, u32[]{:S(2)}) collective-permute-start(bf16[4,256,128]{2,1,0:T(8,128)(2,1)S(1)} %get-tuple-element.45), channel_id=1, source_target_pairs={{1,7},{3,1},{5,3},{7,5},{9,15},{11,9},{13,11},{15,13},{17,23},{19,... | collective-permute-start | bytes 786440 | tf_op jit(solution)/shard_map/ppermute | solution.py:271
  165.2 32.0 %collective-permute-start.30 = (bf16[8,256,128]{2,1,0:T(8,128)(2,1)}, bf16[8,256,128]{2,1,0:T(8,128)(2,1)}, u32[]{:S(2)}, u32[]{:S(2)}) collective-permute-start(bf16[8,256,128]{2,1,0:T(8,128)(2,1)} %pad_maximum_fusion.3), channel_id=1, source_target_pairs={{0,8},{1,7},{2,10},{3,1},{4,12},{5,3},{6,14},{7,5},{8,16},{9,15},{... | collective-permute-start | bytes 1572872 | tf_op jit(solution)/shard_map/ppermute | solution.py:271
  167.9 29.3 %collective-permute-start.29 = (bf16[8,256,128]{2,1,0:T(8,128)(2,1)}, bf16[8,256,128]{2,1,0:T(8,128)(2,1)S(1)}, u32[]{:S(2)}, u32[]{:S(2)}) collective-permute-start(bf16[8,256,128]{2,1,0:T(8,128)(2,1)} %shard_map.109), channel_id=1, source_target_pairs={{0,120},{1,3},{2,122},{3,5},{4,124},{5,7},{6,126},{7,1},{8,0},{9,1... | collective-permute-start | bytes 1572872 | tf_op jit(solution)/shard_map/ppermute | solution.py:271
  176.0 20.5 %collective-permute-start.32 = (f32[128,256]{1,0:T(8,128)S(1)}, f32[128,256]{1,0:T(8,128)S(1)}, u32[]{:S(2)}, u32[]{:S(2)}) collective-permute-start(f32[128,256]{1,0:T(8,128)S(1)} %add.158), channel_id=1, source_target_pairs={{0,1},{1,0},{2,3},{3,2},{4,5},{5,4},{6,7},{7,6},{8,9},{9,8},{10,11... | collective-permute-start | bytes 393224 | tf_op jit(solution)/shard_map/ppermute | solution.py:280
  (35 other events, 206.0 us)

commit v5 on v3

v5 whole, which is shorter than its diff:
```python
import functools

import jax
import jax.numpy as jnp
import numpy as np
from jax import lax
from jax.experimental import pallas as pl
from jax.experimental.pallas import tpu as pltpu
from jax.sharding import PartitionSpec as P

bf16, f32 = jnp.bfloat16, jnp.float32

FWD_SLOTS = 24
BWD_SLOTS = 12
STAGES = 8
CHUNK = 8


def layout(own, core):
    half = own // 2

    def shards(*keys):
        return [(p, dy, i) for p, dy in keys for i in range(own)]

    if core == 0:
        last = shards((1, 2), (0, 2), (2, 2))
        middle = shards((1, 1), (0, 1), (2, 1), (1, 3), (0, 3), (2, 3))
        first = [None] * own + shards((1, 0), (0, 0), (2, 0))
    else:
        last = shards((0, 2)) + [None] * half + shards((2, 2)) + [None] * half
        middle = shards((0, 0), (0, 1), (0, 3), (2, 0), (2, 1), (2, 3))
        first = shards((1, 2), (1, 0), (1, 1), (1, 3))
    return last, middle, first


def kernel(n_in, n_out, idx, cnt, values, *refs):
    parts = refs[:n_in]
    w_ref, cot_ref, out_ref, wg_ref = refs[n_in : n_in + 4]
    outs = refs[n_in + 4 : n_in + 4 + n_out]
    a_ref, win, acc, stage, in_sem, a_sem, out_sem = refs[n_in + 4 + n_out :]
    n_tiles, _, tile, _ = a_ref.shape
    width = w_ref.shape[0]
    copies, row = [], 0
    for k, part in enumerate(parts):
        rows = part.shape[0]
        copies.append(pltpu.make_async_copy(part, win.at[pl.ds(row, rows)], in_sem.at[k]))
        row += rows
    blocks = [pltpu.make_async_copy(values.at[t], a_ref.at[t], a_sem.at[t]) for t in range(n_tiles)]
    for copy in copies + blocks:
        copy.start()
    wg_ref[...] = jnp.zeros_like(wg_ref)

    def zero(i, _):
        acc[pl.ds(i * 8, 8)] = jnp.zeros((8,) + acc.shape[1:], f32)
        return 0

    lax.fori_loop(0, acc.shape[0] // 8, zero, 0)
    for copy in copies:
        copy.wait()

    def row_tile(t, _):
        pltpu.make_async_copy(values.at[t], a_ref.at[t], a_sem.at[t]).wait()
        n = cnt[t]

        def lanes(k0, count):
            got = []
            for j in range(count):
                a = a_ref[t, k0 + j]
                got.append(jnp.where(k0 + j < n, a, jnp.zeros_like(a)))
            return jnp.concatenate(got, axis=1)

        def forward(i, af):
            k0 = i * FWD_SLOTS
            rows = [
                win[pl.ds(pl.multiple_of(idx[t, k0 + j] * tile, tile), tile), :]
                for j in range(FWD_SLOTS)
            ]
            return af + jnp.dot(
                lanes(k0, FWD_SLOTS), jnp.concatenate(rows, axis=0), preferred_element_type=f32
            )

        at = pl.ds(pl.multiple_of(t * tile, tile), tile)
        trips = (n + FWD_SLOTS - 1) // FWD_SLOTS
        af = lax.fori_loop(0, trips, forward, jnp.zeros((tile, width), f32)).astype(bf16)
        pre = jnp.dot(af, w_ref[...], preferred_element_type=f32)
        sig = jax.nn.sigmoid(pre)
        out_ref[at, :] = (pre * sig).astype(bf16)
        g = (cot_ref[at, :].astype(f32) * sig * (1.0 + pre * (1.0 - sig))).astype(bf16)
        wg_ref[...] += lax.dot_general(
            af, g, (((0,), (0,)), ((), ())), preferred_element_type=f32
        )
        gwt = lax.dot_general(
            w_ref[...], g, (((1,), (1,)), ((), ())), preferred_element_type=f32
        ).astype(bf16)

        def backward(i, _):
            k0 = i * BWD_SLOTS
            r = jnp.dot(gwt, lanes(k0, BWD_SLOTS), preferred_element_type=f32)
            for j in range(BWD_SLOTS):
                acc[idx[t, k0 + j]] += r[:, j * tile : (j + 1) * tile]
            return 0

        lax.fori_loop(0, (n + BWD_SLOTS - 1) // BWD_SLOTS, backward, 0)
        return 0

    lax.fori_loop(0, n_tiles, row_tile, 0)
    stages, chunk = stage.shape[:2]

    def copy(slot, out, at):
        return pltpu.make_async_copy(stage.at[slot], out.at[pl.ds(at, chunk)], out_sem.at[slot])

    done = 0
    for out in outs:
        steps = out.shape[0] // chunk

        def emit(i, _, out=out, done=done):
            number = done + i
            slot = lax.rem(number, stages)

            @pl.when(number >= stages)
            def _():
                copy(slot, out, 0).wait()

            stage[slot] = acc[pl.ds(number * chunk, chunk)].astype(bf16)
            copy(slot, out, i * chunk).start()
            return 0

        lax.fori_loop(0, steps, emit, 0)
        done += steps
    for slot in range(stages):
        copy(slot, outs[0], 0).wait()


def layer(idx, cnt, tile_values, parts, weight, cotangent, groups):
    nt, _, tile, _ = tile_values.shape
    width = weight.shape[0]
    n_win = 2 * sum(groups)
    smem = pl.BlockSpec(memory_space=pltpu.SMEM)
    vmem = pl.BlockSpec(memory_space=pltpu.VMEM)
    anywhere = pl.BlockSpec(memory_space=pl.ANY)
    return pl.pallas_call(
        functools.partial(kernel, len(parts), 2 * len(groups)),
        in_specs=[smem, smem] + [anywhere] * (1 + len(parts)) + [vmem, vmem],
        out_specs=[vmem, vmem] + [anywhere] * (2 * len(groups)),
        scratch_shapes=[
            pltpu.VMEM(tile_values.shape, bf16),
            pltpu.VMEM((n_win * tile, width), bf16),
            pltpu.VMEM((n_win, width, tile), f32),
            pltpu.VMEM((STAGES, CHUNK, width, tile), bf16),
            pltpu.SemaphoreType.DMA((len(parts),)),
            pltpu.SemaphoreType.DMA((nt,)),
            pltpu.SemaphoreType.DMA((STAGES,)),
        ],
        out_shape=[
            jax.ShapeDtypeStruct((nt * tile, width), bf16),
            jax.ShapeDtypeStruct((width, width), f32),
        ]
        + [jax.ShapeDtypeStruct((g, width, tile), bf16) for _ in range(2) for g in groups],
        compiler_params=pltpu.CompilerParams(vmem_limit_bytes=60 * 2**20),
        cost_estimate=pl.CostEstimate(
            flops=4 * tile_values.size * width,
            bytes_accessed=6 * tile_values.size,
            transcendentals=0,
        ),
    )(idx, cnt, tile_values, *parts, weight, cotangent)


def tied(x, *earlier):
    return pl.pallas_call(
        lambda *refs: None,
        in_specs=[pl.BlockSpec(memory_space=pl.ANY)] * (1 + len(earlier)),
        out_specs=pl.BlockSpec(memory_space=pl.ANY),
        out_shape=jax.ShapeDtypeStruct(x.shape, x.dtype),
        input_output_aliases={0: 0},
    )(x, *earlier)


def never(*earlier):
    out = False
    for x in earlier:
        v = x[(0,) * x.ndim]
        out |= (v != v) & (v == v)
    return out


def near(group, rep, axis, step, n_rows, n_rep):
    if axis == "z":
        return (group + step) % n_rows * n_rep + rep
    return group * n_rep + (rep + 2 * step) % n_rep


def moved(x, moves, back=False):
    n_rows, n_rep = lax.axis_size("rows"), lax.axis_size("rep")
    pairs = []
    for group in range(n_rows):
        for rep in range(n_rep):
            if moves[rep % 2]:
                source = near(group, rep, *moves[rep % 2], n_rows, n_rep)
                pairs.append((source, group * n_rep + rep))
    if back:
        pairs = [(target, source) for source, target in pairs]
    return lax.ppermute(x, ("rows", "rep"), pairs)


FIRST_UP, FIRST_DOWN = (("z", -1), ("y", 1)), (("z", 1), ("y", -1))
HALF_UP, HALF_DOWN = (None, ("y", 1)), (None, ("y", -1))
NEXT_UP, NEXT_DOWN = (("y", 1), ("z", -1)), (("y", -1), ("z", 1))


def from_core(x):
    return lax.ppermute(x, "rep", [(i, i ^ 1) for i in range(lax.axis_size("rep"))])


def gather(features, core):
    rows = features.shape[0]
    half = rows // 2
    up, down = moved(features, FIRST_UP), moved(features, FIRST_DOWN)
    near3 = jnp.concatenate([features, up, down])
    far = jnp.concatenate([moved(up[:half], HALF_UP), moved(down[half:], HALF_DOWN)])
    up, down = moved(near3, NEXT_UP), moved(near3, NEXT_DOWN)
    crossing = jnp.concatenate([far, far[:half]])
    swapped = from_core(near3)
    first = (core == 0) | never(swapped)
    last_up = moved(jnp.where(first, up[: 3 * half], crossing), NEXT_UP)
    last_down = moved(jnp.where(first, down[3 * half :], crossing), NEXT_DOWN)
    mine = [last_up, last_down, up, down, far]
    return mine + [near3] + [from_core(x) for x in mine] + [swapped]


class Steps:
    def __init__(self, term, core):
        height = term.shape[0] // 2
        low, high = term[:height], term[height:]
        self.got = from_core(jnp.where(core == 0, high, low))
        self.x = jnp.where(core == 0, low, high) + self.got
        self.left = [
            (axis, bit)
            for axis, first in (("rep", 2), ("rows", 1))
            for bit in (1 << k for k in range(10))
            if first <= bit < lax.axis_size(axis)
        ]

    def go(self, count):
        for axis, bit in self.left[:count]:
            pairs = [(i, i ^ bit) for i in range(lax.axis_size(axis))]
            self.got = lax.ppermute(self.x, axis, pairs)
            self.x = self.x + self.got
        self.left = self.left[count:]

    def after(self, *earlier):
        self.x = jnp.where(never(*earlier), 0.0, self.x)

    def whole(self, core):
        self.go(len(self.left))
        other = from_core(self.x)
        halves = [self.x, other], [other, self.x]
        return jnp.where(core == 0, *(jnp.concatenate(h) for h in halves))


def scatter(mine, other, own, core, steps):
    half = own // 2
    cut = 3 * half
    last = (mine[0].astype(f32) + from_core(other[0]).astype(f32)).astype(bf16)
    begun = last[:1, :8]
    middle, first = (
        m.astype(f32) + from_core(tied(o, begun)).astype(f32)
        for m, o in zip(mine[1:], other[1:])
    )
    last_up = moved(last[:cut], NEXT_UP, back=True).astype(f32)
    last_down = moved(last[cut:], NEXT_DOWN, back=True).astype(f32)
    steps.go(2)
    up, down = middle[: 2 * cut], middle[2 * cut :]
    along = ((core == 0) | never(steps.x)).astype(f32)
    up = jnp.concatenate([up[:cut] + along * last_up, up[cut:]]).astype(bf16)
    down = jnp.concatenate([down[:cut], down[cut:] + along * last_down]).astype(bf16)
    across = (core != 0).astype(f32)
    far = (first[:own] + across * (last_up[:own] + last_down[:own])).astype(bf16)
    next_up, next_down = moved(up, NEXT_UP, back=True), moved(down, NEXT_DOWN, back=True)
    half_up = moved(far[:half], HALF_UP, back=True)
    half_down = moved(far[half:], HALF_DOWN, back=True)
    steps.go(1)
    steps.after(half_up, half_down)
    steps.go(2)
    near3 = first[own:] + next_up.astype(f32) + next_down.astype(f32)
    home, up, down = near3[:own], near3[own : 2 * own], near3[2 * own :]
    none = never(steps.x)
    up = jnp.concatenate([up[:half] + half_up.astype(f32), up[half:]])
    down = jnp.concatenate([down[:half], down[half:] + half_down.astype(f32)])
    up, down = (jnp.where(none, 0.0, x).astype(bf16) for x in (up, down))
    return (
        home
        + moved(up, FIRST_UP, back=True).astype(f32)
        + moved(down, FIRST_DOWN, back=True).astype(f32)
    )


def local(features, weight, tile_values, tile_cols, tile_live, cotangent):
    n_rows, n_rep = lax.axis_size("rows"), lax.axis_size("rep")
    rep = lax.axis_index("rep")
    node_dev, width = features.shape
    tile = tile_values.shape[2]
    own = node_dev // tile
    group_tiles = own * n_rep
    core = rep % 2
    plans = [layout(own, c) for c in range(2)]
    groups = [len(keys) for keys in plans[0]]
    table = np.zeros((2, 3, n_rep // 2, own), np.int32)
    for c, plan in enumerate(plans):
        for at, key in enumerate(sum(plan, [])):
            if key:
                table[(c, *key)] = at
    place = jnp.mod(tile_cols // group_tiles - lax.axis_index("rows") + 1, n_rows)
    inner = tile_cols % group_tiles
    owner = inner // own
    dy = jnp.mod(owner // 2 - rep // 2, n_rep // 2)
    key = (((owner % 2) * 3 + place) * (n_rep // 2) + dy) * own + inner % own
    hit = key[:, :, None] == jnp.arange(table.size, dtype=jnp.int32)
    at = jnp.sum(jnp.where(hit, jnp.asarray(table.reshape(-1)), 0), axis=2)
    idx = jnp.mod(owner + rep, 2) * sum(groups) + at
    cnt = jnp.sum(tile_live, axis=1)

    parts = gather(features, core)
    output, term, *grads = layer(idx, cnt, tile_values, parts, weight, cotangent, groups)
    steps = Steps(term, core)
    total = scatter(grads[: len(groups)], grads[len(groups) :], own, core, steps)
    weight_grad = steps.whole(core)
    feature_grad = jnp.swapaxes(total, 1, 2).reshape(node_dev, width).astype(bf16)
    return (output, feature_grad, weight_grad)


def solution(mesh):
    placed = (
        P(("rows", "rep"), None),
        P(),
        P(("rows", "rep"), None, None, None),
        P(("rows", "rep"), None),
        P(("rows", "rep"), None),
        P(("rows", "rep"), None),
    )
    return jax.shard_map(
        local,
        mesh=mesh,
        in_specs=placed,
        out_specs=(P(("rows", "rep"), None), P(("rows", "rep"), None), P()),
        check_vma=False,
    )
```

time: 194 us -> 189 us (0.974)
  waiting for transfers between devices: 85.2 us -> 66.1 us
  between operations: 1.05 us -> 14 us
  starting transfers between devices: 53 us -> 43.2 us
  local copies, waits for them, and re-layouts: 7.5 us -> 16 us
  Pallas kernels: 28.7 us -> 32.3 us
  other arithmetic: 17.1 us -> 14.8 us
    ppermute x6, waiting for transfers between devices: 43.3 us -> 34.2 us  [go(): self.got = lax.ppermute(self.x, axis, pairs)]
    ppermute x16, waiting for transfers between devices: 31.5 us -> 24.3 us  [moved(): return lax.ppermute(x, ('rows', 'rep'), pairs)]
    ppermute x16, starting transfers between devices: 31 us -> 25.8 us  [moved(): return lax.ppermute(x, ('rows', 'rep'), pairs)]
    ppermute x6, starting transfers between devices: 6.94 us -> 2.29 us  [go(): self.got = lax.ppermute(self.x, axis, pairs)]
    slice x2 -> x7, local copies, waits for them, and re-layouts: 0.08 us -> 3.86 us  [the longest x5 3.24 us: never(): v = x[(0,) * x.ndim]]
    pallas_call x1 -> x3, Pallas kernels: 28.7 us -> 32.3 us  [the longest x1 32.3 us: layer(): pl.pallas_call(functools.partial(kernel, len(parts), 2 * len(groups)), in...]
    unnamed x21, local copies, waits for them, and re-layouts: 2.84 us -> 6 us
    ppermute x11, waiting for transfers between devices: 10.4 us -> 7.61 us  [from_core(): lax.ppermute(x, 'rep', [(i, i ^ 1) for i in range(lax.axis_size('rep'))])]
  transfers between devices with their start and end apart: 33 -> 33, of which waited for: 15 -> 16; matrix products, arithmetic and copies ran while one was open for 12% -> 11% of each run, Pallas kernels for 0% -> 0%
where the time goes in v5:
time: 189 us; the launch traced here: 186 us
  waiting for transfers between devices  66.1 us (35%)
  starting transfers between devices  43.2 us (23%)
  Pallas kernels  32.3 us (17%)
  local copies, waits for them, and re-layouts  16 us (8%)
  other arithmetic  14.8 us (8%)
  between operations  14 us (7%)
    ppermute x6, waiting for transfers between devices, go(): self.got = lax.ppermute(self.x, axis, pairs)  34.2 us
    pallas_call x1, Pallas kernels, layer(): pl.pallas_call(functools.partial(kernel, len(parts), 2 * len(groups)), in...  32.3 us
    ppermute x16, starting transfers between devices, moved(): return lax.ppermute(x, ('rows', 'rep'), pairs)  25.8 us
    ppermute x16, waiting for transfers between devices, moved(): return lax.ppermute(x, ('rows', 'rep'), pairs)  24.3 us
    ppermute x11, starting transfers between devices, from_core(): lax.ppermute(x, 'rep', [(i, i ^ 1) for i in range(lax.axis_size('rep'))])  15.1 us
    ppermute x11, waiting for transfers between devices, from_core(): lax.ppermute(x, 'rep', [(i, i ^ 1) for i in range(lax.axis_size('rep'))])  7.61 us
    unnamed x21, local copies, waits for them, and re-layouts  6 us
  transfers between devices with their start and end apart: 33, of which 16 were waited for; matrix products, arithmetic and copies ran while one was open for 11% of the time, Pallas kernels for 0%

profile of v5, /device:TPU:0, one launch (start us, length us, event | category | flops | bytes accessed | tf_op | source)
XLA Modules:
  0.0 186.4 jit_solution(14071048787790655439)
XLA Ops:
  0.6 2.1 %collective-permute-start = (bf16[1024,256]{1,0:T(8,128)(2,1)}, bf16[1024,256]{1,0:T(8,128)(2,1)S(1)}, u32[]{:S(2)}, u32[]{:S(2)}) collective-permute-start(bf16[1024,256]{1,0:T(8,128)(2,1)} %param.7), channel_id=1, source_target_pairs={{120,0},{3,1},{122,2},{5,3},{124,4},{7,5},{126,6},{1,7},{0,8},{11,... | collective-permute-start | bytes 1572872 | tf_op jit(solution)/shard_map/ppermute | solution.py:202
  2.7 4.4 %collective-permute-start.1 = (bf16[1024,256]{1,0:T(8,128)(2,1)}, bf16[1024,256]{1,0:T(8,128)(2,1)S(1)}, u32[]{:S(2)}, u32[]{:S(2)}) collective-permute-start(bf16[1024,256]{1,0:T(8,128)(2,1)} %param.7), channel_id=1, source_target_pairs={{8,0},{7,1},{10,2},{1,3},{12,4},{3,5},{14,6},{5,7},{16,8},{15,9},{... | collective-permute-start | bytes 1572872 | tf_op jit(solution)/shard_map/ppermute | solution.py:202
  7.1 1.9 %constant_dynamic-update-slice_fusion.2 = bf16[3072,256]{1,0:T(8,128)(2,1)} fusion(bf16[1024,256]{1,0:T(8,128)(2,1)} %param.7), kind=kLoop, calls=%fused_computation.35 | loop fusion | bytes 1048576
  9.0 5.3 %collective-permute-done = bf16[1024,256]{1,0:T(8,128)(2,1)S(1)} collective-permute-done((bf16[1024,256]{1,0:T(8,128)(2,1)}, bf16[1024,256]{1,0:T(8,128)(2,1)S(1)}, u32[]{:S(2)}, u32[]{:S(2)}) %collective-permute-start) | collective-permute-done | bytes 524320 | tf_op jit(solution)/shard_map/ppermute | solution.py:202
  30.0 10.7 %collective-permute-done.7.refs_3_ = bf16[3072,256]{1,0:T(8,128)(2,1)S(1)} collective-permute-done((bf16[3072,256]{1,0:T(8,128)(2,1)}, bf16[3072,256]{1,0:T(8,128)(2,1)S(1)}, u32[]{:S(2)}, u32[]{:S(2)}) %collective-permute-start.7) | collective-permute-done | bytes 1572896 | tf_op jit(solution)/shard_map/ppermute | solution.py:202
  44.5 7.2 %collective-permute-start.12 = (bf16[3072,256]{1,0:T(8,128)(2,1)S(1)}, bf16[3072,256]{1,0:T(8,128)(2,1)}, u32[]{:S(2)}, u32[]{:S(2)}) collective-permute-start(bf16[3072,256]{1,0:T(8,128)(2,1)S(1)} %collective-permute-done.7.refs_3_), channel_id=1, source_target_pairs={{0,1},{1,0},{2,3},{3,2},{4,5},{5,4},{6,7},{7,6},{8,9},{9,8},{10,11... | collective-permute-start | bytes 4718600 | tf_op jit(solution)/shard_map/ppermute | solution.py:211
  51.8 4.5 %collective-permute-done.8.refs_1_ = bf16[1536,256]{1,0:T(8,128)(2,1)} collective-permute-done((bf16[1536,256]{1,0:T(8,128)(2,1)S(1)}, bf16[1536,256]{1,0:T(8,128)(2,1)}, u32[]{:S(2)}, u32[]{:S(2)}) %collective-permute-start.8) | collective-permute-done | bytes 786464 | tf_op jit(solution)/shard_map/ppermute | solution.py:202
  56.3 4.4 %collective-permute-start.10 = (bf16[1536,256]{1,0:T(8,128)(2,1)}, bf16[1536,256]{1,0:T(8,128)(2,1)}, u32[]{:S(2)}, u32[]{:S(2)}) collective-permute-start(bf16[1536,256]{1,0:T(8,128)(2,1)} %collective-permute-done.8.refs_1_), channel_id=1, source_target_pairs={{0,1},{1,0},{2,3},{3,2},{4,5},{5,4},{6,7},{7,6},{8,9},{9,8},{10,11... | collective-permute-start | bytes 2359304 | tf_op jit(solution)/shard_map/ppermute | solution.py:211
  60.7 3.3 %collective-permute-done.6.refs_0_ = bf16[1536,256]{1,0:T(8,128)(2,1)} collective-permute-done((bf16[1536,256]{1,0:T(8,128)(2,1)S(1)}, bf16[1536,256]{1,0:T(8,128)(2,1)}, u32[]{:S(2)}, u32[]{:S(2)}) %collective-permute-start.6) | collective-permute-done | bytes 786464 | tf_op jit(solution)/shard_map/ppermute | solution.py:202
  63.9 2.6 %collective-permute-start.9 = (bf16[1536,256]{1,0:T(8,128)(2,1)}, bf16[1536,256]{1,0:T(8,128)(2,1)}, u32[]{:S(2)}, u32[]{:S(2)}) collective-permute-start(bf16[1536,256]{1,0:T(8,128)(2,1)} %collective-permute-done.6.refs_0_), channel_id=1, source_target_pairs={{0,1},{1,0},{2,3},{3,2},{4,5},{5,4},{6,7},{7,6},{8,9},{9,8},{10,11... | collective-permute-start | bytes 2359304 | tf_op jit(solution)/shard_map/ppermute | solution.py:211
  70.2 32.3 %shard_map.94 = (bf16[1024,256]{1,0:T(8,128)(2,1)}, f32[256,256]{1,0:T(8,128)}, bf16[24,256,128]{2,1,0:T(8,128)(2,1)}, bf16[48,256,128]{2,1,0:T(8,128)(2,1)}, bf...) custom-call(s32[8,48]{1,0:T(8,128)} %fusion.13.idx, ...), custom_call_target="tpu_custom_call" | custom-call | flops 6442450944 | bytes 37748736 | tf_op jit(solution)/shard_map/pallas_call | solution.py:141
  102.6 3.6 %collective-permute-done.14 = bf16[24,256,128]{2,1,0:T(8,128)(2,1)S(1)} collective-permute-done((bf16[24,256,128]{2,1,0:T(8,128)(2,1)}, bf16[24,256,128]{2,1,0:T(8,128)(2,1)S(1)}, u32[]{:S(2)}, u32[]{:S(2)}) %collective-permute-start.14) | collective-permute-done | bytes 1572896 | tf_op jit(solution)/shard_map/ppermute | solution.py:211
  106.2 1.9 %add_convert_fusion = bf16[24,256,128]{2,1,0:T(8,128)(2,1)S(1)} fusion(bf16[24,256,128]{2,1,0:T(8,128)(2,1)S(1)} %collective-permute-done.14, bf16[24,256,128]{2,1,0:T(8,128)(2,1)} %get-tuple-element.14), kind=kLoop, calls=%fused_computation.4 | loop fusion | flops 3145728 | bytes 4718592 | tf_op jit(solution)/shard_map/convert_element_type | solution.py:263
  109.3 2.9 %collective-permute-start.22 = (bf16[12,256,128]{2,1,0:T(8,128)(2,1)S(1)}, bf16[12,256,128]{2,1,0:T(8,128)(2,1)S(1)}, u32[]{:S(2)}, u32[]{:S(2)}) collective-permute-start(bf16[12,256,128]{2,1,0:T(8,128)(2,1)S(1)} %get-tuple-element.30), channel_id=1, source_target_pairs={{0,6},{1,9},{2,0},{3,11},{4,2},{5,13},{6,4},{7,15},{8,14},{9,17},{... | collective-permute-start | bytes 2359304 | tf_op jit(solution)/shard_map/ppermute | solution.py:202
  115.3 10.2 %collective-permute-done.18 = f32[128,256]{1,0:T(8,128)S(1)} collective-permute-done((f32[128,256]{1,0:T(8,128)S(1)}, f32[128,256]{1,0:T(8,128)S(1)}, u32[]{:S(2)}, u32[]{:S(2)}) %collective-permute-start.18) | collective-permute-done | bytes 131104 | tf_op jit(solution)/shard_map/ppermute | solution.py:246
  127.2 4.9 %collective-permute-done.19 = f32[128,256]{1,0:T(8,128)S(1)} collective-permute-done((f32[128,256]{1,0:T(8,128)S(1)}, f32[128,256]{1,0:T(8,128)S(1)}, u32[]{:S(2)}, u32[]{:S(2)}) %collective-permute-start.19) | collective-permute-done | bytes 131104 | tf_op jit(solution)/shard_map/ppermute | solution.py:246
  137.1 3.2 %fusion.31 = (bf16[48,256,128]{2,1,0:T(8,128)(2,1)S(1)}, f32[48,256,128]{2,1,0:T(8,128)S(1)}) fusion(bf16[48,256,128]{2,1,0:T(8,128)(2,1)} %collective-permute-done.16, bf16[48,256,128]{2,1,0:T(8,128)(2,1)S(1)} %copy-done.2), kind=kLoop, calls=%fused_computation.88 | loop fusion | flops 6291456 | bytes 15728640 | tf_op jit(solution)/shard_map/convert.5
  141.5 2.1 %collective-permute-start.21 = (bf16[24,256,128]{2,1,0:T(8,128)(2,1)S(1)}, bf16[24,256,128]{2,1,0:T(8,128)(2,1)S(1)}, u32[]{:S(2)}, u32[]{:S(2)}) collective-permute-start(bf16[24,256,128]{2,1,0:T(8,128)(2,1)S(1)} %pad_maximum_fusion), channel_id=1, source_target_pairs={{0,2},{1,121},{2,4},{3,123},{4,6},{5,125},{6,0},{7,127},{8,10},{9,... | collective-permute-start | bytes 4718600 | tf_op jit(solution)/shard_map/ppermute | solution.py:202
  143.6 2.3 %convert_add_fusion.1 = f32[32,256,128]{2,1,0:T(8,128)S(1)} fusion(bf16[32,256,128]{2,1,0:T(8,128)(2,1)} %collective-permute-done.15, bf16[32,256,128]{2,1,0:T(8,128)(2,1)S(1)} %copy-done.3), kind=kLoop, calls=%fused_computation.1 | loop fusion | flops 3145728 | bytes 8388608 | tf_op jit(solution)/shard_map/add | solution.py:266
  154.1 6.5 %collective-permute-done.27 = f32[128,256]{1,0:T(8,128)S(1)} collective-permute-done((f32[128,256]{1,0:T(8,128)S(1)}, f32[128,256]{1,0:T(8,128)S(1)}, u32[]{:S(2)}, u32[]{:S(2)}) %collective-permute-start.27) | collective-permute-done | bytes 131104 | tf_op jit(solution)/shard_map/ppermute | solution.py:246
  160.7 5.0 %collective-permute-done.28 = f32[128,256]{1,0:T(8,128)S(1)} collective-permute-done((f32[128,256]{1,0:T(8,128)S(1)}, f32[128,256]{1,0:T(8,128)S(1)}, u32[]{:S(2)}, u32[]{:S(2)}) %collective-permute-start.28) | collective-permute-done | bytes 131104 | tf_op jit(solution)/shard_map/ppermute | solution.py:246
  169.8 2.8 %collective-permute-start.30 = (bf16[8,256,128]{2,1,0:T(8,128)(2,1)S(1)}, bf16[8,256,128]{2,1,0:T(8,128)(2,1)S(1)}, u32[]{:S(2)}, u32[]{:S(2)}) collective-permute-start(bf16[8,256,128]{2,1,0:T(8,128)(2,1)S(1)} %fusion.9), channel_id=1, source_target_pairs={{0,8},{1,7},{2,10},{3,1},{4,12},{5,3},{6,14},{7,5},{8,16},{9,15},{... | collective-permute-start | bytes 1572872 | tf_op jit(solution)/shard_map/ppermute | solution.py:202
  172.7 2.7 %collective-permute-start.29 = (bf16[8,256,128]{2,1,0:T(8,128)(2,1)S(1)}, bf16[8,256,128]{2,1,0:T(8,128)(2,1)S(1)}, u32[]{:S(2)}, u32[]{:S(2)}) collective-permute-start(bf16[8,256,128]{2,1,0:T(8,128)(2,1)S(1)} %fusion.8), channel_id=1, source_target_pairs={{0,120},{1,3},{2,122},{3,5},{4,124},{5,7},{6,126},{7,1},{8,0},{9,1... | collective-permute-start | bytes 1572872 | tf_op jit(solution)/shard_map/ppermute | solution.py:202
  175.4 7.5 %collective-permute-done.31 = f32[128,256]{1,0:T(8,128)S(1)} collective-permute-done((f32[128,256]{1,0:T(8,128)S(1)}, f32[128,256]{1,0:T(8,128)S(1)}, u32[]{:S(2)}, u32[]{:S(2)}) %collective-permute-start.31) | collective-permute-done | bytes 131104 | tf_op jit(solution)/shard_map/ppermute | solution.py:246
  (109 shorter events, 38.1 us)
Async XLA Ops:
  0.6 13.8 %collective-permute-start = (bf16[1024,256]{1,0:T(8,128)(2,1)}, bf16[1024,256]{1,0:T(8,128)(2,1)S(1)}, u32[]{:S(2)}, u32[]{:S(2)}) collective-permute-start(bf16[1024,256]{1,0:T(8,128)(2,1)} %param.7), channel_id=1, source_target_pairs={{120,0},{3,1},{122,2},{5,3},{124,4},{7,5},{126,6},{1,7},{0,8},{11,... | collective-permute-start | bytes 1572872 | tf_op jit(solution)/shard_map/ppermute | solution.py:202
  2.7 12.5 %collective-permute-start.1 = (bf16[1024,256]{1,0:T(8,128)(2,1)}, bf16[1024,256]{1,0:T(8,128)(2,1)S(1)}, u32[]{:S(2)}, u32[]{:S(2)}) collective-permute-start(bf16[1024,256]{1,0:T(8,128)(2,1)} %param.7), channel_id=1, source_target_pairs={{8,0},{7,1},{10,2},{1,3},{12,4},{3,5},{14,6},{5,7},{16,8},{15,9},{... | collective-permute-start | bytes 1572872 | tf_op jit(solution)/shard_map/ppermute | solution.py:202
  16.1 10.1 %collective-permute-start.2 = (bf16[3072,256]{1,0:T(8,128)(2,1)}, bf16[3072,256]{1,0:T(8,128)(2,1)}, u32[]{:S(2)}, u32[]{:S(2)}) collective-permute-start(bf16[3072,256]{1,0:T(8,128)(2,1)} %constant_dynamic-update-slice_fusion.refs_5_), channel_id=1, source_target_pairs={{0,1},{1,0},{2,3},{3,2},{4,5},{5,4},{6,7},{7,6},{8,9},{9,8},{10,11... | collective-permute-start | bytes 4718600 | tf_op jit(solution)/shard_map/ppermute | solution.py:211
  16.1 24.6 %collective-permute-start.7 = (bf16[3072,256]{1,0:T(8,128)(2,1)}, bf16[3072,256]{1,0:T(8,128)(2,1)S(1)}, u32[]{:S(2)}, u32[]{:S(2)}) collective-permute-start(bf16[3072,256]{1,0:T(8,128)(2,1)} %constant_dynamic-update-slice_fusion.refs_5_), channel_id=1, source_target_pairs={{6,0},{9,1},{0,2},{11,3},{2,4},{13,5},{4,6},{15,7},{14,8},{17,9},{... | collective-permute-start | bytes 4718600 | tf_op jit(solution)/shard_map/ppermute | solution.py:202
  17.6 23.4 %collective-permute-start.3 = (bf16[3072,256]{1,0:T(8,128)(2,1)}, bf16[3072,256]{1,0:T(8,128)(2,1)S(1)}, u32[]{:S(2)}, u32[]{:S(2)}) collective-permute-start(bf16[3072,256]{1,0:T(8,128)(2,1)} %constant_dynamic-update-slice_fusion.refs_5_), channel_id=1, source_target_pairs={{2,0},{121,1},{4,2},{123,3},{6,4},{125,5},{0,6},{127,7},{10,8},{1,... | collective-permute-start | bytes 4718600 | tf_op jit(solution)/shard_map/ppermute | solution.py:202
  42.9 13.4 %collective-permute-start.8 = (bf16[1536,256]{1,0:T(8,128)(2,1)S(1)}, bf16[1536,256]{1,0:T(8,128)(2,1)}, u32[]{:S(2)}, u32[]{:S(2)}) collective-permute-start(bf16[1536,256]{1,0:T(8,128)(2,1)S(1)} %get-tuple-element.31), channel_id=1, source_target_pairs={{6,0},{9,1},{0,2},{11,3},{2,4},{13,5},{4,6},{15,7},{14,8},{17,9},{... | collective-permute-start | bytes 2359304 | tf_op jit(solution)/shard_map/ppermute | solution.py:202
  44.5 24.9 %collective-permute-start.12 = (bf16[3072,256]{1,0:T(8,128)(2,1)S(1)}, bf16[3072,256]{1,0:T(8,128)(2,1)}, u32[]{:S(2)}, u32[]{:S(2)}) collective-permute-start(bf16[3072,256]{1,0:T(8,128)(2,1)S(1)} %collective-permute-done.7.refs_3_), channel_id=1, source_target_pairs={{0,1},{1,0},{2,3},{3,2},{4,5},{5,4},{6,7},{7,6},{8,9},{9,8},{10,11... | collective-permute-start | bytes 4718600 | tf_op jit(solution)/shard_map/ppermute | solution.py:211
  51.8 17.7 %collective-permute-start.11 = (bf16[3072,256]{1,0:T(8,128)(2,1)S(1)}, bf16[3072,256]{1,0:T(8,128)(2,1)}, u32[]{:S(2)}, u32[]{:S(2)}) collective-permute-start(bf16[3072,256]{1,0:T(8,128)(2,1)S(1)} %collective-permute-done.3.refs_2_), channel_id=1, source_target_pairs={{0,1},{1,0},{2,3},{3,2},{4,5},{5,4},{6,7},{7,6},{8,9},{9,8},{10,11... | collective-permute-start | bytes 4718600 | tf_op jit(solution)/shard_map/ppermute | solution.py:211
  51.8 12.1 %collective-permute-start.6 = (bf16[1536,256]{1,0:T(8,128)(2,1)S(1)}, bf16[1536,256]{1,0:T(8,128)(2,1)}, u32[]{:S(2)}, u32[]{:S(2)}) collective-permute-start(bf16[1536,256]{1,0:T(8,128)(2,1)S(1)} %get-tuple-element.32), channel_id=1, source_target_pairs={{2,0},{121,1},{4,2},{123,3},{6,4},{125,5},{0,6},{127,7},{10,8},{1,... | collective-permute-start | bytes 2359304 | tf_op jit(solution)/shard_map/ppermute | solution.py:202
  56.3 13.1 %collective-permute-start.10 = (bf16[1536,256]{1,0:T(8,128)(2,1)}, bf16[1536,256]{1,0:T(8,128)(2,1)}, u32[]{:S(2)}, u32[]{:S(2)}) collective-permute-start(bf16[1536,256]{1,0:T(8,128)(2,1)} %collective-permute-done.8.refs_1_), channel_id=1, source_target_pairs={{0,1},{1,0},{2,3},{3,2},{4,5},{5,4},{6,7},{7,6},{8,9},{9,8},{10,11... | collective-permute-start | bytes 2359304 | tf_op jit(solution)/shard_map/ppermute | solution.py:211
  63.9 5.5 %collective-permute-start.9 = (bf16[1536,256]{1,0:T(8,128)(2,1)}, bf16[1536,256]{1,0:T(8,128)(2,1)}, u32[]{:S(2)}, u32[]{:S(2)}) collective-permute-start(bf16[1536,256]{1,0:T(8,128)(2,1)} %collective-permute-done.6.refs_0_), channel_id=1, source_target_pairs={{0,1},{1,0},{2,3},{3,2},{4,5},{5,4},{6,7},{7,6},{8,9},{9,8},{10,11... | collective-permute-start | bytes 2359304 | tf_op jit(solution)/shard_map/ppermute | solution.py:211
  108.7 26.9 %collective-permute-start.16 = (bf16[48,256,128]{2,1,0:T(8,128)(2,1)}, bf16[48,256,128]{2,1,0:T(8,128)(2,1)}, u32[]{:S(2)}, u32[]{:S(2)}) collective-permute-start(bf16[48,256,128]{2,1,0:T(8,128)(2,1)} %shard_map.96), channel_id=1, source_target_pairs={{0,1},{1,0},{2,3},{3,2},{4,5},{5,4},{6,7},{7,6},{8,9},{9,8},{10,11... | collective-permute-start | bytes 9437192 | tf_op jit(solution)/shard_map/ppermute | solution.py:211
  109.0 26.4 %collective-permute-start.20 = (bf16[12,256,128]{2,1,0:T(8,128)(2,1)S(1)}, bf16[12,256,128]{2,1,0:T(8,128)(2,1)S(1)}, u32[]{:S(2)}, u32[]{:S(2)}) collective-permute-start(bf16[12,256,128]{2,1,0:T(8,128)(2,1)S(1)} %get-tuple-element.29), channel_id=1, source_target_pairs={{0,2},{1,121},{2,4},{3,123},{4,6},{5,125},{6,0},{7,127},{8,10},{9,... | collective-permute-start | bytes 2359304 | tf_op jit(solution)/shard_map/ppermute | solution.py:202
  109.3 25.9 %collective-permute-start.22 = (bf16[12,256,128]{2,1,0:T(8,128)(2,1)S(1)}, bf16[12,256,128]{2,1,0:T(8,128)(2,1)S(1)}, u32[]{:S(2)}, u32[]{:S(2)}) collective-permute-start(bf16[12,256,128]{2,1,0:T(8,128)(2,1)S(1)} %get-tuple-element.30), channel_id=1, source_target_pairs={{0,6},{1,9},{2,0},{3,11},{4,2},{5,13},{6,4},{7,15},{8,14},{9,17},{... | collective-permute-start | bytes 2359304 | tf_op jit(solution)/shard_map/ppermute | solution.py:202
  113.0 30.7 %collective-permute-start.15 = (bf16[32,256,128]{2,1,0:T(8,128)(2,1)}, bf16[32,256,128]{2,1,0:T(8,128)(2,1)}, u32[]{:S(2)}, u32[]{:S(2)}) collective-permute-start(bf16[32,256,128]{2,1,0:T(8,128)(2,1)} %shard_map.95), channel_id=1, source_target_pairs={{0,1},{1,0},{2,3},{3,2},{4,5},{5,4},{6,7},{7,6},{8,9},{9,8},{10,11... | collective-permute-start | bytes 6291464 | tf_op jit(solution)/shard_map/ppermute | solution.py:211
  115.0 10.6 %collective-permute-start.18 = (f32[128,256]{1,0:T(8,128)S(1)}, f32[128,256]{1,0:T(8,128)S(1)}, u32[]{:S(2)}, u32[]{:S(2)}) collective-permute-start(f32[128,256]{1,0:T(8,128)S(1)} %select_add_fusion), channel_id=1, source_target_pairs={{0,2},{1,3},{2,0},{3,1},{4,6},{5,7},{6,4},{7,5},{8,10},{9,11},{10,... | collective-permute-start | bytes 393224 | tf_op jit(solution)/shard_map/ppermute | solution.py:246
  125.6 6.6 %collective-permute-start.19 = (f32[128,256]{1,0:T(8,128)S(1)}, f32[128,256]{1,0:T(8,128)S(1)}, u32[]{:S(2)}, u32[]{:S(2)}) collective-permute-start(f32[128,256]{1,0:T(8,128)S(1)} %add.134), channel_id=1, source_target_pairs={{0,4},{1,5},{2,6},{3,7},{4,0},{5,1},{6,2},{7,3},{8,12},{9,13},{10,... | collective-permute-start | bytes 393224 | tf_op jit(solution)/shard_map/ppermute | solution.py:246
  141.1 27.7 %collective-permute-start.23 = (bf16[24,256,128]{2,1,0:T(8,128)(2,1)S(1)}, bf16[24,256,128]{2,1,0:T(8,128)(2,1)S(1)}, u32[]{:S(2)}, u32[]{:S(2)}) collective-permute-start(bf16[24,256,128]{2,1,0:T(8,128)(2,1)S(1)} %pad_maximum_fusion.1), channel_id=1, source_target_pairs={{0,6},{1,9},{2,0},{3,11},{4,2},{5,13},{6,4},{7,15},{8,14},{9,17},{... | collective-permute-start | bytes 4718600 | tf_op jit(solution)/shard_map/ppermute | solution.py:202
  141.5 27.3 %collective-permute-start.21 = (bf16[24,256,128]{2,1,0:T(8,128)(2,1)S(1)}, bf16[24,256,128]{2,1,0:T(8,128)(2,1)S(1)}, u32[]{:S(2)}, u32[]{:S(2)}) collective-permute-start(bf16[24,256,128]{2,1,0:T(8,128)(2,1)S(1)} %pad_maximum_fusion), channel_id=1, source_target_pairs={{0,2},{1,121},{2,4},{3,123},{4,6},{5,125},{6,0},{7,127},{8,10},{9,... | collective-permute-start | bytes 4718600 | tf_op jit(solution)/shard_map/ppermute | solution.py:202
  147.5 6.5 %collective-permute-start.26 = (f32[128,256]{1,0:T(8,128)S(1)}, f32[128,256]{1,0:T(8,128)S(1)}, u32[]{:S(2)}, u32[]{:S(2)}) collective-permute-start(f32[128,256]{1,0:T(8,128)S(1)} %add.135), channel_id=1, source_target_pairs={{0,8},{8,0},{16,24},{24,16},{32,40},{40,32},{48,56},{56,48},{64,72... | collective-permute-start | bytes 393224 | tf_op jit(solution)/shard_map/ppermute | solution.py:246
  154.1 6.6 %collective-permute-start.27 = (f32[128,256]{1,0:T(8,128)S(1)}, f32[128,256]{1,0:T(8,128)S(1)}, u32[]{:S(2)}, u32[]{:S(2)}) collective-permute-start(f32[128,256]{1,0:T(8,128)S(1)} %add_select_fusion), channel_id=1, source_target_pairs={{0,16},{8,24},{16,0},{24,8},{32,48},{40,56},{48,32},{56,40},{64,80... | collective-permute-start | bytes 393224 | tf_op jit(solution)/shard_map/ppermute | solution.py:246
  169.8 15.4 %collective-permute-start.30 = (bf16[8,256,128]{2,1,0:T(8,128)(2,1)S(1)}, bf16[8,256,128]{2,1,0:T(8,128)(2,1)S(1)}, u32[]{:S(2)}, u32[]{:S(2)}) collective-permute-start(bf16[8,256,128]{2,1,0:T(8,128)(2,1)S(1)} %fusion.9), channel_id=1, source_target_pairs={{0,8},{1,7},{2,10},{3,1},{4,12},{5,3},{6,14},{7,5},{8,16},{9,15},{... | collective-permute-start | bytes 1572872 | tf_op jit(solution)/shard_map/ppermute | solution.py:202
  172.7 12.5 %collective-permute-start.29 = (bf16[8,256,128]{2,1,0:T(8,128)(2,1)S(1)}, bf16[8,256,128]{2,1,0:T(8,128)(2,1)S(1)}, u32[]{:S(2)}, u32[]{:S(2)}) collective-permute-start(bf16[8,256,128]{2,1,0:T(8,128)(2,1)S(1)} %fusion.8), channel_id=1, source_target_pairs={{0,120},{1,3},{2,122},{3,5},{4,124},{5,7},{6,126},{7,1},{8,0},{9,1... | collective-permute-start | bytes 1572872 | tf_op jit(solution)/shard_map/ppermute | solution.py:202
  175.4 7.5 %collective-permute-start.31 = (f32[128,256]{1,0:T(8,128)S(1)}, f32[128,256]{1,0:T(8,128)S(1)}, u32[]{:S(2)}, u32[]{:S(2)}) collective-permute-start(f32[128,256]{1,0:T(8,128)S(1)} %add.144), channel_id=1, source_target_pairs={{0,64},{8,72},{16,80},{24,88},{32,96},{40,104},{48,112},{56,120},{... | collective-permute-start | bytes 393224 | tf_op jit(solution)/shard_map/ppermute | solution.py:246
  (18 other events, 158.8 us)

commit v6 on v5

--- a/solution.py
+++ b/solution.py
@@ -220,78 +220,105 @@
     up, down = moved(near3, NEXT_UP), moved(near3, NEXT_DOWN)
     crossing = jnp.concatenate([far, far[:half]])
     swapped = from_core(near3)
-    first = (core == 0) | never(swapped)
+    swapped_far = from_core(far)
+    first = (core == 0) | never(swapped, swapped_far)
     last_up = moved(jnp.where(first, up[: 3 * half], crossing), NEXT_UP)
     last_down = moved(jnp.where(first, down[3 * half :], crossing), NEXT_DOWN)
-    mine = [last_up, last_down, up, down, far]
-    return mine + [near3] + [from_core(x) for x in mine] + [swapped]
+    mine = [last_up, last_down, up, down]
+    return mine + [far, near3] + [from_core(x) for x in mine] + [swapped_far, swapped]
+
+
+def others(x, axis, group, stride):
+    count = lax.axis_size(axis)
+    got = []
+    for step in range(1, group):
+        pairs = []
+        for i in range(count):
+            digit = i // stride % group
+            source = i + ((digit + step) % group - digit) * stride
+            pairs.append((source, i))
+        got.append((step, pairs))
+    return [lax.ppermute(x(step), axis, pairs) for step, pairs in got]
 
 
 class Steps:
-    def __init__(self, term, core):
+    def __init__(self, term, core, y):
         height = term.shape[0] // 2
         low, high = term[:height], term[height:]
-        self.got = from_core(jnp.where(core == 0, high, low))
-        self.x = jnp.where(core == 0, low, high) + self.got
-        self.left = [
-            (axis, bit)
-            for axis, first in (("rep", 2), ("rows", 1))
-            for bit in (1 << k for k in range(10))
-            if first <= bit < lax.axis_size(axis)
-        ]
-
-    def go(self, count):
-        for axis, bit in self.left[:count]:
-            pairs = [(i, i ^ bit) for i in range(lax.axis_size(axis))]
-            self.got = lax.ppermute(self.x, axis, pairs)
-            self.x = self.x + self.got
-        self.left = self.left[count:]
+        half = jnp.where(core == 0, low, high) + from_core(jnp.where(core == 0, high, low))
+        self.core, self.y, self.n_y = core, y, lax.axis_size("rep") // 2
+        self.x = half.reshape(self.n_y, height // self.n_y, term.shape[1])
+
+    def piece(self, at):
+        return lax.dynamic_index_in_dim(self.x, jnp.mod(at, self.n_y), 0, keepdims=False)
+
+    def scatter(self):
+        got = others(lambda step: self.piece(self.y - step), "rep", self.n_y, 2)
+        self.x = sum(got, self.piece(self.y))
+
+    def sum_rows(self, stride):
+        self.x = sum(others(lambda step: self.x, "rows", 4, stride), self.x)
+
+    def gather(self):
+        got = others(lambda step: self.x, "rep", self.n_y, 2)
+        blocks = jnp.zeros((self.n_y,) + self.x.shape, f32)
+        for step, block in enumerate([self.x, *got]):
+            at = jnp.mod(self.y + step, self.n_y)
+            blocks = lax.dynamic_update_index_in_dim(blocks, block, at, 0)
+        self.x = blocks.reshape(-1, self.x.shape[1])
+
+    def whole(self):
+        other = from_core(self.x)
+        halves = [self.x, other], [other, self.x]
+        return jnp.where(self.core == 0, *(jnp.concatenate(h) for h in halves))
 
     def after(self, *earlier):
         self.x = jnp.where(never(*earlier), 0.0, self.x)
 
-    def whole(self, core):
-        self.go(len(self.left))
-        other = from_core(self.x)
-        halves = [self.x, other], [other, self.x]
-        return jnp.where(core == 0, *(jnp.concatenate(h) for h in halves))
+
+def total(*terms):
+    return sum(x.astype(f32) for x in terms).astype(bf16)
+
+
+def widened(x, size, at):
+    return jnp.pad(x, ((at, size - at - x.shape[0]), (0, 0), (0, 0)))
 
 
 def scatter(mine, other, own, core, steps):
     half = own // 2
     cut = 3 * half
-    last = (mine[0].astype(f32) + from_core(other[0]).astype(f32)).astype(bf16)
-    begun = last[:1, :8]
-    middle, first = (
-        m.astype(f32) + from_core(tied(o, begun)).astype(f32)
-        for m, o in zip(mine[1:], other[1:])
-    )
-    last_up = moved(last[:cut], NEXT_UP, back=True).astype(f32)
-    last_down = moved(last[cut:], NEXT_DOWN, back=True).astype(f32)
-    steps.go(2)
-    up, down = middle[: 2 * cut], middle[2 * cut :]
-    along = ((core == 0) | never(steps.x)).astype(f32)
-    up = jnp.concatenate([up[:cut] + along * last_up, up[cut:]]).astype(bf16)
-    down = jnp.concatenate([down[:cut], down[cut:] + along * last_down]).astype(bf16)
-    across = (core != 0).astype(f32)
-    far = (first[:own] + across * (last_up[:own] + last_down[:own])).astype(bf16)
-    next_up, next_down = moved(up, NEXT_UP, back=True), moved(down, NEXT_DOWN, back=True)
+    last = total(mine[0], from_core(other[0]))
+    middle = from_core(tied(other[1], last[:1, :8], steps.x[:1, :8]))
+    last_up = moved(last[:cut], NEXT_UP, back=True)
+    last_down = moved(last[cut:], NEXT_DOWN, back=True)
+    first = from_core(tied(other[2], last[:1, :8], steps.x[:1, :8]))
+    steps.after(last_up, last_down)
+    steps.scatter()
+    along = core == 0
+    zero = jnp.zeros((), bf16)
+    to_up = jnp.where(along, widened(last_up, 2 * cut, 0), zero)
+    to_down = jnp.where(along, widened(last_down, 2 * cut, cut), zero)
+    next_up = total(mine[1][: 2 * cut], middle[: 2 * cut], to_up)
+    next_down = total(mine[1][2 * cut :], middle[2 * cut :], to_down)
+    next_up, next_down = moved(next_up, NEXT_UP, back=True), moved(next_down, NEXT_DOWN, back=True)
+    far = [jnp.where(along, zero, x[:own]) for x in (last_up, last_down)]
+    far = total(mine[2][:own], first[:own], *far)
     half_up = moved(far[:half], HALF_UP, back=True)
     half_down = moved(far[half:], HALF_DOWN, back=True)
-    steps.go(1)
     steps.after(half_up, half_down)
-    steps.go(2)
-    near3 = first[own:] + next_up.astype(f32) + next_down.astype(f32)
-    home, up, down = near3[:own], near3[own : 2 * own], near3[2 * own :]
+    steps.sum_rows(1)
+    steps.sum_rows(4)
     none = never(steps.x)
-    up = jnp.concatenate([up[:half] + half_up.astype(f32), up[half:]])
-    down = jnp.concatenate([down[:half], down[half:] + half_down.astype(f32)])
-    up, down = (jnp.where(none, 0.0, x).astype(bf16) for x in (up, down))
-    return (
-        home
-        + moved(up, FIRST_UP, back=True).astype(f32)
-        + moved(down, FIRST_DOWN, back=True).astype(f32)
-    )
+    steps.gather()
+
+    def near(k):
+        at = slice(k * own, (k + 1) * own)
+        return [mine[2][own:][at], first[own:][at], next_up[at], next_down[at]]
+
+    up = total(*near(1), jnp.where(none, zero, widened(half_up, own, 0)))
+    down = total(*near(2), jnp.where(none, zero, widened(half_down, own, half)))
+    ends = moved(up, FIRST_UP, back=True), moved(down, FIRST_DOWN, back=True)
+    return total(*near(0), *ends)
 
 
 def local(features, weight, tile_values, tile_cols, tile_live, cotangent):
@@ -321,10 +348,10 @@
 
     parts = gather(features, core)
     output, term, *grads = layer(idx, cnt, tile_values, parts, weight, cotangent, groups)
-    steps = Steps(term, core)
-    total = scatter(grads[: len(groups)], grads[len(groups) :], own, core, steps)
-    weight_grad = steps.whole(core)
-    feature_grad = jnp.swapaxes(total, 1, 2).reshape(node_dev, width).astype(bf16)
+    steps = Steps(term, core, rep // 2)
+    grad = scatter(grads[: len(groups)], grads[len(groups) :], own, core, steps)
+    weight_grad = steps.whole()
+    feature_grad = jnp.swapaxes(grad, 1, 2).reshape(node_dev, width)
     return (output, feature_grad, weight_grad)
 
 

time: 189 us -> 204 us (1.079)
  starting transfers between devices: 43.2 us -> 62.1 us
  between operations: 14 us -> 19.2 us
  waiting for transfers between devices: 66.1 us -> 60.9 us
  Pallas kernels: 32.3 us -> 27.9 us
  other arithmetic: 14.8 us -> 18.8 us
  local copies, waits for them, and re-layouts: 16 us -> 13.4 us
    ppermute x11, starting transfers between devices: 15.1 us -> 28.3 us  [from_core(): lax.ppermute(x, 'rep', [(i, i ^ 1) for i in range(lax.axis_size('rep'))])]
    ppermute x6 -> x12, waiting for transfers between devices: 34.2 us -> 22.1 us  [others(): return [lax.ppermute(x(step), axis, pairs) for step, pairs in got]]
    ppermute x6 -> x12, starting transfers between devices: 2.29 us -> 10.7 us  [others(): return [lax.ppermute(x(step), axis, pairs) for step, pairs in got]]
    ppermute x16, waiting for transfers between devices: 24.3 us -> 32.5 us  [moved(): return lax.ppermute(x, ('rows', 'rep'), pairs)]
    convert_element_type x7 -> x4, other arithmetic: 2.7 us -> 10.8 us  [total(): return sum((x.astype(f32) for x in terms)).astype(bf16)]
    pallas_call x1, Pallas kernels: 32.3 us -> 27.9 us  [layer(): pl.pallas_call(functools.partial(kernel, len(parts), 2 * len(groups)), in...]
    another operation x2 -> x0, other arithmetic: 3.67 us -> none
    ppermute x16, starting transfers between devices: 25.8 us -> 23.1 us  [moved(): return lax.ppermute(x, ('rows', 'rep'), pairs)]
  transfers between devices with their start and end apart: 33 -> 39, of which waited for: 16 -> 18; matrix products, arithmetic and copies ran while one was open for 11% -> 10% of each run, Pallas kernels for 0% -> 0%
where the time goes in v6:
time: 204 us; the launch traced here: 202 us
  starting transfers between devices  62.1 us (30%)
  waiting for transfers between devices  60.9 us (30%)
  Pallas kernels  27.9 us (14%)
  between operations  19.2 us (9%)
  other arithmetic  18.8 us (9%)
  local copies, waits for them, and re-layouts  13.4 us (7%)
    ppermute x16, waiting for transfers between devices, moved(): return lax.ppermute(x, ('rows', 'rep'), pairs)  32.5 us
    ppermute x11, starting transfers between devices, from_core(): lax.ppermute(x, 'rep', [(i, i ^ 1) for i in range(lax.axis_size('rep'))])  28.3 us
    pallas_call x1, Pallas kernels, layer(): pl.pallas_call(functools.partial(kernel, len(parts), 2 * len(groups)), in...  27.9 us
    ppermute x16, starting transfers between devices, moved(): return lax.ppermute(x, ('rows', 'rep'), pairs)  23.1 us
    ppermute x12, waiting for transfers between devices, others(): return [lax.ppermute(x(step), axis, pairs) for step, pairs in got]  22.1 us
    convert_element_type x4, other arithmetic, total(): return sum((x.astype(f32) for x in terms)).astype(bf16)  10.8 us
    ppermute x12, starting transfers between devices, others(): return [lax.ppermute(x(step), axis, pairs) for step, pairs in got]  10.7 us
    ppermute x11, waiting for transfers between devices, from_core(): lax.ppermute(x, 'rep', [(i, i ^ 1) for i in range(lax.axis_size('rep'))])  6.37 us
  transfers between devices with their start and end apart: 39, of which 18 were waited for; matrix products, arithmetic and copies ran while one was open for 10% of the time, Pallas kernels for 0%

profile of v6, /device:TPU:0, one launch (start us, length us, event | category | flops | bytes accessed | tf_op | source)
XLA Modules:
  0.0 202.4 jit_solution(6272955885973352378)
XLA Ops:
  0.6 2.1 %collective-permute-start = (bf16[1024,256]{1,0:T(8,128)(2,1)}, bf16[1024,256]{1,0:T(8,128)(2,1)S(1)}, u32[]{:S(2)}, u32[]{:S(2)}) collective-permute-start(bf16[1024,256]{1,0:T(8,128)(2,1)} %param.7), channel_id=1, source_target_pairs={{120,0},{3,1},{122,2},{5,3},{124,4},{7,5},{126,6},{1,7},{0,8},{11,... | collective-permute-start | bytes 1572872 | tf_op jit(solution)/shard_map/ppermute | solution.py:202
  2.7 4.4 %collective-permute-start.1 = (bf16[1024,256]{1,0:T(8,128)(2,1)}, bf16[1024,256]{1,0:T(8,128)(2,1)S(1)}, u32[]{:S(2)}, u32[]{:S(2)}) collective-permute-start(bf16[1024,256]{1,0:T(8,128)(2,1)} %param.7), channel_id=1, source_target_pairs={{8,0},{7,1},{10,2},{1,3},{12,4},{3,5},{14,6},{5,7},{16,8},{15,9},{... | collective-permute-start | bytes 1572872 | tf_op jit(solution)/shard_map/ppermute | solution.py:202
  7.1 1.9 constant_dynamic-update-slice_fusion.2
  9.0 5.3 %collective-permute-done = bf16[1024,256]{1,0:T(8,128)(2,1)S(1)} collective-permute-done((bf16[1024,256]{1,0:T(8,128)(2,1)}, bf16[1024,256]{1,0:T(8,128)(2,1)S(1)}, u32[]{:S(2)}, u32[]{:S(2)}) %collective-permute-start) | collective-permute-done | bytes 524320 | tf_op jit(solution)/shard_map/ppermute | solution.py:202
  16.1 3.0 %collective-permute-start.6 = (bf16[3072,256]{1,0:T(8,128)(2,1)}, bf16[3072,256]{1,0:T(8,128)(2,1)S(1)}, u32[]{:S(2)}, u32[]{:S(2)}) collective-permute-start(bf16[3072,256]{1,0:T(8,128)(2,1)} %constant_dynamic-update-slice_fusion.refs_5_), channel_id=1, source_target_pairs={{2,0},{121,1},{4,2},{123,3},{6,4},{125,5},{0,6},{127,7},{10,8},{1,... | collective-permute-start | bytes 4718600 | tf_op jit(solution)/shard_map/ppermute | solution.py:202
  22.2 16.2 %collective-permute-start.5 = (bf16[1024,256]{1,0:T(8,128)(2,1)}, bf16[1024,256]{1,0:T(8,128)(2,1)}, u32[]{:S(2)}, u32[]{:S(2)}) collective-permute-start(bf16[1024,256]{1,0:T(8,128)(2,1)} %get-tuple-element.31.refs_4_), channel_id=1, source_target_pairs={{0,1},{1,0},{2,3},{3,2},{4,5},{5,4},{6,7},{7,6},{8,9},{9,8},{10,11... | collective-permute-start | bytes 1572872 | tf_op jit(solution)/shard_map/ppermute | solution.py:211
  49.8 2.0 collective-permute-start.9
  51.8 3.1 %collective-permute-start.12 = (bf16[3072,256]{1,0:T(8,128)(2,1)S(1)}, bf16[3072,256]{1,0:T(8,128)(2,1)}, u32[]{:S(2)}, u32[]{:S(2)}) collective-permute-start(bf16[3072,256]{1,0:T(8,128)(2,1)S(1)} %collective-permute-done.6.refs_2_), channel_id=1, source_target_pairs={{0,1},{1,0},{2,3},{3,2},{4,5},{5,4},{6,7},{7,6},{8,9},{9,8},{10,11... | collective-permute-start | bytes 4718600 | tf_op jit(solution)/shard_map/ppermute | solution.py:211
  55.1 6.8 %collective-permute-done.7.refs_0_ = bf16[1536,256]{1,0:T(8,128)(2,1)} collective-permute-done((bf16[1536,256]{1,0:T(8,128)(2,1)S(1)}, bf16[1536,256]{1,0:T(8,128)(2,1)}, u32[]{:S(2)}, u32[]{:S(2)}) %collective-permute-start.7) | collective-permute-done | bytes 786464 | tf_op jit(solution)/shard_map/ppermute | solution.py:202
  61.9 2.5 %collective-permute-start.10 = (bf16[1536,256]{1,0:T(8,128)(2,1)}, bf16[1536,256]{1,0:T(8,128)(2,1)}, u32[]{:S(2)}, u32[]{:S(2)}) collective-permute-start(bf16[1536,256]{1,0:T(8,128)(2,1)} %collective-permute-done.7.refs_0_), channel_id=1, source_target_pairs={{0,1},{1,0},{2,3},{3,2},{4,5},{5,4},{6,7},{7,6},{8,9},{9,8},{10,11... | collective-permute-start | bytes 2359304 | tf_op jit(solution)/shard_map/ppermute | solution.py:211
  67.8 27.9 %shard_map.94 = (bf16[1024,256]{1,0:T(8,128)(2,1)}, f32[256,256]{1,0:T(8,128)}, bf16[24,256,128]{2,1,0:T(8,128)(2,1)}, bf16[48,256,128]{2,1,0:T(8,128)(2,1)}, bf...) custom-call(s32[8,48]{1,0:T(8,128)} %fusion.6.idx, ...), custom_call_target="tpu_custom_call" | custom-call | flops 6442450944 | bytes 37748736 | tf_op jit(solution)/shard_map/pallas_call | solution.py:141
  95.7 5.7 %collective-permute-start.14 = (bf16[24,256,128]{2,1,0:T(8,128)(2,1)}, bf16[24,256,128]{2,1,0:T(8,128)(2,1)S(1)}, u32[]{:S(2)}, u32[]{:S(2)}) collective-permute-start(bf16[24,256,128]{2,1,0:T(8,128)(2,1)} %get-tuple-element.15), channel_id=1, source_target_pairs={{0,1},{1,0},{2,3},{3,2},{4,5},{5,4},{6,7},{7,6},{8,9},{9,8},{10,11... | collective-permute-start | bytes 4718600 | tf_op jit(solution)/shard_map/ppermute | solution.py:211
  102.5 2.1 %collective-permute-done.15 = f32[128,256]{1,0:T(8,128)S(1)} collective-permute-done((f32[128,256]{1,0:T(8,128)S(1)}, f32[128,256]{1,0:T(8,128)S(1)}, u32[]{:S(2)}, u32[]{:S(2)}) %collective-permute-start.15) | collective-permute-done | bytes 131104 | tf_op jit(solution)/shard_map/ppermute | solution.py:211
  109.4 2.0 collective-permute-start.18
  111.5 10.0 %collective-permute-done.20 = bf16[12,256,128]{2,1,0:T(8,128)(2,1)S(1)} collective-permute-done((bf16[12,256,128]{2,1,0:T(8,128)(2,1)S(1)}, bf16[12,256,128]{2,1,0:T(8,128)(2,1)S(1)}, u32[]{:S(2)}, u32[]{:S(2)}) %collective-permute-start.20) | collective-permute-done | bytes 786464 | tf_op jit(solution)/shard_map/ppermute | solution.py:202
  129.2 4.8 %add_convert_fusion.1 = (bf16[24,256,128]{2,1,0:T(8,128)(2,1)}, bf16[24,256,128]{2,1,0:T(8,128)(2,1)}) fusion(bf16[48,256,128]{2,1,0:T(8,128)(2,1)} %collective-permute-done.17, bf16[12,256,128]{2,1,0:T(8,128)(2,1)S(1)} %collective-permute-done.18, bf16[48,256,128]{2,1,0:T(8,128)(2,1)} %get-tuple-element.17, pred[]{:T(512)S(6)} %eq.68, ...), kind=kLoop, calls=%fused_computation.1 | loop fusion | flops 11010048 | bytes 11010049 | tf_op jit(solution)/shard_map/convert_element_type | solution.py:280
  134.0 3.2 %collective-permute-start.21 = (bf16[24,256,128]{2,1,0:T(8,128)(2,1)}, bf16[24,256,128]{2,1,0:T(8,128)(2,1)}, u32[]{:S(2)}, u32[]{:S(2)}) collective-permute-start(bf16[24,256,128]{2,1,0:T(8,128)(2,1)} %get-tuple-element.24), channel_id=1, source_target_pairs={{0,6},{1,9},{2,0},{3,11},{4,2},{5,13},{6,4},{7,15},{8,14},{9,17},{... | collective-permute-start | bytes 4718600 | tf_op jit(solution)/shard_map/ppermute | solution.py:202
  147.1 12.5 %collective-permute-done.24 = f32[32,256]{1,0:T(8,128)S(1)} collective-permute-done((f32[32,256]{1,0:T(8,128)S(1)}, f32[32,256]{1,0:T(8,128)S(1)}, u32[]{:S(2)}, u32[]{:S(2)}) %collective-permute-start.24) | collective-permute-done | bytes 32800 | tf_op jit(solution)/shard_map/ppermute | solution.py:241
  170.8 1.9 collective-permute-done.31
  173.5 3.3 %collective-permute-start.35 = (f32[32,256]{1,0:T(8,128)S(1)}, f32[32,256]{1,0:T(8,128)S(1)}, u32[]{:S(2)}, u32[]{:S(2)}) collective-permute-start(f32[32,256]{1,0:T(8,128)S(1)} %get-tuple-element.20), channel_id=1, source_target_pairs={{2,0},{3,1},{4,2},{5,3},{6,4},{7,5},{0,6},{1,7},{10,8},{11,9},{12,... | collective-permute-start | bytes 98312 | tf_op jit(solution)/shard_map/ppermute | solution.py:241
  181.0 2.6 %add_convert_fusion.5 = (bf16[8,256,128]{2,1,0:T(8,128)(2,1)S(1)}, bf16[8,256,128]{2,1,0:T(8,128)(2,1)S(1)}) fusion(bf16[24,256,128]{2,1,0:T(8,128)(2,1)} %collective-permute-done.21, bf16[24,256,128]{2,1,0:T(8,128)(2,1)} %collective-permute-done.19, bf16[32,256,128]{2,1,0:T(8,128)(2,1)} %collective-permute-done.16, ...), kind=kLoop, calls=%fused_computation.5 | loop fusion | flops 5767168 | bytes 5767169 | tf_op jit(solution)/shard_map/convert_element_type | solution.py:280
  183.6 3.5 %collective-permute-start.33 = (bf16[8,256,128]{2,1,0:T(8,128)(2,1)S(1)}, bf16[8,256,128]{2,1,0:T(8,128)(2,1)S(1)}, u32[]{:S(2)}, u32[]{:S(2)}) collective-permute-start(bf16[8,256,128]{2,1,0:T(8,128)(2,1)S(1)} %get-tuple-element.21), channel_id=1, source_target_pairs={{0,120},{1,3},{2,122},{3,5},{4,124},{5,7},{6,126},{7,1},{8,0},{9,1... | collective-permute-start | bytes 1572872 | tf_op jit(solution)/shard_map/ppermute | solution.py:202
  189.3 4.5 %collective-permute-done.33 = bf16[8,256,128]{2,1,0:T(8,128)(2,1)S(1)} collective-permute-done((bf16[8,256,128]{2,1,0:T(8,128)(2,1)S(1)}, bf16[8,256,128]{2,1,0:T(8,128)(2,1)S(1)}, u32[]{:S(2)}, u32[]{:S(2)}) %collective-permute-start.33) | collective-permute-done | bytes 524320 | tf_op jit(solution)/shard_map/ppermute | solution.py:202
  193.8 5.8 %collective-permute-done.34 = bf16[8,256,128]{2,1,0:T(8,128)(2,1)S(1)} collective-permute-done((bf16[8,256,128]{2,1,0:T(8,128)(2,1)S(1)}, bf16[8,256,128]{2,1,0:T(8,128)(2,1)S(1)}, u32[]{:S(2)}, u32[]{:S(2)}) %collective-permute-start.34) | collective-permute-done | bytes 524320 | tf_op jit(solution)/shard_map/ppermute | solution.py:202
  (111 shorter events, 45.7 us)
Async XLA Ops:
  0.6 13.8 %collective-permute-start = (bf16[1024,256]{1,0:T(8,128)(2,1)}, bf16[1024,256]{1,0:T(8,128)(2,1)S(1)}, u32[]{:S(2)}, u32[]{:S(2)}) collective-permute-start(bf16[1024,256]{1,0:T(8,128)(2,1)} %param.7), channel_id=1, source_target_pairs={{120,0},{3,1},{122,2},{5,3},{124,4},{7,5},{126,6},{1,7},{0,8},{11,... | collective-permute-start | bytes 1572872 | tf_op jit(solution)/shard_map/ppermute | solution.py:202
  2.7 12.5 %collective-permute-start.1 = (bf16[1024,256]{1,0:T(8,128)(2,1)}, bf16[1024,256]{1,0:T(8,128)(2,1)S(1)}, u32[]{:S(2)}, u32[]{:S(2)}) collective-permute-start(bf16[1024,256]{1,0:T(8,128)(2,1)} %param.7), channel_id=1, source_target_pairs={{8,0},{7,1},{10,2},{1,3},{12,4},{3,5},{14,6},{5,7},{16,8},{15,9},{... | collective-permute-start | bytes 1572872 | tf_op jit(solution)/shard_map/ppermute | solution.py:202
  16.1 27.9 %collective-permute-start.2 = (bf16[3072,256]{1,0:T(8,128)(2,1)}, bf16[3072,256]{1,0:T(8,128)(2,1)}, u32[]{:S(2)}, u32[]{:S(2)}) collective-permute-start(bf16[3072,256]{1,0:T(8,128)(2,1)} %constant_dynamic-update-slice_fusion.refs_5_), channel_id=1, source_target_pairs={{0,1},{1,0},{2,3},{3,2},{4,5},{5,4},{6,7},{7,6},{8,9},{9,8},{10,11... | collective-permute-start | bytes 4718600 | tf_op jit(solution)/shard_map/ppermute | solution.py:211
  16.1 31.8 %collective-permute-start.6 = (bf16[3072,256]{1,0:T(8,128)(2,1)}, bf16[3072,256]{1,0:T(8,128)(2,1)S(1)}, u32[]{:S(2)}, u32[]{:S(2)}) collective-permute-start(bf16[3072,256]{1,0:T(8,128)(2,1)} %constant_dynamic-update-slice_fusion.refs_5_), channel_id=1, source_target_pairs={{2,0},{121,1},{4,2},{123,3},{6,4},{125,5},{0,6},{127,7},{10,8},{1,... | collective-permute-start | bytes 4718600 | tf_op jit(solution)/shard_map/ppermute | solution.py:202
  19.1 28.8 %collective-permute-start.8 = (bf16[3072,256]{1,0:T(8,128)(2,1)}, bf16[3072,256]{1,0:T(8,128)(2,1)S(1)}, u32[]{:S(2)}, u32[]{:S(2)}) collective-permute-start(bf16[3072,256]{1,0:T(8,128)(2,1)} %constant_dynamic-update-slice_fusion.refs_5_), channel_id=1, source_target_pairs={{6,0},{9,1},{0,2},{11,3},{2,4},{13,5},{4,6},{15,7},{14,8},{17,9},{... | collective-permute-start | bytes 4718600 | tf_op jit(solution)/shard_map/ppermute | solution.py:202
  22.2 18.1 %collective-permute-start.5 = (bf16[1024,256]{1,0:T(8,128)(2,1)}, bf16[1024,256]{1,0:T(8,128)(2,1)}, u32[]{:S(2)}, u32[]{:S(2)}) collective-permute-start(bf16[1024,256]{1,0:T(8,128)(2,1)} %get-tuple-element.31.refs_4_), channel_id=1, source_target_pairs={{0,1},{1,0},{2,3},{3,2},{4,5},{5,4},{6,7},{7,6},{8,9},{9,8},{10,11... | collective-permute-start | bytes 1572872 | tf_op jit(solution)/shard_map/ppermute | solution.py:211
  49.7 12.2 %collective-permute-start.7 = (bf16[1536,256]{1,0:T(8,128)(2,1)S(1)}, bf16[1536,256]{1,0:T(8,128)(2,1)}, u32[]{:S(2)}, u32[]{:S(2)}) collective-permute-start(bf16[1536,256]{1,0:T(8,128)(2,1)S(1)} %get-tuple-element.28), channel_id=1, source_target_pairs={{2,0},{121,1},{4,2},{123,3},{6,4},{125,5},{0,6},{127,7},{10,8},{1,... | collective-permute-start | bytes 2359304 | tf_op jit(solution)/shard_map/ppermute | solution.py:202
  49.8 14.6 %collective-permute-start.9 = (bf16[1536,256]{1,0:T(8,128)(2,1)S(1)}, bf16[1536,256]{1,0:T(8,128)(2,1)}, u32[]{:S(2)}, u32[]{:S(2)}) collective-permute-start(bf16[1536,256]{1,0:T(8,128)(2,1)S(1)} %get-tuple-element.27), channel_id=1, source_target_pairs={{6,0},{9,1},{0,2},{11,3},{2,4},{13,5},{4,6},{15,7},{14,8},{17,9},{... | collective-permute-start | bytes 2359304 | tf_op jit(solution)/shard_map/ppermute | solution.py:202
  51.8 16.0 %collective-permute-start.12 = (bf16[3072,256]{1,0:T(8,128)(2,1)S(1)}, bf16[3072,256]{1,0:T(8,128)(2,1)}, u32[]{:S(2)}, u32[]{:S(2)}) collective-permute-start(bf16[3072,256]{1,0:T(8,128)(2,1)S(1)} %collective-permute-done.6.refs_2_), channel_id=1, source_target_pairs={{0,1},{1,0},{2,3},{3,2},{4,5},{5,4},{6,7},{7,6},{8,9},{9,8},{10,11... | collective-permute-start | bytes 4718600 | tf_op jit(solution)/shard_map/ppermute | solution.py:211
  55.0 12.9 %collective-permute-start.13 = (bf16[3072,256]{1,0:T(8,128)(2,1)S(1)}, bf16[3072,256]{1,0:T(8,128)(2,1)}, u32[]{:S(2)}, u32[]{:S(2)}) collective-permute-start(bf16[3072,256]{1,0:T(8,128)(2,1)S(1)} %collective-permute-done.8.refs_3_), channel_id=1, source_target_pairs={{0,1},{1,0},{2,3},{3,2},{4,5},{5,4},{6,7},{7,6},{8,9},{9,8},{10,11... | collective-permute-start | bytes 4718600 | tf_op jit(solution)/shard_map/ppermute | solution.py:211
  95.7 10.5 %collective-permute-start.14 = (bf16[24,256,128]{2,1,0:T(8,128)(2,1)}, bf16[24,256,128]{2,1,0:T(8,128)(2,1)S(1)}, u32[]{:S(2)}, u32[]{:S(2)}) collective-permute-start(bf16[24,256,128]{2,1,0:T(8,128)(2,1)} %get-tuple-element.15), channel_id=1, source_target_pairs={{0,1},{1,0},{2,3},{3,2},{4,5},{5,4},{6,7},{7,6},{8,9},{9,8},{10,11... | collective-permute-start | bytes 4718600 | tf_op jit(solution)/shard_map/ppermute | solution.py:211
  108.7 20.5 %collective-permute-start.17 = (bf16[48,256,128]{2,1,0:T(8,128)(2,1)}, bf16[48,256,128]{2,1,0:T(8,128)(2,1)}, u32[]{:S(2)}, u32[]{:S(2)}) collective-permute-start(bf16[48,256,128]{2,1,0:T(8,128)(2,1)} %shard_map.96), channel_id=1, source_target_pairs={{0,1},{1,0},{2,3},{3,2},{4,5},{5,4},{6,7},{7,6},{8,9},{9,8},{10,11... | collective-permute-start | bytes 9437192 | tf_op jit(solution)/shard_map/ppermute | solution.py:211
  109.1 18.6 %collective-permute-start.16 = (bf16[32,256,128]{2,1,0:T(8,128)(2,1)}, bf16[32,256,128]{2,1,0:T(8,128)(2,1)}, u32[]{:S(2)}, u32[]{:S(2)}) collective-permute-start(bf16[32,256,128]{2,1,0:T(8,128)(2,1)} %shard_map.95), channel_id=1, source_target_pairs={{0,1},{1,0},{2,3},{3,2},{4,5},{5,4},{6,7},{7,6},{8,9},{9,8},{10,11... | collective-permute-start | bytes 6291464 | tf_op jit(solution)/shard_map/ppermute | solution.py:211
  109.4 12.1 %collective-permute-start.20 = (bf16[12,256,128]{2,1,0:T(8,128)(2,1)S(1)}, bf16[12,256,128]{2,1,0:T(8,128)(2,1)S(1)}, u32[]{:S(2)}, u32[]{:S(2)}) collective-permute-start(bf16[12,256,128]{2,1,0:T(8,128)(2,1)S(1)} %get-tuple-element.26), channel_id=1, source_target_pairs={{0,6},{1,9},{2,0},{3,11},{4,2},{5,13},{6,4},{7,15},{8,14},{9,17},{... | collective-permute-start | bytes 2359304 | tf_op jit(solution)/shard_map/ppermute | solution.py:202
  109.4 15.1 %collective-permute-start.18 = (bf16[12,256,128]{2,1,0:T(8,128)(2,1)S(1)}, bf16[12,256,128]{2,1,0:T(8,128)(2,1)S(1)}, u32[]{:S(2)}, u32[]{:S(2)}) collective-permute-start(bf16[12,256,128]{2,1,0:T(8,128)(2,1)S(1)} %get-tuple-element.25), channel_id=1, source_target_pairs={{0,2},{1,121},{2,4},{3,123},{4,6},{5,125},{6,0},{7,127},{8,10},{9,... | collective-permute-start | bytes 2359304 | tf_op jit(solution)/shard_map/ppermute | solution.py:202
  134.0 46.9 %collective-permute-start.19 = (bf16[24,256,128]{2,1,0:T(8,128)(2,1)}, bf16[24,256,128]{2,1,0:T(8,128)(2,1)}, u32[]{:S(2)}, u32[]{:S(2)}) collective-permute-start(bf16[24,256,128]{2,1,0:T(8,128)(2,1)} %get-tuple-element.23), channel_id=1, source_target_pairs={{0,2},{1,121},{2,4},{3,123},{4,6},{5,125},{6,0},{7,127},{8,10},{9,... | collective-permute-start | bytes 4718600 | tf_op jit(solution)/shard_map/ppermute | solution.py:202
  134.0 46.9 %collective-permute-start.21 = (bf16[24,256,128]{2,1,0:T(8,128)(2,1)}, bf16[24,256,128]{2,1,0:T(8,128)(2,1)}, u32[]{:S(2)}, u32[]{:S(2)}) collective-permute-start(bf16[24,256,128]{2,1,0:T(8,128)(2,1)} %get-tuple-element.24), channel_id=1, source_target_pairs={{0,6},{1,9},{2,0},{3,11},{4,2},{5,13},{6,4},{7,15},{8,14},{9,17},{... | collective-permute-start | bytes 4718600 | tf_op jit(solution)/shard_map/ppermute | solution.py:202
  138.7 20.9 %collective-permute-start.24 = (f32[32,256]{1,0:T(8,128)S(1)}, f32[32,256]{1,0:T(8,128)S(1)}, u32[]{:S(2)}, u32[]{:S(2)}) collective-permute-start(f32[32,256]{1,0:T(8,128)S(1)} %get-tuple-element.35), channel_id=1, source_target_pairs={{2,0},{3,1},{4,2},{5,3},{6,4},{7,5},{0,6},{1,7},{10,8},{11,9},{12,... | collective-permute-start | bytes 98312 | tf_op jit(solution)/shard_map/ppermute | solution.py:241
  138.8 20.8 %collective-permute-start.25 = (f32[32,256]{1,0:T(8,128)S(1)}, f32[32,256]{1,0:T(8,128)S(1)}, u32[]{:S(2)}, u32[]{:S(2)}) collective-permute-start(f32[32,256]{1,0:T(8,128)S(1)} %get-tuple-element.37), channel_id=1, source_target_pairs={{4,0},{5,1},{6,2},{7,3},{0,4},{1,5},{2,6},{3,7},{12,8},{13,9},{14,... | collective-permute-start | bytes 98312 | tf_op jit(solution)/shard_map/ppermute | solution.py:241
  139.7 20.3 %collective-permute-start.26 = (f32[32,256]{1,0:T(8,128)S(1)}, f32[32,256]{1,0:T(8,128)S(1)}, u32[]{:S(2)}, u32[]{:S(2)}) collective-permute-start(f32[32,256]{1,0:T(8,128)S(1)} %get-tuple-element.36), channel_id=1, source_target_pairs={{6,0},{7,1},{0,2},{1,3},{2,4},{3,5},{4,6},{5,7},{14,8},{15,9},{8,1... | collective-permute-start | bytes 98312 | tf_op jit(solution)/shard_map/ppermute | solution.py:241
  176.8 10.3 %collective-permute-start.36 = (f32[32,256]{1,0:T(8,128)S(1)}, f32[32,256]{1,0:T(8,128)S(1)}, u32[]{:S(2)}, u32[]{:S(2)}) collective-permute-start(f32[32,256]{1,0:T(8,128)S(1)} %get-tuple-element.20), channel_id=1, source_target_pairs={{4,0},{5,1},{6,2},{7,3},{0,4},{1,5},{2,6},{3,7},{12,8},{13,9},{14,... | collective-permute-start | bytes 98312 | tf_op jit(solution)/shard_map/ppermute | solution.py:241
  176.8 10.3 %collective-permute-start.37 = (f32[32,256]{1,0:T(8,128)S(1)}, f32[32,256]{1,0:T(8,128)S(1)}, u32[]{:S(2)}, u32[]{:S(2)}) collective-permute-start(f32[32,256]{1,0:T(8,128)S(1)} %get-tuple-element.20), channel_id=1, source_target_pairs={{6,0},{7,1},{0,2},{1,3},{2,4},{3,5},{4,6},{5,7},{14,8},{15,9},{8,1... | collective-permute-start | bytes 98312 | tf_op jit(solution)/shard_map/ppermute | solution.py:241
  183.6 10.2 %collective-permute-start.33 = (bf16[8,256,128]{2,1,0:T(8,128)(2,1)S(1)}, bf16[8,256,128]{2,1,0:T(8,128)(2,1)S(1)}, u32[]{:S(2)}, u32[]{:S(2)}) collective-permute-start(bf16[8,256,128]{2,1,0:T(8,128)(2,1)S(1)} %get-tuple-element.21), channel_id=1, source_target_pairs={{0,120},{1,3},{2,122},{3,5},{4,124},{5,7},{6,126},{7,1},{8,0},{9,1... | collective-permute-start | bytes 1572872 | tf_op jit(solution)/shard_map/ppermute | solution.py:202
  187.1 12.5 %collective-permute-start.34 = (bf16[8,256,128]{2,1,0:T(8,128)(2,1)S(1)}, bf16[8,256,128]{2,1,0:T(8,128)(2,1)S(1)}, u32[]{:S(2)}, u32[]{:S(2)}) collective-permute-start(bf16[8,256,128]{2,1,0:T(8,128)(2,1)S(1)} %get-tuple-element.22), channel_id=1, source_target_pairs={{0,8},{1,7},{2,10},{3,1},{4,12},{5,3},{6,14},{7,5},{8,16},{9,15},{... | collective-permute-start | bytes 1572872 | tf_op jit(solution)/shard_map/ppermute | solution.py:202
  (21 other events, 166.2 us)

commit v7 on v6

--- a/solution.py
+++ b/solution.py
@@ -175,14 +175,6 @@
     )(x, *earlier)
 
 
-def never(*earlier):
-    out = False
-    for x in earlier:
-        v = x[(0,) * x.ndim]
-        out |= (v != v) & (v == v)
-    return out
-
-
 def near(group, rep, axis, step, n_rows, n_rep):
     if axis == "z":
         return (group + step) % n_rows * n_rep + rep
@@ -221,59 +213,42 @@
     crossing = jnp.concatenate([far, far[:half]])
     swapped = from_core(near3)
     swapped_far = from_core(far)
-    first = (core == 0) | never(swapped, swapped_far)
-    last_up = moved(jnp.where(first, up[: 3 * half], crossing), NEXT_UP)
-    last_down = moved(jnp.where(first, down[3 * half :], crossing), NEXT_DOWN)
+    to_up = jnp.where(core == 0, up[: 3 * half], crossing)
+    to_down = jnp.where(core == 0, down[3 * half :], crossing)
+    last_up = moved(tied(to_up, swapped, swapped_far), NEXT_UP)
+    last_down = moved(to_down, NEXT_DOWN)
     mine = [last_up, last_down, up, down]
     return mine + [far, near3] + [from_core(x) for x in mine] + [swapped_far, swapped]
 
 
-def others(x, axis, group, stride):
-    count = lax.axis_size(axis)
-    got = []
-    for step in range(1, group):
-        pairs = []
-        for i in range(count):
-            digit = i // stride % group
-            source = i + ((digit + step) % group - digit) * stride
-            pairs.append((source, i))
-        got.append((step, pairs))
-    return [lax.ppermute(x(step), axis, pairs) for step, pairs in got]
-
-
 class Steps:
-    def __init__(self, term, core, y):
+    def __init__(self, term, core):
         height = term.shape[0] // 2
         low, high = term[:height], term[height:]
-        half = jnp.where(core == 0, low, high) + from_core(jnp.where(core == 0, high, low))
-        self.core, self.y, self.n_y = core, y, lax.axis_size("rep") // 2
-        self.x = half.reshape(self.n_y, height // self.n_y, term.shape[1])
-
-    def piece(self, at):
-        return lax.dynamic_index_in_dim(self.x, jnp.mod(at, self.n_y), 0, keepdims=False)
-
-    def scatter(self):
-        got = others(lambda step: self.piece(self.y - step), "rep", self.n_y, 2)
-        self.x = sum(got, self.piece(self.y))
-
-    def sum_rows(self, stride):
-        self.x = sum(others(lambda step: self.x, "rows", 4, stride), self.x)
-
-    def gather(self):
-        got = others(lambda step: self.x, "rep", self.n_y, 2)
-        blocks = jnp.zeros((self.n_y,) + self.x.shape, f32)
-        for step, block in enumerate([self.x, *got]):
-            at = jnp.mod(self.y + step, self.n_y)
-            blocks = lax.dynamic_update_index_in_dim(blocks, block, at, 0)
-        self.x = blocks.reshape(-1, self.x.shape[1])
+        self.x = jnp.where(core == 0, low, high) + from_core(jnp.where(core == 0, high, low))
+        self.core = core
+        self.left = [
+            (axis, bit)
+            for axis, first in (("rep", 2), ("rows", 1))
+            for bit in (1 << k for k in range(10))
+            if first <= bit < lax.axis_size(axis)
+        ]
+
+    def go(self, count):
+        for axis, bit in self.left[:count]:
+            pairs = [(i, i ^ bit) for i in range(lax.axis_size(axis))]
+            rounded = lax.reduce_precision(self.x, 8, 7)
+            self.x = rounded + lax.ppermute(rounded.astype(bf16), axis, pairs).astype(f32)
+        self.left = self.left[count:]
+
+    def after(self, *earlier):
+        self.x = tied(self.x, *earlier)
 
     def whole(self):
+        self.go(len(self.left))
         other = from_core(self.x)
         halves = [self.x, other], [other, self.x]
         return jnp.where(self.core == 0, *(jnp.concatenate(h) for h in halves))
-
-    def after(self, *earlier):
-        self.x = jnp.where(never(*earlier), 0.0, self.x)
 
 
 def total(*terms):
@@ -292,31 +267,29 @@
     last_up = moved(last[:cut], NEXT_UP, back=True)
     last_down = moved(last[cut:], NEXT_DOWN, back=True)
     first = from_core(tied(other[2], last[:1, :8], steps.x[:1, :8]))
-    steps.after(last_up, last_down)
-    steps.scatter()
+    steps.go(2)
     along = core == 0
     zero = jnp.zeros((), bf16)
     to_up = jnp.where(along, widened(last_up, 2 * cut, 0), zero)
     to_down = jnp.where(along, widened(last_down, 2 * cut, cut), zero)
     next_up = total(mine[1][: 2 * cut], middle[: 2 * cut], to_up)
     next_down = total(mine[1][2 * cut :], middle[2 * cut :], to_down)
-    next_up, next_down = moved(next_up, NEXT_UP, back=True), moved(next_down, NEXT_DOWN, back=True)
+    next_up = moved(tied(next_up, steps.x), NEXT_UP, back=True)
+    next_down = moved(next_down, NEXT_DOWN, back=True)
     far = [jnp.where(along, zero, x[:own]) for x in (last_up, last_down)]
     far = total(mine[2][:own], first[:own], *far)
     half_up = moved(far[:half], HALF_UP, back=True)
     half_down = moved(far[half:], HALF_DOWN, back=True)
-    steps.after(half_up, half_down)
-    steps.sum_rows(1)
-    steps.sum_rows(4)
-    none = never(steps.x)
-    steps.gather()
+    steps.go(1)
+    steps.after(half_up[:1, :8], half_down[:1, :8])
+    steps.go(2)
 
     def near(k):
         at = slice(k * own, (k + 1) * own)
         return [mine[2][own:][at], first[own:][at], next_up[at], next_down[at]]
 
-    up = total(*near(1), jnp.where(none, zero, widened(half_up, own, 0)))
-    down = total(*near(2), jnp.where(none, zero, widened(half_down, own, half)))
+    up = tied(total(*near(1), widened(half_up, own, 0)), steps.x)
+    down = total(*near(2), widened(half_down, own, half))
     ends = moved(up, FIRST_UP, back=True), moved(down, FIRST_DOWN, back=True)
     return total(*near(0), *ends)
 
@@ -348,7 +321,7 @@
 
     parts = gather(features, core)
     output, term, *grads = layer(idx, cnt, tile_values, parts, weight, cotangent, groups)
-    steps = Steps(term, core, rep // 2)
+    steps = Steps(term, core)
     grad = scatter(grads[: len(groups)], grads[len(groups) :], own, core, steps)
     weight_grad = steps.whole()
     feature_grad = jnp.swapaxes(grad, 1, 2).reshape(node_dev, width)

time: 204 us -> 179 us (0.88)
  between operations: 19.2 us -> 0.86 us
  waiting for transfers between devices: 60.9 us -> 54.8 us
  other arithmetic: 18.8 us -> 24.3 us
  starting transfers between devices: 62.1 us -> 59 us
    ppermute x16, waiting for transfers between devices: 32.5 us -> 23.5 us  [moved(): return lax.ppermute(x, ('rows', 'rep'), pairs)]
    ppermute x12 -> x6, waiting for transfers between devices: 22.1 us -> 27.3 us  [go(): lax.ppermute(rounded.astype(bf16), axis, pairs).astype(f32)]
    convert_element_type x0 -> x6, other arithmetic: none -> 5.13 us  [go(): rounded.astype(bf16)]
    slice x7 -> x2, local copies, waits for them, and re-layouts: 4.86 us -> 1.12 us  [scatter(): steps.after(half_up[:1, :8], half_down[:1, :8])]
    ppermute x11, starting transfers between devices: 28.3 us -> 25.7 us  [from_core(): lax.ppermute(x, 'rep', [(i, i ^ 1) for i in range(lax.axis_size('rep'))])]
    ppermute x11, waiting for transfers between devices: 6.37 us -> 4.03 us  [from_core(): lax.ppermute(x, 'rep', [(i, i ^ 1) for i in range(lax.axis_size('rep'))])]
    ppermute x12 -> x6, starting transfers between devices: 10.7 us -> 8.46 us  [go(): lax.ppermute(rounded.astype(bf16), axis, pairs).astype(f32)]
    unnamed x15 -> x27, local copies, waits for them, and re-layouts: 3.64 us -> 5.07 us
  transfers between devices with their start and end apart: 39 -> 33, of which waited for: 18 -> 14; matrix products, arithmetic and copies ran while one was open for 10% -> 16% of each run, Pallas kernels for 0% -> 0%
where the time goes in v7:
time: 179 us; the launch traced here: 177 us
  starting transfers between devices  59 us (33%)
  waiting for transfers between devices  54.8 us (31%)
  Pallas kernels  26.7 us (15%)
  other arithmetic  24.3 us (14%)
  local copies, waits for them, and re-layouts  11.7 us (7%)
    ppermute x6, waiting for transfers between devices, go(): lax.ppermute(rounded.astype(bf16), axis, pairs).astype(f32)  27.3 us
    pallas_call x1, Pallas kernels, layer(): pl.pallas_call(functools.partial(kernel, len(parts), 2 * len(groups)), in...  26.7 us
    ppermute x11, starting transfers between devices, from_core(): lax.ppermute(x, 'rep', [(i, i ^ 1) for i in range(lax.axis_size('rep'))])  25.7 us
    ppermute x16, starting transfers between devices, moved(): return lax.ppermute(x, ('rows', 'rep'), pairs)  24.8 us
    ppermute x16, waiting for transfers between devices, moved(): return lax.ppermute(x, ('rows', 'rep'), pairs)  23.5 us
    convert_element_type x4, other arithmetic, total(): return sum((x.astype(f32) for x in terms)).astype(bf16)  10.8 us
    ppermute x6, starting transfers between devices, go(): lax.ppermute(rounded.astype(bf16), axis, pairs).astype(f32)  8.46 us
    convert_element_type x6, other arithmetic, go(): rounded.astype(bf16)  5.13 us
  transfers between devices with their start and end apart: 33, of which 14 were waited for; matrix products, arithmetic and copies ran while one was open for 16% of the time, Pallas kernels for 0%

profile of v7, /device:TPU:0, one launch (start us, length us, event | category | flops | bytes accessed | tf_op | source)
XLA Modules:
  0.0 177.3 jit_solution(8100707070682890542)
XLA Ops:
  0.6 2.1 %collective-permute-start = (bf16[1024,256]{1,0:T(8,128)(2,1)}, bf16[1024,256]{1,0:T(8,128)(2,1)S(1)}, u32[]{:S(2)}, u32[]{:S(2)}) collective-permute-start(bf16[1024,256]{1,0:T(8,128)(2,1)} %param.7), channel_id=1, source_target_pairs={{120,0},{3,1},{122,2},{5,3},{124,4},{7,5},{126,6},{1,7},{0,8},{11,... | collective-permute-start | bytes 1572872 | tf_op jit(solution)/shard_map/ppermute | solution.py:194
  2.7 4.4 %collective-permute-start.1 = (bf16[1024,256]{1,0:T(8,128)(2,1)}, bf16[1024,256]{1,0:T(8,128)(2,1)S(1)}, u32[]{:S(2)}, u32[]{:S(2)}) collective-permute-start(bf16[1024,256]{1,0:T(8,128)(2,1)} %param.7), channel_id=1, source_target_pairs={{8,0},{7,1},{10,2},{1,3},{12,4},{3,5},{14,6},{5,7},{16,8},{15,9},{... | collective-permute-start | bytes 1572872 | tf_op jit(solution)/shard_map/ppermute | solution.py:194
  9.0 5.4 %collective-permute-done = bf16[1024,256]{1,0:T(8,128)(2,1)S(1)} collective-permute-done((bf16[1024,256]{1,0:T(8,128)(2,1)}, bf16[1024,256]{1,0:T(8,128)(2,1)S(1)}, u32[]{:S(2)}, u32[]{:S(2)}) %collective-permute-start) | collective-permute-done | bytes 524320 | tf_op jit(solution)/shard_map/ppermute | solution.py:194
  24.4 13.0 %collective-permute-start.6 = (bf16[1024,256]{1,0:T(8,128)(2,1)S(1)}, bf16[1024,256]{1,0:T(8,128)(2,1)S(1)}, u32[]{:S(2)}, u32[]{:S(2)}) collective-permute-start(bf16[1024,256]{1,0:T(8,128)(2,1)S(1)} %get-tuple-element.35.refs_4_), channel_id=1, source_target_pairs={{0,1},{1,0},{2,3},{3,2},{4,5},{5,4},{6,7},{7,6},{8,9},{9,8},{10,11... | collective-permute-start | bytes 1572872 | tf_op jit(solution)/shard_map/ppermute | solution.py:203
  37.5 3.2 %collective-permute-done.8.refs_3_ = bf16[3072,256]{1,0:T(8,128)(2,1)S(1)} collective-permute-done((bf16[3072,256]{1,0:T(8,128)(2,1)}, bf16[3072,256]{1,0:T(8,128)(2,1)S(1)}, u32[]{:S(2)}, u32[]{:S(2)}) %collective-permute-start.8) | collective-permute-done | bytes 1572896 | tf_op jit(solution)/shard_map/ppermute | solution.py:194
  41.2 2.5 %slice_select_fusion = (bf16[1536,256]{1,0:T(8,128)(2,1)}, bf16[1536,256]{1,0:T(8,128)(2,1)}) fusion(bf16[1536,256]{1,0:T(8,128)(2,1)S(1)} %constant_dynamic-update-slice_fusion.3, bf16[3072,256]{1,0:T(8,128)(2,1)S(1)} %collective-permute-done.8.refs_3_, pred[]{:T(512)S(6)} %eq.33, bf16[3072,256]{1,0:T(8,128)(2,1)} %collective-permute-done.2.refs_2_), kind=kLoop, calls=%fused_computation.7 | loop fusion | flops 786432 | bytes 3932161 | tf_op jit(solution)/shard_map/jit(_where)/select_n | solution.py:217
  45.7 2.8 %collective-permute-start.7 = (bf16[1536,256]{1,0:T(8,128)(2,1)}, bf16[1536,256]{1,0:T(8,128)(2,1)}, u32[]{:S(2)}, u32[]{:S(2)}) collective-permute-start(bf16[1536,256]{1,0:T(8,128)(2,1)} %shard_map.94), channel_id=1, source_target_pairs={{2,0},{121,1},{4,2},{123,3},{6,4},{125,5},{0,6},{127,7},{10,8},{1,... | collective-permute-start | bytes 2359304 | tf_op jit(solution)/shard_map/ppermute | solution.py:194
  48.5 4.8 %collective-permute-start.12 = (bf16[3072,256]{1,0:T(8,128)(2,1)}, bf16[3072,256]{1,0:T(8,128)(2,1)}, u32[]{:S(2)}, u32[]{:S(2)}) collective-permute-start(bf16[3072,256]{1,0:T(8,128)(2,1)} %collective-permute-done.2.refs_2_), channel_id=1, source_target_pairs={{0,1},{1,0},{2,3},{3,2},{4,5},{5,4},{6,7},{7,6},{8,9},{9,8},{10,11... | collective-permute-start | bytes 4718600 | tf_op jit(solution)/shard_map/ppermute | solution.py:203
  53.3 5.0 %collective-permute-done.7.refs_0_ = bf16[1536,256]{1,0:T(8,128)(2,1)} collective-permute-done((bf16[1536,256]{1,0:T(8,128)(2,1)}, bf16[1536,256]{1,0:T(8,128)(2,1)}, u32[]{:S(2)}, u32[]{:S(2)}) %collective-permute-start.7) | collective-permute-done | bytes 786464 | tf_op jit(solution)/shard_map/ppermute | solution.py:194
  58.3 3.4 %collective-permute-start.10 = (bf16[1536,256]{1,0:T(8,128)(2,1)}, bf16[1536,256]{1,0:T(8,128)(2,1)}, u32[]{:S(2)}, u32[]{:S(2)}) collective-permute-start(bf16[1536,256]{1,0:T(8,128)(2,1)} %collective-permute-done.7.refs_0_), channel_id=1, source_target_pairs={{0,1},{1,0},{2,3},{3,2},{4,5},{5,4},{6,7},{7,6},{8,9},{9,8},{10,11... | collective-permute-start | bytes 2359304 | tf_op jit(solution)/shard_map/ppermute | solution.py:203
  65.3 26.7 %shard_map.95 = (bf16[1024,256]{1,0:T(8,128)(2,1)}, f32[256,256]{1,0:T(8,128)}, bf16[24,256,128]{2,1,0:T(8,128)(2,1)}, bf16[48,256,128]{2,1,0:T(8,128)(2,1)}, bf...) custom-call(s32[8,48]{1,0:T(8,128)} %fusion.5.idx, ...), custom_call_target="tpu_custom_call" | custom-call | flops 6442450944 | bytes 37748736 | tf_op jit(solution)/shard_map/pallas_call | solution.py:141
  94.9 2.1 %collective-permute-done.15 = f32[128,256]{1,0:T(8,128)S(1)} collective-permute-done((f32[128,256]{1,0:T(8,128)S(1)}, f32[128,256]{1,0:T(8,128)S(1)}, u32[]{:S(2)}, u32[]{:S(2)}) %collective-permute-start.15) | collective-permute-done | bytes 131104 | tf_op jit(solution)/shard_map/ppermute | solution.py:203
  102.9 2.1 %collective-permute-start.22 = (bf16[12,256,128]{2,1,0:T(8,128)(2,1)S(1)}, bf16[12,256,128]{2,1,0:T(8,128)(2,1)S(1)}, u32[]{:S(2)}, u32[]{:S(2)}) collective-permute-start(bf16[12,256,128]{2,1,0:T(8,128)(2,1)S(1)} %get-tuple-element.30), channel_id=1, source_target_pairs={{0,6},{1,9},{2,0},{3,11},{4,2},{5,13},{6,4},{7,15},{8,14},{9,17},{... | collective-permute-start | bytes 2359304 | tf_op jit(solution)/shard_map/ppermute | solution.py:194
  105.0 12.0 %collective-permute-done.19 = bf16[128,256]{1,0:T(8,128)(2,1)S(1)} collective-permute-done((bf16[128,256]{1,0:T(8,128)(2,1)S(1)}, bf16[128,256]{1,0:T(8,128)(2,1)S(1)}, u32[]{:S(2)}, u32[]{:S(2)}) %collective-permute-start.19) | collective-permute-done | bytes 65568 | tf_op jit(solution)/shard_map/ppermute | solution.py:241
  117.0 2.0 %collective-permute-start.20 = (bf16[128,256]{1,0:T(8,128)(2,1)S(1)}, bf16[128,256]{1,0:T(8,128)(2,1)S(1)}, u32[]{:S(2)}, u32[]{:S(2)}) collective-permute-start(bf16[128,256]{1,0:T(8,128)(2,1)S(1)} %fusion.1), channel_id=1, source_target_pairs={{0,4},{1,5},{2,6},{3,7},{4,0},{5,1},{6,2},{7,3},{8,12},{9,13},{10,... | collective-permute-start | bytes 196616 | tf_op jit(solution)/shard_map/ppermute | solution.py:241
  119.0 3.9 %collective-permute-done.20 = bf16[128,256]{1,0:T(8,128)(2,1)S(1)} collective-permute-done((bf16[128,256]{1,0:T(8,128)(2,1)S(1)}, bf16[128,256]{1,0:T(8,128)(2,1)S(1)}, u32[]{:S(2)}, u32[]{:S(2)}) %collective-permute-start.20) | collective-permute-done | bytes 65568 | tf_op jit(solution)/shard_map/ppermute | solution.py:241
  123.5 4.4 %collective-permute-start.25 = (bf16[128,256]{1,0:T(8,128)(2,1)S(1)}, bf16[128,256]{1,0:T(8,128)(2,1)S(1)}, u32[]{:S(2)}, u32[]{:S(2)}) collective-permute-start(bf16[128,256]{1,0:T(8,128)(2,1)S(1)} %get-tuple-element.21), channel_id=1, source_target_pairs={{0,8},{8,0},{16,24},{24,16},{32,40},{40,32},{48,56},{56,48},{64,72... | collective-permute-start | bytes 196616 | tf_op jit(solution)/shard_map/ppermute | solution.py:241
  128.0 4.0 %add_convert_fusion.1 = (bf16[24,256,128]{2,1,0:T(8,128)(2,1)}, bf16[24,256,128]{2,1,0:T(8,128)(2,1)}) fusion(bf16[48,256,128]{2,1,0:T(8,128)(2,1)} %collective-permute-done.17, bf16[12,256,128]{2,1,0:T(8,128)(2,1)S(1)} %collective-permute-done.18, bf16[48,256,128]{2,1,0:T(8,128)(2,1)S(1)} %copy-done.2, pred[]{:T(512)S(6)} %eq.33, ...), kind=kLoop, calls=%fused_computation.1 | loop fusion | flops 11010048 | bytes 11010049 | tf_op jit(solution)/shard_map/convert_element_type | solution.py:255
  132.0 3.2 %collective-permute-start.23 = (bf16[24,256,128]{2,1,0:T(8,128)(2,1)}, bf16[24,256,128]{2,1,0:T(8,128)(2,1)}, u32[]{:S(2)}, u32[]{:S(2)}) collective-permute-start(bf16[24,256,128]{2,1,0:T(8,128)(2,1)} %get-tuple-element.28), channel_id=1, source_target_pairs={{0,6},{1,9},{2,0},{3,11},{4,2},{5,13},{6,4},{7,15},{8,14},{9,17},{... | collective-permute-start | bytes 4718600 | tf_op jit(solution)/shard_map/ppermute | solution.py:194
  141.6 7.2 %collective-permute-done.27 = bf16[128,256]{1,0:T(8,128)(2,1)S(1)} collective-permute-done((bf16[128,256]{1,0:T(8,128)(2,1)S(1)}, bf16[128,256]{1,0:T(8,128)(2,1)S(1)}, u32[]{:S(2)}, u32[]{:S(2)}) %collective-permute-start.27) | collective-permute-done | bytes 65568 | tf_op jit(solution)/shard_map/ppermute | solution.py:241
  149.9 4.3 %collective-permute-done.28 = bf16[128,256]{1,0:T(8,128)(2,1)S(1)} collective-permute-done((bf16[128,256]{1,0:T(8,128)(2,1)S(1)}, bf16[128,256]{1,0:T(8,128)(2,1)S(1)}, u32[]{:S(2)}, u32[]{:S(2)}) %collective-permute-start.28) | collective-permute-done | bytes 65568 | tf_op jit(solution)/shard_map/ppermute | solution.py:241
  157.4 3.3 %add_convert_fusion.5 = (bf16[8,256,128]{2,1,0:T(8,128)(2,1)}, bf16[8,256,128]{2,1,0:T(8,128)(2,1)S(1)}) fusion(bf16[24,256,128]{2,1,0:T(8,128)(2,1)} %collective-permute-done.23, bf16[24,256,128]{2,1,0:T(8,128)(2,1)} %collective-permute-done.21, bf16[32,256,128]{2,1,0:T(8,128)(2,1)} %collective-permute-done.16, ...), kind=kLoop, calls=%fused_computation.5 | loop fusion | flops 5242880 | bytes 5767168 | tf_op jit(solution)/shard_map/convert_element_type | solution.py:255
  165.5 4.6 %collective-permute-done.29 = bf16[8,256,128]{2,1,0:T(8,128)(2,1)S(1)} collective-permute-done((bf16[8,256,128]{2,1,0:T(8,128)(2,1)}, bf16[8,256,128]{2,1,0:T(8,128)(2,1)S(1)}, u32[]{:S(2)}, u32[]{:S(2)}) %collective-permute-start.29) | collective-permute-done | bytes 524320 | tf_op jit(solution)/shard_map/ppermute | solution.py:194
  170.1 4.4 %collective-permute-done.30 = bf16[8,256,128]{2,1,0:T(8,128)(2,1)S(1)} collective-permute-done((bf16[8,256,128]{2,1,0:T(8,128)(2,1)S(1)}, bf16[8,256,128]{2,1,0:T(8,128)(2,1)S(1)}, u32[]{:S(2)}, u32[]{:S(2)}) %collective-permute-start.30) | collective-permute-done | bytes 524320 | tf_op jit(solution)/shard_map/ppermute | solution.py:194
  (108 shorter events, 45.6 us)
Async XLA Ops:
  0.6 13.8 %collective-permute-start = (bf16[1024,256]{1,0:T(8,128)(2,1)}, bf16[1024,256]{1,0:T(8,128)(2,1)S(1)}, u32[]{:S(2)}, u32[]{:S(2)}) collective-permute-start(bf16[1024,256]{1,0:T(8,128)(2,1)} %param.7), channel_id=1, source_target_pairs={{120,0},{3,1},{122,2},{5,3},{124,4},{7,5},{126,6},{1,7},{0,8},{11,... | collective-permute-start | bytes 1572872 | tf_op jit(solution)/shard_map/ppermute | solution.py:194
  2.7 12.5 %collective-permute-start.1 = (bf16[1024,256]{1,0:T(8,128)(2,1)}, bf16[1024,256]{1,0:T(8,128)(2,1)S(1)}, u32[]{:S(2)}, u32[]{:S(2)}) collective-permute-start(bf16[1024,256]{1,0:T(8,128)(2,1)} %param.7), channel_id=1, source_target_pairs={{8,0},{7,1},{10,2},{1,3},{12,4},{3,5},{14,6},{5,7},{16,8},{15,9},{... | collective-permute-start | bytes 1572872 | tf_op jit(solution)/shard_map/ppermute | solution.py:194
  16.1 24.6 %collective-permute-start.8 = (bf16[3072,256]{1,0:T(8,128)(2,1)}, bf16[3072,256]{1,0:T(8,128)(2,1)S(1)}, u32[]{:S(2)}, u32[]{:S(2)}) collective-permute-start(bf16[3072,256]{1,0:T(8,128)(2,1)} %constant_dynamic-update-slice_fusion.refs_5_), channel_id=1, source_target_pairs={{6,0},{9,1},{0,2},{11,3},{2,4},{13,5},{4,6},{15,7},{14,8},{17,9},{... | collective-permute-start | bytes 4718600 | tf_op jit(solution)/shard_map/ppermute | solution.py:194
  17.6 23.5 %collective-permute-start.2 = (bf16[3072,256]{1,0:T(8,128)(2,1)}, bf16[3072,256]{1,0:T(8,128)(2,1)}, u32[]{:S(2)}, u32[]{:S(2)}) collective-permute-start(bf16[3072,256]{1,0:T(8,128)(2,1)} %constant_dynamic-update-slice_fusion.refs_5_), channel_id=1, source_target_pairs={{2,0},{121,1},{4,2},{123,3},{6,4},{125,5},{0,6},{127,7},{10,8},{1,... | collective-permute-start | bytes 4718600 | tf_op jit(solution)/shard_map/ppermute | solution.py:194
  19.3 24.4 %collective-permute-start.5 = (bf16[3072,256]{1,0:T(8,128)(2,1)}, bf16[3072,256]{1,0:T(8,128)(2,1)S(1)}, u32[]{:S(2)}, u32[]{:S(2)}) collective-permute-start(bf16[3072,256]{1,0:T(8,128)(2,1)} %constant_dynamic-update-slice_fusion.refs_5_), channel_id=1, source_target_pairs={{0,1},{1,0},{2,3},{3,2},{4,5},{5,4},{6,7},{7,6},{8,9},{9,8},{10,11... | collective-permute-start | bytes 4718600 | tf_op jit(solution)/shard_map/ppermute | solution.py:203
  24.4 19.3 %collective-permute-start.6 = (bf16[1024,256]{1,0:T(8,128)(2,1)S(1)}, bf16[1024,256]{1,0:T(8,128)(2,1)S(1)}, u32[]{:S(2)}, u32[]{:S(2)}) collective-permute-start(bf16[1024,256]{1,0:T(8,128)(2,1)S(1)} %get-tuple-element.35.refs_4_), channel_id=1, source_target_pairs={{0,1},{1,0},{2,3},{3,2},{4,5},{5,4},{6,7},{7,6},{8,9},{9,8},{10,11... | collective-permute-start | bytes 1572872 | tf_op jit(solution)/shard_map/ppermute | solution.py:203
  45.7 12.6 %collective-permute-start.7 = (bf16[1536,256]{1,0:T(8,128)(2,1)}, bf16[1536,256]{1,0:T(8,128)(2,1)}, u32[]{:S(2)}, u32[]{:S(2)}) collective-permute-start(bf16[1536,256]{1,0:T(8,128)(2,1)} %shard_map.94), channel_id=1, source_target_pairs={{2,0},{121,1},{4,2},{123,3},{6,4},{125,5},{0,6},{127,7},{10,8},{1,... | collective-permute-start | bytes 2359304 | tf_op jit(solution)/shard_map/ppermute | solution.py:194
  48.5 15.7 %collective-permute-start.13 = (bf16[3072,256]{1,0:T(8,128)(2,1)S(1)}, bf16[3072,256]{1,0:T(8,128)(2,1)S(1)}, u32[]{:S(2)}, u32[]{:S(2)}) collective-permute-start(bf16[3072,256]{1,0:T(8,128)(2,1)S(1)} %collective-permute-done.8.refs_3_), channel_id=1, source_target_pairs={{0,1},{1,0},{2,3},{3,2},{4,5},{5,4},{6,7},{7,6},{8,9},{9,8},{10,11... | collective-permute-start | bytes 4718600 | tf_op jit(solution)/shard_map/ppermute | solution.py:203
  48.5 13.5 %collective-permute-start.9 = (bf16[1536,256]{1,0:T(8,128)(2,1)}, bf16[1536,256]{1,0:T(8,128)(2,1)}, u32[]{:S(2)}, u32[]{:S(2)}) collective-permute-start(bf16[1536,256]{1,0:T(8,128)(2,1)} %get-tuple-element.31), channel_id=1, source_target_pairs={{6,0},{9,1},{0,2},{11,3},{2,4},{13,5},{4,6},{15,7},{14,8},{17,9},{... | collective-permute-start | bytes 2359304 | tf_op jit(solution)/shard_map/ppermute | solution.py:194
  48.5 16.6 %collective-permute-start.12 = (bf16[3072,256]{1,0:T(8,128)(2,1)}, bf16[3072,256]{1,0:T(8,128)(2,1)}, u32[]{:S(2)}, u32[]{:S(2)}) collective-permute-start(bf16[3072,256]{1,0:T(8,128)(2,1)} %collective-permute-done.2.refs_2_), channel_id=1, source_target_pairs={{0,1},{1,0},{2,3},{3,2},{4,5},{5,4},{6,7},{7,6},{8,9},{9,8},{10,11... | collective-permute-start | bytes 4718600 | tf_op jit(solution)/shard_map/ppermute | solution.py:203
  58.3 5.9 %collective-permute-start.10 = (bf16[1536,256]{1,0:T(8,128)(2,1)}, bf16[1536,256]{1,0:T(8,128)(2,1)}, u32[]{:S(2)}, u32[]{:S(2)}) collective-permute-start(bf16[1536,256]{1,0:T(8,128)(2,1)} %collective-permute-done.7.refs_0_), channel_id=1, source_target_pairs={{0,1},{1,0},{2,3},{3,2},{4,5},{5,4},{6,7},{7,6},{8,9},{9,8},{10,11... | collective-permute-start | bytes 2359304 | tf_op jit(solution)/shard_map/ppermute | solution.py:203
  92.1 6.5 %collective-permute-start.14 = (bf16[24,256,128]{2,1,0:T(8,128)(2,1)}, bf16[24,256,128]{2,1,0:T(8,128)(2,1)S(1)}, u32[]{:S(2)}, u32[]{:S(2)}) collective-permute-start(bf16[24,256,128]{2,1,0:T(8,128)(2,1)} %get-tuple-element.15), channel_id=1, source_target_pairs={{0,1},{1,0},{2,3},{3,2},{4,5},{5,4},{6,7},{7,6},{8,9},{9,8},{10,11... | collective-permute-start | bytes 4718600 | tf_op jit(solution)/shard_map/ppermute | solution.py:203
  101.1 26.9 %collective-permute-start.17 = (bf16[48,256,128]{2,1,0:T(8,128)(2,1)}, bf16[48,256,128]{2,1,0:T(8,128)(2,1)}, u32[]{:S(2)}, u32[]{:S(2)}) collective-permute-start(bf16[48,256,128]{2,1,0:T(8,128)(2,1)} %shard_map.97), channel_id=1, source_target_pairs={{0,1},{1,0},{2,3},{3,2},{4,5},{5,4},{6,7},{7,6},{8,9},{9,8},{10,11... | collective-permute-start | bytes 9437192 | tf_op jit(solution)/shard_map/ppermute | solution.py:203
  101.4 33.8 %collective-permute-start.16 = (bf16[32,256,128]{2,1,0:T(8,128)(2,1)}, bf16[32,256,128]{2,1,0:T(8,128)(2,1)}, u32[]{:S(2)}, u32[]{:S(2)}) collective-permute-start(bf16[32,256,128]{2,1,0:T(8,128)(2,1)} %shard_map.96), channel_id=1, source_target_pairs={{0,1},{1,0},{2,3},{3,2},{4,5},{5,4},{6,7},{7,6},{8,9},{9,8},{10,11... | collective-permute-start | bytes 6291464 | tf_op jit(solution)/shard_map/ppermute | solution.py:203
  101.7 26.2 %collective-permute-start.18 = (bf16[12,256,128]{2,1,0:T(8,128)(2,1)S(1)}, bf16[12,256,128]{2,1,0:T(8,128)(2,1)S(1)}, u32[]{:S(2)}, u32[]{:S(2)}) collective-permute-start(bf16[12,256,128]{2,1,0:T(8,128)(2,1)S(1)} %get-tuple-element.29), channel_id=1, source_target_pairs={{0,2},{1,121},{2,4},{3,123},{4,6},{5,125},{6,0},{7,127},{8,10},{9,... | collective-permute-start | bytes 2359304 | tf_op jit(solution)/shard_map/ppermute | solution.py:194
  102.9 25.1 %collective-permute-start.22 = (bf16[12,256,128]{2,1,0:T(8,128)(2,1)S(1)}, bf16[12,256,128]{2,1,0:T(8,128)(2,1)S(1)}, u32[]{:S(2)}, u32[]{:S(2)}) collective-permute-start(bf16[12,256,128]{2,1,0:T(8,128)(2,1)S(1)} %get-tuple-element.30), channel_id=1, source_target_pairs={{0,6},{1,9},{2,0},{3,11},{4,2},{5,13},{6,4},{7,15},{8,14},{9,17},{... | collective-permute-start | bytes 2359304 | tf_op jit(solution)/shard_map/ppermute | solution.py:194
  105.0 12.0 %collective-permute-start.19 = (bf16[128,256]{1,0:T(8,128)(2,1)S(1)}, bf16[128,256]{1,0:T(8,128)(2,1)S(1)}, u32[]{:S(2)}, u32[]{:S(2)}) collective-permute-start(bf16[128,256]{1,0:T(8,128)(2,1)S(1)} %get-tuple-element.23), channel_id=1, source_target_pairs={{0,2},{1,3},{2,0},{3,1},{4,6},{5,7},{6,4},{7,5},{8,10},{9,11},{10,... | collective-permute-start | bytes 196616 | tf_op jit(solution)/shard_map/ppermute | solution.py:241
  123.5 15.0 %collective-permute-start.25 = (bf16[128,256]{1,0:T(8,128)(2,1)S(1)}, bf16[128,256]{1,0:T(8,128)(2,1)S(1)}, u32[]{:S(2)}, u32[]{:S(2)}) collective-permute-start(bf16[128,256]{1,0:T(8,128)(2,1)S(1)} %get-tuple-element.21), channel_id=1, source_target_pairs={{0,8},{8,0},{16,24},{24,16},{32,40},{40,32},{48,56},{56,48},{64,72... | collective-permute-start | bytes 196616 | tf_op jit(solution)/shard_map/ppermute | solution.py:241
  132.0 25.4 %collective-permute-start.21 = (bf16[24,256,128]{2,1,0:T(8,128)(2,1)}, bf16[24,256,128]{2,1,0:T(8,128)(2,1)}, u32[]{:S(2)}, u32[]{:S(2)}) collective-permute-start(bf16[24,256,128]{2,1,0:T(8,128)(2,1)} %shard_map.98), channel_id=1, source_target_pairs={{0,2},{1,121},{2,4},{3,123},{4,6},{5,125},{6,0},{7,127},{8,10},{9,... | collective-permute-start | bytes 4718600 | tf_op jit(solution)/shard_map/ppermute | solution.py:194
  132.0 25.4 %collective-permute-start.23 = (bf16[24,256,128]{2,1,0:T(8,128)(2,1)}, bf16[24,256,128]{2,1,0:T(8,128)(2,1)}, u32[]{:S(2)}, u32[]{:S(2)}) collective-permute-start(bf16[24,256,128]{2,1,0:T(8,128)(2,1)} %get-tuple-element.28), channel_id=1, source_target_pairs={{0,6},{1,9},{2,0},{3,11},{4,2},{5,13},{6,4},{7,15},{8,14},{9,17},{... | collective-permute-start | bytes 4718600 | tf_op jit(solution)/shard_map/ppermute | solution.py:194
  141.3 7.6 %collective-permute-start.27 = (bf16[128,256]{1,0:T(8,128)(2,1)S(1)}, bf16[128,256]{1,0:T(8,128)(2,1)S(1)}, u32[]{:S(2)}, u32[]{:S(2)}) collective-permute-start(bf16[128,256]{1,0:T(8,128)(2,1)S(1)} %reduce-precision_convert_fusion.1), channel_id=1, source_target_pairs={{0,16},{8,24},{16,0},{24,8},{32,48},{40,56},{48,32},{56,40},{64,80... | collective-permute-start | bytes 196616 | tf_op jit(solution)/shard_map/ppermute | solution.py:241
  155.7 7.0 %collective-permute-start.31 = (bf16[128,256]{1,0:T(8,128)(2,1)S(1)}, bf16[128,256]{1,0:T(8,128)(2,1)S(1)}, u32[]{:S(2)}, u32[]{:S(2)}) collective-permute-start(bf16[128,256]{1,0:T(8,128)(2,1)S(1)} %get-tuple-element.19), channel_id=1, source_target_pairs={{0,64},{8,72},{16,80},{24,88},{32,96},{40,104},{48,112},{56,120},{... | collective-permute-start | bytes 196616 | tf_op jit(solution)/shard_map/ppermute | solution.py:241
  160.7 9.4 %collective-permute-start.29 = (bf16[8,256,128]{2,1,0:T(8,128)(2,1)}, bf16[8,256,128]{2,1,0:T(8,128)(2,1)S(1)}, u32[]{:S(2)}, u32[]{:S(2)}) collective-permute-start(bf16[8,256,128]{2,1,0:T(8,128)(2,1)} %shard_map.100), channel_id=1, source_target_pairs={{0,120},{1,3},{2,122},{3,5},{4,124},{5,7},{6,126},{7,1},{8,0},{9,1... | collective-permute-start | bytes 1572872 | tf_op jit(solution)/shard_map/ppermute | solution.py:194
  162.0 12.5 %collective-permute-start.30 = (bf16[8,256,128]{2,1,0:T(8,128)(2,1)S(1)}, bf16[8,256,128]{2,1,0:T(8,128)(2,1)S(1)}, u32[]{:S(2)}, u32[]{:S(2)}) collective-permute-start(bf16[8,256,128]{2,1,0:T(8,128)(2,1)S(1)} %get-tuple-element.26), channel_id=1, source_target_pairs={{0,8},{1,7},{2,10},{3,1},{4,12},{5,3},{6,14},{7,5},{8,16},{9,15},{... | collective-permute-start | bytes 1572872 | tf_op jit(solution)/shard_map/ppermute | solution.py:194
  (21 other events, 165.7 us)

commit v8 on v7

--- a/solution.py
+++ b/solution.py
@@ -11,7 +11,7 @@
 bf16, f32 = jnp.bfloat16, jnp.float32
 
 FWD_SLOTS = 24
-BWD_SLOTS = 12
+BWD_SLOTS = 24
 STAGES = 8
 CHUNK = 8
 
@@ -215,7 +215,7 @@
     swapped_far = from_core(far)
     to_up = jnp.where(core == 0, up[: 3 * half], crossing)
     to_down = jnp.where(core == 0, down[3 * half :], crossing)
-    last_up = moved(tied(to_up, swapped, swapped_far), NEXT_UP)
+    last_up = moved(tied(to_up, swapped[:8], swapped_far[:8]), NEXT_UP)
     last_down = moved(to_down, NEXT_DOWN)
     mine = [last_up, last_down, up, down]
     return mine + [far, near3] + [from_core(x) for x in mine] + [swapped_far, swapped]
@@ -225,7 +225,7 @@
     def __init__(self, term, core):
         height = term.shape[0] // 2
         low, high = term[:height], term[height:]
-        self.x = jnp.where(core == 0, low, high) + from_core(jnp.where(core == 0, high, low))
+        self.mine, self.other = jnp.where(core == 0, low, high), jnp.where(core == 0, high, low)
         self.core = core
         self.left = [
             (axis, bit)
@@ -234,6 +234,9 @@
             if first <= bit < lax.axis_size(axis)
         ]
 
+    def begin(self, *earlier):
+        self.x = self.mine + from_core(tied(self.other, *earlier))
+
     def go(self, count):
         for axis, bit in self.left[:count]:
             pairs = [(i, i ^ bit) for i in range(lax.axis_size(axis))]
@@ -263,11 +266,13 @@
     half = own // 2
     cut = 3 * half
     last = total(mine[0], from_core(other[0]))
-    middle = from_core(tied(other[1], last[:1, :8], steps.x[:1, :8]))
+    begun = last[:1, :8]
+    middle = from_core(tied(other[1], begun))
     last_up = moved(last[:cut], NEXT_UP, back=True)
     last_down = moved(last[cut:], NEXT_DOWN, back=True)
-    first = from_core(tied(other[2], last[:1, :8], steps.x[:1, :8]))
-    steps.go(2)
+    first = from_core(tied(other[2], begun))
+    steps.begin(begun)
+    steps.go(1)
     along = core == 0
     zero = jnp.zeros((), bf16)
     to_up = jnp.where(along, widened(last_up, 2 * cut, 0), zero)
@@ -290,6 +295,7 @@
 
     up = tied(total(*near(1), widened(half_up, own, 0)), steps.x)
     down = total(*near(2), widened(half_down, own, half))
+    steps.after(down[:1, :8])
     ends = moved(up, FIRST_UP, back=True), moved(down, FIRST_DOWN, back=True)
     return total(*near(0), *ends)
 

time: 179 us -> 183 us (1.022); the launches traced: 177 us -> 183 us
  Pallas kernels: 26.7 us -> 30.1 us
  waiting for transfers between devices: 54.8 us -> 51.6 us
  starting transfers between devices: 59 us -> 61.7 us
  other arithmetic: 24.3 us -> 27 us
    ppermute x16, starting transfers between devices: 24.8 us -> 29.6 us  [moved(): return lax.ppermute(x, ('rows', 'rep'), pairs)]
    ppermute x11, waiting for transfers between devices: 4.03 us -> 8.74 us  [from_core(): lax.ppermute(x, 'rep', [(i, i ^ 1) for i in range(lax.axis_size('rep'))])]
    ppermute x6, starting transfers between devices: 8.46 us -> 4.09 us  [go(): lax.ppermute(rounded.astype(bf16), axis, pairs).astype(f32)]
    ppermute x16, waiting for transfers between devices: 23.5 us -> 19.4 us  [moved(): return lax.ppermute(x, ('rows', 'rep'), pairs)]
    ppermute x6, waiting for transfers between devices: 27.3 us -> 23.5 us  [go(): lax.ppermute(rounded.astype(bf16), axis, pairs).astype(f32)]
    pallas_call x1, Pallas kernels: 26.7 us -> 30.1 us  [layer(): pl.pallas_call(functools.partial(kernel, len(parts), 2 * len(groups)), in...]
    slice x2 -> x4, local copies, waits for them, and re-layouts: 1.09 us -> 3.72 us  [the longest x2 2.55 us: gather(): last_up = moved(tied(to_up, swapped[:8], swapped_far[:8]), NEXT_UP)]
    add x2 -> x3, other arithmetic: 0.69 us -> 3.2 us  [go(): rounded + lax.ppermute(rounded.astype(bf16), axis, pairs).astype(f32)]
  transfers between devices with their start and end apart: 33 -> 33, of which waited for: 14 -> 15; matrix products, arithmetic and copies ran while one was open for 16% -> 13% of each run, Pallas kernels for 0% -> 0%
where the time goes in v8:
time: 183 us
  starting transfers between devices  61.7 us (34%)
  waiting for transfers between devices  51.6 us (28%)
  Pallas kernels  30.1 us (16%)
  other arithmetic  27 us (15%)
  local copies, waits for them, and re-layouts  12 us (7%)
    pallas_call x1, Pallas kernels, layer(): pl.pallas_call(functools.partial(kernel, len(parts), 2 * len(groups)), in...  30.1 us
    ppermute x16, starting transfers between devices, moved(): return lax.ppermute(x, ('rows', 'rep'), pairs)  29.6 us
    ppermute x11, starting transfers between devices, from_core(): lax.ppermute(x, 'rep', [(i, i ^ 1) for i in range(lax.axis_size('rep'))])  28 us
    ppermute x6, waiting for transfers between devices, go(): lax.ppermute(rounded.astype(bf16), axis, pairs).astype(f32)  23.5 us
    ppermute x16, waiting for transfers between devices, moved(): return lax.ppermute(x, ('rows', 'rep'), pairs)  19.4 us
    convert_element_type x4, other arithmetic, total(): return sum((x.astype(f32) for x in terms)).astype(bf16)  11.6 us
    ppermute x11, waiting for transfers between devices, from_core(): lax.ppermute(x, 'rep', [(i, i ^ 1) for i in range(lax.axis_size('rep'))])  8.74 us
    convert_element_type x6, other arithmetic, go(): rounded.astype(bf16)  4.38 us
  transfers between devices with their start and end apart: 33, of which 15 were waited for; matrix products, arithmetic and copies ran while one was open for 13% of the time, Pallas kernels for 0%

profile of v8, /device:TPU:0, one launch (start us, length us, event | category | flops | bytes accessed | tf_op | source)
XLA Modules:
  0.0 183.4 jit_solution(15627552226940058212)
XLA Ops:
  0.6 2.1 %collective-permute-start = (bf16[1024,256]{1,0:T(8,128)(2,1)}, bf16[1024,256]{1,0:T(8,128)(2,1)S(1)}, u32[]{:S(2)}, u32[]{:S(2)}) collective-permute-start(bf16[1024,256]{1,0:T(8,128)(2,1)} %param.7), channel_id=1, source_target_pairs={{120,0},{3,1},{122,2},{5,3},{124,4},{7,5},{126,6},{1,7},{0,8},{11,... | collective-permute-start | bytes 1572872 | tf_op jit(solution)/shard_map/ppermute | solution.py:194
  2.7 4.4 %collective-permute-start.1 = (bf16[1024,256]{1,0:T(8,128)(2,1)}, bf16[1024,256]{1,0:T(8,128)(2,1)S(1)}, u32[]{:S(2)}, u32[]{:S(2)}) collective-permute-start(bf16[1024,256]{1,0:T(8,128)(2,1)} %param.7), channel_id=1, source_target_pairs={{8,0},{7,1},{10,2},{1,3},{12,4},{3,5},{14,6},{5,7},{16,8},{15,9},{... | collective-permute-start | bytes 1572872 | tf_op jit(solution)/shard_map/ppermute | solution.py:194
  7.1 1.9 %constant_dynamic-update-slice_fusion.2 = bf16[3072,256]{1,0:T(8,128)(2,1)} fusion(bf16[1024,256]{1,0:T(8,128)(2,1)} %param.7), kind=kLoop, calls=%fused_computation.30 | loop fusion | bytes 1048576
  9.0 5.3 %collective-permute-done = bf16[1024,256]{1,0:T(8,128)(2,1)S(1)} collective-permute-done((bf16[1024,256]{1,0:T(8,128)(2,1)}, bf16[1024,256]{1,0:T(8,128)(2,1)S(1)}, u32[]{:S(2)}, u32[]{:S(2)}) %collective-permute-start) | collective-permute-done | bytes 524320 | tf_op jit(solution)/shard_map/ppermute | solution.py:194
  22.4 15.5 %collective-permute-start.6 = (bf16[1024,256]{1,0:T(8,128)(2,1)}, bf16[1024,256]{1,0:T(8,128)(2,1)}, u32[]{:S(2)}, u32[]{:S(2)}) collective-permute-start(bf16[1024,256]{1,0:T(8,128)(2,1)} %get-tuple-element.33.refs_4_), channel_id=1, source_target_pairs={{0,1},{1,0},{2,3},{3,2},{4,5},{5,4},{6,7},{7,6},{8,9},{9,8},{10,11... | collective-permute-start | bytes 1572872 | tf_op jit(solution)/shard_map/ppermute | solution.py:203
  42.3 3.0 %slice_select_fusion = (bf16[1536,256]{1,0:T(8,128)(2,1)}, bf16[1536,256]{1,0:T(8,128)(2,1)}) fusion(bf16[1536,256]{1,0:T(8,128)(2,1)} %constant_dynamic-update-slice_fusion.3, bf16[3072,256]{1,0:T(8,128)(2,1)S(1)} %collective-permute-done.8.refs_3_, pred[]{:T(512)S(6)} %eq.33, bf16[3072,256]{1,0:T(8,128)(2,1)S(1)} %collective-permute-done.2.refs_2_), kind=kLoop, calls=%fused_computation.7 | loop fusion | flops 786432 | bytes 3932161 | tf_op jit(solution)/shard_map/jit(_where)/select_n | solution.py:217
  48.4 3.4 %collective-permute-start.12 = (bf16[3072,256]{1,0:T(8,128)(2,1)S(1)}, bf16[3072,256]{1,0:T(8,128)(2,1)}, u32[]{:S(2)}, u32[]{:S(2)}) collective-permute-start(bf16[3072,256]{1,0:T(8,128)(2,1)S(1)} %collective-permute-done.2.refs_2_), channel_id=1, source_target_pairs={{0,1},{1,0},{2,3},{3,2},{4,5},{5,4},{6,7},{7,6},{8,9},{9,8},{10,11... | collective-permute-start | bytes 4718600 | tf_op jit(solution)/shard_map/ppermute | solution.py:203
  51.9 5.9 %collective-permute-done.7.refs_0_ = bf16[1536,256]{1,0:T(8,128)(2,1)} collective-permute-done((bf16[1536,256]{1,0:T(8,128)(2,1)}, bf16[1536,256]{1,0:T(8,128)(2,1)}, u32[]{:S(2)}, u32[]{:S(2)}) %collective-permute-start.7) | collective-permute-done | bytes 786464 | tf_op jit(solution)/shard_map/ppermute | solution.py:194
  57.7 3.5 %collective-permute-start.10 = (bf16[1536,256]{1,0:T(8,128)(2,1)}, bf16[1536,256]{1,0:T(8,128)(2,1)}, u32[]{:S(2)}, u32[]{:S(2)}) collective-permute-start(bf16[1536,256]{1,0:T(8,128)(2,1)} %collective-permute-done.7.refs_0_), channel_id=1, source_target_pairs={{0,1},{1,0},{2,3},{3,2},{4,5},{5,4},{6,7},{7,6},{8,9},{9,8},{10,11... | collective-permute-start | bytes 2359304 | tf_op jit(solution)/shard_map/ppermute | solution.py:203
  64.6 30.1 %shard_map.95 = (bf16[1024,256]{1,0:T(8,128)(2,1)}, f32[256,256]{1,0:T(8,128)}, bf16[24,256,128]{2,1,0:T(8,128)(2,1)}, bf16[48,256,128]{2,1,0:T(8,128)(2,1)}, bf...) custom-call(s32[8,48]{1,0:T(8,128)} %fusion.5.idx, ...), custom_call_target="tpu_custom_call" | custom-call | flops 6442450944 | bytes 37748736 | tf_op jit(solution)/shard_map/pallas_call | solution.py:141
  94.8 3.6 %collective-permute-done.14 = bf16[24,256,128]{2,1,0:T(8,128)(2,1)S(1)} collective-permute-done((bf16[24,256,128]{2,1,0:T(8,128)(2,1)}, bf16[24,256,128]{2,1,0:T(8,128)(2,1)S(1)}, u32[]{:S(2)}, u32[]{:S(2)}) %collective-permute-start.14) | collective-permute-done | bytes 1572896 | tf_op jit(solution)/shard_map/ppermute | solution.py:203
  101.5 3.7 %collective-permute-start.17 = (bf16[12,256,128]{2,1,0:T(8,128)(2,1)S(1)}, bf16[12,256,128]{2,1,0:T(8,128)(2,1)S(1)}, u32[]{:S(2)}, u32[]{:S(2)}) collective-permute-start(bf16[12,256,128]{2,1,0:T(8,128)(2,1)S(1)} %get-tuple-element.27), channel_id=1, source_target_pairs={{0,2},{1,121},{2,4},{3,123},{4,6},{5,125},{6,0},{7,127},{8,10},{9,... | collective-permute-start | bytes 2359304 | tf_op jit(solution)/shard_map/ppermute | solution.py:194
  107.4 2.0 %collective-permute-start.18 = (f32[128,256]{1,0:T(8,128)}, f32[128,256]{1,0:T(8,128)S(1)}, u32[]{:S(2)}, u32[]{:S(2)}) collective-permute-start(f32[128,256]{1,0:T(8,128)} %shard_map.98), channel_id=1, source_target_pairs={{0,1},{1,0},{2,3},{3,2},{4,5},{5,4},{6,7},{7,6},{8,9},{9,8},{10,11... | collective-permute-start | bytes 393224 | tf_op jit(solution)/shard_map/ppermute | solution.py:203
  110.9 7.8 %collective-permute-done.19 = bf16[128,256]{1,0:T(8,128)(2,1)S(1)} collective-permute-done((bf16[128,256]{1,0:T(8,128)(2,1)S(1)}, bf16[128,256]{1,0:T(8,128)(2,1)S(1)}, u32[]{:S(2)}, u32[]{:S(2)}) %collective-permute-start.19) | collective-permute-done | bytes 65568 | tf_op jit(solution)/shard_map/ppermute | solution.py:244
  119.3 2.9 %collective-permute-start.24 = (bf16[128,256]{1,0:T(8,128)(2,1)S(1)}, bf16[128,256]{1,0:T(8,128)(2,1)S(1)}, u32[]{:S(2)}, u32[]{:S(2)}) collective-permute-start(bf16[128,256]{1,0:T(8,128)(2,1)S(1)} %get-tuple-element.19), channel_id=1, source_target_pairs={{0,4},{1,5},{2,6},{3,7},{4,0},{5,1},{6,2},{7,3},{8,12},{9,13},{10,... | collective-permute-start | bytes 196616 | tf_op jit(solution)/shard_map/ppermute | solution.py:244
  122.2 4.8 %add_convert_fusion.1 = (bf16[24,256,128]{2,1,0:T(8,128)(2,1)}, bf16[24,256,128]{2,1,0:T(8,128)(2,1)}) fusion(bf16[48,256,128]{2,1,0:T(8,128)(2,1)} %collective-permute-done.16, bf16[12,256,128]{2,1,0:T(8,128)(2,1)S(1)} %collective-permute-done.17, bf16[48,256,128]{2,1,0:T(8,128)(2,1)} %get-tuple-element.16, pred[]{:T(512)S(6)} %eq.33, ...), kind=kLoop, calls=%fused_computation.1 | loop fusion | flops 11010048 | bytes 11010049 | tf_op jit(solution)/shard_map/convert_element_type | solution.py:258
  127.0 3.2 %collective-permute-start.22 = (bf16[24,256,128]{2,1,0:T(8,128)(2,1)}, bf16[24,256,128]{2,1,0:T(8,128)(2,1)}, u32[]{:S(2)}, u32[]{:S(2)}) collective-permute-start(bf16[24,256,128]{2,1,0:T(8,128)(2,1)} %get-tuple-element.26), channel_id=1, source_target_pairs={{0,6},{1,9},{2,0},{3,11},{4,2},{5,13},{6,4},{7,15},{8,14},{9,17},{... | collective-permute-start | bytes 4718600 | tf_op jit(solution)/shard_map/ppermute | solution.py:194
  136.4 5.0 %collective-permute-done.26 = bf16[128,256]{1,0:T(8,128)(2,1)S(1)} collective-permute-done((bf16[128,256]{1,0:T(8,128)(2,1)S(1)}, bf16[128,256]{1,0:T(8,128)(2,1)S(1)}, u32[]{:S(2)}, u32[]{:S(2)}) %collective-permute-start.26) | collective-permute-done | bytes 65568 | tf_op jit(solution)/shard_map/ppermute | solution.py:244
  142.5 6.5 %collective-permute-done.27 = bf16[128,256]{1,0:T(8,128)(2,1)S(1)} collective-permute-done((bf16[128,256]{1,0:T(8,128)(2,1)S(1)}, bf16[128,256]{1,0:T(8,128)(2,1)S(1)}, u32[]{:S(2)}, u32[]{:S(2)}) %collective-permute-start.27) | collective-permute-done | bytes 65568 | tf_op jit(solution)/shard_map/ppermute | solution.py:244
  151.8 3.3 %add_convert_fusion.5 = (bf16[8,256,128]{2,1,0:T(8,128)(2,1)}, bf16[8,256,128]{2,1,0:T(8,128)(2,1)S(1)}) fusion(bf16[24,256,128]{2,1,0:T(8,128)(2,1)} %collective-permute-done.22, bf16[24,256,128]{2,1,0:T(8,128)(2,1)} %collective-permute-done.20, bf16[32,256,128]{2,1,0:T(8,128)(2,1)} %collective-permute-done.15, ...), kind=kLoop, calls=%fused_computation.5 | loop fusion | flops 5242880 | bytes 5767168 | tf_op jit(solution)/shard_map/convert_element_type | solution.py:258
  156.7 4.3 %collective-permute-done.30 = bf16[128,256]{1,0:T(8,128)(2,1)S(1)} collective-permute-done((bf16[128,256]{1,0:T(8,128)(2,1)S(1)}, bf16[128,256]{1,0:T(8,128)(2,1)S(1)}, u32[]{:S(2)}, u32[]{:S(2)}) %collective-permute-start.30) | collective-permute-done | bytes 65568 | tf_op jit(solution)/shard_map/ppermute | solution.py:244
  162.7 5.4 %collective-permute-start.28 = (bf16[8,256,128]{2,1,0:T(8,128)(2,1)}, bf16[8,256,128]{2,1,0:T(8,128)(2,1)S(1)}, u32[]{:S(2)}, u32[]{:S(2)}) collective-permute-start(bf16[8,256,128]{2,1,0:T(8,128)(2,1)} %shard_map.101), channel_id=1, source_target_pairs={{0,120},{1,3},{2,122},{3,5},{4,124},{5,7},{6,126},{7,1},{8,0},{9,1... | collective-permute-start | bytes 1572872 | tf_op jit(solution)/shard_map/ppermute | solution.py:194
  169.0 3.0 %collective-permute-start.32 = (f32[128,256]{1,0:T(8,128)S(1)}, f32[128,256]{1,0:T(8,128)S(1)}, u32[]{:S(2)}, u32[]{:S(2)}) collective-permute-start(f32[128,256]{1,0:T(8,128)S(1)} %convert_add_fusion), channel_id=1, source_target_pairs={{0,1},{1,0},{2,3},{3,2},{4,5},{5,4},{6,7},{7,6},{8,9},{9,8},{10,11... | collective-permute-start | bytes 393224 | tf_op jit(solution)/shard_map/ppermute | solution.py:203
  175.1 5.5 %collective-permute-done.29 = bf16[8,256,128]{2,1,0:T(8,128)(2,1)S(1)} collective-permute-done((bf16[8,256,128]{2,1,0:T(8,128)(2,1)S(1)}, bf16[8,256,128]{2,1,0:T(8,128)(2,1)S(1)}, u32[]{:S(2)}, u32[]{:S(2)}) %collective-permute-start.29) | collective-permute-done | bytes 524320 | tf_op jit(solution)/shard_map/ppermute | solution.py:194
  (105 shorter events, 46.4 us)
Async XLA Ops:
  0.6 13.8 %collective-permute-start = (bf16[1024,256]{1,0:T(8,128)(2,1)}, bf16[1024,256]{1,0:T(8,128)(2,1)S(1)}, u32[]{:S(2)}, u32[]{:S(2)}) collective-permute-start(bf16[1024,256]{1,0:T(8,128)(2,1)} %param.7), channel_id=1, source_target_pairs={{120,0},{3,1},{122,2},{5,3},{124,4},{7,5},{126,6},{1,7},{0,8},{11,... | collective-permute-start | bytes 1572872 | tf_op jit(solution)/shard_map/ppermute | solution.py:194
  2.7 12.5 %collective-permute-start.1 = (bf16[1024,256]{1,0:T(8,128)(2,1)}, bf16[1024,256]{1,0:T(8,128)(2,1)S(1)}, u32[]{:S(2)}, u32[]{:S(2)}) collective-permute-start(bf16[1024,256]{1,0:T(8,128)(2,1)} %param.7), channel_id=1, source_target_pairs={{8,0},{7,1},{10,2},{1,3},{12,4},{3,5},{14,6},{5,7},{16,8},{15,9},{... | collective-permute-start | bytes 1572872 | tf_op jit(solution)/shard_map/ppermute | solution.py:194
  16.0 25.0 %collective-permute-start.5 = (bf16[3072,256]{1,0:T(8,128)(2,1)}, bf16[3072,256]{1,0:T(8,128)(2,1)}, u32[]{:S(2)}, u32[]{:S(2)}) collective-permute-start(bf16[3072,256]{1,0:T(8,128)(2,1)} %constant_dynamic-update-slice_fusion.refs_5_), channel_id=1, source_target_pairs={{0,1},{1,0},{2,3},{3,2},{4,5},{5,4},{6,7},{7,6},{8,9},{9,8},{10,11... | collective-permute-start | bytes 4718600 | tf_op jit(solution)/shard_map/ppermute | solution.py:203
  16.1 26.2 %collective-permute-start.8 = (bf16[3072,256]{1,0:T(8,128)(2,1)}, bf16[3072,256]{1,0:T(8,128)(2,1)S(1)}, u32[]{:S(2)}, u32[]{:S(2)}) collective-permute-start(bf16[3072,256]{1,0:T(8,128)(2,1)} %constant_dynamic-update-slice_fusion.refs_5_), channel_id=1, source_target_pairs={{6,0},{9,1},{0,2},{11,3},{2,4},{13,5},{4,6},{15,7},{14,8},{17,9},{... | collective-permute-start | bytes 4718600 | tf_op jit(solution)/shard_map/ppermute | solution.py:194
  17.6 24.7 %collective-permute-start.2 = (bf16[3072,256]{1,0:T(8,128)(2,1)}, bf16[3072,256]{1,0:T(8,128)(2,1)S(1)}, u32[]{:S(2)}, u32[]{:S(2)}) collective-permute-start(bf16[3072,256]{1,0:T(8,128)(2,1)} %constant_dynamic-update-slice_fusion.refs_5_), channel_id=1, source_target_pairs={{2,0},{121,1},{4,2},{123,3},{6,4},{125,5},{0,6},{127,7},{10,8},{1,... | collective-permute-start | bytes 4718600 | tf_op jit(solution)/shard_map/ppermute | solution.py:194
  22.4 17.4 %collective-permute-start.6 = (bf16[1024,256]{1,0:T(8,128)(2,1)}, bf16[1024,256]{1,0:T(8,128)(2,1)}, u32[]{:S(2)}, u32[]{:S(2)}) collective-permute-start(bf16[1024,256]{1,0:T(8,128)(2,1)} %get-tuple-element.33.refs_4_), channel_id=1, source_target_pairs={{0,1},{1,0},{2,3},{3,2},{4,5},{5,4},{6,7},{7,6},{8,9},{9,8},{10,11... | collective-permute-start | bytes 1572872 | tf_op jit(solution)/shard_map/ppermute | solution.py:203
  45.4 12.4 %collective-permute-start.7 = (bf16[1536,256]{1,0:T(8,128)(2,1)}, bf16[1536,256]{1,0:T(8,128)(2,1)}, u32[]{:S(2)}, u32[]{:S(2)}) collective-permute-start(bf16[1536,256]{1,0:T(8,128)(2,1)} %shard_map.94), channel_id=1, source_target_pairs={{2,0},{121,1},{4,2},{123,3},{6,4},{125,5},{0,6},{127,7},{10,8},{1,... | collective-permute-start | bytes 2359304 | tf_op jit(solution)/shard_map/ppermute | solution.py:194
  47.0 15.8 %collective-permute-start.13 = (bf16[3072,256]{1,0:T(8,128)(2,1)S(1)}, bf16[3072,256]{1,0:T(8,128)(2,1)}, u32[]{:S(2)}, u32[]{:S(2)}) collective-permute-start(bf16[3072,256]{1,0:T(8,128)(2,1)S(1)} %collective-permute-done.8.refs_3_), channel_id=1, source_target_pairs={{0,1},{1,0},{2,3},{3,2},{4,5},{5,4},{6,7},{7,6},{8,9},{9,8},{10,11... | collective-permute-start | bytes 4718600 | tf_op jit(solution)/shard_map/ppermute | solution.py:203
  47.0 14.2 %collective-permute-start.9 = (bf16[1536,256]{1,0:T(8,128)(2,1)}, bf16[1536,256]{1,0:T(8,128)(2,1)}, u32[]{:S(2)}, u32[]{:S(2)}) collective-permute-start(bf16[1536,256]{1,0:T(8,128)(2,1)} %get-tuple-element.29), channel_id=1, source_target_pairs={{6,0},{9,1},{0,2},{11,3},{2,4},{13,5},{4,6},{15,7},{14,8},{17,9},{... | collective-permute-start | bytes 2359304 | tf_op jit(solution)/shard_map/ppermute | solution.py:194
  48.4 16.2 %collective-permute-start.12 = (bf16[3072,256]{1,0:T(8,128)(2,1)S(1)}, bf16[3072,256]{1,0:T(8,128)(2,1)}, u32[]{:S(2)}, u32[]{:S(2)}) collective-permute-start(bf16[3072,256]{1,0:T(8,128)(2,1)S(1)} %collective-permute-done.2.refs_2_), channel_id=1, source_target_pairs={{0,1},{1,0},{2,3},{3,2},{4,5},{5,4},{6,7},{7,6},{8,9},{9,8},{10,11... | collective-permute-start | bytes 4718600 | tf_op jit(solution)/shard_map/ppermute | solution.py:203
  57.7 5.7 %collective-permute-start.10 = (bf16[1536,256]{1,0:T(8,128)(2,1)}, bf16[1536,256]{1,0:T(8,128)(2,1)}, u32[]{:S(2)}, u32[]{:S(2)}) collective-permute-start(bf16[1536,256]{1,0:T(8,128)(2,1)} %collective-permute-done.7.refs_0_), channel_id=1, source_target_pairs={{0,1},{1,0},{2,3},{3,2},{4,5},{5,4},{6,7},{7,6},{8,9},{9,8},{10,11... | collective-permute-start | bytes 2359304 | tf_op jit(solution)/shard_map/ppermute | solution.py:203
  100.9 21.3 %collective-permute-start.16 = (bf16[48,256,128]{2,1,0:T(8,128)(2,1)}, bf16[48,256,128]{2,1,0:T(8,128)(2,1)}, u32[]{:S(2)}, u32[]{:S(2)}) collective-permute-start(bf16[48,256,128]{2,1,0:T(8,128)(2,1)} %shard_map.97), channel_id=1, source_target_pairs={{0,1},{1,0},{2,3},{3,2},{4,5},{5,4},{6,7},{7,6},{8,9},{9,8},{10,11... | collective-permute-start | bytes 9437192 | tf_op jit(solution)/shard_map/ppermute | solution.py:203
  101.0 29.3 %collective-permute-start.15 = (bf16[32,256,128]{2,1,0:T(8,128)(2,1)}, bf16[32,256,128]{2,1,0:T(8,128)(2,1)}, u32[]{:S(2)}, u32[]{:S(2)}) collective-permute-start(bf16[32,256,128]{2,1,0:T(8,128)(2,1)} %shard_map.96), channel_id=1, source_target_pairs={{0,1},{1,0},{2,3},{3,2},{4,5},{5,4},{6,7},{7,6},{8,9},{9,8},{10,11... | collective-permute-start | bytes 6291464 | tf_op jit(solution)/shard_map/ppermute | solution.py:203
  101.5 20.7 %collective-permute-start.17 = (bf16[12,256,128]{2,1,0:T(8,128)(2,1)S(1)}, bf16[12,256,128]{2,1,0:T(8,128)(2,1)S(1)}, u32[]{:S(2)}, u32[]{:S(2)}) collective-permute-start(bf16[12,256,128]{2,1,0:T(8,128)(2,1)S(1)} %get-tuple-element.27), channel_id=1, source_target_pairs={{0,2},{1,121},{2,4},{3,123},{4,6},{5,125},{6,0},{7,127},{8,10},{9,... | collective-permute-start | bytes 2359304 | tf_op jit(solution)/shard_map/ppermute | solution.py:194
  105.2 17.0 %collective-permute-start.21 = (bf16[12,256,128]{2,1,0:T(8,128)(2,1)S(1)}, bf16[12,256,128]{2,1,0:T(8,128)(2,1)S(1)}, u32[]{:S(2)}, u32[]{:S(2)}) collective-permute-start(bf16[12,256,128]{2,1,0:T(8,128)(2,1)S(1)} %get-tuple-element.28), channel_id=1, source_target_pairs={{0,6},{1,9},{2,0},{3,11},{4,2},{5,13},{6,4},{7,15},{8,14},{9,17},{... | collective-permute-start | bytes 2359304 | tf_op jit(solution)/shard_map/ppermute | solution.py:194
  110.7 7.9 %collective-permute-start.19 = (bf16[128,256]{1,0:T(8,128)(2,1)S(1)}, bf16[128,256]{1,0:T(8,128)(2,1)S(1)}, u32[]{:S(2)}, u32[]{:S(2)}) collective-permute-start(bf16[128,256]{1,0:T(8,128)(2,1)S(1)} %get-tuple-element.21), channel_id=1, source_target_pairs={{0,2},{1,3},{2,0},{3,1},{4,6},{5,7},{6,4},{7,5},{8,10},{9,11},{10,... | collective-permute-start | bytes 196616 | tf_op jit(solution)/shard_map/ppermute | solution.py:244
  119.3 14.3 %collective-permute-start.24 = (bf16[128,256]{1,0:T(8,128)(2,1)S(1)}, bf16[128,256]{1,0:T(8,128)(2,1)S(1)}, u32[]{:S(2)}, u32[]{:S(2)}) collective-permute-start(bf16[128,256]{1,0:T(8,128)(2,1)S(1)} %get-tuple-element.19), channel_id=1, source_target_pairs={{0,4},{1,5},{2,6},{3,7},{4,0},{5,1},{6,2},{7,3},{8,12},{9,13},{10,... | collective-permute-start | bytes 196616 | tf_op jit(solution)/shard_map/ppermute | solution.py:244
  127.0 24.8 %collective-permute-start.20 = (bf16[24,256,128]{2,1,0:T(8,128)(2,1)}, bf16[24,256,128]{2,1,0:T(8,128)(2,1)}, u32[]{:S(2)}, u32[]{:S(2)}) collective-permute-start(bf16[24,256,128]{2,1,0:T(8,128)(2,1)} %shard_map.99), channel_id=1, source_target_pairs={{0,2},{1,121},{2,4},{3,123},{4,6},{5,125},{6,0},{7,127},{8,10},{9,... | collective-permute-start | bytes 4718600 | tf_op jit(solution)/shard_map/ppermute | solution.py:194
  127.0 24.7 %collective-permute-start.22 = (bf16[24,256,128]{2,1,0:T(8,128)(2,1)}, bf16[24,256,128]{2,1,0:T(8,128)(2,1)}, u32[]{:S(2)}, u32[]{:S(2)}) collective-permute-start(bf16[24,256,128]{2,1,0:T(8,128)(2,1)} %get-tuple-element.26), channel_id=1, source_target_pairs={{0,6},{1,9},{2,0},{3,11},{4,2},{5,13},{6,4},{7,15},{8,14},{9,17},{... | collective-permute-start | bytes 4718600 | tf_op jit(solution)/shard_map/ppermute | solution.py:194
  136.3 5.1 %collective-permute-start.26 = (bf16[128,256]{1,0:T(8,128)(2,1)S(1)}, bf16[128,256]{1,0:T(8,128)(2,1)S(1)}, u32[]{:S(2)}, u32[]{:S(2)}) collective-permute-start(bf16[128,256]{1,0:T(8,128)(2,1)S(1)} %reduce-precision_convert_fusion.1), channel_id=1, source_target_pairs={{0,8},{8,0},{16,24},{24,16},{32,40},{40,32},{48,56},{56,48},{64,72... | collective-permute-start | bytes 196616 | tf_op jit(solution)/shard_map/ppermute | solution.py:244
  142.4 6.5 %collective-permute-start.27 = (bf16[128,256]{1,0:T(8,128)(2,1)S(1)}, bf16[128,256]{1,0:T(8,128)(2,1)S(1)}, u32[]{:S(2)}, u32[]{:S(2)}) collective-permute-start(bf16[128,256]{1,0:T(8,128)(2,1)S(1)} %fusion.1), channel_id=1, source_target_pairs={{0,16},{8,24},{16,0},{24,8},{32,48},{40,56},{48,32},{56,40},{64,80... | collective-permute-start | bytes 196616 | tf_op jit(solution)/shard_map/ppermute | solution.py:244
  161.9 6.2 %collective-permute-start.31 = (bf16[128,256]{1,0:T(8,128)(2,1)S(1)}, bf16[128,256]{1,0:T(8,128)(2,1)S(1)}, u32[]{:S(2)}, u32[]{:S(2)}) collective-permute-start(bf16[128,256]{1,0:T(8,128)(2,1)S(1)} %fusion.2), channel_id=1, source_target_pairs={{0,64},{8,72},{16,80},{24,88},{32,96},{40,104},{48,112},{56,120},{... | collective-permute-start | bytes 196616 | tf_op jit(solution)/shard_map/ppermute | solution.py:244
  162.7 12.4 %collective-permute-start.28 = (bf16[8,256,128]{2,1,0:T(8,128)(2,1)}, bf16[8,256,128]{2,1,0:T(8,128)(2,1)S(1)}, u32[]{:S(2)}, u32[]{:S(2)}) collective-permute-start(bf16[8,256,128]{2,1,0:T(8,128)(2,1)} %shard_map.101), channel_id=1, source_target_pairs={{0,120},{1,3},{2,122},{3,5},{4,124},{5,7},{6,126},{7,1},{8,0},{9,1... | collective-permute-start | bytes 1572872 | tf_op jit(solution)/shard_map/ppermute | solution.py:194
  168.1 12.5 %collective-permute-start.29 = (bf16[8,256,128]{2,1,0:T(8,128)(2,1)S(1)}, bf16[8,256,128]{2,1,0:T(8,128)(2,1)S(1)}, u32[]{:S(2)}, u32[]{:S(2)}) collective-permute-start(bf16[8,256,128]{2,1,0:T(8,128)(2,1)S(1)} %get-tuple-element.24), channel_id=1, source_target_pairs={{0,8},{1,7},{2,10},{3,1},{4,12},{5,3},{6,14},{7,5},{8,16},{9,15},{... | collective-permute-start | bytes 1572872 | tf_op jit(solution)/shard_map/ppermute | solution.py:194
  (17 other events, 114.9 us)

commit v9 on v8

--- a/solution.py
+++ b/solution.py
@@ -287,7 +287,7 @@
     half_down = moved(far[half:], HALF_DOWN, back=True)
     steps.go(1)
     steps.after(half_up[:1, :8], half_down[:1, :8])
-    steps.go(2)
+    steps.go(3)
 
     def near(k):
         at = slice(k * own, (k + 1) * own)
@@ -295,7 +295,6 @@
 
     up = tied(total(*near(1), widened(half_up, own, 0)), steps.x)
     down = total(*near(2), widened(half_down, own, half))
-    steps.after(down[:1, :8])
     ends = moved(up, FIRST_UP, back=True), moved(down, FIRST_DOWN, back=True)
     return total(*near(0), *ends)
 

time: 183 us -> 179 us (0.978); the launches traced: 183 us -> 177 us
  waiting for transfers between devices: 51.6 us -> 47.7 us
  starting transfers between devices: 61.7 us -> 64.6 us
  other arithmetic: 27 us -> 24.4 us
  Pallas kernels: 30.1 us -> 28 us
    ppermute x16, waiting for transfers between devices: 19.4 us -> 15.7 us  [moved(): return lax.ppermute(x, ('rows', 'rep'), pairs)]
    add x3 -> x2, other arithmetic: 3.2 us -> 0.69 us  [go(): rounded + lax.ppermute(rounded.astype(bf16), axis, pairs).astype(f32)]
    pallas_call x1, Pallas kernels: 30.1 us -> 28 us  [layer(): pl.pallas_call(functools.partial(kernel, len(parts), 2 * len(groups)), in...]
    ppermute x11, starting transfers between devices: 28 us -> 30.1 us  [from_core(): lax.ppermute(x, 'rep', [(i, i ^ 1) for i in range(lax.axis_size('rep'))])]
  transfers between devices with their start and end apart: 33 -> 33, of which waited for: 15 -> 14; matrix products, arithmetic and copies ran while one was open for 13% -> 15% of each run, Pallas kernels for 0% -> 0%
where the time goes in v9:
time: 179 us; the launch traced here: 177 us
  starting transfers between devices  64.6 us (36%)
  waiting for transfers between devices  47.7 us (27%)
  Pallas kernels  28 us (16%)
  other arithmetic  24.4 us (14%)
  local copies, waits for them, and re-layouts  11.5 us (6%)
    ppermute x11, starting transfers between devices, from_core(): lax.ppermute(x, 'rep', [(i, i ^ 1) for i in range(lax.axis_size('rep'))])  30.1 us
    ppermute x16, starting transfers between devices, moved(): return lax.ppermute(x, ('rows', 'rep'), pairs)  29.3 us
    pallas_call x1, Pallas kernels, layer(): pl.pallas_call(functools.partial(kernel, len(parts), 2 * len(groups)), in...  28 us
    ppermute x6, waiting for transfers between devices, go(): lax.ppermute(rounded.astype(bf16), axis, pairs).astype(f32)  23.7 us
    ppermute x16, waiting for transfers between devices, moved(): return lax.ppermute(x, ('rows', 'rep'), pairs)  15.7 us
    convert_element_type x4, other arithmetic, total(): return sum((x.astype(f32) for x in terms)).astype(bf16)  10.8 us
    ppermute x11, waiting for transfers between devices, from_core(): lax.ppermute(x, 'rep', [(i, i ^ 1) for i in range(lax.axis_size('rep'))])  8.31 us
    ppermute x6, starting transfers between devices, go(): lax.ppermute(rounded.astype(bf16), axis, pairs).astype(f32)  5.22 us
  transfers between devices with their start and end apart: 33, of which 14 were waited for; matrix products, arithmetic and copies ran while one was open for 15% of the time, Pallas kernels for 0%

profile of v9, /device:TPU:0, one launch (start us, length us, event | category | flops | bytes accessed | tf_op | source)
XLA Modules:
  0.0 177.1 jit_solution(2290298120116085380)
XLA Ops:
  0.6 2.1 %collective-permute-start = (bf16[1024,256]{1,0:T(8,128)(2,1)}, bf16[1024,256]{1,0:T(8,128)(2,1)S(1)}, u32[]{:S(2)}, u32[]{:S(2)}) collective-permute-start(bf16[1024,256]{1,0:T(8,128)(2,1)} %param.7), channel_id=1, source_target_pairs={{120,0},{3,1},{122,2},{5,3},{124,4},{7,5},{126,6},{1,7},{0,8},{11,... | collective-permute-start | bytes 1572872 | tf_op jit(solution)/shard_map/ppermute | solution.py:194
  2.7 4.4 %collective-permute-start.1 = (bf16[1024,256]{1,0:T(8,128)(2,1)}, bf16[1024,256]{1,0:T(8,128)(2,1)S(1)}, u32[]{:S(2)}, u32[]{:S(2)}) collective-permute-start(bf16[1024,256]{1,0:T(8,128)(2,1)} %param.7), channel_id=1, source_target_pairs={{8,0},{7,1},{10,2},{1,3},{12,4},{3,5},{14,6},{5,7},{16,8},{15,9},{... | collective-permute-start | bytes 1572872 | tf_op jit(solution)/shard_map/ppermute | solution.py:194
  7.1 1.9 %constant_dynamic-update-slice_fusion.2 = bf16[3072,256]{1,0:T(8,128)(2,1)} fusion(bf16[1024,256]{1,0:T(8,128)(2,1)} %param.7), kind=kLoop, calls=%fused_computation.30 | loop fusion | bytes 1048576
  9.0 5.4 %collective-permute-done = bf16[1024,256]{1,0:T(8,128)(2,1)S(1)} collective-permute-done((bf16[1024,256]{1,0:T(8,128)(2,1)}, bf16[1024,256]{1,0:T(8,128)(2,1)S(1)}, u32[]{:S(2)}, u32[]{:S(2)}) %collective-permute-start) | collective-permute-done | bytes 524320 | tf_op jit(solution)/shard_map/ppermute | solution.py:194
  22.4 15.5 %collective-permute-start.6 = (bf16[1024,256]{1,0:T(8,128)(2,1)}, bf16[1024,256]{1,0:T(8,128)(2,1)}, u32[]{:S(2)}, u32[]{:S(2)}) collective-permute-start(bf16[1024,256]{1,0:T(8,128)(2,1)} %get-tuple-element.35.refs_4_), channel_id=1, source_target_pairs={{0,1},{1,0},{2,3},{3,2},{4,5},{5,4},{6,7},{7,6},{8,9},{9,8},{10,11... | collective-permute-start | bytes 1572872 | tf_op jit(solution)/shard_map/ppermute | solution.py:203
  42.3 3.0 %slice_select_fusion = (bf16[1536,256]{1,0:T(8,128)(2,1)}, bf16[1536,256]{1,0:T(8,128)(2,1)}) fusion(bf16[1536,256]{1,0:T(8,128)(2,1)} %constant_dynamic-update-slice_fusion.3, bf16[3072,256]{1,0:T(8,128)(2,1)S(1)} %collective-permute-done.8.refs_3_, pred[]{:T(512)S(6)} %eq.33, bf16[3072,256]{1,0:T(8,128)(2,1)S(1)} %collective-permute-done.2.refs_2_), kind=kLoop, calls=%fused_computation.7 | loop fusion | flops 786432 | bytes 3932161 | tf_op jit(solution)/shard_map/jit(_where)/select_n | solution.py:217
  48.4 3.4 %collective-permute-start.12 = (bf16[3072,256]{1,0:T(8,128)(2,1)S(1)}, bf16[3072,256]{1,0:T(8,128)(2,1)}, u32[]{:S(2)}, u32[]{:S(2)}) collective-permute-start(bf16[3072,256]{1,0:T(8,128)(2,1)S(1)} %collective-permute-done.2.refs_2_), channel_id=1, source_target_pairs={{0,1},{1,0},{2,3},{3,2},{4,5},{5,4},{6,7},{7,6},{8,9},{9,8},{10,11... | collective-permute-start | bytes 4718600 | tf_op jit(solution)/shard_map/ppermute | solution.py:203
  51.8 5.9 %collective-permute-done.7.refs_0_ = bf16[1536,256]{1,0:T(8,128)(2,1)} collective-permute-done((bf16[1536,256]{1,0:T(8,128)(2,1)}, bf16[1536,256]{1,0:T(8,128)(2,1)}, u32[]{:S(2)}, u32[]{:S(2)}) %collective-permute-start.7) | collective-permute-done | bytes 786464 | tf_op jit(solution)/shard_map/ppermute | solution.py:194
  57.7 3.5 %collective-permute-start.10 = (bf16[1536,256]{1,0:T(8,128)(2,1)}, bf16[1536,256]{1,0:T(8,128)(2,1)}, u32[]{:S(2)}, u32[]{:S(2)}) collective-permute-start(bf16[1536,256]{1,0:T(8,128)(2,1)} %collective-permute-done.7.refs_0_), channel_id=1, source_target_pairs={{0,1},{1,0},{2,3},{3,2},{4,5},{5,4},{6,7},{7,6},{8,9},{9,8},{10,11... | collective-permute-start | bytes 2359304 | tf_op jit(solution)/shard_map/ppermute | solution.py:203
  64.6 28.0 %shard_map.95 = (bf16[1024,256]{1,0:T(8,128)(2,1)}, f32[256,256]{1,0:T(8,128)}, bf16[24,256,128]{2,1,0:T(8,128)(2,1)}, bf16[48,256,128]{2,1,0:T(8,128)(2,1)}, bf...) custom-call(s32[8,48]{1,0:T(8,128)} %fusion.5.idx, ...), custom_call_target="tpu_custom_call" | custom-call | flops 6442450944 | bytes 37748736 | tf_op jit(solution)/shard_map/pallas_call | solution.py:141
  93.1 3.2 %collective-permute-done.14 = bf16[24,256,128]{2,1,0:T(8,128)(2,1)S(1)} collective-permute-done((bf16[24,256,128]{2,1,0:T(8,128)(2,1)}, bf16[24,256,128]{2,1,0:T(8,128)(2,1)S(1)}, u32[]{:S(2)}, u32[]{:S(2)}) %collective-permute-start.14) | collective-permute-done | bytes 1572896 | tf_op jit(solution)/shard_map/ppermute | solution.py:203
  96.3 1.9 %add_convert_fusion.2 = bf16[24,256,128]{2,1,0:T(8,128)(2,1)S(1)} fusion(bf16[24,256,128]{2,1,0:T(8,128)(2,1)S(1)} %collective-permute-done.14, bf16[24,256,128]{2,1,0:T(8,128)(2,1)} %get-tuple-element.14), kind=kLoop, calls=%fused_computation.2 | loop fusion | flops 3145728 | bytes 4718592 | tf_op jit(solution)/shard_map/convert_element_type | solution.py:258
  99.5 3.7 %collective-permute-start.17 = (bf16[12,256,128]{2,1,0:T(8,128)(2,1)S(1)}, bf16[12,256,128]{2,1,0:T(8,128)(2,1)S(1)}, u32[]{:S(2)}, u32[]{:S(2)}) collective-permute-start(bf16[12,256,128]{2,1,0:T(8,128)(2,1)S(1)} %get-tuple-element.29), channel_id=1, source_target_pairs={{0,2},{1,121},{2,4},{3,123},{4,6},{5,125},{6,0},{7,127},{8,10},{9,... | collective-permute-start | bytes 2359304 | tf_op jit(solution)/shard_map/ppermute | solution.py:194
  103.2 4.6 %collective-permute-start.21 = (bf16[12,256,128]{2,1,0:T(8,128)(2,1)S(1)}, bf16[12,256,128]{2,1,0:T(8,128)(2,1)S(1)}, u32[]{:S(2)}, u32[]{:S(2)}) collective-permute-start(bf16[12,256,128]{2,1,0:T(8,128)(2,1)S(1)} %get-tuple-element.30), channel_id=1, source_target_pairs={{0,6},{1,9},{2,0},{3,11},{4,2},{5,13},{6,4},{7,15},{8,14},{9,17},{... | collective-permute-start | bytes 2359304 | tf_op jit(solution)/shard_map/ppermute | solution.py:194
  111.6 7.6 %collective-permute-done.19 = bf16[128,256]{1,0:T(8,128)(2,1)S(1)} collective-permute-done((bf16[128,256]{1,0:T(8,128)(2,1)S(1)}, bf16[128,256]{1,0:T(8,128)(2,1)S(1)}, u32[]{:S(2)}, u32[]{:S(2)}) %collective-permute-start.19) | collective-permute-done | bytes 65568 | tf_op jit(solution)/shard_map/ppermute | solution.py:244
  119.9 4.0 %collective-permute-start.24 = (bf16[128,256]{1,0:T(8,128)(2,1)S(1)}, bf16[128,256]{1,0:T(8,128)(2,1)S(1)}, u32[]{:S(2)}, u32[]{:S(2)}) collective-permute-start(bf16[128,256]{1,0:T(8,128)(2,1)S(1)} %get-tuple-element.21), channel_id=1, source_target_pairs={{0,4},{1,5},{2,6},{3,7},{4,0},{5,1},{6,2},{7,3},{8,12},{9,13},{10,... | collective-permute-start | bytes 196616 | tf_op jit(solution)/shard_map/ppermute | solution.py:244
  125.5 4.0 %add_convert_fusion.1 = (bf16[24,256,128]{2,1,0:T(8,128)(2,1)}, bf16[24,256,128]{2,1,0:T(8,128)(2,1)}) fusion(bf16[48,256,128]{2,1,0:T(8,128)(2,1)} %collective-permute-done.16, bf16[12,256,128]{2,1,0:T(8,128)(2,1)S(1)} %collective-permute-done.17, bf16[48,256,128]{2,1,0:T(8,128)(2,1)S(1)} %copy-done.2, pred[]{:T(512)S(6)} %eq.33, ...), kind=kLoop, calls=%fused_computation.1 | loop fusion | flops 11010048 | bytes 11010049 | tf_op jit(solution)/shard_map/convert_element_type | solution.py:258
  129.6 3.2 %collective-permute-start.22 = (bf16[24,256,128]{2,1,0:T(8,128)(2,1)}, bf16[24,256,128]{2,1,0:T(8,128)(2,1)}, u32[]{:S(2)}, u32[]{:S(2)}) collective-permute-start(bf16[24,256,128]{2,1,0:T(8,128)(2,1)} %get-tuple-element.28), channel_id=1, source_target_pairs={{0,6},{1,9},{2,0},{3,11},{4,2},{5,13},{6,4},{7,15},{8,14},{9,17},{... | collective-permute-start | bytes 4718600 | tf_op jit(solution)/shard_map/ppermute | solution.py:194
  137.3 5.0 %collective-permute-done.26 = bf16[128,256]{1,0:T(8,128)(2,1)S(1)} collective-permute-done((bf16[128,256]{1,0:T(8,128)(2,1)S(1)}, bf16[128,256]{1,0:T(8,128)(2,1)S(1)}, u32[]{:S(2)}, u32[]{:S(2)}) %collective-permute-start.26) | collective-permute-done | bytes 65568 | tf_op jit(solution)/shard_map/ppermute | solution.py:244
  143.3 6.5 %collective-permute-done.27 = bf16[128,256]{1,0:T(8,128)(2,1)S(1)} collective-permute-done((bf16[128,256]{1,0:T(8,128)(2,1)S(1)}, bf16[128,256]{1,0:T(8,128)(2,1)S(1)}, u32[]{:S(2)}, u32[]{:S(2)}) %collective-permute-start.27) | collective-permute-done | bytes 65568 | tf_op jit(solution)/shard_map/ppermute | solution.py:244
  150.8 4.3 %collective-permute-done.28 = bf16[128,256]{1,0:T(8,128)(2,1)S(1)} collective-permute-done((bf16[128,256]{1,0:T(8,128)(2,1)S(1)}, bf16[128,256]{1,0:T(8,128)(2,1)S(1)}, u32[]{:S(2)}, u32[]{:S(2)}) %collective-permute-start.28) | collective-permute-done | bytes 65568 | tf_op jit(solution)/shard_map/ppermute | solution.py:244
  156.7 3.4 %add_convert_fusion.5 = (bf16[8,256,128]{2,1,0:T(8,128)(2,1)}, bf16[8,256,128]{2,1,0:T(8,128)(2,1)S(1)}) fusion(bf16[24,256,128]{2,1,0:T(8,128)(2,1)} %collective-permute-done.22, bf16[24,256,128]{2,1,0:T(8,128)(2,1)} %collective-permute-done.20, bf16[32,256,128]{2,1,0:T(8,128)(2,1)} %collective-permute-done.15, ...), kind=kLoop, calls=%fused_computation.5 | loop fusion | flops 5242880 | bytes 5767168 | tf_op jit(solution)/shard_map/convert_element_type | solution.py:258
  162.5 5.7 %collective-permute-start.32 = (f32[128,256]{1,0:T(8,128)S(1)}, f32[128,256]{1,0:T(8,128)S(1)}, u32[]{:S(2)}, u32[]{:S(2)}) collective-permute-start(f32[128,256]{1,0:T(8,128)S(1)} %convert_add_fusion), channel_id=1, source_target_pairs={{0,1},{1,0},{2,3},{3,2},{4,5},{5,4},{6,7},{7,6},{8,9},{9,8},{10,11... | collective-permute-start | bytes 393224 | tf_op jit(solution)/shard_map/ppermute | solution.py:203
  169.9 4.5 %collective-permute-done.30 = bf16[8,256,128]{2,1,0:T(8,128)(2,1)S(1)} collective-permute-done((bf16[8,256,128]{2,1,0:T(8,128)(2,1)S(1)}, bf16[8,256,128]{2,1,0:T(8,128)(2,1)S(1)}, u32[]{:S(2)}, u32[]{:S(2)}) %collective-permute-start.30) | collective-permute-done | bytes 524320 | tf_op jit(solution)/shard_map/ppermute | solution.py:194
  (106 shorter events, 41.6 us)
Async XLA Ops:
  0.6 13.8 %collective-permute-start = (bf16[1024,256]{1,0:T(8,128)(2,1)}, bf16[1024,256]{1,0:T(8,128)(2,1)S(1)}, u32[]{:S(2)}, u32[]{:S(2)}) collective-permute-start(bf16[1024,256]{1,0:T(8,128)(2,1)} %param.7), channel_id=1, source_target_pairs={{120,0},{3,1},{122,2},{5,3},{124,4},{7,5},{126,6},{1,7},{0,8},{11,... | collective-permute-start | bytes 1572872 | tf_op jit(solution)/shard_map/ppermute | solution.py:194
  2.7 12.5 %collective-permute-start.1 = (bf16[1024,256]{1,0:T(8,128)(2,1)}, bf16[1024,256]{1,0:T(8,128)(2,1)S(1)}, u32[]{:S(2)}, u32[]{:S(2)}) collective-permute-start(bf16[1024,256]{1,0:T(8,128)(2,1)} %param.7), channel_id=1, source_target_pairs={{8,0},{7,1},{10,2},{1,3},{12,4},{3,5},{14,6},{5,7},{16,8},{15,9},{... | collective-permute-start | bytes 1572872 | tf_op jit(solution)/shard_map/ppermute | solution.py:194
  16.1 25.0 %collective-permute-start.5 = (bf16[3072,256]{1,0:T(8,128)(2,1)}, bf16[3072,256]{1,0:T(8,128)(2,1)}, u32[]{:S(2)}, u32[]{:S(2)}) collective-permute-start(bf16[3072,256]{1,0:T(8,128)(2,1)} %constant_dynamic-update-slice_fusion.refs_5_), channel_id=1, source_target_pairs={{0,1},{1,0},{2,3},{3,2},{4,5},{5,4},{6,7},{7,6},{8,9},{9,8},{10,11... | collective-permute-start | bytes 4718600 | tf_op jit(solution)/shard_map/ppermute | solution.py:203
  16.1 26.2 %collective-permute-start.8 = (bf16[3072,256]{1,0:T(8,128)(2,1)}, bf16[3072,256]{1,0:T(8,128)(2,1)S(1)}, u32[]{:S(2)}, u32[]{:S(2)}) collective-permute-start(bf16[3072,256]{1,0:T(8,128)(2,1)} %constant_dynamic-update-slice_fusion.refs_5_), channel_id=1, source_target_pairs={{6,0},{9,1},{0,2},{11,3},{2,4},{13,5},{4,6},{15,7},{14,8},{17,9},{... | collective-permute-start | bytes 4718600 | tf_op jit(solution)/shard_map/ppermute | solution.py:194
  17.7 24.7 %collective-permute-start.2 = (bf16[3072,256]{1,0:T(8,128)(2,1)}, bf16[3072,256]{1,0:T(8,128)(2,1)S(1)}, u32[]{:S(2)}, u32[]{:S(2)}) collective-permute-start(bf16[3072,256]{1,0:T(8,128)(2,1)} %constant_dynamic-update-slice_fusion.refs_5_), channel_id=1, source_target_pairs={{2,0},{121,1},{4,2},{123,3},{6,4},{125,5},{0,6},{127,7},{10,8},{1,... | collective-permute-start | bytes 4718600 | tf_op jit(solution)/shard_map/ppermute | solution.py:194
  22.4 17.4 %collective-permute-start.6 = (bf16[1024,256]{1,0:T(8,128)(2,1)}, bf16[1024,256]{1,0:T(8,128)(2,1)}, u32[]{:S(2)}, u32[]{:S(2)}) collective-permute-start(bf16[1024,256]{1,0:T(8,128)(2,1)} %get-tuple-element.35.refs_4_), channel_id=1, source_target_pairs={{0,1},{1,0},{2,3},{3,2},{4,5},{5,4},{6,7},{7,6},{8,9},{9,8},{10,11... | collective-permute-start | bytes 1572872 | tf_op jit(solution)/shard_map/ppermute | solution.py:203
  45.4 12.4 %collective-permute-start.7 = (bf16[1536,256]{1,0:T(8,128)(2,1)}, bf16[1536,256]{1,0:T(8,128)(2,1)}, u32[]{:S(2)}, u32[]{:S(2)}) collective-permute-start(bf16[1536,256]{1,0:T(8,128)(2,1)} %shard_map.94), channel_id=1, source_target_pairs={{2,0},{121,1},{4,2},{123,3},{6,4},{125,5},{0,6},{127,7},{10,8},{1,... | collective-permute-start | bytes 2359304 | tf_op jit(solution)/shard_map/ppermute | solution.py:194
  47.0 15.9 %collective-permute-start.13 = (bf16[3072,256]{1,0:T(8,128)(2,1)S(1)}, bf16[3072,256]{1,0:T(8,128)(2,1)}, u32[]{:S(2)}, u32[]{:S(2)}) collective-permute-start(bf16[3072,256]{1,0:T(8,128)(2,1)S(1)} %collective-permute-done.8.refs_3_), channel_id=1, source_target_pairs={{0,1},{1,0},{2,3},{3,2},{4,5},{5,4},{6,7},{7,6},{8,9},{9,8},{10,11... | collective-permute-start | bytes 4718600 | tf_op jit(solution)/shard_map/ppermute | solution.py:203
  47.0 14.2 %collective-permute-start.9 = (bf16[1536,256]{1,0:T(8,128)(2,1)}, bf16[1536,256]{1,0:T(8,128)(2,1)}, u32[]{:S(2)}, u32[]{:S(2)}) collective-permute-start(bf16[1536,256]{1,0:T(8,128)(2,1)} %get-tuple-element.31), channel_id=1, source_target_pairs={{6,0},{9,1},{0,2},{11,3},{2,4},{13,5},{4,6},{15,7},{14,8},{17,9},{... | collective-permute-start | bytes 2359304 | tf_op jit(solution)/shard_map/ppermute | solution.py:194
  48.4 16.2 %collective-permute-start.12 = (bf16[3072,256]{1,0:T(8,128)(2,1)S(1)}, bf16[3072,256]{1,0:T(8,128)(2,1)}, u32[]{:S(2)}, u32[]{:S(2)}) collective-permute-start(bf16[3072,256]{1,0:T(8,128)(2,1)S(1)} %collective-permute-done.2.refs_2_), channel_id=1, source_target_pairs={{0,1},{1,0},{2,3},{3,2},{4,5},{5,4},{6,7},{7,6},{8,9},{9,8},{10,11... | collective-permute-start | bytes 4718600 | tf_op jit(solution)/shard_map/ppermute | solution.py:203
  57.7 5.7 %collective-permute-start.10 = (bf16[1536,256]{1,0:T(8,128)(2,1)}, bf16[1536,256]{1,0:T(8,128)(2,1)}, u32[]{:S(2)}, u32[]{:S(2)}) collective-permute-start(bf16[1536,256]{1,0:T(8,128)(2,1)} %collective-permute-done.7.refs_0_), channel_id=1, source_target_pairs={{0,1},{1,0},{2,3},{3,2},{4,5},{5,4},{6,7},{7,6},{8,9},{9,8},{10,11... | collective-permute-start | bytes 2359304 | tf_op jit(solution)/shard_map/ppermute | solution.py:203
  98.8 26.7 %collective-permute-start.16 = (bf16[48,256,128]{2,1,0:T(8,128)(2,1)}, bf16[48,256,128]{2,1,0:T(8,128)(2,1)}, u32[]{:S(2)}, u32[]{:S(2)}) collective-permute-start(bf16[48,256,128]{2,1,0:T(8,128)(2,1)} %shard_map.97), channel_id=1, source_target_pairs={{0,1},{1,0},{2,3},{3,2},{4,5},{5,4},{6,7},{7,6},{8,9},{9,8},{10,11... | collective-permute-start | bytes 9437192 | tf_op jit(solution)/shard_map/ppermute | solution.py:203
  99.2 24.8 %collective-permute-start.15 = (bf16[32,256,128]{2,1,0:T(8,128)(2,1)}, bf16[32,256,128]{2,1,0:T(8,128)(2,1)}, u32[]{:S(2)}, u32[]{:S(2)}) collective-permute-start(bf16[32,256,128]{2,1,0:T(8,128)(2,1)} %shard_map.96), channel_id=1, source_target_pairs={{0,1},{1,0},{2,3},{3,2},{4,5},{5,4},{6,7},{7,6},{8,9},{9,8},{10,11... | collective-permute-start | bytes 6291464 | tf_op jit(solution)/shard_map/ppermute | solution.py:203
  99.5 24.5 %collective-permute-start.17 = (bf16[12,256,128]{2,1,0:T(8,128)(2,1)S(1)}, bf16[12,256,128]{2,1,0:T(8,128)(2,1)S(1)}, u32[]{:S(2)}, u32[]{:S(2)}) collective-permute-start(bf16[12,256,128]{2,1,0:T(8,128)(2,1)S(1)} %get-tuple-element.29), channel_id=1, source_target_pairs={{0,2},{1,121},{2,4},{3,123},{4,6},{5,125},{6,0},{7,127},{8,10},{9,... | collective-permute-start | bytes 2359304 | tf_op jit(solution)/shard_map/ppermute | solution.py:194
  103.2 20.8 %collective-permute-start.21 = (bf16[12,256,128]{2,1,0:T(8,128)(2,1)S(1)}, bf16[12,256,128]{2,1,0:T(8,128)(2,1)S(1)}, u32[]{:S(2)}, u32[]{:S(2)}) collective-permute-start(bf16[12,256,128]{2,1,0:T(8,128)(2,1)S(1)} %get-tuple-element.30), channel_id=1, source_target_pairs={{0,6},{1,9},{2,0},{3,11},{4,2},{5,13},{6,4},{7,15},{8,14},{9,17},{... | collective-permute-start | bytes 2359304 | tf_op jit(solution)/shard_map/ppermute | solution.py:194
  110.7 8.5 %collective-permute-start.19 = (bf16[128,256]{1,0:T(8,128)(2,1)S(1)}, bf16[128,256]{1,0:T(8,128)(2,1)S(1)}, u32[]{:S(2)}, u32[]{:S(2)}) collective-permute-start(bf16[128,256]{1,0:T(8,128)(2,1)S(1)} %get-tuple-element.23), channel_id=1, source_target_pairs={{0,2},{1,3},{2,0},{3,1},{4,6},{5,7},{6,4},{7,5},{8,10},{9,11},{10,... | collective-permute-start | bytes 196616 | tf_op jit(solution)/shard_map/ppermute | solution.py:244
  119.9 14.5 %collective-permute-start.24 = (bf16[128,256]{1,0:T(8,128)(2,1)S(1)}, bf16[128,256]{1,0:T(8,128)(2,1)S(1)}, u32[]{:S(2)}, u32[]{:S(2)}) collective-permute-start(bf16[128,256]{1,0:T(8,128)(2,1)S(1)} %get-tuple-element.21), channel_id=1, source_target_pairs={{0,4},{1,5},{2,6},{3,7},{4,0},{5,1},{6,2},{7,3},{8,12},{9,13},{10,... | collective-permute-start | bytes 196616 | tf_op jit(solution)/shard_map/ppermute | solution.py:244
  129.5 27.2 %collective-permute-start.20 = (bf16[24,256,128]{2,1,0:T(8,128)(2,1)}, bf16[24,256,128]{2,1,0:T(8,128)(2,1)}, u32[]{:S(2)}, u32[]{:S(2)}) collective-permute-start(bf16[24,256,128]{2,1,0:T(8,128)(2,1)} %shard_map.99), channel_id=1, source_target_pairs={{0,2},{1,121},{2,4},{3,123},{4,6},{5,125},{6,0},{7,127},{8,10},{9,... | collective-permute-start | bytes 4718600 | tf_op jit(solution)/shard_map/ppermute | solution.py:194
  129.6 27.1 %collective-permute-start.22 = (bf16[24,256,128]{2,1,0:T(8,128)(2,1)}, bf16[24,256,128]{2,1,0:T(8,128)(2,1)}, u32[]{:S(2)}, u32[]{:S(2)}) collective-permute-start(bf16[24,256,128]{2,1,0:T(8,128)(2,1)} %get-tuple-element.28), channel_id=1, source_target_pairs={{0,6},{1,9},{2,0},{3,11},{4,2},{5,13},{6,4},{7,15},{8,14},{9,17},{... | collective-permute-start | bytes 4718600 | tf_op jit(solution)/shard_map/ppermute | solution.py:194
  143.2 6.6 %collective-permute-start.27 = (bf16[128,256]{1,0:T(8,128)(2,1)S(1)}, bf16[128,256]{1,0:T(8,128)(2,1)S(1)}, u32[]{:S(2)}, u32[]{:S(2)}) collective-permute-start(bf16[128,256]{1,0:T(8,128)(2,1)S(1)} %fusion.2), channel_id=1, source_target_pairs={{0,16},{8,24},{16,0},{24,8},{32,48},{40,56},{48,32},{56,40},{64,80... | collective-permute-start | bytes 196616 | tf_op jit(solution)/shard_map/ppermute | solution.py:244
  156.7 5.8 %collective-permute-start.31 = (bf16[128,256]{1,0:T(8,128)(2,1)S(1)}, bf16[128,256]{1,0:T(8,128)(2,1)S(1)}, u32[]{:S(2)}, u32[]{:S(2)}) collective-permute-start(bf16[128,256]{1,0:T(8,128)(2,1)S(1)} %get-tuple-element.19), channel_id=1, source_target_pairs={{0,64},{8,72},{16,80},{24,88},{32,96},{40,104},{48,112},{56,120},{... | collective-permute-start | bytes 196616 | tf_op jit(solution)/shard_map/ppermute | solution.py:244
  160.1 9.8 %collective-permute-start.29 = (bf16[8,256,128]{2,1,0:T(8,128)(2,1)}, bf16[8,256,128]{2,1,0:T(8,128)(2,1)S(1)}, u32[]{:S(2)}, u32[]{:S(2)}) collective-permute-start(bf16[8,256,128]{2,1,0:T(8,128)(2,1)} %shard_map.101), channel_id=1, source_target_pairs={{0,120},{1,3},{2,122},{3,5},{4,124},{5,7},{6,126},{7,1},{8,0},{9,1... | collective-permute-start | bytes 1572872 | tf_op jit(solution)/shard_map/ppermute | solution.py:194
  161.8 12.5 %collective-permute-start.30 = (bf16[8,256,128]{2,1,0:T(8,128)(2,1)S(1)}, bf16[8,256,128]{2,1,0:T(8,128)(2,1)S(1)}, u32[]{:S(2)}, u32[]{:S(2)}) collective-permute-start(bf16[8,256,128]{2,1,0:T(8,128)(2,1)S(1)} %get-tuple-element.26), channel_id=1, source_target_pairs={{0,8},{1,7},{2,10},{3,1},{4,12},{5,3},{6,14},{7,5},{8,16},{9,15},{... | collective-permute-start | bytes 1572872 | tf_op jit(solution)/shard_map/ppermute | solution.py:194
  162.5 6.7 %collective-permute-start.32 = (f32[128,256]{1,0:T(8,128)S(1)}, f32[128,256]{1,0:T(8,128)S(1)}, u32[]{:S(2)}, u32[]{:S(2)}) collective-permute-start(f32[128,256]{1,0:T(8,128)S(1)} %convert_add_fusion), channel_id=1, source_target_pairs={{0,1},{1,0},{2,3},{3,2},{4,5},{5,4},{6,7},{7,6},{8,9},{9,8},{10,11... | collective-permute-start | bytes 393224 | tf_op jit(solution)/shard_map/ppermute | solution.py:203
  (19 other events, 147.3 us)

commit v10 on v8

--- a/solution.py
+++ b/solution.py
@@ -10,7 +10,7 @@
 
 bf16, f32 = jnp.bfloat16, jnp.float32
 
-FWD_SLOTS = 24
+FWD_SLOTS = 48
 BWD_SLOTS = 24
 STAGES = 8
 CHUNK = 8
@@ -225,7 +225,8 @@
     def __init__(self, term, core):
         height = term.shape[0] // 2
         low, high = term[:height], term[height:]
-        self.mine, self.other = jnp.where(core == 0, low, high), jnp.where(core == 0, high, low)
+        self.mine = jnp.where(core == 0, low, high)
+        self.got = from_core(jnp.where(core == 0, high, low))
         self.core = core
         self.left = [
             (axis, bit)
@@ -235,7 +236,7 @@
         ]
 
     def begin(self, *earlier):
-        self.x = self.mine + from_core(tied(self.other, *earlier))
+        self.x = self.mine + tied(self.got, *earlier)
 
     def go(self, count):
         for axis, bit in self.left[:count]:
@@ -285,7 +286,7 @@
     far = total(mine[2][:own], first[:own], *far)
     half_up = moved(far[:half], HALF_UP, back=True)
     half_down = moved(far[half:], HALF_DOWN, back=True)
-    steps.go(1)
+    steps.go(2)
     steps.after(half_up[:1, :8], half_down[:1, :8])
     steps.go(2)
 
@@ -295,7 +296,6 @@
 
     up = tied(total(*near(1), widened(half_up, own, 0)), steps.x)
     down = total(*near(2), widened(half_down, own, half))
-    steps.after(down[:1, :8])
     ends = moved(up, FIRST_UP, back=True), moved(down, FIRST_DOWN, back=True)
     return total(*near(0), *ends)
 

time: 183 us -> 179 us (0.978)
  starting transfers between devices: 61.7 us -> 58.9 us
  other arithmetic: 27 us -> 24.5 us
    ppermute x11, starting transfers between devices: 28 us -> 24.3 us  [from_core(): lax.ppermute(x, 'rep', [(i, i ^ 1) for i in range(lax.axis_size('rep'))])]
    ppermute x16, waiting for transfers between devices: 19.4 us -> 23.1 us  [moved(): return lax.ppermute(x, ('rows', 'rep'), pairs)]
    add x3 -> x2, other arithmetic: 3.2 us -> 0.7 us  [go(): rounded + lax.ppermute(rounded.astype(bf16), axis, pairs).astype(f32)]
    ppermute x6, starting transfers between devices: 4.09 us -> 6.3 us  [go(): lax.ppermute(rounded.astype(bf16), axis, pairs).astype(f32)]
    ppermute x6, waiting for transfers between devices: 23.5 us -> 21.5 us  [go(): lax.ppermute(rounded.astype(bf16), axis, pairs).astype(f32)]
    unnamed x19 -> x25, local copies, waits for them, and re-layouts: 3.63 us -> 5.11 us
  transfers between devices with their start and end apart: 33 -> 33, of which waited for: 15 -> 15; matrix products, arithmetic and copies ran while one was open for 13% -> 15% of each run, Pallas kernels for 0% -> 0%
where the time goes in v10:
time: 179 us; the launch traced here: 178 us
  starting transfers between devices  58.9 us (33%)
  waiting for transfers between devices  51.8 us (29%)
  Pallas kernels  29.3 us (16%)
  other arithmetic  24.5 us (14%)
  local copies, waits for them, and re-layouts  12.9 us (7%)
    pallas_call x1, Pallas kernels, layer(): pl.pallas_call(functools.partial(kernel, len(parts), 2 * len(groups)), in...  29.3 us
    ppermute x16, starting transfers between devices, moved(): return lax.ppermute(x, ('rows', 'rep'), pairs)  28.3 us
    ppermute x11, starting transfers between devices, from_core(): lax.ppermute(x, 'rep', [(i, i ^ 1) for i in range(lax.axis_size('rep'))])  24.3 us
    ppermute x16, waiting for transfers between devices, moved(): return lax.ppermute(x, ('rows', 'rep'), pairs)  23.1 us
    ppermute x6, waiting for transfers between devices, go(): lax.ppermute(rounded.astype(bf16), axis, pairs).astype(f32)  21.5 us
    convert_element_type x4, other arithmetic, total(): return sum((x.astype(f32) for x in terms)).astype(bf16)  11.6 us
    ppermute x11, waiting for transfers between devices, from_core(): lax.ppermute(x, 'rep', [(i, i ^ 1) for i in range(lax.axis_size('rep'))])  7.15 us
    ppermute x6, starting transfers between devices, go(): lax.ppermute(rounded.astype(bf16), axis, pairs).astype(f32)  6.3 us
  transfers between devices with their start and end apart: 33, of which 15 were waited for; matrix products, arithmetic and copies ran while one was open for 15% of the time, Pallas kernels for 0%

profile of v10, /device:TPU:0, one launch (start us, length us, event | category | flops | bytes accessed | tf_op | source)
XLA Modules:
  0.0 178.3 jit_solution(10619956187802089709)
XLA Ops:
  0.6 2.1 %collective-permute-start = (bf16[1024,256]{1,0:T(8,128)(2,1)}, bf16[1024,256]{1,0:T(8,128)(2,1)S(1)}, u32[]{:S(2)}, u32[]{:S(2)}) collective-permute-start(bf16[1024,256]{1,0:T(8,128)(2,1)} %param.7), channel_id=1, source_target_pairs={{120,0},{3,1},{122,2},{5,3},{124,4},{7,5},{126,6},{1,7},{0,8},{11,... | collective-permute-start | bytes 1572872 | tf_op jit(solution)/shard_map/ppermute | solution.py:194
  2.7 4.4 %collective-permute-start.1 = (bf16[1024,256]{1,0:T(8,128)(2,1)}, bf16[1024,256]{1,0:T(8,128)(2,1)S(1)}, u32[]{:S(2)}, u32[]{:S(2)}) collective-permute-start(bf16[1024,256]{1,0:T(8,128)(2,1)} %param.7), channel_id=1, source_target_pairs={{8,0},{7,1},{10,2},{1,3},{12,4},{3,5},{14,6},{5,7},{16,8},{15,9},{... | collective-permute-start | bytes 1572872 | tf_op jit(solution)/shard_map/ppermute | solution.py:194
  7.1 1.9 %constant_dynamic-update-slice_fusion.2 = bf16[3072,256]{1,0:T(8,128)(2,1)} fusion(bf16[1024,256]{1,0:T(8,128)(2,1)} %param.7), kind=kLoop, calls=%fused_computation.30 | loop fusion | bytes 1048576
  9.0 5.3 %collective-permute-done = bf16[1024,256]{1,0:T(8,128)(2,1)S(1)} collective-permute-done((bf16[1024,256]{1,0:T(8,128)(2,1)}, bf16[1024,256]{1,0:T(8,128)(2,1)S(1)}, u32[]{:S(2)}, u32[]{:S(2)}) %collective-permute-start) | collective-permute-done | bytes 524320 | tf_op jit(solution)/shard_map/ppermute | solution.py:194
  22.4 15.5 %collective-permute-start.6 = (bf16[1024,256]{1,0:T(8,128)(2,1)}, bf16[1024,256]{1,0:T(8,128)(2,1)}, u32[]{:S(2)}, u32[]{:S(2)}) collective-permute-start(bf16[1024,256]{1,0:T(8,128)(2,1)} %get-tuple-element.35.refs_4_), channel_id=1, source_target_pairs={{0,1},{1,0},{2,3},{3,2},{4,5},{5,4},{6,7},{7,6},{8,9},{9,8},{10,11... | collective-permute-start | bytes 1572872 | tf_op jit(solution)/shard_map/ppermute | solution.py:203
  42.3 3.0 %slice_select_fusion = (bf16[1536,256]{1,0:T(8,128)(2,1)}, bf16[1536,256]{1,0:T(8,128)(2,1)}) fusion(bf16[1536,256]{1,0:T(8,128)(2,1)} %constant_dynamic-update-slice_fusion.3, bf16[3072,256]{1,0:T(8,128)(2,1)S(1)} %collective-permute-done.8.refs_3_, pred[]{:T(512)S(6)} %eq.33, bf16[3072,256]{1,0:T(8,128)(2,1)S(1)} %collective-permute-done.2.refs_2_), kind=kLoop, calls=%fused_computation.7 | loop fusion | flops 786432 | bytes 3932161 | tf_op jit(solution)/shard_map/jit(_where)/select_n | solution.py:217
  48.4 3.4 %collective-permute-start.12 = (bf16[3072,256]{1,0:T(8,128)(2,1)S(1)}, bf16[3072,256]{1,0:T(8,128)(2,1)}, u32[]{:S(2)}, u32[]{:S(2)}) collective-permute-start(bf16[3072,256]{1,0:T(8,128)(2,1)S(1)} %collective-permute-done.2.refs_2_), channel_id=1, source_target_pairs={{0,1},{1,0},{2,3},{3,2},{4,5},{5,4},{6,7},{7,6},{8,9},{9,8},{10,11... | collective-permute-start | bytes 4718600 | tf_op jit(solution)/shard_map/ppermute | solution.py:203
  51.8 5.9 %collective-permute-done.7.refs_0_ = bf16[1536,256]{1,0:T(8,128)(2,1)} collective-permute-done((bf16[1536,256]{1,0:T(8,128)(2,1)}, bf16[1536,256]{1,0:T(8,128)(2,1)}, u32[]{:S(2)}, u32[]{:S(2)}) %collective-permute-start.7) | collective-permute-done | bytes 786464 | tf_op jit(solution)/shard_map/ppermute | solution.py:194
  57.7 3.5 %collective-permute-start.10 = (bf16[1536,256]{1,0:T(8,128)(2,1)}, bf16[1536,256]{1,0:T(8,128)(2,1)}, u32[]{:S(2)}, u32[]{:S(2)}) collective-permute-start(bf16[1536,256]{1,0:T(8,128)(2,1)} %collective-permute-done.7.refs_0_), channel_id=1, source_target_pairs={{0,1},{1,0},{2,3},{3,2},{4,5},{5,4},{6,7},{7,6},{8,9},{9,8},{10,11... | collective-permute-start | bytes 2359304 | tf_op jit(solution)/shard_map/ppermute | solution.py:203
  64.6 29.3 %shard_map.95 = (bf16[1024,256]{1,0:T(8,128)(2,1)}, f32[256,256]{1,0:T(8,128)}, bf16[24,256,128]{2,1,0:T(8,128)(2,1)}, bf16[48,256,128]{2,1,0:T(8,128)(2,1)}, bf...) custom-call(s32[8,48]{1,0:T(8,128)} %fusion.5.idx, ...), custom_call_target="tpu_custom_call" | custom-call | flops 6442450944 | bytes 37748736 | tf_op jit(solution)/shard_map/pallas_call | solution.py:141
  94.4 3.2 %collective-permute-done.14 = bf16[24,256,128]{2,1,0:T(8,128)(2,1)S(1)} collective-permute-done((bf16[24,256,128]{2,1,0:T(8,128)(2,1)}, bf16[24,256,128]{2,1,0:T(8,128)(2,1)S(1)}, u32[]{:S(2)}, u32[]{:S(2)}) %collective-permute-start.14) | collective-permute-done | bytes 1572896 | tf_op jit(solution)/shard_map/ppermute | solution.py:203
  101.8 2.3 %collective-permute-start.17 = (bf16[12,256,128]{2,1,0:T(8,128)(2,1)S(1)}, bf16[12,256,128]{2,1,0:T(8,128)(2,1)S(1)}, u32[]{:S(2)}, u32[]{:S(2)}) collective-permute-start(bf16[12,256,128]{2,1,0:T(8,128)(2,1)S(1)} %get-tuple-element.29), channel_id=1, source_target_pairs={{0,2},{1,121},{2,4},{3,123},{4,6},{5,125},{6,0},{7,127},{8,10},{9,... | collective-permute-start | bytes 2359304 | tf_op jit(solution)/shard_map/ppermute | solution.py:194
  104.1 4.7 %collective-permute-start.21 = (bf16[12,256,128]{2,1,0:T(8,128)(2,1)S(1)}, bf16[12,256,128]{2,1,0:T(8,128)(2,1)S(1)}, u32[]{:S(2)}, u32[]{:S(2)}) collective-permute-start(bf16[12,256,128]{2,1,0:T(8,128)(2,1)S(1)} %get-tuple-element.30), channel_id=1, source_target_pairs={{0,6},{1,9},{2,0},{3,11},{4,2},{5,13},{6,4},{7,15},{8,14},{9,17},{... | collective-permute-start | bytes 2359304 | tf_op jit(solution)/shard_map/ppermute | solution.py:194
  110.5 7.8 %collective-permute-done.19 = bf16[128,256]{1,0:T(8,128)(2,1)S(1)} collective-permute-done((bf16[128,256]{1,0:T(8,128)(2,1)S(1)}, bf16[128,256]{1,0:T(8,128)(2,1)S(1)}, u32[]{:S(2)}, u32[]{:S(2)}) %collective-permute-start.19) | collective-permute-done | bytes 65568 | tf_op jit(solution)/shard_map/ppermute | solution.py:245
  118.4 6.0 %collective-permute-start.24 = (bf16[128,256]{1,0:T(8,128)(2,1)S(1)}, bf16[128,256]{1,0:T(8,128)(2,1)S(1)}, u32[]{:S(2)}, u32[]{:S(2)}) collective-permute-start(bf16[128,256]{1,0:T(8,128)(2,1)S(1)} %get-tuple-element.21), channel_id=1, source_target_pairs={{0,4},{1,5},{2,6},{3,7},{4,0},{5,1},{6,2},{7,3},{8,12},{9,13},{10,... | collective-permute-start | bytes 196616 | tf_op jit(solution)/shard_map/ppermute | solution.py:245
  124.4 2.2 %collective-permute-done.24 = bf16[128,256]{1,0:T(8,128)(2,1)S(1)} collective-permute-done((bf16[128,256]{1,0:T(8,128)(2,1)S(1)}, bf16[128,256]{1,0:T(8,128)(2,1)S(1)}, u32[]{:S(2)}, u32[]{:S(2)}) %collective-permute-start.24) | collective-permute-done | bytes 65568 | tf_op jit(solution)/shard_map/ppermute | solution.py:245
  127.3 4.8 %add_convert_fusion.1 = (bf16[24,256,128]{2,1,0:T(8,128)(2,1)}, bf16[24,256,128]{2,1,0:T(8,128)(2,1)}) fusion(bf16[48,256,128]{2,1,0:T(8,128)(2,1)} %collective-permute-done.16, bf16[12,256,128]{2,1,0:T(8,128)(2,1)S(1)} %collective-permute-done.17, bf16[48,256,128]{2,1,0:T(8,128)(2,1)} %get-tuple-element.16, pred[]{:T(512)S(6)} %eq.33, ...), kind=kLoop, calls=%fused_computation.1 | loop fusion | flops 11010048 | bytes 11010049 | tf_op jit(solution)/shard_map/convert_element_type | solution.py:259
  132.2 3.2 %collective-permute-start.22 = (bf16[24,256,128]{2,1,0:T(8,128)(2,1)}, bf16[24,256,128]{2,1,0:T(8,128)(2,1)}, u32[]{:S(2)}, u32[]{:S(2)}) collective-permute-start(bf16[24,256,128]{2,1,0:T(8,128)(2,1)} %get-tuple-element.28), channel_id=1, source_target_pairs={{0,6},{1,9},{2,0},{3,11},{4,2},{5,13},{6,4},{7,15},{8,14},{9,17},{... | collective-permute-start | bytes 4718600 | tf_op jit(solution)/shard_map/ppermute | solution.py:194
  141.4 7.2 %collective-permute-done.27 = bf16[128,256]{1,0:T(8,128)(2,1)S(1)} collective-permute-done((bf16[128,256]{1,0:T(8,128)(2,1)S(1)}, bf16[128,256]{1,0:T(8,128)(2,1)S(1)}, u32[]{:S(2)}, u32[]{:S(2)}) %collective-permute-start.27) | collective-permute-done | bytes 65568 | tf_op jit(solution)/shard_map/ppermute | solution.py:245
  149.7 4.3 %collective-permute-done.28 = bf16[128,256]{1,0:T(8,128)(2,1)S(1)} collective-permute-done((bf16[128,256]{1,0:T(8,128)(2,1)S(1)}, bf16[128,256]{1,0:T(8,128)(2,1)S(1)}, u32[]{:S(2)}, u32[]{:S(2)}) %collective-permute-start.28) | collective-permute-done | bytes 65568 | tf_op jit(solution)/shard_map/ppermute | solution.py:245
  157.2 3.3 %add_convert_fusion.5 = (bf16[8,256,128]{2,1,0:T(8,128)(2,1)}, bf16[8,256,128]{2,1,0:T(8,128)(2,1)S(1)}) fusion(bf16[24,256,128]{2,1,0:T(8,128)(2,1)} %collective-permute-done.22, bf16[24,256,128]{2,1,0:T(8,128)(2,1)} %collective-permute-done.20, bf16[32,256,128]{2,1,0:T(8,128)(2,1)} %collective-permute-done.15, ...), kind=kLoop, calls=%fused_computation.5 | loop fusion | flops 5242880 | bytes 5767168 | tf_op jit(solution)/shard_map/convert_element_type | solution.py:259
  160.6 2.4 %collective-permute-start.29 = (bf16[8,256,128]{2,1,0:T(8,128)(2,1)}, bf16[8,256,128]{2,1,0:T(8,128)(2,1)S(1)}, u32[]{:S(2)}, u32[]{:S(2)}) collective-permute-start(bf16[8,256,128]{2,1,0:T(8,128)(2,1)} %shard_map.101), channel_id=1, source_target_pairs={{0,120},{1,3},{2,122},{3,5},{4,124},{5,7},{6,126},{7,1},{8,0},{9,1... | collective-permute-start | bytes 1572872 | tf_op jit(solution)/shard_map/ppermute | solution.py:194
  165.4 4.6 %collective-permute-done.29 = bf16[8,256,128]{2,1,0:T(8,128)(2,1)S(1)} collective-permute-done((bf16[8,256,128]{2,1,0:T(8,128)(2,1)}, bf16[8,256,128]{2,1,0:T(8,128)(2,1)S(1)}, u32[]{:S(2)}, u32[]{:S(2)}) %collective-permute-start.29) | collective-permute-done | bytes 524320 | tf_op jit(solution)/shard_map/ppermute | solution.py:194
  170.0 5.5 %collective-permute-done.30 = bf16[8,256,128]{2,1,0:T(8,128)(2,1)S(1)} collective-permute-done((bf16[8,256,128]{2,1,0:T(8,128)(2,1)S(1)}, bf16[8,256,128]{2,1,0:T(8,128)(2,1)S(1)}, u32[]{:S(2)}, u32[]{:S(2)}) %collective-permute-start.30) | collective-permute-done | bytes 524320 | tf_op jit(solution)/shard_map/ppermute | solution.py:194
  (108 shorter events, 41.3 us)
Async XLA Ops:
  0.6 13.8 %collective-permute-start = (bf16[1024,256]{1,0:T(8,128)(2,1)}, bf16[1024,256]{1,0:T(8,128)(2,1)S(1)}, u32[]{:S(2)}, u32[]{:S(2)}) collective-permute-start(bf16[1024,256]{1,0:T(8,128)(2,1)} %param.7), channel_id=1, source_target_pairs={{120,0},{3,1},{122,2},{5,3},{124,4},{7,5},{126,6},{1,7},{0,8},{11,... | collective-permute-start | bytes 1572872 | tf_op jit(solution)/shard_map/ppermute | solution.py:194
  2.7 12.5 %collective-permute-start.1 = (bf16[1024,256]{1,0:T(8,128)(2,1)}, bf16[1024,256]{1,0:T(8,128)(2,1)S(1)}, u32[]{:S(2)}, u32[]{:S(2)}) collective-permute-start(bf16[1024,256]{1,0:T(8,128)(2,1)} %param.7), channel_id=1, source_target_pairs={{8,0},{7,1},{10,2},{1,3},{12,4},{3,5},{14,6},{5,7},{16,8},{15,9},{... | collective-permute-start | bytes 1572872 | tf_op jit(solution)/shard_map/ppermute | solution.py:194
  16.1 25.0 %collective-permute-start.5 = (bf16[3072,256]{1,0:T(8,128)(2,1)}, bf16[3072,256]{1,0:T(8,128)(2,1)}, u32[]{:S(2)}, u32[]{:S(2)}) collective-permute-start(bf16[3072,256]{1,0:T(8,128)(2,1)} %constant_dynamic-update-slice_fusion.refs_5_), channel_id=1, source_target_pairs={{0,1},{1,0},{2,3},{3,2},{4,5},{5,4},{6,7},{7,6},{8,9},{9,8},{10,11... | collective-permute-start | bytes 4718600 | tf_op jit(solution)/shard_map/ppermute | solution.py:203
  16.1 26.2 %collective-permute-start.8 = (bf16[3072,256]{1,0:T(8,128)(2,1)}, bf16[3072,256]{1,0:T(8,128)(2,1)S(1)}, u32[]{:S(2)}, u32[]{:S(2)}) collective-permute-start(bf16[3072,256]{1,0:T(8,128)(2,1)} %constant_dynamic-update-slice_fusion.refs_5_), channel_id=1, source_target_pairs={{6,0},{9,1},{0,2},{11,3},{2,4},{13,5},{4,6},{15,7},{14,8},{17,9},{... | collective-permute-start | bytes 4718600 | tf_op jit(solution)/shard_map/ppermute | solution.py:194
  17.6 24.7 %collective-permute-start.2 = (bf16[3072,256]{1,0:T(8,128)(2,1)}, bf16[3072,256]{1,0:T(8,128)(2,1)S(1)}, u32[]{:S(2)}, u32[]{:S(2)}) collective-permute-start(bf16[3072,256]{1,0:T(8,128)(2,1)} %constant_dynamic-update-slice_fusion.refs_5_), channel_id=1, source_target_pairs={{2,0},{121,1},{4,2},{123,3},{6,4},{125,5},{0,6},{127,7},{10,8},{1,... | collective-permute-start | bytes 4718600 | tf_op jit(solution)/shard_map/ppermute | solution.py:194
  22.4 17.4 %collective-permute-start.6 = (bf16[1024,256]{1,0:T(8,128)(2,1)}, bf16[1024,256]{1,0:T(8,128)(2,1)}, u32[]{:S(2)}, u32[]{:S(2)}) collective-permute-start(bf16[1024,256]{1,0:T(8,128)(2,1)} %get-tuple-element.35.refs_4_), channel_id=1, source_target_pairs={{0,1},{1,0},{2,3},{3,2},{4,5},{5,4},{6,7},{7,6},{8,9},{9,8},{10,11... | collective-permute-start | bytes 1572872 | tf_op jit(solution)/shard_map/ppermute | solution.py:203
  45.4 12.4 %collective-permute-start.7 = (bf16[1536,256]{1,0:T(8,128)(2,1)}, bf16[1536,256]{1,0:T(8,128)(2,1)}, u32[]{:S(2)}, u32[]{:S(2)}) collective-permute-start(bf16[1536,256]{1,0:T(8,128)(2,1)} %shard_map.94), channel_id=1, source_target_pairs={{2,0},{121,1},{4,2},{123,3},{6,4},{125,5},{0,6},{127,7},{10,8},{1,... | collective-permute-start | bytes 2359304 | tf_op jit(solution)/shard_map/ppermute | solution.py:194
  47.0 15.8 %collective-permute-start.13 = (bf16[3072,256]{1,0:T(8,128)(2,1)S(1)}, bf16[3072,256]{1,0:T(8,128)(2,1)}, u32[]{:S(2)}, u32[]{:S(2)}) collective-permute-start(bf16[3072,256]{1,0:T(8,128)(2,1)S(1)} %collective-permute-done.8.refs_3_), channel_id=1, source_target_pairs={{0,1},{1,0},{2,3},{3,2},{4,5},{5,4},{6,7},{7,6},{8,9},{9,8},{10,11... | collective-permute-start | bytes 4718600 | tf_op jit(solution)/shard_map/ppermute | solution.py:203
  47.0 14.2 %collective-permute-start.9 = (bf16[1536,256]{1,0:T(8,128)(2,1)}, bf16[1536,256]{1,0:T(8,128)(2,1)}, u32[]{:S(2)}, u32[]{:S(2)}) collective-permute-start(bf16[1536,256]{1,0:T(8,128)(2,1)} %get-tuple-element.31), channel_id=1, source_target_pairs={{6,0},{9,1},{0,2},{11,3},{2,4},{13,5},{4,6},{15,7},{14,8},{17,9},{... | collective-permute-start | bytes 2359304 | tf_op jit(solution)/shard_map/ppermute | solution.py:194
  48.4 16.2 %collective-permute-start.12 = (bf16[3072,256]{1,0:T(8,128)(2,1)S(1)}, bf16[3072,256]{1,0:T(8,128)(2,1)}, u32[]{:S(2)}, u32[]{:S(2)}) collective-permute-start(bf16[3072,256]{1,0:T(8,128)(2,1)S(1)} %collective-permute-done.2.refs_2_), channel_id=1, source_target_pairs={{0,1},{1,0},{2,3},{3,2},{4,5},{5,4},{6,7},{7,6},{8,9},{9,8},{10,11... | collective-permute-start | bytes 4718600 | tf_op jit(solution)/shard_map/ppermute | solution.py:203
  100.1 27.2 %collective-permute-start.16 = (bf16[48,256,128]{2,1,0:T(8,128)(2,1)}, bf16[48,256,128]{2,1,0:T(8,128)(2,1)}, u32[]{:S(2)}, u32[]{:S(2)}) collective-permute-start(bf16[48,256,128]{2,1,0:T(8,128)(2,1)} %shard_map.97), channel_id=1, source_target_pairs={{0,1},{1,0},{2,3},{3,2},{4,5},{5,4},{6,7},{7,6},{8,9},{9,8},{10,11... | collective-permute-start | bytes 9437192 | tf_op jit(solution)/shard_map/ppermute | solution.py:203
  100.5 35.0 %collective-permute-start.15 = (bf16[32,256,128]{2,1,0:T(8,128)(2,1)}, bf16[32,256,128]{2,1,0:T(8,128)(2,1)}, u32[]{:S(2)}, u32[]{:S(2)}) collective-permute-start(bf16[32,256,128]{2,1,0:T(8,128)(2,1)} %shard_map.96), channel_id=1, source_target_pairs={{0,1},{1,0},{2,3},{3,2},{4,5},{5,4},{6,7},{7,6},{8,9},{9,8},{10,11... | collective-permute-start | bytes 6291464 | tf_op jit(solution)/shard_map/ppermute | solution.py:203
  101.4 7.4 %collective-permute-start.18 = (f32[128,256]{1,0:T(8,128)S(1)}, f32[128,256]{1,0:T(8,128)S(1)}, u32[]{:S(2)}, u32[]{:S(2)}) collective-permute-start(f32[128,256]{1,0:T(8,128)S(1)} %slice_select_fusion.4), channel_id=1, source_target_pairs={{0,1},{1,0},{2,3},{3,2},{4,5},{5,4},{6,7},{7,6},{8,9},{9,8},{10,11... | collective-permute-start | bytes 393224 | tf_op jit(solution)/shard_map/ppermute | solution.py:203
  101.8 25.5 %collective-permute-start.17 = (bf16[12,256,128]{2,1,0:T(8,128)(2,1)S(1)}, bf16[12,256,128]{2,1,0:T(8,128)(2,1)S(1)}, u32[]{:S(2)}, u32[]{:S(2)}) collective-permute-start(bf16[12,256,128]{2,1,0:T(8,128)(2,1)S(1)} %get-tuple-element.29), channel_id=1, source_target_pairs={{0,2},{1,121},{2,4},{3,123},{4,6},{5,125},{6,0},{7,127},{8,10},{9,... | collective-permute-start | bytes 2359304 | tf_op jit(solution)/shard_map/ppermute | solution.py:194
  104.1 23.2 %collective-permute-start.21 = (bf16[12,256,128]{2,1,0:T(8,128)(2,1)S(1)}, bf16[12,256,128]{2,1,0:T(8,128)(2,1)S(1)}, u32[]{:S(2)}, u32[]{:S(2)}) collective-permute-start(bf16[12,256,128]{2,1,0:T(8,128)(2,1)S(1)} %get-tuple-element.30), channel_id=1, source_target_pairs={{0,6},{1,9},{2,0},{3,11},{4,2},{5,13},{6,4},{7,15},{8,14},{9,17},{... | collective-permute-start | bytes 2359304 | tf_op jit(solution)/shard_map/ppermute | solution.py:194
  110.4 7.9 %collective-permute-start.19 = (bf16[128,256]{1,0:T(8,128)(2,1)S(1)}, bf16[128,256]{1,0:T(8,128)(2,1)S(1)}, u32[]{:S(2)}, u32[]{:S(2)}) collective-permute-start(bf16[128,256]{1,0:T(8,128)(2,1)S(1)} %get-tuple-element.23), channel_id=1, source_target_pairs={{0,2},{1,3},{2,0},{3,1},{4,6},{5,7},{6,4},{7,5},{8,10},{9,11},{10,... | collective-permute-start | bytes 196616 | tf_op jit(solution)/shard_map/ppermute | solution.py:245
  118.4 8.3 %collective-permute-start.24 = (bf16[128,256]{1,0:T(8,128)(2,1)S(1)}, bf16[128,256]{1,0:T(8,128)(2,1)S(1)}, u32[]{:S(2)}, u32[]{:S(2)}) collective-permute-start(bf16[128,256]{1,0:T(8,128)(2,1)S(1)} %get-tuple-element.21), channel_id=1, source_target_pairs={{0,4},{1,5},{2,6},{3,7},{4,0},{5,1},{6,2},{7,3},{8,12},{9,13},{10,... | collective-permute-start | bytes 196616 | tf_op jit(solution)/shard_map/ppermute | solution.py:245
  127.3 11.3 %collective-permute-start.25 = (bf16[128,256]{1,0:T(8,128)(2,1)}, bf16[128,256]{1,0:T(8,128)(2,1)S(1)}, u32[]{:S(2)}, u32[]{:S(2)}) collective-permute-start(bf16[128,256]{1,0:T(8,128)(2,1)} %fusion.1), channel_id=1, source_target_pairs={{0,8},{8,0},{16,24},{24,16},{32,40},{40,32},{48,56},{56,48},{64,72... | collective-permute-start | bytes 196616 | tf_op jit(solution)/shard_map/ppermute | solution.py:245
  132.2 24.3 %collective-permute-start.20 = (bf16[24,256,128]{2,1,0:T(8,128)(2,1)}, bf16[24,256,128]{2,1,0:T(8,128)(2,1)}, u32[]{:S(2)}, u32[]{:S(2)}) collective-permute-start(bf16[24,256,128]{2,1,0:T(8,128)(2,1)} %shard_map.99), channel_id=1, source_target_pairs={{0,2},{1,121},{2,4},{3,123},{4,6},{5,125},{6,0},{7,127},{8,10},{9,... | collective-permute-start | bytes 4718600 | tf_op jit(solution)/shard_map/ppermute | solution.py:194
  132.2 25.0 %collective-permute-start.22 = (bf16[24,256,128]{2,1,0:T(8,128)(2,1)}, bf16[24,256,128]{2,1,0:T(8,128)(2,1)}, u32[]{:S(2)}, u32[]{:S(2)}) collective-permute-start(bf16[24,256,128]{2,1,0:T(8,128)(2,1)} %get-tuple-element.28), channel_id=1, source_target_pairs={{0,6},{1,9},{2,0},{3,11},{4,2},{5,13},{6,4},{7,15},{8,14},{9,17},{... | collective-permute-start | bytes 4718600 | tf_op jit(solution)/shard_map/ppermute | solution.py:194
  141.4 7.3 %collective-permute-start.27 = (bf16[128,256]{1,0:T(8,128)(2,1)S(1)}, bf16[128,256]{1,0:T(8,128)(2,1)S(1)}, u32[]{:S(2)}, u32[]{:S(2)}) collective-permute-start(bf16[128,256]{1,0:T(8,128)(2,1)S(1)} %reduce-precision_convert_fusion.1), channel_id=1, source_target_pairs={{0,16},{8,24},{16,0},{24,8},{32,48},{40,56},{48,32},{56,40},{64,80... | collective-permute-start | bytes 196616 | tf_op jit(solution)/shard_map/ppermute | solution.py:245
  155.5 7.5 %collective-permute-start.31 = (bf16[128,256]{1,0:T(8,128)(2,1)S(1)}, bf16[128,256]{1,0:T(8,128)(2,1)S(1)}, u32[]{:S(2)}, u32[]{:S(2)}) collective-permute-start(bf16[128,256]{1,0:T(8,128)(2,1)S(1)} %get-tuple-element.19), channel_id=1, source_target_pairs={{0,64},{8,72},{16,80},{24,88},{32,96},{40,104},{48,112},{56,120},{... | collective-permute-start | bytes 196616 | tf_op jit(solution)/shard_map/ppermute | solution.py:245
  160.6 9.4 %collective-permute-start.29 = (bf16[8,256,128]{2,1,0:T(8,128)(2,1)}, bf16[8,256,128]{2,1,0:T(8,128)(2,1)S(1)}, u32[]{:S(2)}, u32[]{:S(2)}) collective-permute-start(bf16[8,256,128]{2,1,0:T(8,128)(2,1)} %shard_map.101), channel_id=1, source_target_pairs={{0,120},{1,3},{2,122},{3,5},{4,124},{5,7},{6,126},{7,1},{8,0},{9,1... | collective-permute-start | bytes 1572872 | tf_op jit(solution)/shard_map/ppermute | solution.py:194
  163.0 12.5 %collective-permute-start.30 = (bf16[8,256,128]{2,1,0:T(8,128)(2,1)S(1)}, bf16[8,256,128]{2,1,0:T(8,128)(2,1)S(1)}, u32[]{:S(2)}, u32[]{:S(2)}) collective-permute-start(bf16[8,256,128]{2,1,0:T(8,128)(2,1)S(1)} %get-tuple-element.26), channel_id=1, source_target_pairs={{0,8},{1,7},{2,10},{3,1},{4,12},{5,3},{6,14},{7,5},{8,16},{9,15},{... | collective-permute-start | bytes 1572872 | tf_op jit(solution)/shard_map/ppermute | solution.py:194
  (20 other events, 131.9 us)

commit v11 on v10

--- a/solution.py
+++ b/solution.py
@@ -286,7 +286,7 @@
     far = total(mine[2][:own], first[:own], *far)
     half_up = moved(far[:half], HALF_UP, back=True)
     half_down = moved(far[half:], HALF_DOWN, back=True)
-    steps.go(2)
+    steps.go(1)
     steps.after(half_up[:1, :8], half_down[:1, :8])
     steps.go(2)
 
@@ -297,6 +297,9 @@
     up = tied(total(*near(1), widened(half_up, own, 0)), steps.x)
     down = total(*near(2), widened(half_down, own, half))
     ends = moved(up, FIRST_UP, back=True), moved(down, FIRST_DOWN, back=True)
+    steps.after(down[:1, :8])
+    steps.go(2)
+    steps.after(ends[0][:1, :8])
     return total(*near(0), *ends)
 
 

time: 179 us -> 180 us (level)
  waiting for transfers between devices: 51.8 us -> 46 us
  other arithmetic: 24.5 us -> 28.1 us
  Pallas kernels: 29.3 us -> 31.2 us
    ppermute x16, waiting for transfers between devices: 23.1 us -> 13.2 us  [moved(): return lax.ppermute(x, ('rows', 'rep'), pairs)]
    ppermute x11, starting transfers between devices: 24.3 us -> 28.8 us  [from_core(): lax.ppermute(x, 'rep', [(i, i ^ 1) for i in range(lax.axis_size('rep'))])]
    ppermute x6, starting transfers between devices: 6.3 us -> 2.03 us  [go(): lax.ppermute(rounded.astype(bf16), axis, pairs).astype(f32)]
    add x2 -> x3, other arithmetic: 0.7 us -> 3.85 us  [go(): rounded + lax.ppermute(rounded.astype(bf16), axis, pairs).astype(f32)]
    ppermute x11, waiting for transfers between devices: 7.15 us -> 9.79 us  [from_core(): lax.ppermute(x, 'rep', [(i, i ^ 1) for i in range(lax.axis_size('rep'))])]
    pallas_call x1, Pallas kernels: 29.3 us -> 31.2 us  [layer(): pl.pallas_call(functools.partial(kernel, len(parts), 2 * len(groups)), in...]
    unnamed x25 -> x23, local copies, waits for them, and re-layouts: 5.11 us -> 4.29 us
  transfers between devices with their start and end apart: 33 -> 33, of which waited for: 15 -> 14; matrix products, arithmetic and copies ran while one was open for 15% -> 16% of each run, Pallas kernels for 0% -> 0%
where the time goes in v11:
time: 180 us; the launch traced here: 178 us
  starting transfers between devices  58.3 us (32%)
  waiting for transfers between devices  46 us (26%)
  Pallas kernels  31.2 us (17%)
  other arithmetic  28.1 us (16%)
  local copies, waits for them, and re-layouts  13.3 us (7%)
    pallas_call x1, Pallas kernels, layer(): pl.pallas_call(functools.partial(kernel, len(parts), 2 * len(groups)), in...  31.2 us
    ppermute x11, starting transfers between devices, from_core(): lax.ppermute(x, 'rep', [(i, i ^ 1) for i in range(lax.axis_size('rep'))])  28.8 us
    ppermute x16, starting transfers between devices, moved(): return lax.ppermute(x, ('rows', 'rep'), pairs)  27.5 us
    ppermute x6, waiting for transfers between devices, go(): lax.ppermute(rounded.astype(bf16), axis, pairs).astype(f32)  23 us
    ppermute x16, waiting for transfers between devices, moved(): return lax.ppermute(x, ('rows', 'rep'), pairs)  13.2 us
    convert_element_type x4, other arithmetic, total(): return sum((x.astype(f32) for x in terms)).astype(bf16)  11.6 us
    ppermute x11, waiting for transfers between devices, from_core(): lax.ppermute(x, 'rep', [(i, i ^ 1) for i in range(lax.axis_size('rep'))])  9.79 us
    convert_element_type x6, other arithmetic, go(): rounded.astype(bf16)  5.28 us
  transfers between devices with their start and end apart: 33, of which 14 were waited for; matrix products, arithmetic and copies ran while one was open for 16% of the time, Pallas kernels for 0%

profile of v11, /device:TPU:0, one launch (start us, length us, event | category | flops | bytes accessed | tf_op | source)
XLA Modules:
  0.0 177.8 jit_solution(17966058106070519713)
XLA Ops:
  0.6 2.1 %collective-permute-start = (bf16[1024,256]{1,0:T(8,128)(2,1)}, bf16[1024,256]{1,0:T(8,128)(2,1)S(1)}, u32[]{:S(2)}, u32[]{:S(2)}) collective-permute-start(bf16[1024,256]{1,0:T(8,128)(2,1)} %param.7), channel_id=1, source_target_pairs={{120,0},{3,1},{122,2},{5,3},{124,4},{7,5},{126,6},{1,7},{0,8},{11,... | collective-permute-start | bytes 1572872 | tf_op jit(solution)/shard_map/ppermute | solution.py:194
  2.7 4.4 %collective-permute-start.1 = (bf16[1024,256]{1,0:T(8,128)(2,1)}, bf16[1024,256]{1,0:T(8,128)(2,1)S(1)}, u32[]{:S(2)}, u32[]{:S(2)}) collective-permute-start(bf16[1024,256]{1,0:T(8,128)(2,1)} %param.7), channel_id=1, source_target_pairs={{8,0},{7,1},{10,2},{1,3},{12,4},{3,5},{14,6},{5,7},{16,8},{15,9},{... | collective-permute-start | bytes 1572872 | tf_op jit(solution)/shard_map/ppermute | solution.py:194
  7.1 1.9 %constant_dynamic-update-slice_fusion.2 = bf16[3072,256]{1,0:T(8,128)(2,1)} fusion(bf16[1024,256]{1,0:T(8,128)(2,1)} %param.7), kind=kLoop, calls=%fused_computation.30 | loop fusion | bytes 1048576
  9.0 5.4 %collective-permute-done = bf16[1024,256]{1,0:T(8,128)(2,1)S(1)} collective-permute-done((bf16[1024,256]{1,0:T(8,128)(2,1)}, bf16[1024,256]{1,0:T(8,128)(2,1)S(1)}, u32[]{:S(2)}, u32[]{:S(2)}) %collective-permute-start) | collective-permute-done | bytes 524320 | tf_op jit(solution)/shard_map/ppermute | solution.py:194
  22.4 15.5 %collective-permute-start.6 = (bf16[1024,256]{1,0:T(8,128)(2,1)}, bf16[1024,256]{1,0:T(8,128)(2,1)}, u32[]{:S(2)}, u32[]{:S(2)}) collective-permute-start(bf16[1024,256]{1,0:T(8,128)(2,1)} %get-tuple-element.33.refs_4_), channel_id=1, source_target_pairs={{0,1},{1,0},{2,3},{3,2},{4,5},{5,4},{6,7},{7,6},{8,9},{9,8},{10,11... | collective-permute-start | bytes 1572872 | tf_op jit(solution)/shard_map/ppermute | solution.py:203
  42.3 3.0 %slice_select_fusion = (bf16[1536,256]{1,0:T(8,128)(2,1)}, bf16[1536,256]{1,0:T(8,128)(2,1)}) fusion(bf16[1536,256]{1,0:T(8,128)(2,1)} %constant_dynamic-update-slice_fusion.3, bf16[3072,256]{1,0:T(8,128)(2,1)S(1)} %collective-permute-done.8.refs_3_, pred[]{:T(512)S(6)} %eq.33, bf16[3072,256]{1,0:T(8,128)(2,1)S(1)} %collective-permute-done.2.refs_2_), kind=kLoop, calls=%fused_computation.7 | loop fusion | flops 786432 | bytes 3932161 | tf_op jit(solution)/shard_map/jit(_where)/select_n | solution.py:217
  48.4 3.4 %collective-permute-start.12 = (bf16[3072,256]{1,0:T(8,128)(2,1)S(1)}, bf16[3072,256]{1,0:T(8,128)(2,1)}, u32[]{:S(2)}, u32[]{:S(2)}) collective-permute-start(bf16[3072,256]{1,0:T(8,128)(2,1)S(1)} %collective-permute-done.2.refs_2_), channel_id=1, source_target_pairs={{0,1},{1,0},{2,3},{3,2},{4,5},{5,4},{6,7},{7,6},{8,9},{9,8},{10,11... | collective-permute-start | bytes 4718600 | tf_op jit(solution)/shard_map/ppermute | solution.py:203
  51.9 5.9 %collective-permute-done.7.refs_0_ = bf16[1536,256]{1,0:T(8,128)(2,1)} collective-permute-done((bf16[1536,256]{1,0:T(8,128)(2,1)}, bf16[1536,256]{1,0:T(8,128)(2,1)}, u32[]{:S(2)}, u32[]{:S(2)}) %collective-permute-start.7) | collective-permute-done | bytes 786464 | tf_op jit(solution)/shard_map/ppermute | solution.py:194
  57.7 3.5 %collective-permute-start.10 = (bf16[1536,256]{1,0:T(8,128)(2,1)}, bf16[1536,256]{1,0:T(8,128)(2,1)}, u32[]{:S(2)}, u32[]{:S(2)}) collective-permute-start(bf16[1536,256]{1,0:T(8,128)(2,1)} %collective-permute-done.7.refs_0_), channel_id=1, source_target_pairs={{0,1},{1,0},{2,3},{3,2},{4,5},{5,4},{6,7},{7,6},{8,9},{9,8},{10,11... | collective-permute-start | bytes 2359304 | tf_op jit(solution)/shard_map/ppermute | solution.py:203
  64.6 31.2 %shard_map.95 = (bf16[1024,256]{1,0:T(8,128)(2,1)}, f32[256,256]{1,0:T(8,128)}, bf16[24,256,128]{2,1,0:T(8,128)(2,1)}, bf16[48,256,128]{2,1,0:T(8,128)(2,1)}, bf...) custom-call(s32[8,48]{1,0:T(8,128)} %fusion.5.idx, ...), custom_call_target="tpu_custom_call" | custom-call | flops 6442450944 | bytes 37748736 | tf_op jit(solution)/shard_map/pallas_call | solution.py:141
  96.9 3.2 %collective-permute-done.14 = bf16[24,256,128]{2,1,0:T(8,128)(2,1)S(1)} collective-permute-done((bf16[24,256,128]{2,1,0:T(8,128)(2,1)}, bf16[24,256,128]{2,1,0:T(8,128)(2,1)S(1)}, u32[]{:S(2)}, u32[]{:S(2)}) %collective-permute-start.14) | collective-permute-done | bytes 1572896 | tf_op jit(solution)/shard_map/ppermute | solution.py:203
  100.2 1.9 %add_convert_fusion.2 = bf16[24,256,128]{2,1,0:T(8,128)(2,1)S(1)} fusion(bf16[24,256,128]{2,1,0:T(8,128)(2,1)S(1)} %collective-permute-done.14, bf16[24,256,128]{2,1,0:T(8,128)(2,1)} %get-tuple-element.14), kind=kLoop, calls=%fused_computation.2 | loop fusion | flops 3145728 | bytes 4718592 | tf_op jit(solution)/shard_map/convert_element_type | solution.py:259
  103.3 2.3 %collective-permute-start.17 = (bf16[12,256,128]{2,1,0:T(8,128)(2,1)S(1)}, bf16[12,256,128]{2,1,0:T(8,128)(2,1)S(1)}, u32[]{:S(2)}, u32[]{:S(2)}) collective-permute-start(bf16[12,256,128]{2,1,0:T(8,128)(2,1)S(1)} %get-tuple-element.27), channel_id=1, source_target_pairs={{0,2},{1,121},{2,4},{3,123},{4,6},{5,125},{6,0},{7,127},{8,10},{9,... | collective-permute-start | bytes 2359304 | tf_op jit(solution)/shard_map/ppermute | solution.py:194
  107.8 3.7 %collective-permute-done.18.refs_0_ = f32[128,256]{1,0:T(8,128)S(1)} collective-permute-done((f32[128,256]{1,0:T(8,128)S(1)}, f32[128,256]{1,0:T(8,128)S(1)}, u32[]{:S(2)}, u32[]{:S(2)}) %collective-permute-start.18) | collective-permute-done | bytes 131104 | tf_op jit(solution)/shard_map/ppermute | solution.py:203
  113.2 5.8 %collective-permute-done.19 = bf16[128,256]{1,0:T(8,128)(2,1)S(1)} collective-permute-done((bf16[128,256]{1,0:T(8,128)(2,1)S(1)}, bf16[128,256]{1,0:T(8,128)(2,1)S(1)}, u32[]{:S(2)}, u32[]{:S(2)}) %collective-permute-start.19) | collective-permute-done | bytes 65568 | tf_op jit(solution)/shard_map/ppermute | solution.py:245
  121.3 4.8 %add_convert_fusion.1 = (bf16[24,256,128]{2,1,0:T(8,128)(2,1)}, bf16[24,256,128]{2,1,0:T(8,128)(2,1)}) fusion(bf16[48,256,128]{2,1,0:T(8,128)(2,1)} %collective-permute-done.16, bf16[12,256,128]{2,1,0:T(8,128)(2,1)S(1)} %collective-permute-done.17, bf16[48,256,128]{2,1,0:T(8,128)(2,1)} %get-tuple-element.16, pred[]{:T(512)S(6)} %eq.33, ...), kind=kLoop, calls=%fused_computation.1 | loop fusion | flops 11010048 | bytes 11010049 | tf_op jit(solution)/shard_map/convert_element_type | solution.py:259
  126.3 3.1 %collective-permute-start.22 = (bf16[24,256,128]{2,1,0:T(8,128)(2,1)}, bf16[24,256,128]{2,1,0:T(8,128)(2,1)}, u32[]{:S(2)}, u32[]{:S(2)}) collective-permute-start(bf16[24,256,128]{2,1,0:T(8,128)(2,1)} %get-tuple-element.26), channel_id=1, source_target_pairs={{0,6},{1,9},{2,0},{3,11},{4,2},{5,13},{6,4},{7,15},{8,14},{9,17},{... | collective-permute-start | bytes 4718600 | tf_op jit(solution)/shard_map/ppermute | solution.py:194
  135.4 5.0 %collective-permute-done.26 = bf16[128,256]{1,0:T(8,128)(2,1)S(1)} collective-permute-done((bf16[128,256]{1,0:T(8,128)(2,1)S(1)}, bf16[128,256]{1,0:T(8,128)(2,1)S(1)}, u32[]{:S(2)}, u32[]{:S(2)}) %collective-permute-start.26) | collective-permute-done | bytes 65568 | tf_op jit(solution)/shard_map/ppermute | solution.py:245
  141.4 6.5 %collective-permute-done.27 = bf16[128,256]{1,0:T(8,128)(2,1)S(1)} collective-permute-done((bf16[128,256]{1,0:T(8,128)(2,1)S(1)}, bf16[128,256]{1,0:T(8,128)(2,1)S(1)}, u32[]{:S(2)}, u32[]{:S(2)}) %collective-permute-start.27) | collective-permute-done | bytes 65568 | tf_op jit(solution)/shard_map/ppermute | solution.py:245
  150.9 3.3 %add_convert_fusion.5 = (bf16[8,256,128]{2,1,0:T(8,128)(2,1)}, bf16[8,256,128]{2,1,0:T(8,128)(2,1)S(1)}) fusion(bf16[24,256,128]{2,1,0:T(8,128)(2,1)} %collective-permute-done.22, bf16[24,256,128]{2,1,0:T(8,128)(2,1)} %collective-permute-done.20, bf16[32,256,128]{2,1,0:T(8,128)(2,1)} %collective-permute-done.15, ...), kind=kLoop, calls=%fused_computation.5 | loop fusion | flops 5242880 | bytes 5767168 | tf_op jit(solution)/shard_map/convert_element_type | solution.py:259
  155.8 5.3 %collective-permute-start.28 = (bf16[8,256,128]{2,1,0:T(8,128)(2,1)}, bf16[8,256,128]{2,1,0:T(8,128)(2,1)S(1)}, u32[]{:S(2)}, u32[]{:S(2)}) collective-permute-start(bf16[8,256,128]{2,1,0:T(8,128)(2,1)} %shard_map.101), channel_id=1, source_target_pairs={{0,120},{1,3},{2,122},{3,5},{4,124},{5,7},{6,126},{7,1},{8,0},{9,1... | collective-permute-start | bytes 1572872 | tf_op jit(solution)/shard_map/ppermute | solution.py:194
  162.1 5.8 %collective-permute-done.31 = bf16[128,256]{1,0:T(8,128)(2,1)S(1)} collective-permute-done((bf16[128,256]{1,0:T(8,128)(2,1)S(1)}, bf16[128,256]{1,0:T(8,128)(2,1)S(1)}, u32[]{:S(2)}, u32[]{:S(2)}) %collective-permute-start.31) | collective-permute-done | bytes 65568 | tf_op jit(solution)/shard_map/ppermute | solution.py:245
  170.2 3.6 %collective-permute-start.32 = (f32[128,256]{1,0:T(8,128)}, f32[128,256]{1,0:T(8,128)S(1)}, u32[]{:S(2)}, u32[]{:S(2)}) collective-permute-start(f32[128,256]{1,0:T(8,128)} %shard_map.103), channel_id=1, source_target_pairs={{0,1},{1,0},{2,3},{3,2},{4,5},{5,4},{6,7},{7,6},{8,9},{9,8},{10,11... | collective-permute-start | bytes 393224 | tf_op jit(solution)/shard_map/ppermute | solution.py:203
  174.1 1.9 %fusion = bf16[8,128,256]{1,2,0:T(8,128)(2,1)S(1)} fusion(bf16[8,256,128]{2,1,0:T(8,128)(2,1)} %collective-permute-done.29, bf16[8,256,128]{2,1,0:T(8,128)(2,1)S(1)} %collective-permute-done.28, bf16[24,256,128]{2,1,0:T(8,128)(2,1)} %collective-permute-done.22, bf16[24,256,128]{2,1,0:T(8,128)(2,1)} %collective-permute-done.20, ...), kind=kLoop, calls=%fused_computation.9 | loop fusion | flops 3145728 | bytes 3670016 | tf_op jit(solution)/shard_map/transpose | solution.py:336
  (111 shorter events, 44.5 us)
Async XLA Ops:
  0.6 13.8 %collective-permute-start = (bf16[1024,256]{1,0:T(8,128)(2,1)}, bf16[1024,256]{1,0:T(8,128)(2,1)S(1)}, u32[]{:S(2)}, u32[]{:S(2)}) collective-permute-start(bf16[1024,256]{1,0:T(8,128)(2,1)} %param.7), channel_id=1, source_target_pairs={{120,0},{3,1},{122,2},{5,3},{124,4},{7,5},{126,6},{1,7},{0,8},{11,... | collective-permute-start | bytes 1572872 | tf_op jit(solution)/shard_map/ppermute | solution.py:194
  2.7 12.5 %collective-permute-start.1 = (bf16[1024,256]{1,0:T(8,128)(2,1)}, bf16[1024,256]{1,0:T(8,128)(2,1)S(1)}, u32[]{:S(2)}, u32[]{:S(2)}) collective-permute-start(bf16[1024,256]{1,0:T(8,128)(2,1)} %param.7), channel_id=1, source_target_pairs={{8,0},{7,1},{10,2},{1,3},{12,4},{3,5},{14,6},{5,7},{16,8},{15,9},{... | collective-permute-start | bytes 1572872 | tf_op jit(solution)/shard_map/ppermute | solution.py:194
  16.1 25.0 %collective-permute-start.5 = (bf16[3072,256]{1,0:T(8,128)(2,1)}, bf16[3072,256]{1,0:T(8,128)(2,1)}, u32[]{:S(2)}, u32[]{:S(2)}) collective-permute-start(bf16[3072,256]{1,0:T(8,128)(2,1)} %constant_dynamic-update-slice_fusion.refs_5_), channel_id=1, source_target_pairs={{0,1},{1,0},{2,3},{3,2},{4,5},{5,4},{6,7},{7,6},{8,9},{9,8},{10,11... | collective-permute-start | bytes 4718600 | tf_op jit(solution)/shard_map/ppermute | solution.py:203
  16.1 26.2 %collective-permute-start.8 = (bf16[3072,256]{1,0:T(8,128)(2,1)}, bf16[3072,256]{1,0:T(8,128)(2,1)S(1)}, u32[]{:S(2)}, u32[]{:S(2)}) collective-permute-start(bf16[3072,256]{1,0:T(8,128)(2,1)} %constant_dynamic-update-slice_fusion.refs_5_), channel_id=1, source_target_pairs={{6,0},{9,1},{0,2},{11,3},{2,4},{13,5},{4,6},{15,7},{14,8},{17,9},{... | collective-permute-start | bytes 4718600 | tf_op jit(solution)/shard_map/ppermute | solution.py:194
  17.6 24.7 %collective-permute-start.2 = (bf16[3072,256]{1,0:T(8,128)(2,1)}, bf16[3072,256]{1,0:T(8,128)(2,1)S(1)}, u32[]{:S(2)}, u32[]{:S(2)}) collective-permute-start(bf16[3072,256]{1,0:T(8,128)(2,1)} %constant_dynamic-update-slice_fusion.refs_5_), channel_id=1, source_target_pairs={{2,0},{121,1},{4,2},{123,3},{6,4},{125,5},{0,6},{127,7},{10,8},{1,... | collective-permute-start | bytes 4718600 | tf_op jit(solution)/shard_map/ppermute | solution.py:194
  22.4 17.4 %collective-permute-start.6 = (bf16[1024,256]{1,0:T(8,128)(2,1)}, bf16[1024,256]{1,0:T(8,128)(2,1)}, u32[]{:S(2)}, u32[]{:S(2)}) collective-permute-start(bf16[1024,256]{1,0:T(8,128)(2,1)} %get-tuple-element.33.refs_4_), channel_id=1, source_target_pairs={{0,1},{1,0},{2,3},{3,2},{4,5},{5,4},{6,7},{7,6},{8,9},{9,8},{10,11... | collective-permute-start | bytes 1572872 | tf_op jit(solution)/shard_map/ppermute | solution.py:203
  45.4 12.4 %collective-permute-start.7 = (bf16[1536,256]{1,0:T(8,128)(2,1)}, bf16[1536,256]{1,0:T(8,128)(2,1)}, u32[]{:S(2)}, u32[]{:S(2)}) collective-permute-start(bf16[1536,256]{1,0:T(8,128)(2,1)} %shard_map.94), channel_id=1, source_target_pairs={{2,0},{121,1},{4,2},{123,3},{6,4},{125,5},{0,6},{127,7},{10,8},{1,... | collective-permute-start | bytes 2359304 | tf_op jit(solution)/shard_map/ppermute | solution.py:194
  47.0 15.9 %collective-permute-start.13 = (bf16[3072,256]{1,0:T(8,128)(2,1)S(1)}, bf16[3072,256]{1,0:T(8,128)(2,1)}, u32[]{:S(2)}, u32[]{:S(2)}) collective-permute-start(bf16[3072,256]{1,0:T(8,128)(2,1)S(1)} %collective-permute-done.8.refs_3_), channel_id=1, source_target_pairs={{0,1},{1,0},{2,3},{3,2},{4,5},{5,4},{6,7},{7,6},{8,9},{9,8},{10,11... | collective-permute-start | bytes 4718600 | tf_op jit(solution)/shard_map/ppermute | solution.py:203
  47.0 14.2 %collective-permute-start.9 = (bf16[1536,256]{1,0:T(8,128)(2,1)}, bf16[1536,256]{1,0:T(8,128)(2,1)}, u32[]{:S(2)}, u32[]{:S(2)}) collective-permute-start(bf16[1536,256]{1,0:T(8,128)(2,1)} %get-tuple-element.29), channel_id=1, source_target_pairs={{6,0},{9,1},{0,2},{11,3},{2,4},{13,5},{4,6},{15,7},{14,8},{17,9},{... | collective-permute-start | bytes 2359304 | tf_op jit(solution)/shard_map/ppermute | solution.py:194
  48.4 16.2 %collective-permute-start.12 = (bf16[3072,256]{1,0:T(8,128)(2,1)S(1)}, bf16[3072,256]{1,0:T(8,128)(2,1)}, u32[]{:S(2)}, u32[]{:S(2)}) collective-permute-start(bf16[3072,256]{1,0:T(8,128)(2,1)S(1)} %collective-permute-done.2.refs_2_), channel_id=1, source_target_pairs={{0,1},{1,0},{2,3},{3,2},{4,5},{5,4},{6,7},{7,6},{8,9},{9,8},{10,11... | collective-permute-start | bytes 4718600 | tf_op jit(solution)/shard_map/ppermute | solution.py:203
  57.7 5.8 %collective-permute-start.10 = (bf16[1536,256]{1,0:T(8,128)(2,1)}, bf16[1536,256]{1,0:T(8,128)(2,1)}, u32[]{:S(2)}, u32[]{:S(2)}) collective-permute-start(bf16[1536,256]{1,0:T(8,128)(2,1)} %collective-permute-done.7.refs_0_), channel_id=1, source_target_pairs={{0,1},{1,0},{2,3},{3,2},{4,5},{5,4},{6,7},{7,6},{8,9},{9,8},{10,11... | collective-permute-start | bytes 2359304 | tf_op jit(solution)/shard_map/ppermute | solution.py:203
  102.7 18.6 %collective-permute-start.16 = (bf16[48,256,128]{2,1,0:T(8,128)(2,1)}, bf16[48,256,128]{2,1,0:T(8,128)(2,1)}, u32[]{:S(2)}, u32[]{:S(2)}) collective-permute-start(bf16[48,256,128]{2,1,0:T(8,128)(2,1)} %shard_map.97), channel_id=1, source_target_pairs={{0,1},{1,0},{2,3},{3,2},{4,5},{5,4},{6,7},{7,6},{8,9},{9,8},{10,11... | collective-permute-start | bytes 9437192 | tf_op jit(solution)/shard_map/ppermute | solution.py:203
  103.0 26.3 %collective-permute-start.15 = (bf16[32,256,128]{2,1,0:T(8,128)(2,1)}, bf16[32,256,128]{2,1,0:T(8,128)(2,1)}, u32[]{:S(2)}, u32[]{:S(2)}) collective-permute-start(bf16[32,256,128]{2,1,0:T(8,128)(2,1)} %shard_map.96), channel_id=1, source_target_pairs={{0,1},{1,0},{2,3},{3,2},{4,5},{5,4},{6,7},{7,6},{8,9},{9,8},{10,11... | collective-permute-start | bytes 6291464 | tf_op jit(solution)/shard_map/ppermute | solution.py:203
  103.3 18.0 %collective-permute-start.17 = (bf16[12,256,128]{2,1,0:T(8,128)(2,1)S(1)}, bf16[12,256,128]{2,1,0:T(8,128)(2,1)S(1)}, u32[]{:S(2)}, u32[]{:S(2)}) collective-permute-start(bf16[12,256,128]{2,1,0:T(8,128)(2,1)S(1)} %get-tuple-element.27), channel_id=1, source_target_pairs={{0,2},{1,121},{2,4},{3,123},{4,6},{5,125},{6,0},{7,127},{8,10},{9,... | collective-permute-start | bytes 2359304 | tf_op jit(solution)/shard_map/ppermute | solution.py:194
  105.6 15.7 %collective-permute-start.21 = (bf16[12,256,128]{2,1,0:T(8,128)(2,1)S(1)}, bf16[12,256,128]{2,1,0:T(8,128)(2,1)S(1)}, u32[]{:S(2)}, u32[]{:S(2)}) collective-permute-start(bf16[12,256,128]{2,1,0:T(8,128)(2,1)S(1)} %get-tuple-element.28), channel_id=1, source_target_pairs={{0,6},{1,9},{2,0},{3,11},{4,2},{5,13},{6,4},{7,15},{8,14},{9,17},{... | collective-permute-start | bytes 2359304 | tf_op jit(solution)/shard_map/ppermute | solution.py:194
  113.1 5.9 %collective-permute-start.19 = (bf16[128,256]{1,0:T(8,128)(2,1)S(1)}, bf16[128,256]{1,0:T(8,128)(2,1)S(1)}, u32[]{:S(2)}, u32[]{:S(2)}) collective-permute-start(bf16[128,256]{1,0:T(8,128)(2,1)S(1)} %get-tuple-element.21), channel_id=1, source_target_pairs={{0,2},{1,3},{2,0},{3,1},{4,6},{5,7},{6,4},{7,5},{8,10},{9,11},{10,... | collective-permute-start | bytes 196616 | tf_op jit(solution)/shard_map/ppermute | solution.py:245
  119.7 12.8 %collective-permute-start.24 = (bf16[128,256]{1,0:T(8,128)(2,1)S(1)}, bf16[128,256]{1,0:T(8,128)(2,1)S(1)}, u32[]{:S(2)}, u32[]{:S(2)}) collective-permute-start(bf16[128,256]{1,0:T(8,128)(2,1)S(1)} %get-tuple-element.19), channel_id=1, source_target_pairs={{0,4},{1,5},{2,6},{3,7},{4,0},{5,1},{6,2},{7,3},{8,12},{9,13},{10,... | collective-permute-start | bytes 196616 | tf_op jit(solution)/shard_map/ppermute | solution.py:245
  126.1 24.8 %collective-permute-start.20 = (bf16[24,256,128]{2,1,0:T(8,128)(2,1)}, bf16[24,256,128]{2,1,0:T(8,128)(2,1)}, u32[]{:S(2)}, u32[]{:S(2)}) collective-permute-start(bf16[24,256,128]{2,1,0:T(8,128)(2,1)} %shard_map.99), channel_id=1, source_target_pairs={{0,2},{1,121},{2,4},{3,123},{4,6},{5,125},{6,0},{7,127},{8,10},{9,... | collective-permute-start | bytes 4718600 | tf_op jit(solution)/shard_map/ppermute | solution.py:194
  126.3 24.6 %collective-permute-start.22 = (bf16[24,256,128]{2,1,0:T(8,128)(2,1)}, bf16[24,256,128]{2,1,0:T(8,128)(2,1)}, u32[]{:S(2)}, u32[]{:S(2)}) collective-permute-start(bf16[24,256,128]{2,1,0:T(8,128)(2,1)} %get-tuple-element.26), channel_id=1, source_target_pairs={{0,6},{1,9},{2,0},{3,11},{4,2},{5,13},{6,4},{7,15},{8,14},{9,17},{... | collective-permute-start | bytes 4718600 | tf_op jit(solution)/shard_map/ppermute | solution.py:194
  141.3 6.6 %collective-permute-start.27 = (bf16[128,256]{1,0:T(8,128)(2,1)S(1)}, bf16[128,256]{1,0:T(8,128)(2,1)S(1)}, u32[]{:S(2)}, u32[]{:S(2)}) collective-permute-start(bf16[128,256]{1,0:T(8,128)(2,1)S(1)} %fusion.1), channel_id=1, source_target_pairs={{0,16},{8,24},{16,0},{24,8},{32,48},{40,56},{48,32},{56,40},{64,80... | collective-permute-start | bytes 196616 | tf_op jit(solution)/shard_map/ppermute | solution.py:245
  155.8 13.8 %collective-permute-start.28 = (bf16[8,256,128]{2,1,0:T(8,128)(2,1)}, bf16[8,256,128]{2,1,0:T(8,128)(2,1)S(1)}, u32[]{:S(2)}, u32[]{:S(2)}) collective-permute-start(bf16[8,256,128]{2,1,0:T(8,128)(2,1)} %shard_map.101), channel_id=1, source_target_pairs={{0,120},{1,3},{2,122},{3,5},{4,124},{5,7},{6,126},{7,1},{8,0},{9,1... | collective-permute-start | bytes 1572872 | tf_op jit(solution)/shard_map/ppermute | solution.py:194
  161.1 13.0 %collective-permute-start.29 = (bf16[8,256,128]{2,1,0:T(8,128)(2,1)S(1)}, bf16[8,256,128]{2,1,0:T(8,128)(2,1)}, u32[]{:S(2)}, u32[]{:S(2)}) collective-permute-start(bf16[8,256,128]{2,1,0:T(8,128)(2,1)S(1)} %get-tuple-element.24), channel_id=1, source_target_pairs={{0,8},{1,7},{2,10},{3,1},{4,12},{5,3},{6,14},{7,5},{8,16},{9,15},{... | collective-permute-start | bytes 1572872 | tf_op jit(solution)/shard_map/ppermute | solution.py:194
  162.1 5.8 %collective-permute-start.31 = (bf16[128,256]{1,0:T(8,128)(2,1)S(1)}, bf16[128,256]{1,0:T(8,128)(2,1)S(1)}, u32[]{:S(2)}, u32[]{:S(2)}) collective-permute-start(bf16[128,256]{1,0:T(8,128)(2,1)S(1)} %fusion.2), channel_id=1, source_target_pairs={{0,64},{8,72},{16,80},{24,88},{32,96},{40,104},{48,112},{56,120},{... | collective-permute-start | bytes 196616 | tf_op jit(solution)/shard_map/ppermute | solution.py:245
  170.2 6.9 %collective-permute-start.32 = (f32[128,256]{1,0:T(8,128)}, f32[128,256]{1,0:T(8,128)S(1)}, u32[]{:S(2)}, u32[]{:S(2)}) collective-permute-start(f32[128,256]{1,0:T(8,128)} %shard_map.103), channel_id=1, source_target_pairs={{0,1},{1,0},{2,3},{3,2},{4,5},{5,4},{6,7},{7,6},{8,9},{9,8},{10,11... | collective-permute-start | bytes 393224 | tf_op jit(solution)/shard_map/ppermute | solution.py:203
  (19 other events, 124.4 us)

commit v12 on v10

--- a/solution.py
+++ b/solution.py
@@ -228,21 +228,23 @@
         self.mine = jnp.where(core == 0, low, high)
         self.got = from_core(jnp.where(core == 0, high, low))
         self.core = core
-        self.left = [
-            (axis, bit)
-            for axis, first in (("rep", 2), ("rows", 1))
-            for bit in (1 << k for k in range(10))
-            if first <= bit < lax.axis_size(axis)
-        ]
+        self.left = [("rep", (2,)), ("rep", (4,)), ("rows", (1, 2)), ("rows", (4, 8))]
 
     def begin(self, *earlier):
         self.x = self.mine + tied(self.got, *earlier)
 
     def go(self, count):
-        for axis, bit in self.left[:count]:
-            pairs = [(i, i ^ bit) for i in range(lax.axis_size(axis))]
-            rounded = lax.reduce_precision(self.x, 8, 7)
-            self.x = rounded + lax.ppermute(rounded.astype(bf16), axis, pairs).astype(f32)
+        for axis, bits in self.left[:count]:
+            own = lax.reduce_precision(self.x, 8, 7)
+            sent = own.astype(bf16)
+
+            def taken(bit, axis=axis, sent=sent):
+                pairs = [(i, i ^ bit) for i in range(lax.axis_size(axis))]
+                return lax.ppermute(sent, axis, pairs).astype(f32)
+
+            self.x = own + taken(bits[0])
+            if len(bits) > 1:
+                self.x += taken(bits[1]) + taken(bits[0] | bits[1])
         self.left = self.left[count:]
 
     def after(self, *earlier):
@@ -286,7 +288,7 @@
     far = total(mine[2][:own], first[:own], *far)
     half_up = moved(far[:half], HALF_UP, back=True)
     half_down = moved(far[half:], HALF_DOWN, back=True)
-    steps.go(2)
+    steps.go(1)
     steps.after(half_up[:1, :8], half_down[:1, :8])
     steps.go(2)
 

time: 179 us -> 185 us (1.034)
  waiting for transfers between devices: 51.8 us -> 55.8 us
  Pallas kernels: 29.3 us -> 31.9 us
    ppermute x6 -> x8, starting transfers between devices: 6.3 us -> 11.1 us  [taken(): return lax.ppermute(sent, axis, pairs).astype(f32)]
    ppermute x16, starting transfers between devices: 28.3 us -> 24.2 us  [moved(): return lax.ppermute(x, ('rows', 'rep'), pairs)]
    ppermute x6 -> x8, waiting for transfers between devices: 21.5 us -> 25.1 us  [taken(): return lax.ppermute(sent, axis, pairs).astype(f32)]
    ppermute x11, waiting for transfers between devices: 7.15 us -> 9.81 us  [from_core(): lax.ppermute(x, 'rep', [(i, i ^ 1) for i in range(lax.axis_size('rep'))])]
    pallas_call x1, Pallas kernels: 29.3 us -> 31.9 us  [layer(): pl.pallas_call(functools.partial(kernel, len(parts), 2 * len(groups)), in...]
    ppermute x16, waiting for transfers between devices: 23.1 us -> 20.8 us  [moved(): return lax.ppermute(x, ('rows', 'rep'), pairs)]
    convert_element_type x6 -> x4, other arithmetic: 5.02 us -> 3.46 us  [go(): sent = own.astype(bf16)]
    unnamed x25 -> x23, local copies, waits for them, and re-layouts: 5.11 us -> 4.3 us
  transfers between devices with their start and end apart: 33 -> 35, of which waited for: 15 -> 14; matrix products, arithmetic and copies ran while one was open for 15% -> 13% of each run, Pallas kernels for 0% -> 0%
where the time goes in v12:
time: 185 us; the launch traced here: 184 us
  starting transfers between devices  58.4 us (32%)
  waiting for transfers between devices  55.8 us (30%)
  Pallas kernels  31.9 us (17%)
  other arithmetic  24.6 us (13%)
  local copies, waits for them, and re-layouts  12.1 us (7%)
    pallas_call x1, Pallas kernels, layer(): pl.pallas_call(functools.partial(kernel, len(parts), 2 * len(groups)), in...  31.9 us
    ppermute x8, waiting for transfers between devices, taken(): return lax.ppermute(sent, axis, pairs).astype(f32)  25.1 us
    ppermute x16, starting transfers between devices, moved(): return lax.ppermute(x, ('rows', 'rep'), pairs)  24.2 us
    ppermute x11, starting transfers between devices, from_core(): lax.ppermute(x, 'rep', [(i, i ^ 1) for i in range(lax.axis_size('rep'))])  23.1 us
    ppermute x16, waiting for transfers between devices, moved(): return lax.ppermute(x, ('rows', 'rep'), pairs)  20.8 us
    convert_element_type x4, other arithmetic, total(): return sum((x.astype(f32) for x in terms)).astype(bf16)  11.7 us
    ppermute x8, starting transfers between devices, taken(): return lax.ppermute(sent, axis, pairs).astype(f32)  11.1 us
    ppermute x11, waiting for transfers between devices, from_core(): lax.ppermute(x, 'rep', [(i, i ^ 1) for i in range(lax.axis_size('rep'))])  9.81 us
  transfers between devices with their start and end apart: 35, of which 14 were waited for; matrix products, arithmetic and copies ran while one was open for 13% of the time, Pallas kernels for 0%

profile of v12, /device:TPU:0, one launch (start us, length us, event | category | flops | bytes accessed | tf_op | source)
XLA Modules:
  0.0 183.6 jit_solution(5952659154079044355)
XLA Ops:
  0.6 2.1 %collective-permute-start = (bf16[1024,256]{1,0:T(8,128)(2,1)}, bf16[1024,256]{1,0:T(8,128)(2,1)S(1)}, u32[]{:S(2)}, u32[]{:S(2)}) collective-permute-start(bf16[1024,256]{1,0:T(8,128)(2,1)} %param.7), channel_id=1, source_target_pairs={{120,0},{3,1},{122,2},{5,3},{124,4},{7,5},{126,6},{1,7},{0,8},{11,... | collective-permute-start | bytes 1572872 | tf_op jit(solution)/shard_map/ppermute | solution.py:194
  2.7 4.4 %collective-permute-start.1 = (bf16[1024,256]{1,0:T(8,128)(2,1)}, bf16[1024,256]{1,0:T(8,128)(2,1)S(1)}, u32[]{:S(2)}, u32[]{:S(2)}) collective-permute-start(bf16[1024,256]{1,0:T(8,128)(2,1)} %param.7), channel_id=1, source_target_pairs={{8,0},{7,1},{10,2},{1,3},{12,4},{3,5},{14,6},{5,7},{16,8},{15,9},{... | collective-permute-start | bytes 1572872 | tf_op jit(solution)/shard_map/ppermute | solution.py:194
  7.1 1.9 %constant_dynamic-update-slice_fusion.2 = bf16[3072,256]{1,0:T(8,128)(2,1)} fusion(bf16[1024,256]{1,0:T(8,128)(2,1)} %param.7), kind=kLoop, calls=%fused_computation.25 | loop fusion | bytes 1048576
  9.0 5.3 %collective-permute-done = bf16[1024,256]{1,0:T(8,128)(2,1)S(1)} collective-permute-done((bf16[1024,256]{1,0:T(8,128)(2,1)}, bf16[1024,256]{1,0:T(8,128)(2,1)S(1)}, u32[]{:S(2)}, u32[]{:S(2)}) %collective-permute-start) | collective-permute-done | bytes 524320 | tf_op jit(solution)/shard_map/ppermute | solution.py:194
  22.4 15.5 %collective-permute-start.6 = (bf16[1024,256]{1,0:T(8,128)(2,1)}, bf16[1024,256]{1,0:T(8,128)(2,1)}, u32[]{:S(2)}, u32[]{:S(2)}) collective-permute-start(bf16[1024,256]{1,0:T(8,128)(2,1)} %get-tuple-element.33.refs_4_), channel_id=1, source_target_pairs={{0,1},{1,0},{2,3},{3,2},{4,5},{5,4},{6,7},{7,6},{8,9},{9,8},{10,11... | collective-permute-start | bytes 1572872 | tf_op jit(solution)/shard_map/ppermute | solution.py:203
  42.3 3.0 %slice_select_fusion = (bf16[1536,256]{1,0:T(8,128)(2,1)}, bf16[1536,256]{1,0:T(8,128)(2,1)}) fusion(bf16[1536,256]{1,0:T(8,128)(2,1)} %constant_dynamic-update-slice_fusion.3, bf16[3072,256]{1,0:T(8,128)(2,1)S(1)} %collective-permute-done.8.refs_3_, pred[]{:T(512)S(6)} %eq.33, bf16[3072,256]{1,0:T(8,128)(2,1)S(1)} %collective-permute-done.2.refs_2_), kind=kLoop, calls=%fused_computation.7 | loop fusion | flops 786432 | bytes 3932161 | tf_op jit(solution)/shard_map/jit(_where)/select_n | solution.py:217
  48.4 3.4 %collective-permute-start.12 = (bf16[3072,256]{1,0:T(8,128)(2,1)S(1)}, bf16[3072,256]{1,0:T(8,128)(2,1)}, u32[]{:S(2)}, u32[]{:S(2)}) collective-permute-start(bf16[3072,256]{1,0:T(8,128)(2,1)S(1)} %collective-permute-done.2.refs_2_), channel_id=1, source_target_pairs={{0,1},{1,0},{2,3},{3,2},{4,5},{5,4},{6,7},{7,6},{8,9},{9,8},{10,11... | collective-permute-start | bytes 4718600 | tf_op jit(solution)/shard_map/ppermute | solution.py:203
  51.8 5.9 %collective-permute-done.7.refs_0_ = bf16[1536,256]{1,0:T(8,128)(2,1)} collective-permute-done((bf16[1536,256]{1,0:T(8,128)(2,1)}, bf16[1536,256]{1,0:T(8,128)(2,1)}, u32[]{:S(2)}, u32[]{:S(2)}) %collective-permute-start.7) | collective-permute-done | bytes 786464 | tf_op jit(solution)/shard_map/ppermute | solution.py:194
  57.7 3.5 %collective-permute-start.10 = (bf16[1536,256]{1,0:T(8,128)(2,1)}, bf16[1536,256]{1,0:T(8,128)(2,1)}, u32[]{:S(2)}, u32[]{:S(2)}) collective-permute-start(bf16[1536,256]{1,0:T(8,128)(2,1)} %collective-permute-done.7.refs_0_), channel_id=1, source_target_pairs={{0,1},{1,0},{2,3},{3,2},{4,5},{5,4},{6,7},{7,6},{8,9},{9,8},{10,11... | collective-permute-start | bytes 2359304 | tf_op jit(solution)/shard_map/ppermute | solution.py:203
  64.6 31.9 %shard_map.95 = (bf16[1024,256]{1,0:T(8,128)(2,1)}, f32[256,256]{1,0:T(8,128)}, bf16[24,256,128]{2,1,0:T(8,128)(2,1)}, bf16[48,256,128]{2,1,0:T(8,128)(2,1)}, bf...) custom-call(s32[8,48]{1,0:T(8,128)} %fusion.3.idx, ...), custom_call_target="tpu_custom_call" | custom-call | flops 6442450944 | bytes 37748736 | tf_op jit(solution)/shard_map/pallas_call | solution.py:141
  96.6 3.6 %collective-permute-done.14 = bf16[24,256,128]{2,1,0:T(8,128)(2,1)S(1)} collective-permute-done((bf16[24,256,128]{2,1,0:T(8,128)(2,1)}, bf16[24,256,128]{2,1,0:T(8,128)(2,1)S(1)}, u32[]{:S(2)}, u32[]{:S(2)}) %collective-permute-start.14) | collective-permute-done | bytes 1572896 | tf_op jit(solution)/shard_map/ppermute | solution.py:203
  100.2 1.9 %add_convert_fusion.2 = bf16[24,256,128]{2,1,0:T(8,128)(2,1)S(1)} fusion(bf16[24,256,128]{2,1,0:T(8,128)(2,1)S(1)} %collective-permute-done.14, bf16[24,256,128]{2,1,0:T(8,128)(2,1)} %get-tuple-element.14), kind=kLoop, calls=%fused_computation.2 | loop fusion | flops 3145728 | bytes 4718592 | tf_op jit(solution)/shard_map/convert_element_type | solution.py:261
  104.3 2.3 %collective-permute-start.21 = (bf16[12,256,128]{2,1,0:T(8,128)(2,1)S(1)}, bf16[12,256,128]{2,1,0:T(8,128)(2,1)S(1)}, u32[]{:S(2)}, u32[]{:S(2)}) collective-permute-start(bf16[12,256,128]{2,1,0:T(8,128)(2,1)S(1)} %get-tuple-element.28), channel_id=1, source_target_pairs={{0,6},{1,9},{2,0},{3,11},{4,2},{5,13},{6,4},{7,15},{8,14},{9,17},{... | collective-permute-start | bytes 2359304 | tf_op jit(solution)/shard_map/ppermute | solution.py:194
  106.8 1.9 %collective-permute-done.18.refs_0_ = f32[128,256]{1,0:T(8,128)S(1)} collective-permute-done((f32[128,256]{1,0:T(8,128)S(1)}, f32[128,256]{1,0:T(8,128)S(1)}, u32[]{:S(2)}, u32[]{:S(2)}) %collective-permute-start.18) | collective-permute-done | bytes 131104 | tf_op jit(solution)/shard_map/ppermute | solution.py:203
  111.3 6.4 %collective-permute-done.19 = bf16[128,256]{1,0:T(8,128)(2,1)S(1)} collective-permute-done((bf16[128,256]{1,0:T(8,128)(2,1)S(1)}, bf16[128,256]{1,0:T(8,128)(2,1)S(1)}, u32[]{:S(2)}, u32[]{:S(2)}) %collective-permute-start.19) | collective-permute-done | bytes 65568 | tf_op jit(solution)/shard_map/ppermute | solution.py:243
  120.2 4.8 %add_convert_fusion.1 = (bf16[24,256,128]{2,1,0:T(8,128)(2,1)}, bf16[24,256,128]{2,1,0:T(8,128)(2,1)}) fusion(bf16[48,256,128]{2,1,0:T(8,128)(2,1)} %collective-permute-done.16, bf16[12,256,128]{2,1,0:T(8,128)(2,1)S(1)} %collective-permute-done.17, bf16[48,256,128]{2,1,0:T(8,128)(2,1)} %get-tuple-element.16, pred[]{:T(512)S(6)} %eq.33, ...), kind=kLoop, calls=%fused_computation.1 | loop fusion | flops 11010048 | bytes 11010049 | tf_op jit(solution)/shard_map/convert_element_type | solution.py:261
  125.0 3.2 %collective-permute-start.22 = (bf16[24,256,128]{2,1,0:T(8,128)(2,1)}, bf16[24,256,128]{2,1,0:T(8,128)(2,1)}, u32[]{:S(2)}, u32[]{:S(2)}) collective-permute-start(bf16[24,256,128]{2,1,0:T(8,128)(2,1)} %get-tuple-element.26), channel_id=1, source_target_pairs={{0,6},{1,9},{2,0},{3,11},{4,2},{5,13},{6,4},{7,15},{8,14},{9,17},{... | collective-permute-start | bytes 4718600 | tf_op jit(solution)/shard_map/ppermute | solution.py:194
  135.0 3.3 %collective-permute-start.26 = (bf16[128,256]{1,0:T(8,128)(2,1)S(1)}, bf16[128,256]{1,0:T(8,128)(2,1)S(1)}, u32[]{:S(2)}, u32[]{:S(2)}) collective-permute-start(bf16[128,256]{1,0:T(8,128)(2,1)S(1)} %reduce-precision_convert_fusion), channel_id=1, source_target_pairs={{0,8},{8,0},{16,24},{24,16},{32,40},{40,32},{48,56},{56,48},{64,72... | collective-permute-start | bytes 196616 | tf_op jit(solution)/shard_map/ppermute | solution.py:243
  138.3 15.5 %collective-permute-done.28 = bf16[128,256]{1,0:T(8,128)(2,1)S(1)} collective-permute-done((bf16[128,256]{1,0:T(8,128)(2,1)S(1)}, bf16[128,256]{1,0:T(8,128)(2,1)S(1)}, u32[]{:S(2)}, u32[]{:S(2)}) %collective-permute-start.28) | collective-permute-done | bytes 65568 | tf_op jit(solution)/shard_map/ppermute | solution.py:243
  154.9 4.0 %collective-permute-start.29 = (bf16[128,256]{1,0:T(8,128)(2,1)S(1)}, bf16[128,256]{1,0:T(8,128)(2,1)S(1)}, u32[]{:S(2)}, u32[]{:S(2)}) collective-permute-start(bf16[128,256]{1,0:T(8,128)(2,1)S(1)} %fusion.21), channel_id=1, source_target_pairs={{0,32},{8,40},{16,48},{24,56},{32,0},{40,8},{48,16},{56,24},{64,96... | collective-permute-start | bytes 196616 | tf_op jit(solution)/shard_map/ppermute | solution.py:243
  158.9 2.6 %collective-permute-done.31 = bf16[128,256]{1,0:T(8,128)(2,1)S(1)} collective-permute-done((bf16[128,256]{1,0:T(8,128)(2,1)S(1)}, bf16[128,256]{1,0:T(8,128)(2,1)S(1)}, u32[]{:S(2)}, u32[]{:S(2)}) %collective-permute-start.31) | collective-permute-done | bytes 65568 | tf_op jit(solution)/shard_map/ppermute | solution.py:243
  163.8 3.4 %add_convert_fusion.5 = (bf16[8,256,128]{2,1,0:T(8,128)(2,1)}, bf16[8,256,128]{2,1,0:T(8,128)(2,1)S(1)}) fusion(bf16[24,256,128]{2,1,0:T(8,128)(2,1)} %collective-permute-done.22, bf16[24,256,128]{2,1,0:T(8,128)(2,1)} %collective-permute-done.20, bf16[32,256,128]{2,1,0:T(8,128)(2,1)} %collective-permute-done.15, ...), kind=kLoop, calls=%fused_computation.5 | loop fusion | flops 5242880 | bytes 5767168 | tf_op jit(solution)/shard_map/convert_element_type | solution.py:261
  171.2 5.3 %collective-permute-done.32 = bf16[8,256,128]{2,1,0:T(8,128)(2,1)S(1)} collective-permute-done((bf16[8,256,128]{2,1,0:T(8,128)(2,1)}, bf16[8,256,128]{2,1,0:T(8,128)(2,1)S(1)}, u32[]{:S(2)}, u32[]{:S(2)}) %collective-permute-start.32) | collective-permute-done | bytes 524320 | tf_op jit(solution)/shard_map/ppermute | solution.py:194
  176.5 4.3 %collective-permute-done.33 = bf16[8,256,128]{2,1,0:T(8,128)(2,1)S(1)} collective-permute-done((bf16[8,256,128]{2,1,0:T(8,128)(2,1)S(1)}, bf16[8,256,128]{2,1,0:T(8,128)(2,1)S(1)}, u32[]{:S(2)}, u32[]{:S(2)}) %collective-permute-start.33) | collective-permute-done | bytes 524320 | tf_op jit(solution)/shard_map/ppermute | solution.py:194
  (108 shorter events, 43.2 us)
Async XLA Ops:
  0.6 13.8 %collective-permute-start = (bf16[1024,256]{1,0:T(8,128)(2,1)}, bf16[1024,256]{1,0:T(8,128)(2,1)S(1)}, u32[]{:S(2)}, u32[]{:S(2)}) collective-permute-start(bf16[1024,256]{1,0:T(8,128)(2,1)} %param.7), channel_id=1, source_target_pairs={{120,0},{3,1},{122,2},{5,3},{124,4},{7,5},{126,6},{1,7},{0,8},{11,... | collective-permute-start | bytes 1572872 | tf_op jit(solution)/shard_map/ppermute | solution.py:194
  2.7 12.5 %collective-permute-start.1 = (bf16[1024,256]{1,0:T(8,128)(2,1)}, bf16[1024,256]{1,0:T(8,128)(2,1)S(1)}, u32[]{:S(2)}, u32[]{:S(2)}) collective-permute-start(bf16[1024,256]{1,0:T(8,128)(2,1)} %param.7), channel_id=1, source_target_pairs={{8,0},{7,1},{10,2},{1,3},{12,4},{3,5},{14,6},{5,7},{16,8},{15,9},{... | collective-permute-start | bytes 1572872 | tf_op jit(solution)/shard_map/ppermute | solution.py:194
  16.1 25.0 %collective-permute-start.5 = (bf16[3072,256]{1,0:T(8,128)(2,1)}, bf16[3072,256]{1,0:T(8,128)(2,1)}, u32[]{:S(2)}, u32[]{:S(2)}) collective-permute-start(bf16[3072,256]{1,0:T(8,128)(2,1)} %constant_dynamic-update-slice_fusion.refs_5_), channel_id=1, source_target_pairs={{0,1},{1,0},{2,3},{3,2},{4,5},{5,4},{6,7},{7,6},{8,9},{9,8},{10,11... | collective-permute-start | bytes 4718600 | tf_op jit(solution)/shard_map/ppermute | solution.py:203
  16.1 26.2 %collective-permute-start.8 = (bf16[3072,256]{1,0:T(8,128)(2,1)}, bf16[3072,256]{1,0:T(8,128)(2,1)S(1)}, u32[]{:S(2)}, u32[]{:S(2)}) collective-permute-start(bf16[3072,256]{1,0:T(8,128)(2,1)} %constant_dynamic-update-slice_fusion.refs_5_), channel_id=1, source_target_pairs={{6,0},{9,1},{0,2},{11,3},{2,4},{13,5},{4,6},{15,7},{14,8},{17,9},{... | collective-permute-start | bytes 4718600 | tf_op jit(solution)/shard_map/ppermute | solution.py:194
  17.6 24.7 %collective-permute-start.2 = (bf16[3072,256]{1,0:T(8,128)(2,1)}, bf16[3072,256]{1,0:T(8,128)(2,1)S(1)}, u32[]{:S(2)}, u32[]{:S(2)}) collective-permute-start(bf16[3072,256]{1,0:T(8,128)(2,1)} %constant_dynamic-update-slice_fusion.refs_5_), channel_id=1, source_target_pairs={{2,0},{121,1},{4,2},{123,3},{6,4},{125,5},{0,6},{127,7},{10,8},{1,... | collective-permute-start | bytes 4718600 | tf_op jit(solution)/shard_map/ppermute | solution.py:194
  22.4 17.4 %collective-permute-start.6 = (bf16[1024,256]{1,0:T(8,128)(2,1)}, bf16[1024,256]{1,0:T(8,128)(2,1)}, u32[]{:S(2)}, u32[]{:S(2)}) collective-permute-start(bf16[1024,256]{1,0:T(8,128)(2,1)} %get-tuple-element.33.refs_4_), channel_id=1, source_target_pairs={{0,1},{1,0},{2,3},{3,2},{4,5},{5,4},{6,7},{7,6},{8,9},{9,8},{10,11... | collective-permute-start | bytes 1572872 | tf_op jit(solution)/shard_map/ppermute | solution.py:203
  45.4 12.4 %collective-permute-start.7 = (bf16[1536,256]{1,0:T(8,128)(2,1)}, bf16[1536,256]{1,0:T(8,128)(2,1)}, u32[]{:S(2)}, u32[]{:S(2)}) collective-permute-start(bf16[1536,256]{1,0:T(8,128)(2,1)} %shard_map.94), channel_id=1, source_target_pairs={{2,0},{121,1},{4,2},{123,3},{6,4},{125,5},{0,6},{127,7},{10,8},{1,... | collective-permute-start | bytes 2359304 | tf_op jit(solution)/shard_map/ppermute | solution.py:194
  47.0 15.8 %collective-permute-start.13 = (bf16[3072,256]{1,0:T(8,128)(2,1)S(1)}, bf16[3072,256]{1,0:T(8,128)(2,1)}, u32[]{:S(2)}, u32[]{:S(2)}) collective-permute-start(bf16[3072,256]{1,0:T(8,128)(2,1)S(1)} %collective-permute-done.8.refs_3_), channel_id=1, source_target_pairs={{0,1},{1,0},{2,3},{3,2},{4,5},{5,4},{6,7},{7,6},{8,9},{9,8},{10,11... | collective-permute-start | bytes 4718600 | tf_op jit(solution)/shard_map/ppermute | solution.py:203
  47.0 14.2 %collective-permute-start.9 = (bf16[1536,256]{1,0:T(8,128)(2,1)}, bf16[1536,256]{1,0:T(8,128)(2,1)}, u32[]{:S(2)}, u32[]{:S(2)}) collective-permute-start(bf16[1536,256]{1,0:T(8,128)(2,1)} %get-tuple-element.29), channel_id=1, source_target_pairs={{6,0},{9,1},{0,2},{11,3},{2,4},{13,5},{4,6},{15,7},{14,8},{17,9},{... | collective-permute-start | bytes 2359304 | tf_op jit(solution)/shard_map/ppermute | solution.py:194
  48.4 16.2 %collective-permute-start.12 = (bf16[3072,256]{1,0:T(8,128)(2,1)S(1)}, bf16[3072,256]{1,0:T(8,128)(2,1)}, u32[]{:S(2)}, u32[]{:S(2)}) collective-permute-start(bf16[3072,256]{1,0:T(8,128)(2,1)S(1)} %collective-permute-done.2.refs_2_), channel_id=1, source_target_pairs={{0,1},{1,0},{2,3},{3,2},{4,5},{5,4},{6,7},{7,6},{8,9},{9,8},{10,11... | collective-permute-start | bytes 4718600 | tf_op jit(solution)/shard_map/ppermute | solution.py:203
  102.7 17.5 %collective-permute-start.16 = (bf16[48,256,128]{2,1,0:T(8,128)(2,1)}, bf16[48,256,128]{2,1,0:T(8,128)(2,1)}, u32[]{:S(2)}, u32[]{:S(2)}) collective-permute-start(bf16[48,256,128]{2,1,0:T(8,128)(2,1)} %shard_map.97), channel_id=1, source_target_pairs={{0,1},{1,0},{2,3},{3,2},{4,5},{5,4},{6,7},{7,6},{8,9},{9,8},{10,11... | collective-permute-start | bytes 9437192 | tf_op jit(solution)/shard_map/ppermute | solution.py:203
  102.8 25.4 %collective-permute-start.15 = (bf16[32,256,128]{2,1,0:T(8,128)(2,1)}, bf16[32,256,128]{2,1,0:T(8,128)(2,1)}, u32[]{:S(2)}, u32[]{:S(2)}) collective-permute-start(bf16[32,256,128]{2,1,0:T(8,128)(2,1)} %shard_map.96), channel_id=1, source_target_pairs={{0,1},{1,0},{2,3},{3,2},{4,5},{5,4},{6,7},{7,6},{8,9},{9,8},{10,11... | collective-permute-start | bytes 6291464 | tf_op jit(solution)/shard_map/ppermute | solution.py:203
  103.3 16.8 %collective-permute-start.17 = (bf16[12,256,128]{2,1,0:T(8,128)(2,1)S(1)}, bf16[12,256,128]{2,1,0:T(8,128)(2,1)S(1)}, u32[]{:S(2)}, u32[]{:S(2)}) collective-permute-start(bf16[12,256,128]{2,1,0:T(8,128)(2,1)S(1)} %get-tuple-element.27), channel_id=1, source_target_pairs={{0,2},{1,121},{2,4},{3,123},{4,6},{5,125},{6,0},{7,127},{8,10},{9,... | collective-permute-start | bytes 2359304 | tf_op jit(solution)/shard_map/ppermute | solution.py:194
  104.3 15.8 %collective-permute-start.21 = (bf16[12,256,128]{2,1,0:T(8,128)(2,1)S(1)}, bf16[12,256,128]{2,1,0:T(8,128)(2,1)S(1)}, u32[]{:S(2)}, u32[]{:S(2)}) collective-permute-start(bf16[12,256,128]{2,1,0:T(8,128)(2,1)S(1)} %get-tuple-element.28), channel_id=1, source_target_pairs={{0,6},{1,9},{2,0},{3,11},{4,2},{5,13},{6,4},{7,15},{8,14},{9,17},{... | collective-permute-start | bytes 2359304 | tf_op jit(solution)/shard_map/ppermute | solution.py:194
  110.3 7.4 %collective-permute-start.19 = (bf16[128,256]{1,0:T(8,128)(2,1)S(1)}, bf16[128,256]{1,0:T(8,128)(2,1)S(1)}, u32[]{:S(2)}, u32[]{:S(2)}) collective-permute-start(bf16[128,256]{1,0:T(8,128)(2,1)S(1)} %get-tuple-element.21), channel_id=1, source_target_pairs={{0,2},{1,3},{2,0},{3,1},{4,6},{5,7},{6,4},{7,5},{8,10},{9,11},{10,... | collective-permute-start | bytes 196616 | tf_op jit(solution)/shard_map/ppermute | solution.py:243
  118.4 13.0 %collective-permute-start.24 = (bf16[128,256]{1,0:T(8,128)(2,1)S(1)}, bf16[128,256]{1,0:T(8,128)(2,1)S(1)}, u32[]{:S(2)}, u32[]{:S(2)}) collective-permute-start(bf16[128,256]{1,0:T(8,128)(2,1)S(1)} %get-tuple-element.19), channel_id=1, source_target_pairs={{0,4},{1,5},{2,6},{3,7},{4,0},{5,1},{6,2},{7,3},{8,12},{9,13},{10,... | collective-permute-start | bytes 196616 | tf_op jit(solution)/shard_map/ppermute | solution.py:243
  125.0 38.8 %collective-permute-start.20 = (bf16[24,256,128]{2,1,0:T(8,128)(2,1)}, bf16[24,256,128]{2,1,0:T(8,128)(2,1)}, u32[]{:S(2)}, u32[]{:S(2)}) collective-permute-start(bf16[24,256,128]{2,1,0:T(8,128)(2,1)} %shard_map.99), channel_id=1, source_target_pairs={{0,2},{1,121},{2,4},{3,123},{4,6},{5,125},{6,0},{7,127},{8,10},{9,... | collective-permute-start | bytes 4718600 | tf_op jit(solution)/shard_map/ppermute | solution.py:194
  125.0 38.8 %collective-permute-start.22 = (bf16[24,256,128]{2,1,0:T(8,128)(2,1)}, bf16[24,256,128]{2,1,0:T(8,128)(2,1)}, u32[]{:S(2)}, u32[]{:S(2)}) collective-permute-start(bf16[24,256,128]{2,1,0:T(8,128)(2,1)} %get-tuple-element.26), channel_id=1, source_target_pairs={{0,6},{1,9},{2,0},{3,11},{4,2},{5,13},{6,4},{7,15},{8,14},{9,17},{... | collective-permute-start | bytes 4718600 | tf_op jit(solution)/shard_map/ppermute | solution.py:194
  134.1 19.7 %collective-permute-start.28 = (bf16[128,256]{1,0:T(8,128)(2,1)S(1)}, bf16[128,256]{1,0:T(8,128)(2,1)S(1)}, u32[]{:S(2)}, u32[]{:S(2)}) collective-permute-start(bf16[128,256]{1,0:T(8,128)(2,1)S(1)} %reduce-precision_convert_fusion), channel_id=1, source_target_pairs={{0,24},{8,16},{16,8},{24,0},{32,56},{40,48},{48,40},{56,32},{64,88... | collective-permute-start | bytes 196616 | tf_op jit(solution)/shard_map/ppermute | solution.py:243
  134.4 19.4 %collective-permute-start.27 = (bf16[128,256]{1,0:T(8,128)(2,1)S(1)}, bf16[128,256]{1,0:T(8,128)(2,1)S(1)}, u32[]{:S(2)}, u32[]{:S(2)}) collective-permute-start(bf16[128,256]{1,0:T(8,128)(2,1)S(1)} %reduce-precision_convert_fusion), channel_id=1, source_target_pairs={{0,16},{8,24},{16,0},{24,8},{32,48},{40,56},{48,32},{56,40},{64,80... | collective-permute-start | bytes 196616 | tf_op jit(solution)/shard_map/ppermute | solution.py:243
  135.0 18.8 %collective-permute-start.26 = (bf16[128,256]{1,0:T(8,128)(2,1)S(1)}, bf16[128,256]{1,0:T(8,128)(2,1)S(1)}, u32[]{:S(2)}, u32[]{:S(2)}) collective-permute-start(bf16[128,256]{1,0:T(8,128)(2,1)S(1)} %reduce-precision_convert_fusion), channel_id=1, source_target_pairs={{0,8},{8,0},{16,24},{24,16},{32,40},{40,32},{48,56},{56,48},{64,72... | collective-permute-start | bytes 196616 | tf_op jit(solution)/shard_map/ppermute | solution.py:243
  154.9 7.2 %collective-permute-start.29 = (bf16[128,256]{1,0:T(8,128)(2,1)S(1)}, bf16[128,256]{1,0:T(8,128)(2,1)S(1)}, u32[]{:S(2)}, u32[]{:S(2)}) collective-permute-start(bf16[128,256]{1,0:T(8,128)(2,1)S(1)} %fusion.21), channel_id=1, source_target_pairs={{0,32},{8,40},{16,48},{24,56},{32,0},{40,8},{48,16},{56,24},{64,96... | collective-permute-start | bytes 196616 | tf_op jit(solution)/shard_map/ppermute | solution.py:243
  167.1 9.4 %collective-permute-start.32 = (bf16[8,256,128]{2,1,0:T(8,128)(2,1)}, bf16[8,256,128]{2,1,0:T(8,128)(2,1)S(1)}, u32[]{:S(2)}, u32[]{:S(2)}) collective-permute-start(bf16[8,256,128]{2,1,0:T(8,128)(2,1)} %shard_map.101), channel_id=1, source_target_pairs={{0,120},{1,3},{2,122},{3,5},{4,124},{5,7},{6,126},{7,1},{8,0},{9,1... | collective-permute-start | bytes 1572872 | tf_op jit(solution)/shard_map/ppermute | solution.py:194
  168.3 12.5 %collective-permute-start.33 = (bf16[8,256,128]{2,1,0:T(8,128)(2,1)S(1)}, bf16[8,256,128]{2,1,0:T(8,128)(2,1)S(1)}, u32[]{:S(2)}, u32[]{:S(2)}) collective-permute-start(bf16[8,256,128]{2,1,0:T(8,128)(2,1)S(1)} %get-tuple-element.24), channel_id=1, source_target_pairs={{0,8},{1,7},{2,10},{3,1},{4,12},{5,3},{6,14},{7,5},{8,16},{9,15},{... | collective-permute-start | bytes 1572872 | tf_op jit(solution)/shard_map/ppermute | solution.py:194
  (21 other events, 143.6 us)

commit v13 on v9

--- a/solution.py
+++ b/solution.py
@@ -10,7 +10,7 @@
 
 bf16, f32 = jnp.bfloat16, jnp.float32
 
-FWD_SLOTS = 24
+FWD_SLOTS = 48
 BWD_SLOTS = 24
 STAGES = 8
 CHUNK = 8

time: 179 us -> 178 us (level)
  starting transfers between devices: 64.6 us -> 59.2 us
  Pallas kernels: 28 us -> 31.9 us
    ppermute x16, starting transfers between devices: 29.3 us -> 25.3 us  [moved(): return lax.ppermute(x, ('rows', 'rep'), pairs)]
    pallas_call x1, Pallas kernels: 28 us -> 31.9 us  [layer(): pl.pallas_call(functools.partial(kernel, len(parts), 2 * len(groups)), in...]
    ppermute x11, waiting for transfers between devices: 8.31 us -> 11.7 us  [from_core(): lax.ppermute(x, 'rep', [(i, i ^ 1) for i in range(lax.axis_size('rep'))])]
    ppermute x6, waiting for transfers between devices: 23.7 us -> 20.9 us  [go(): lax.ppermute(rounded.astype(bf16), axis, pairs).astype(f32)]
  transfers between devices with their start and end apart: 33 -> 33, of which waited for: 14 -> 13; matrix products, arithmetic and copies ran while one was open for 15% -> 15% of each run, Pallas kernels for 0% -> 0%
where the time goes in v13:
time: 178 us; the launch traced here: 176 us
  starting transfers between devices  59.2 us (33%)
  waiting for transfers between devices  48.2 us (27%)
  Pallas kernels  31.9 us (18%)
  other arithmetic  24.4 us (14%)
  local copies, waits for them, and re-layouts  11.5 us (6%)
    pallas_call x1, Pallas kernels, layer(): pl.pallas_call(functools.partial(kernel, len(parts), 2 * len(groups)), in...  31.9 us
    ppermute x11, starting transfers between devices, from_core(): lax.ppermute(x, 'rep', [(i, i ^ 1) for i in range(lax.axis_size('rep'))])  29.5 us
    ppermute x16, starting transfers between devices, moved(): return lax.ppermute(x, ('rows', 'rep'), pairs)  25.3 us
    ppermute x6, waiting for transfers between devices, go(): lax.ppermute(rounded.astype(bf16), axis, pairs).astype(f32)  20.9 us
    ppermute x16, waiting for transfers between devices, moved(): return lax.ppermute(x, ('rows', 'rep'), pairs)  15.7 us
    ppermute x11, waiting for transfers between devices, from_core(): lax.ppermute(x, 'rep', [(i, i ^ 1) for i in range(lax.axis_size('rep'))])  11.7 us
    convert_element_type x4, other arithmetic, total(): return sum((x.astype(f32) for x in terms)).astype(bf16)  10.8 us
    convert_element_type x6, other arithmetic, go(): rounded.astype(bf16)  5.08 us
  transfers between devices with their start and end apart: 33, of which 13 were waited for; matrix products, arithmetic and copies ran while one was open for 15% of the time, Pallas kernels for 0%

profile of v13, /device:TPU:0, one launch (start us, length us, event | category | flops | bytes accessed | tf_op | source)
XLA Modules:
  0.0 176.1 jit_solution(2571126276847842164)
XLA Ops:
  0.6 2.1 %collective-permute-start = (bf16[1024,256]{1,0:T(8,128)(2,1)}, bf16[1024,256]{1,0:T(8,128)(2,1)S(1)}, u32[]{:S(2)}, u32[]{:S(2)}) collective-permute-start(bf16[1024,256]{1,0:T(8,128)(2,1)} %param.7), channel_id=1, source_target_pairs={{120,0},{3,1},{122,2},{5,3},{124,4},{7,5},{126,6},{1,7},{0,8},{11,... | collective-permute-start | bytes 1572872 | tf_op jit(solution)/shard_map/ppermute | solution.py:194
  2.7 4.4 %collective-permute-start.1 = (bf16[1024,256]{1,0:T(8,128)(2,1)}, bf16[1024,256]{1,0:T(8,128)(2,1)S(1)}, u32[]{:S(2)}, u32[]{:S(2)}) collective-permute-start(bf16[1024,256]{1,0:T(8,128)(2,1)} %param.7), channel_id=1, source_target_pairs={{8,0},{7,1},{10,2},{1,3},{12,4},{3,5},{14,6},{5,7},{16,8},{15,9},{... | collective-permute-start | bytes 1572872 | tf_op jit(solution)/shard_map/ppermute | solution.py:194
  7.1 1.9 %constant_dynamic-update-slice_fusion.2 = bf16[3072,256]{1,0:T(8,128)(2,1)} fusion(bf16[1024,256]{1,0:T(8,128)(2,1)} %param.7), kind=kLoop, calls=%fused_computation.30 | loop fusion | bytes 1048576
  9.0 5.4 %collective-permute-done = bf16[1024,256]{1,0:T(8,128)(2,1)S(1)} collective-permute-done((bf16[1024,256]{1,0:T(8,128)(2,1)}, bf16[1024,256]{1,0:T(8,128)(2,1)S(1)}, u32[]{:S(2)}, u32[]{:S(2)}) %collective-permute-start) | collective-permute-done | bytes 524320 | tf_op jit(solution)/shard_map/ppermute | solution.py:194
  22.4 15.5 %collective-permute-start.6 = (bf16[1024,256]{1,0:T(8,128)(2,1)}, bf16[1024,256]{1,0:T(8,128)(2,1)}, u32[]{:S(2)}, u32[]{:S(2)}) collective-permute-start(bf16[1024,256]{1,0:T(8,128)(2,1)} %get-tuple-element.35.refs_4_), channel_id=1, source_target_pairs={{0,1},{1,0},{2,3},{3,2},{4,5},{5,4},{6,7},{7,6},{8,9},{9,8},{10,11... | collective-permute-start | bytes 1572872 | tf_op jit(solution)/shard_map/ppermute | solution.py:203
  42.3 3.0 %slice_select_fusion = (bf16[1536,256]{1,0:T(8,128)(2,1)}, bf16[1536,256]{1,0:T(8,128)(2,1)}) fusion(bf16[1536,256]{1,0:T(8,128)(2,1)} %constant_dynamic-update-slice_fusion.3, bf16[3072,256]{1,0:T(8,128)(2,1)S(1)} %collective-permute-done.8.refs_3_, pred[]{:T(512)S(6)} %eq.33, bf16[3072,256]{1,0:T(8,128)(2,1)S(1)} %collective-permute-done.2.refs_2_), kind=kLoop, calls=%fused_computation.7 | loop fusion | flops 786432 | bytes 3932161 | tf_op jit(solution)/shard_map/jit(_where)/select_n | solution.py:217
  48.4 3.4 %collective-permute-start.12 = (bf16[3072,256]{1,0:T(8,128)(2,1)S(1)}, bf16[3072,256]{1,0:T(8,128)(2,1)}, u32[]{:S(2)}, u32[]{:S(2)}) collective-permute-start(bf16[3072,256]{1,0:T(8,128)(2,1)S(1)} %collective-permute-done.2.refs_2_), channel_id=1, source_target_pairs={{0,1},{1,0},{2,3},{3,2},{4,5},{5,4},{6,7},{7,6},{8,9},{9,8},{10,11... | collective-permute-start | bytes 4718600 | tf_op jit(solution)/shard_map/ppermute | solution.py:203
  51.8 5.9 %collective-permute-done.7.refs_0_ = bf16[1536,256]{1,0:T(8,128)(2,1)} collective-permute-done((bf16[1536,256]{1,0:T(8,128)(2,1)}, bf16[1536,256]{1,0:T(8,128)(2,1)}, u32[]{:S(2)}, u32[]{:S(2)}) %collective-permute-start.7) | collective-permute-done | bytes 786464 | tf_op jit(solution)/shard_map/ppermute | solution.py:194
  57.7 3.5 %collective-permute-start.10 = (bf16[1536,256]{1,0:T(8,128)(2,1)}, bf16[1536,256]{1,0:T(8,128)(2,1)}, u32[]{:S(2)}, u32[]{:S(2)}) collective-permute-start(bf16[1536,256]{1,0:T(8,128)(2,1)} %collective-permute-done.7.refs_0_), channel_id=1, source_target_pairs={{0,1},{1,0},{2,3},{3,2},{4,5},{5,4},{6,7},{7,6},{8,9},{9,8},{10,11... | collective-permute-start | bytes 2359304 | tf_op jit(solution)/shard_map/ppermute | solution.py:203
  64.6 31.9 %shard_map.95 = (bf16[1024,256]{1,0:T(8,128)(2,1)}, f32[256,256]{1,0:T(8,128)}, bf16[24,256,128]{2,1,0:T(8,128)(2,1)}, bf16[48,256,128]{2,1,0:T(8,128)(2,1)}, bf...) custom-call(s32[8,48]{1,0:T(8,128)} %fusion.5.idx, ...), custom_call_target="tpu_custom_call" | custom-call | flops 6442450944 | bytes 37748736 | tf_op jit(solution)/shard_map/pallas_call | solution.py:141
  96.6 3.6 %collective-permute-done.14 = bf16[24,256,128]{2,1,0:T(8,128)(2,1)S(1)} collective-permute-done((bf16[24,256,128]{2,1,0:T(8,128)(2,1)}, bf16[24,256,128]{2,1,0:T(8,128)(2,1)S(1)}, u32[]{:S(2)}, u32[]{:S(2)}) %collective-permute-start.14) | collective-permute-done | bytes 1572896 | tf_op jit(solution)/shard_map/ppermute | solution.py:203
  100.2 1.9 %add_convert_fusion.2 = bf16[24,256,128]{2,1,0:T(8,128)(2,1)S(1)} fusion(bf16[24,256,128]{2,1,0:T(8,128)(2,1)S(1)} %collective-permute-done.14, bf16[24,256,128]{2,1,0:T(8,128)(2,1)} %get-tuple-element.14), kind=kLoop, calls=%fused_computation.2 | loop fusion | flops 3145728 | bytes 4718592 | tf_op jit(solution)/shard_map/convert_element_type | solution.py:258
  107.6 4.2 %collective-permute-done.18 = f32[128,256]{1,0:T(8,128)S(1)} collective-permute-done((f32[128,256]{1,0:T(8,128)}, f32[128,256]{1,0:T(8,128)S(1)}, u32[]{:S(2)}, u32[]{:S(2)}) %collective-permute-start.18) | collective-permute-done | bytes 131104 | tf_op jit(solution)/shard_map/ppermute | solution.py:203
  113.4 5.1 %collective-permute-done.19 = bf16[128,256]{1,0:T(8,128)(2,1)S(1)} collective-permute-done((bf16[128,256]{1,0:T(8,128)(2,1)S(1)}, bf16[128,256]{1,0:T(8,128)(2,1)S(1)}, u32[]{:S(2)}, u32[]{:S(2)}) %collective-permute-start.19) | collective-permute-done | bytes 65568 | tf_op jit(solution)/shard_map/ppermute | solution.py:244
  119.2 2.1 %collective-permute-start.24 = (bf16[128,256]{1,0:T(8,128)(2,1)S(1)}, bf16[128,256]{1,0:T(8,128)(2,1)S(1)}, u32[]{:S(2)}, u32[]{:S(2)}) collective-permute-start(bf16[128,256]{1,0:T(8,128)(2,1)S(1)} %get-tuple-element.21), channel_id=1, source_target_pairs={{0,4},{1,5},{2,6},{3,7},{4,0},{5,1},{6,2},{7,3},{8,12},{9,13},{10,... | collective-permute-start | bytes 196616 | tf_op jit(solution)/shard_map/ppermute | solution.py:244
  123.0 4.0 %add_convert_fusion.1 = (bf16[24,256,128]{2,1,0:T(8,128)(2,1)}, bf16[24,256,128]{2,1,0:T(8,128)(2,1)}) fusion(bf16[48,256,128]{2,1,0:T(8,128)(2,1)} %collective-permute-done.16, bf16[12,256,128]{2,1,0:T(8,128)(2,1)S(1)} %collective-permute-done.17, bf16[48,256,128]{2,1,0:T(8,128)(2,1)S(1)} %copy-done.2, pred[]{:T(512)S(6)} %eq.33, ...), kind=kLoop, calls=%fused_computation.1 | loop fusion | flops 11010048 | bytes 11010049 | tf_op jit(solution)/shard_map/convert_element_type | solution.py:258
  127.1 3.2 %collective-permute-start.22 = (bf16[24,256,128]{2,1,0:T(8,128)(2,1)}, bf16[24,256,128]{2,1,0:T(8,128)(2,1)}, u32[]{:S(2)}, u32[]{:S(2)}) collective-permute-start(bf16[24,256,128]{2,1,0:T(8,128)(2,1)} %get-tuple-element.28), channel_id=1, source_target_pairs={{0,6},{1,9},{2,0},{3,11},{4,2},{5,13},{6,4},{7,15},{8,14},{9,17},{... | collective-permute-start | bytes 4718600 | tf_op jit(solution)/shard_map/ppermute | solution.py:194
  134.7 5.0 %collective-permute-done.26 = bf16[128,256]{1,0:T(8,128)(2,1)S(1)} collective-permute-done((bf16[128,256]{1,0:T(8,128)(2,1)S(1)}, bf16[128,256]{1,0:T(8,128)(2,1)S(1)}, u32[]{:S(2)}, u32[]{:S(2)}) %collective-permute-start.26) | collective-permute-done | bytes 65568 | tf_op jit(solution)/shard_map/ppermute | solution.py:244
  140.8 6.5 %collective-permute-done.27 = bf16[128,256]{1,0:T(8,128)(2,1)S(1)} collective-permute-done((bf16[128,256]{1,0:T(8,128)(2,1)S(1)}, bf16[128,256]{1,0:T(8,128)(2,1)S(1)}, u32[]{:S(2)}, u32[]{:S(2)}) %collective-permute-start.27) | collective-permute-done | bytes 65568 | tf_op jit(solution)/shard_map/ppermute | solution.py:244
  148.3 4.3 %collective-permute-done.28 = bf16[128,256]{1,0:T(8,128)(2,1)S(1)} collective-permute-done((bf16[128,256]{1,0:T(8,128)(2,1)S(1)}, bf16[128,256]{1,0:T(8,128)(2,1)S(1)}, u32[]{:S(2)}, u32[]{:S(2)}) %collective-permute-start.28) | collective-permute-done | bytes 65568 | tf_op jit(solution)/shard_map/ppermute | solution.py:244
  154.4 3.3 %add_convert_fusion.5 = (bf16[8,256,128]{2,1,0:T(8,128)(2,1)}, bf16[8,256,128]{2,1,0:T(8,128)(2,1)S(1)}) fusion(bf16[24,256,128]{2,1,0:T(8,128)(2,1)} %collective-permute-done.22, bf16[24,256,128]{2,1,0:T(8,128)(2,1)} %collective-permute-done.20, bf16[32,256,128]{2,1,0:T(8,128)(2,1)} %collective-permute-done.15, ...), kind=kLoop, calls=%fused_computation.5 | loop fusion | flops 5242880 | bytes 5767168 | tf_op jit(solution)/shard_map/convert_element_type | solution.py:258
  157.8 3.0 %collective-permute-start.29 = (bf16[8,256,128]{2,1,0:T(8,128)(2,1)}, bf16[8,256,128]{2,1,0:T(8,128)(2,1)S(1)}, u32[]{:S(2)}, u32[]{:S(2)}) collective-permute-start(bf16[8,256,128]{2,1,0:T(8,128)(2,1)} %shard_map.101), channel_id=1, source_target_pairs={{0,120},{1,3},{2,122},{3,5},{4,124},{5,7},{6,126},{7,1},{8,0},{9,1... | collective-permute-start | bytes 1572872 | tf_op jit(solution)/shard_map/ppermute | solution.py:194
  160.9 6.3 %collective-permute-start.32 = (f32[128,256]{1,0:T(8,128)S(1)}, f32[128,256]{1,0:T(8,128)S(1)}, u32[]{:S(2)}, u32[]{:S(2)}) collective-permute-start(f32[128,256]{1,0:T(8,128)S(1)} %convert_add_fusion), channel_id=1, source_target_pairs={{0,1},{1,0},{2,3},{3,2},{4,5},{5,4},{6,7},{7,6},{8,9},{9,8},{10,11... | collective-permute-start | bytes 393224 | tf_op jit(solution)/shard_map/ppermute | solution.py:203
  168.9 4.4 %collective-permute-done.30 = bf16[8,256,128]{2,1,0:T(8,128)(2,1)S(1)} collective-permute-done((bf16[8,256,128]{2,1,0:T(8,128)(2,1)S(1)}, bf16[8,256,128]{2,1,0:T(8,128)(2,1)S(1)}, u32[]{:S(2)}, u32[]{:S(2)}) %collective-permute-start.30) | collective-permute-done | bytes 524320 | tf_op jit(solution)/shard_map/ppermute | solution.py:194
  (106 shorter events, 41.3 us)
Async XLA Ops:
  0.6 13.8 %collective-permute-start = (bf16[1024,256]{1,0:T(8,128)(2,1)}, bf16[1024,256]{1,0:T(8,128)(2,1)S(1)}, u32[]{:S(2)}, u32[]{:S(2)}) collective-permute-start(bf16[1024,256]{1,0:T(8,128)(2,1)} %param.7), channel_id=1, source_target_pairs={{120,0},{3,1},{122,2},{5,3},{124,4},{7,5},{126,6},{1,7},{0,8},{11,... | collective-permute-start | bytes 1572872 | tf_op jit(solution)/shard_map/ppermute | solution.py:194
  2.7 12.5 %collective-permute-start.1 = (bf16[1024,256]{1,0:T(8,128)(2,1)}, bf16[1024,256]{1,0:T(8,128)(2,1)S(1)}, u32[]{:S(2)}, u32[]{:S(2)}) collective-permute-start(bf16[1024,256]{1,0:T(8,128)(2,1)} %param.7), channel_id=1, source_target_pairs={{8,0},{7,1},{10,2},{1,3},{12,4},{3,5},{14,6},{5,7},{16,8},{15,9},{... | collective-permute-start | bytes 1572872 | tf_op jit(solution)/shard_map/ppermute | solution.py:194
  16.1 25.0 %collective-permute-start.5 = (bf16[3072,256]{1,0:T(8,128)(2,1)}, bf16[3072,256]{1,0:T(8,128)(2,1)}, u32[]{:S(2)}, u32[]{:S(2)}) collective-permute-start(bf16[3072,256]{1,0:T(8,128)(2,1)} %constant_dynamic-update-slice_fusion.refs_5_), channel_id=1, source_target_pairs={{0,1},{1,0},{2,3},{3,2},{4,5},{5,4},{6,7},{7,6},{8,9},{9,8},{10,11... | collective-permute-start | bytes 4718600 | tf_op jit(solution)/shard_map/ppermute | solution.py:203
  16.1 26.2 %collective-permute-start.8 = (bf16[3072,256]{1,0:T(8,128)(2,1)}, bf16[3072,256]{1,0:T(8,128)(2,1)S(1)}, u32[]{:S(2)}, u32[]{:S(2)}) collective-permute-start(bf16[3072,256]{1,0:T(8,128)(2,1)} %constant_dynamic-update-slice_fusion.refs_5_), channel_id=1, source_target_pairs={{6,0},{9,1},{0,2},{11,3},{2,4},{13,5},{4,6},{15,7},{14,8},{17,9},{... | collective-permute-start | bytes 4718600 | tf_op jit(solution)/shard_map/ppermute | solution.py:194
  17.7 24.7 %collective-permute-start.2 = (bf16[3072,256]{1,0:T(8,128)(2,1)}, bf16[3072,256]{1,0:T(8,128)(2,1)S(1)}, u32[]{:S(2)}, u32[]{:S(2)}) collective-permute-start(bf16[3072,256]{1,0:T(8,128)(2,1)} %constant_dynamic-update-slice_fusion.refs_5_), channel_id=1, source_target_pairs={{2,0},{121,1},{4,2},{123,3},{6,4},{125,5},{0,6},{127,7},{10,8},{1,... | collective-permute-start | bytes 4718600 | tf_op jit(solution)/shard_map/ppermute | solution.py:194
  22.4 17.4 %collective-permute-start.6 = (bf16[1024,256]{1,0:T(8,128)(2,1)}, bf16[1024,256]{1,0:T(8,128)(2,1)}, u32[]{:S(2)}, u32[]{:S(2)}) collective-permute-start(bf16[1024,256]{1,0:T(8,128)(2,1)} %get-tuple-element.35.refs_4_), channel_id=1, source_target_pairs={{0,1},{1,0},{2,3},{3,2},{4,5},{5,4},{6,7},{7,6},{8,9},{9,8},{10,11... | collective-permute-start | bytes 1572872 | tf_op jit(solution)/shard_map/ppermute | solution.py:203
  45.4 12.4 %collective-permute-start.7 = (bf16[1536,256]{1,0:T(8,128)(2,1)}, bf16[1536,256]{1,0:T(8,128)(2,1)}, u32[]{:S(2)}, u32[]{:S(2)}) collective-permute-start(bf16[1536,256]{1,0:T(8,128)(2,1)} %shard_map.94), channel_id=1, source_target_pairs={{2,0},{121,1},{4,2},{123,3},{6,4},{125,5},{0,6},{127,7},{10,8},{1,... | collective-permute-start | bytes 2359304 | tf_op jit(solution)/shard_map/ppermute | solution.py:194
  47.0 15.9 %collective-permute-start.13 = (bf16[3072,256]{1,0:T(8,128)(2,1)S(1)}, bf16[3072,256]{1,0:T(8,128)(2,1)}, u32[]{:S(2)}, u32[]{:S(2)}) collective-permute-start(bf16[3072,256]{1,0:T(8,128)(2,1)S(1)} %collective-permute-done.8.refs_3_), channel_id=1, source_target_pairs={{0,1},{1,0},{2,3},{3,2},{4,5},{5,4},{6,7},{7,6},{8,9},{9,8},{10,11... | collective-permute-start | bytes 4718600 | tf_op jit(solution)/shard_map/ppermute | solution.py:203
  47.0 14.2 %collective-permute-start.9 = (bf16[1536,256]{1,0:T(8,128)(2,1)}, bf16[1536,256]{1,0:T(8,128)(2,1)}, u32[]{:S(2)}, u32[]{:S(2)}) collective-permute-start(bf16[1536,256]{1,0:T(8,128)(2,1)} %get-tuple-element.31), channel_id=1, source_target_pairs={{6,0},{9,1},{0,2},{11,3},{2,4},{13,5},{4,6},{15,7},{14,8},{17,9},{... | collective-permute-start | bytes 2359304 | tf_op jit(solution)/shard_map/ppermute | solution.py:194
  48.4 16.2 %collective-permute-start.12 = (bf16[3072,256]{1,0:T(8,128)(2,1)S(1)}, bf16[3072,256]{1,0:T(8,128)(2,1)}, u32[]{:S(2)}, u32[]{:S(2)}) collective-permute-start(bf16[3072,256]{1,0:T(8,128)(2,1)S(1)} %collective-permute-done.2.refs_2_), channel_id=1, source_target_pairs={{0,1},{1,0},{2,3},{3,2},{4,5},{5,4},{6,7},{7,6},{8,9},{9,8},{10,11... | collective-permute-start | bytes 4718600 | tf_op jit(solution)/shard_map/ppermute | solution.py:203
  57.7 5.7 %collective-permute-start.10 = (bf16[1536,256]{1,0:T(8,128)(2,1)}, bf16[1536,256]{1,0:T(8,128)(2,1)}, u32[]{:S(2)}, u32[]{:S(2)}) collective-permute-start(bf16[1536,256]{1,0:T(8,128)(2,1)} %collective-permute-done.7.refs_0_), channel_id=1, source_target_pairs={{0,1},{1,0},{2,3},{3,2},{4,5},{5,4},{6,7},{7,6},{8,9},{9,8},{10,11... | collective-permute-start | bytes 2359304 | tf_op jit(solution)/shard_map/ppermute | solution.py:203
  102.7 20.3 %collective-permute-start.16 = (bf16[48,256,128]{2,1,0:T(8,128)(2,1)}, bf16[48,256,128]{2,1,0:T(8,128)(2,1)}, u32[]{:S(2)}, u32[]{:S(2)}) collective-permute-start(bf16[48,256,128]{2,1,0:T(8,128)(2,1)} %shard_map.97), channel_id=1, source_target_pairs={{0,1},{1,0},{2,3},{3,2},{4,5},{5,4},{6,7},{7,6},{8,9},{9,8},{10,11... | collective-permute-start | bytes 9437192 | tf_op jit(solution)/shard_map/ppermute | solution.py:203
  102.8 18.6 %collective-permute-start.15 = (bf16[32,256,128]{2,1,0:T(8,128)(2,1)}, bf16[32,256,128]{2,1,0:T(8,128)(2,1)}, u32[]{:S(2)}, u32[]{:S(2)}) collective-permute-start(bf16[32,256,128]{2,1,0:T(8,128)(2,1)} %shard_map.96), channel_id=1, source_target_pairs={{0,1},{1,0},{2,3},{3,2},{4,5},{5,4},{6,7},{7,6},{8,9},{9,8},{10,11... | collective-permute-start | bytes 6291464 | tf_op jit(solution)/shard_map/ppermute | solution.py:203
  103.3 18.1 %collective-permute-start.17 = (bf16[12,256,128]{2,1,0:T(8,128)(2,1)S(1)}, bf16[12,256,128]{2,1,0:T(8,128)(2,1)S(1)}, u32[]{:S(2)}, u32[]{:S(2)}) collective-permute-start(bf16[12,256,128]{2,1,0:T(8,128)(2,1)S(1)} %get-tuple-element.29), channel_id=1, source_target_pairs={{0,2},{1,121},{2,4},{3,123},{4,6},{5,125},{6,0},{7,127},{8,10},{9,... | collective-permute-start | bytes 2359304 | tf_op jit(solution)/shard_map/ppermute | solution.py:194
  105.0 16.4 %collective-permute-start.21 = (bf16[12,256,128]{2,1,0:T(8,128)(2,1)S(1)}, bf16[12,256,128]{2,1,0:T(8,128)(2,1)S(1)}, u32[]{:S(2)}, u32[]{:S(2)}) collective-permute-start(bf16[12,256,128]{2,1,0:T(8,128)(2,1)S(1)} %get-tuple-element.30), channel_id=1, source_target_pairs={{0,6},{1,9},{2,0},{3,11},{4,2},{5,13},{6,4},{7,15},{8,14},{9,17},{... | collective-permute-start | bytes 2359304 | tf_op jit(solution)/shard_map/ppermute | solution.py:194
  111.8 6.8 %collective-permute-start.19 = (bf16[128,256]{1,0:T(8,128)(2,1)S(1)}, bf16[128,256]{1,0:T(8,128)(2,1)S(1)}, u32[]{:S(2)}, u32[]{:S(2)}) collective-permute-start(bf16[128,256]{1,0:T(8,128)(2,1)S(1)} %get-tuple-element.23), channel_id=1, source_target_pairs={{0,2},{1,3},{2,0},{3,1},{4,6},{5,7},{6,4},{7,5},{8,10},{9,11},{10,... | collective-permute-start | bytes 196616 | tf_op jit(solution)/shard_map/ppermute | solution.py:244
  119.2 12.6 %collective-permute-start.24 = (bf16[128,256]{1,0:T(8,128)(2,1)S(1)}, bf16[128,256]{1,0:T(8,128)(2,1)S(1)}, u32[]{:S(2)}, u32[]{:S(2)}) collective-permute-start(bf16[128,256]{1,0:T(8,128)(2,1)S(1)} %get-tuple-element.21), channel_id=1, source_target_pairs={{0,4},{1,5},{2,6},{3,7},{4,0},{5,1},{6,2},{7,3},{8,12},{9,13},{10,... | collective-permute-start | bytes 196616 | tf_op jit(solution)/shard_map/ppermute | solution.py:244
  127.0 27.5 %collective-permute-start.20 = (bf16[24,256,128]{2,1,0:T(8,128)(2,1)}, bf16[24,256,128]{2,1,0:T(8,128)(2,1)}, u32[]{:S(2)}, u32[]{:S(2)}) collective-permute-start(bf16[24,256,128]{2,1,0:T(8,128)(2,1)} %shard_map.99), channel_id=1, source_target_pairs={{0,2},{1,121},{2,4},{3,123},{4,6},{5,125},{6,0},{7,127},{8,10},{9,... | collective-permute-start | bytes 4718600 | tf_op jit(solution)/shard_map/ppermute | solution.py:194
  127.1 27.4 %collective-permute-start.22 = (bf16[24,256,128]{2,1,0:T(8,128)(2,1)}, bf16[24,256,128]{2,1,0:T(8,128)(2,1)}, u32[]{:S(2)}, u32[]{:S(2)}) collective-permute-start(bf16[24,256,128]{2,1,0:T(8,128)(2,1)} %get-tuple-element.28), channel_id=1, source_target_pairs={{0,6},{1,9},{2,0},{3,11},{4,2},{5,13},{6,4},{7,15},{8,14},{9,17},{... | collective-permute-start | bytes 4718600 | tf_op jit(solution)/shard_map/ppermute | solution.py:194
  140.7 6.5 %collective-permute-start.27 = (bf16[128,256]{1,0:T(8,128)(2,1)S(1)}, bf16[128,256]{1,0:T(8,128)(2,1)S(1)}, u32[]{:S(2)}, u32[]{:S(2)}) collective-permute-start(bf16[128,256]{1,0:T(8,128)(2,1)S(1)} %fusion.2), channel_id=1, source_target_pairs={{0,16},{8,24},{16,0},{24,8},{32,48},{40,56},{48,32},{56,40},{64,80... | collective-permute-start | bytes 196616 | tf_op jit(solution)/shard_map/ppermute | solution.py:244
  154.1 6.7 %collective-permute-start.31 = (bf16[128,256]{1,0:T(8,128)(2,1)S(1)}, bf16[128,256]{1,0:T(8,128)(2,1)S(1)}, u32[]{:S(2)}, u32[]{:S(2)}) collective-permute-start(bf16[128,256]{1,0:T(8,128)(2,1)S(1)} %get-tuple-element.19), channel_id=1, source_target_pairs={{0,64},{8,72},{16,80},{24,88},{32,96},{40,104},{48,112},{56,120},{... | collective-permute-start | bytes 196616 | tf_op jit(solution)/shard_map/ppermute | solution.py:244
  157.8 11.1 %collective-permute-start.29 = (bf16[8,256,128]{2,1,0:T(8,128)(2,1)}, bf16[8,256,128]{2,1,0:T(8,128)(2,1)S(1)}, u32[]{:S(2)}, u32[]{:S(2)}) collective-permute-start(bf16[8,256,128]{2,1,0:T(8,128)(2,1)} %shard_map.101), channel_id=1, source_target_pairs={{0,120},{1,3},{2,122},{3,5},{4,124},{5,7},{6,126},{7,1},{8,0},{9,1... | collective-permute-start | bytes 1572872 | tf_op jit(solution)/shard_map/ppermute | solution.py:194
  160.8 12.5 %collective-permute-start.30 = (bf16[8,256,128]{2,1,0:T(8,128)(2,1)S(1)}, bf16[8,256,128]{2,1,0:T(8,128)(2,1)S(1)}, u32[]{:S(2)}, u32[]{:S(2)}) collective-permute-start(bf16[8,256,128]{2,1,0:T(8,128)(2,1)S(1)} %get-tuple-element.26), channel_id=1, source_target_pairs={{0,8},{1,7},{2,10},{3,1},{4,12},{5,3},{6,14},{7,5},{8,16},{9,15},{... | collective-permute-start | bytes 1572872 | tf_op jit(solution)/shard_map/ppermute | solution.py:194
  160.9 7.3 %collective-permute-start.32 = (f32[128,256]{1,0:T(8,128)S(1)}, f32[128,256]{1,0:T(8,128)S(1)}, u32[]{:S(2)}, u32[]{:S(2)}) collective-permute-start(f32[128,256]{1,0:T(8,128)S(1)} %convert_add_fusion), channel_id=1, source_target_pairs={{0,1},{1,0},{2,3},{3,2},{4,5},{5,4},{6,7},{7,6},{8,9},{9,8},{10,11... | collective-permute-start | bytes 393224 | tf_op jit(solution)/shard_map/ppermute | solution.py:203
  (19 other events, 142.1 us)
